TPU v7x, 32 devices: a whole 2x2x4 slice. The times are simulated.
32 devices in a mesh: expert: 4 (over z), zero: 8 (over y, x, core).
Axes of the slice: x: 2, y: 2, z: 4, core: 2. Of those that a mesh axis runs over, the one named last changes fastest.
Arguments:
- tokens: bfloat16 [4096, 2048], P(('expert', 'zero')), may hold values from -6 to 6
- router_weight: bfloat16 [2048, 32], P('zero'), may hold values from -0.25 to 0.25
- expert_ids: int32 [4096, 8], P(('expert', 'zero')), may hold values from 0 to 31, all different within a row; in each aligned block of 128 rows (0 to 127, 128 to 255, ...) at most 40 rows name the same one
- gate_weight: bfloat16 [32, 2048, 768], P(('expert', 'zero')), may hold values from -0.125 to 0.125
- up_weight: bfloat16 [32, 2048, 768], P(('expert', 'zero')), may hold values from -0.125 to 0.125
- down_weight: bfloat16 [32, 768, 2048], P(('expert', 'zero')), may hold values from -0.21875 to 0.21875
Outputs:
- mixed: bfloat16 [4096, 2048], P(('expert', 'zero'))
Inputs may be any that keep to these rules, and one draw needn't show every extreme that they name: `expert_ids`: among the rows of one device no expert is named by more than 40 rows, a bound that some block reaches.
All inputs are finite; a program needn't handle non-finite values.
Results may differ from a plain program's by a relative error of at most 0.0057.
Values may be sent and summed in bfloat16 or wider, within the bound.
No kernel may reach another device: no remote copies, remote signals or barrier semaphores. Data moves between devices by JAX's collectives and lax.ppermute only.
A program may use at most 128 MiB of HBM per device.

v0:
```python
import jax
import jax.numpy as jnp
from jax import lax
from jax.sharding import PartitionSpec as P


def expert_rows(received, gate_weight, up_weight, down_weight):
    shape = received.shape
    rows = received.reshape(-1, shape[-1])
    gate = jnp.dot(rows, gate_weight[0], preferred_element_type=jnp.float32)
    upper = jnp.dot(rows, up_weight[0], preferred_element_type=jnp.float32)
    hidden = (jax.nn.silu(gate) * upper).astype(jnp.bfloat16)
    result = jnp.dot(hidden, down_weight[0], preferred_element_type=jnp.float32).astype(
        jnp.bfloat16
    )
    return result.reshape(shape)


def per_device(tokens, router_weight, expert_ids, gate_weight, up_weight, down_weight):
    tok_rows, width = tokens.shape
    topk = expert_ids.shape[1]
    n_expert = lax.axis_size("expert")
    n_zero = lax.axis_size("zero")
    experts = n_expert * n_zero
    capacity = 5 * tok_rows * topk // (4 * experts)
    logits = jnp.dot(
        tokens,
        lax.all_gather(router_weight, "zero", axis=0, tiled=True),
        preferred_element_type=jnp.float32,
    )
    chosen = jnp.take_along_axis(logits, expert_ids, axis=1)
    weights = jnp.exp(chosen)
    gates = weights / jnp.sum(weights, axis=1, keepdims=True)
    flat_ids = expert_ids.reshape(-1)
    onehot = (flat_ids[:, None] == jnp.arange(experts, dtype=jnp.int32)[None, :]).astype(jnp.int32)
    slot = jnp.sum(jnp.cumsum(onehot, axis=0) * onehot, axis=1) - 1
    position = flat_ids * capacity + slot
    token_num = jnp.arange(tok_rows * topk, dtype=jnp.int32) // topk
    outgoing = jnp.zeros((experts * capacity, width), jnp.bfloat16)
    outgoing = outgoing.at[position].set(tokens[token_num])
    buffer = outgoing.reshape(experts, capacity, width)
    computed = expert_rows(
        lax.all_to_all(buffer, ("expert", "zero"), split_axis=0, concat_axis=0, tiled=True),
        gate_weight,
        up_weight,
        down_weight,
    )
    returned = lax.all_to_all(computed, ("expert", "zero"), split_axis=0, concat_axis=0, tiled=True)
    flat_back = returned.reshape(experts * capacity, width)
    picked = flat_back[position].reshape(tok_rows, topk, width)
    total = jnp.zeros((tok_rows, width), jnp.float32)
    for k in range(topk):
        total = total + gates[:, k : k + 1] * picked[:, k, :].astype(jnp.float32)
    return total.astype(jnp.bfloat16)


def solution(mesh):
    in_specs = (
        P(("expert", "zero"), None),
        P("zero", None),
        P(("expert", "zero"), None),
        P(("expert", "zero"), None, None),
        P(("expert", "zero"), None, None),
        P(("expert", "zero"), None, None),
    )
    out_specs = P(("expert", "zero"), None)
    return jax.shard_map(
        per_device, mesh=mesh, in_specs=in_specs, out_specs=out_specs, check_vma=False
    )
```

profile of v0, /device:TPU:0, one launch (start us, length us, event | category | flops | bytes accessed | tf_op | source)
XLA Modules:
  0.0 334.4 jit_solution(15443680390478995123)
XLA Ops:
  0.0 0.0 copy-start
  0.0 0.9 copy.54
  0.9 0.1 eq.29
  1.0 0.1 eq.25
  1.1 0.7 broadcast_multiply_fusion
  1.8 9.0 %reduce-window.6 = s32[32,8,128]{2,1,0:T(8,128)S(1)} reduce-window(s32[32,8,128]{2,1,0:T(8,128)S(1)} %fusion.18, s32[]{:T(128)} %constant.40.clone.1), window={size=1x1x128 pad=0_0x0_0x127_0}, to_apply=%region_1.2 | reduce-window | flops 4161536 | bytes 262148 | tf_op jit(solution)/shard_map/reduce-window
  10.9 0.1 slice.78
  11.0 0.1 copy.56
  11.1 0.1 copy.57
  11.2 0.1 broadcast_add_fusion
  11.4 0.1 copy.53
  11.5 0.1 mul.110
  11.6 23.9 %scatter_custom_fusion = bf16[1280,2048]{1,0:T(8,128)(2,1)} fusion(s32[1024]{0:T(1024)S(1)} %bitcast.103, bf16[128,2048]{1,0:T(8,128)(2,1)} %param.6, s32[1024]{0:T(1024)S(1)} %broadcast_clamp_fusion.1, bf16[]{:T(256)} %constant.45.clone.1), kind=kCustom, calls=%fused_computation.5 | custom fusion | bytes 5243392 | tf_op jit(solution)/shard_map/scatter | solution.py:40
  35.5 123.4 %all_to_all.10 = bf16[32,40,2048]{2,1,0:T(8,128)(2,1)S(1)} all-to-all(bf16[32,40,2048]{2,1,0:T(8,128)(2,1)} %bitcast.97), channel_id=1, replica_groups=mesh['expert'=4,'zero'=8] {'expert','zero'}, dimensions={0} | all-to-all | bytes 10485760 | tf_op jit(solution)/shard_map/all_to_all | solution.py:43
  159.0 0.0 copy-done.3
  159.0 4.3 %fusion.5 = f32[1280,768]{1,0:T(8,128)S(1)} fusion(bf16[1280,2048]{1,0:T(8,128)(2,1)S(1)} %bitcast.99, bf16[1,2048,768]{2,1,0:T(8,128)(2,1)S(1)} %copy-done.3), kind=kOutput, calls=%fused_computation.11 | convolution fusion | flops 4026531840 | bytes 12320768 | tf_op jit(solution)/shard_map/dot_general | solution.py:10
  163.3 0.0 copy-done.4
  163.3 4.8 %fusion.2 = bf16[1280,768]{1,0:T(8,128)(2,1)S(1)} fusion(bf16[1280,2048]{1,0:T(8,128)(2,1)S(1)} %bitcast.100, f32[1280,768]{1,0:T(8,128)S(1)} %fusion.5, bf16[1,2048,768]{2,1,0:T(8,128)(2,1)S(1)} %copy-done.4), kind=kOutput, calls=%fused_computation.8 | convolution fusion | flops 4032430080 | bytes 14286848 | tf_op jit(solution)/shard_map/dot_general | solution.py:11
  168.1 0.0 copy-done
  168.1 6.1 %convolution_convert_fusion = bf16[1280,2048]{1,0:T(8,128)(2,1)} fusion(bf16[1280,768]{1,0:T(8,128)(2,1)S(1)} %fusion.2, bf16[1,768,2048]{2,1,0:T(8,128)(2,1)S(1)} %copy-done), kind=kOutput, calls=%fused_computation.4 | convolution fusion | flops 4029153280 | bytes 10354688 | tf_op jit(solution)/shard_map/dot_general | solution.py:13
  174.2 3.9 %all-to-all-start.1 = ((bf16[32,40,2048]{2,1,0:T(8,128)(2,1)}), bf16[32,40,2048]{2,1,0:T(8,128)(2,1)}, u32[]{:S(2)}, u32[]{:S(2)}) async-start(bf16[32,40,2048]{2,1,0:T(8,128)(2,1)} %bitcast.98), calls=%async_computation.1 | async-start | bytes 10485760 | tf_op jit(solution)/shard_map/all_to_all | solution.py:48
  178.1 0.0 copy-done.1
  178.1 0.1 copy.51
  178.2 0.1 reshape.166
  178.3 38.5 %all_gather.3 = bf16[2048,32]{0,1:T(8,128)(2,1)S(1)} all-gather(bf16[256,32]{0,1:T(8,128)(2,1)S(1)} %copy-done.2), channel_id=1, replica_groups=mesh['expert'=4,'zero'=8] {'zero'}, dimensions={0}, use_global_device_ids=true | all-gather | bytes 147456 | tf_op jit(solution)/shard_map/all_gather | solution.py:28
  216.8 1.3 fusion.21
  218.1 7.0 %gather_fusion.1 = f32[1024]{0:T(1024)S(1)} fusion(f32[128,32]{0,1:T(8,128)S(1)} %fusion.21, s32[1024]{0:T(1024)S(1)} %reshape.166), kind=kCustom, calls=%fused_computation.2 | custom fusion | bytes 16384 | tf_op jit(solution)/shard_map/jit(take_along_axis)/gather | solution.py:31
  225.1 0.1 reshape.169
  225.4 69.5 %all-to-all-done.1 = bf16[32,40,2048]{2,1,0:T(8,128)(2,1)} async-done(((bf16[32,40,2048]{2,1,0:T(8,128)(2,1)}), bf16[32,40,2048]{2,1,0:T(8,128)(2,1)}, u32[]{:S(2)}, u32[]{:S(2)}) %all-to-all-start.1) | async-done | bytes 5242912 | tf_op jit(solution)/shard_map/all_to_all | solution.py:48
  294.8 12.0 %gather_fusion = bf16[1024,2048]{1,0:T(8,128)(2,1)} fusion(bf16[1280,2048]{1,0:T(8,128)(2,1)} %bitcast.13, s32[1024]{0:T(1024)S(1)} %broadcast_clamp_fusion), kind=kCustom, calls=%fused_computation.1 | custom fusion | bytes 8392704 | tf_op jit(solution)/shard_map/gather | solution.py:50
  306.9 22.1 %fusion.20 = (bf16[128,1,2048]{2,1,0:T(2,128)(2,1)S(1)}, bf16[128,1,2048]{2,1,0:T(2,128)(2,1)S(1)}, bf16[128,1,2048]{2,1,0:T(2,128)(2,1)S(1)}, bf16[128,1,2048]{...) fusion(bf16[128,8,2048]{2,1,0:T(8,128)(2,1)} %bitcast.96), kind=kLoop, calls=%fused_computation.68 | loop fusion | bytes 8388608 | tf_op jit(solution)/shard_map/slice | solution.py:53
  329.0 5.4 %fusion.9 = bf16[128,2048]{1,0:T(8,128)(2,1)} fusion(bf16[128,1,2048]{2,1,0:T(2,128)(2,1)S(1)} %get-tuple-element.12, bf16[128,1,2048]{2,1,0:T(2,128)(2,1)S(1)} %get-tuple-element.6, bf16[128,1,2048]{2,1,0:T(2,128)(2,1)S(1)} %get-tuple-element.7, bf16[128,1,2048]{2,1,0:T(2,128)(2,1)S(1)} %get-tuple-element.8, bf16[128,1,2048]{2,1,0:T(2,128)(2,1)S(1)} %get-tuple-element.9, ...), kind=kLoop, calls=%fused_computation.16 | loop fusion | flops 6291456 | bytes 4722688 | tf_op jit(solution)/shard_map/convert_element_type | solution.py:54
  (19 shorter events, 0.2 us)
Async XLA Ops:
  0.0 168.1 %copy-start = (bf16[1,768,2048]{2,1,0:T(8,128)(2,1)S(1)}, bf16[1,768,2048]{2,1,0:T(8,128)(2,1)}, u32[]{:S(2)}) copy-start(bf16[1,768,2048]{2,1,0:T(8,128)(2,1)} %param.11) | copy-start | bytes 9437188
  35.5 123.4 %copy-start.3 = (bf16[1,2048,768]{2,1,0:T(8,128)(2,1)S(1)}, bf16[1,2048,768]{2,1,0:T(8,128)(2,1)}, u32[]{:S(2)}) copy-start(bf16[1,2048,768]{2,1,0:T(8,128)(2,1)} %param.9) | copy-start | bytes 9437188
  159.0 4.3 %copy-start.4 = (bf16[1,2048,768]{2,1,0:T(8,128)(2,1)S(1)}, bf16[1,2048,768]{2,1,0:T(8,128)(2,1)}, u32[]{:S(2)}) copy-start(bf16[1,2048,768]{2,1,0:T(8,128)(2,1)} %param.10) | copy-start | bytes 9437188
  174.2 3.9 %copy-start.1 = (s32[128,8]{0,1:T(8,128)S(1)}, s32[128,8]{0,1:T(8,128)}, u32[]{:S(2)}) copy-start(s32[128,8]{0,1:T(8,128)} %param.8) | copy-start | bytes 12292
  174.2 4.1 %copy-start.2 = (bf16[256,32]{0,1:T(8,128)(2,1)S(1)}, bf16[256,32]{0,1:T(8,128)(2,1)}, u32[]{:S(2)}) copy-start(bf16[256,32]{0,1:T(8,128)(2,1)} %param.7) | copy-start | bytes 49156
  174.2 120.6 %all-to-all-start.1 = ((bf16[32,40,2048]{2,1,0:T(8,128)(2,1)}), bf16[32,40,2048]{2,1,0:T(8,128)(2,1)}, u32[]{:S(2)}, u32[]{:S(2)}) async-start(bf16[32,40,2048]{2,1,0:T(8,128)(2,1)} %bitcast.98), calls=%async_computation.1 | async-start | bytes 10485760 | tf_op jit(solution)/shard_map/all_to_all | solution.py:48
where the time goes:
time: 335 us; the launch traced here: 334 us
  blocking collectives  162 us (48%)
  waiting for transfers between devices  69.5 us (21%)
  local copies, waits for them, and re-layouts  67.1 us (20%)
  matrix products  16.5 us (5%)
  other arithmetic  15.4 us (5%)
  starting transfers between devices  3.86 us (1%)
    all_to_all x1, blocking collectives, per_device(): lax.all_to_all(buffer, ('expert', 'zero'), split_axis=0, concat_axis=0, t...  123 us
    all_to_all x1, waiting for transfers between devices, per_device(): lax.all_to_all(computed, ('expert', 'zero'), split_axis=0, concat_axis=0,...  69.5 us
    all_gather x1, blocking collectives, per_device(): lax.all_gather(router_weight, 'zero', axis=0, tiled=True)  38.5 us
    scatter x1, local copies, waits for them, and re-layouts, per_device(): outgoing = outgoing.at[position].set(tokens[token_num])  23.9 us
    slice x1, local copies, waits for them, and re-layouts, per_device(): total = total + gates[:, k:k + 1] * picked[:, k, :].astype(jnp.float32)  22.1 us
    gather x1, local copies, waits for them, and re-layouts, per_device(): picked = flat_back[position].reshape(tok_rows, topk, width)  12 us
    another operation x3, other arithmetic  9.15 us
    gather x5, local copies, waits for them, and re-layouts, per_device(): chosen = jnp.take_along_axis(logits, expert_ids, axis=1)  7.36 us
  transfers between devices with their start and end apart: 1, of which 1 were waited for; matrix products, arithmetic and copies ran while one was open for 3% of the time, Pallas kernels for 0%

commit v1 on v0

v1 whole, which is shorter than its diff:
```python
import jax
import jax.numpy as jnp
from jax import lax
from jax.sharding import Mesh
from jax.sharding import PartitionSpec as P

CHUNKS = 2


def capacity_of(tok_rows, topk, experts):
    return 5 * tok_rows * topk // (4 * experts)


def slot_matrix(ids, expert, capacity):
    has = jnp.any(ids == expert, axis=2)
    rows = ids.shape[1]
    before = jnp.arange(rows)[:, None] < jnp.arange(rows)[None, :]
    slot = jnp.dot(
        has.astype(jnp.bfloat16), before.astype(jnp.bfloat16), preferred_element_type=jnp.float32
    ).astype(jnp.int32)
    pick = (slot[:, None, :] == jnp.arange(capacity, dtype=jnp.int32)[None, :, None]) & has[:, None, :]
    return pick


def per_device(tokens, router_weight, expert_ids, gate_weight, up_weight, down_weight):
    tok_rows, width = tokens.shape
    topk = expert_ids.shape[1]
    chips = lax.axis_size("expert") * lax.axis_size("chip")
    cores = lax.axis_size("core")
    experts = chips * cores
    capacity = capacity_of(tok_rows, topk, experts)
    me = (lax.axis_index("expert") * lax.axis_size("chip") + lax.axis_index("chip")) * cores + lax.axis_index("core")
    other = me + 1 - 2 * lax.axis_index("core")
    swap = [(i, cores - 1 - i) for i in range(cores)]

    ids = lax.all_gather(expert_ids, ("expert", "chip"), axis=0, tiled=False)
    router = lax.all_gather(router_weight, ("chip", "core"), axis=0, tiled=True)
    logits = jnp.dot(tokens, router, preferred_element_type=jnp.float32)
    onehot = expert_ids[:, :, None] == jnp.arange(experts, dtype=jnp.int32)[None, None, :]
    chosen = jnp.sum(jnp.where(onehot, logits[:, None, :], 0.0), axis=2)
    weights = jnp.exp(chosen)
    gates = weights / jnp.sum(weights, axis=1, keepdims=True)
    all_gates = lax.all_gather(gates, ("expert", "chip"), axis=0, tiled=False)

    pick_me = slot_matrix(ids, me, capacity)
    pick_other = slot_matrix(ids, other, capacity)

    def gate_rows(expert):
        return jnp.sum(jnp.where(ids == expert, all_gates, 0.0), axis=2)

    picks = jnp.concatenate([pick_me, pick_other], axis=1).astype(jnp.bfloat16)

    step = width // CHUNKS
    gate = up = None
    for c in range(CHUNKS):
        cols = slice(c * step, (c + 1) * step)
        part = lax.all_gather(tokens[:, cols], ("expert", "chip"), axis=0, tiled=False)
        rows = jnp.einsum("bst,btd->bsd", picks, part, preferred_element_type=jnp.float32).astype(jnp.bfloat16)
        mine = rows[:, :capacity]
        theirs = lax.ppermute(rows[:, capacity:], "core", swap)
        x = jnp.concatenate([mine, theirs], axis=0).reshape(2 * chips * capacity, step)
        g = jnp.dot(x, gate_weight[0, cols], preferred_element_type=jnp.float32)
        u = jnp.dot(x, up_weight[0, cols], preferred_element_type=jnp.float32)
        gate = g if gate is None else gate + g
        up = u if up is None else up + u
    hidden = (jax.nn.silu(gate) * up).astype(jnp.bfloat16)

    scale_me = gate_rows(me)[:, None, :] * pick_me
    scale_other = gate_rows(other)[:, None, :] * pick_other
    mix = jnp.concatenate([scale_me, scale_other], axis=1).astype(jnp.bfloat16)
    outs = []
    for c in range(CHUNKS):
        cols = slice(c * step, (c + 1) * step)
        y = jnp.dot(hidden, down_weight[0][:, cols], preferred_element_type=jnp.float32).astype(jnp.bfloat16)
        y = y.reshape(2, chips, capacity, step)
        back = lax.ppermute(y[1], "core", swap)
        both = jnp.concatenate([y[0], back], axis=1)
        partial = jnp.einsum("bst,bsd->btd", mix, both, preferred_element_type=jnp.float32).astype(jnp.bfloat16)
        outs.append(
            lax.psum_scatter(partial, ("expert", "chip"), scatter_dimension=0, tiled=False)
        )
    return jnp.concatenate(outs, axis=1)


def solution(mesh):
    n_expert, n_zero = mesh.devices.shape
    inner = Mesh(mesh.devices.reshape(n_expert, n_zero // 2, 2), ("expert", "chip", "core"))
    everything = ("expert", "chip", "core")
    in_specs = (
        P(everything, None),
        P(("chip", "core"), None),
        P(everything, None),
        P(everything, None, None),
        P(everything, None, None),
        P(everything, None, None),
    )
    return jax.shard_map(
        per_device, mesh=inner, in_specs=in_specs, out_specs=P(everything, None), check_vma=False
    )
```

time: 335 us -> 392 us (1.17)
  waiting for transfers between devices: 69.5 us -> 248 us
  blocking collectives: 162 us -> 88 us
  local copies, waits for them, and re-layouts: 67.1 us -> 5.28 us
  matrix products: 16.5 us -> 30.1 us
  between operations: 0.19 us -> 13.4 us
  other arithmetic: 15.4 us -> 5.01 us
    reduce_scatter x0 -> x2, waiting for transfers between devices: none -> 179 us  [per_device(): lax.psum_scatter(partial, ('expert', 'chip'), scatter_dimension=0, tiled=...]
    all_to_all x1 -> x0, blocking collectives: 123 us -> none  [per_device(): lax.all_to_all(buffer, ('expert', 'zero'), split_axis=0, concat_axis=0, t...]
    all_to_all x1 -> x0, waiting for transfers between devices: 69.5 us -> none  [per_device(): lax.all_to_all(computed, ('expert', 'zero'), split_axis=0, concat_axis=0,...]
    all_gather x0 -> x2, waiting for transfers between devices: none -> 64 us  [per_device(): lax.all_gather(tokens[:, cols], ('expert', 'chip'), axis=0, tiled=False)]
    all_gather x1 -> x3, blocking collectives: 38.5 us -> 88 us  [the longest x1 40.8 us: per_device(): ids = lax.all_gather(expert_ids, ('expert', 'chip'), axis=0, tiled=False)]
    scatter x1 -> x0, local copies, waits for them, and re-layouts: 23.9 us -> none  [per_device(): outgoing = outgoing.at[position].set(tokens[token_num])]
    slice x3 -> x5, local copies, waits for them, and re-layouts: 22.3 us -> 2.87 us  [the longest x1 1.87 us: per_device(): tokens[:, cols]]
    gather x6 -> x0, local copies, waits for them, and re-layouts: 19.4 us -> none  [the longest x1 12 us: per_device(): picked = flat_back[position].reshape(tok_rows, topk, width)]
  transfers between devices with their start and end apart: 1 -> 8, of which waited for: 1 -> 5; matrix products, arithmetic and copies ran while one was open for 3% -> 5% of each run, Pallas kernels for 0% -> 0%
where the time goes in v1:
time: 392 us; the launch traced here: 391 us
  waiting for transfers between devices  248 us (63%)
  blocking collectives  88 us (22%)
  matrix products  30.1 us (8%)
  between operations  13.4 us (3%)
  local copies, waits for them, and re-layouts  5.28 us (1%)
  other arithmetic  5.01 us (1%)
    reduce_scatter x2, waiting for transfers between devices, per_device(): lax.psum_scatter(partial, ('expert', 'chip'), scatter_dimension=0, tiled=...  179 us
    all_gather x2, waiting for transfers between devices, per_device(): lax.all_gather(tokens[:, cols], ('expert', 'chip'), axis=0, tiled=False)  64 us
    all_gather x1, blocking collectives, per_device(): ids = lax.all_gather(expert_ids, ('expert', 'chip'), axis=0, tiled=False)  40.8 us
    all_gather x1, blocking collectives, per_device(): all_gates = lax.all_gather(gates, ('expert', 'chip'), axis=0, tiled=False)  36.3 us
    all_gather x1, blocking collectives, per_device(): router = lax.all_gather(router_weight, ('chip', 'core'), axis=0, tiled=True)  10.9 us
  transfers between devices with their start and end apart: 8, of which 5 were waited for; matrix products, arithmetic and copies ran while one was open for 5% of the time, Pallas kernels for 0%

profile of v1, /device:TPU:0, one launch (start us, length us, event | category | flops | bytes accessed | tf_op | source)
XLA Modules:
  0.0 391.5 jit_solution(5477251595179238912)
XLA Ops:
  6.5 1.9 fusion.31
  8.5 0.7 all-gather.8.cloned.1.call-update
  9.2 10.9 %all_gather.27 = bf16[2048,32]{0,1:T(8,128)(2,1)S(1)} all-gather(bf16[256,32]{0,1:T(8,128)(2,1)} %param.7), channel_id=1, replica_groups=mesh['expert'=4,'chip'=4,'core'=2] {'chip','core'}, dimensions={0}, use_global_device_ids=true | all-gather | bytes 147456 | tf_op jit(solution)/shard_map/all_gather | solution.py:37
  20.2 40.8 %all-gather = s32[2048,8]{0,1:T(8,128)S(1)} all-gather(s32[128,8]{0,1:T(8,128)} %param.8), channel_id=2, replica_groups=mesh['expert'=4,'chip'=4,'core'=2] {'expert','chip'}, dimensions={0}, use_global_device_ids=true | all-gather | bytes 69632 | tf_op jit(solution)/shard_map/all_gather | solution.py:36
  60.9 1.4 fusion.32
  62.3 0.7 select_reduce_fusion
  63.1 36.3 %all_gather.28 = f32[16,128,8]{1,2,0:T(8,128)S(1)} all-gather(f32[1,128,8]{1,2,0:T(8,128)S(1)} %bitcast_divide_fusion), channel_id=1, replica_groups=mesh['expert'=4,'chip'=4,'core'=2] {'expert','chip'}, dimensions={0}, use_global_device_ids=true | all-gather | bytes 69632 | tf_op jit(solution)/shard_map/all_gather | solution.py:43
  100.0 3.1 convolution_convert_fusion.5
  103.1 0.3 fusion.29
  103.5 64.0 %all-gather.8.cloned.1.call-done = bf16[2048,1024]{1,0:T(8,128)(2,1)} async-done(((bf16[128,1024]{1,0:T(8,128)(2,1)}), bf16[2048,1024]{1,0:T(8,128)(2,1)}) %all-gather.8.cloned.1.call-update) | async-done | bytes 4194320 | tf_op jit(solution)/shard_map/all_gather | solution.py:57
  167.5 3.0 convolution_convert_fusion.4
  170.5 0.3 fusion.30
  170.9 1.7 pad_maximum_fusion
  172.6 0.6 copy-done
  173.1 2.2 fusion.13
  175.6 2.2 fusion.11
  177.9 2.2 fusion.8
  180.1 3.0 multiply_convert_fusion
  183.1 2.4 convolution_convert_fusion.1
  185.6 0.2 fusion.27
  185.8 0.6 collective-permute-start.2
  186.6 2.5 collective-permute-done.2
  189.0 3.2 convolution_convert_fusion.3
  192.3 1.8 copy-done.3
  194.1 3.7 convolution_convert_fusion
  197.9 0.2 fusion.28
  198.1 0.4 collective-permute-start.3
  198.6 2.7 collective-permute-done.3
  201.2 3.3 convolution_convert_fusion.2
  204.5 81.6 %reduce-scatter.3.cloned.1.call-done = bf16[1,128,1024]{2,1,0:T(8,128)(2,1)} async-done(((bf16[16,128,1024]{2,1,0:T(8,128)(2,1)}), bf16[1,128,1024]{2,1,0:T(8,128)(2,1)}) %reduce-scatter.3.cloned.1.call-update) | async-done | bytes 262160 | tf_op jit(solution)/shard_map/reduce_scatter | solution.py:80
  286.2 96.9 %reduce-scatter.5.cloned.1.call-done = bf16[1,128,1024]{2,1,0:T(8,128)(2,1)} async-done(((bf16[16,128,1024]{2,1,0:T(8,128)(2,1)}), bf16[1,128,1024]{2,1,0:T(8,128)(2,1)}) %reduce-scatter.5.cloned.1.call-update) | async-done | bytes 262160 | tf_op jit(solution)/shard_map/reduce_scatter | solution.py:80
  383.1 1.9 pad_maximum_fusion.2
  (30 shorter events, 1.4 us)
Async XLA Ops:
  6.5 93.5 %all-gather.6.cloned.1.call-start = ((), (), s32[]{:S(2)}) async-start(), calls=%async_computation.4 | async-start | bytes 4456448 | tf_op jit(solution)/shard_map/all_gather | solution.py:57
  8.4 159.0 %all-gather.8.cloned.1.call-start = ((), (), s32[]{:S(2)}) async-start(), calls=%async_computation.5 | async-start | bytes 4456448 | tf_op jit(solution)/shard_map/all_gather | solution.py:57
  9.2 277.0 %reduce-scatter.3.cloned.1.call-start = ((), (), s32[]{:S(2)}) async-start(), calls=%async_computation.2 | async-start | bytes 4456448 | tf_op jit(solution)/shard_map/reduce_scatter | solution.py:80
  103.4 67.5 %collective-permute-start = (bf16[16,40,1024]{2,1,0:T(8,128)(2,1)S(1)}, bf16[16,40,1024]{2,1,0:T(8,128)(2,1)}, u32[]{:S(2)}, u32[]{:S(2)}) collective-permute-start(bf16[16,40,1024]{2,1,0:T(8,128)(2,1)S(1)} %get-tuple-element.14), channel_id=1, source_target_pairs={{0,1},{1,0},{2,3},{3,2},{4,5},{5,4},{6,7},{7,6},{8,9},{9,8},{10,11... | collective-permute-start | bytes 3932168 | tf_op jit(solution)/shard_map/ppermute | solution.py:60
  170.8 4.6 %collective-permute-start.1 = (bf16[16,40,1024]{2,1,0:T(8,128)(2,1)S(1)}, bf16[16,40,1024]{2,1,0:T(8,128)(2,1)S(1)}, u32[]{:S(2)}, u32[]{:S(2)}) collective-permute-start(bf16[16,40,1024]{2,1,0:T(8,128)(2,1)S(1)} %get-tuple-element.16), channel_id=1, source_target_pairs={{0,1},{1,0},{2,3},{3,2},{4,5},{5,4},{6,7},{7,6},{8,9},{9,8},{10,11... | collective-permute-start | bytes 3932168 | tf_op jit(solution)/shard_map/ppermute | solution.py:60
  170.9 2.3 copy-start
  175.6 2.2 copy-start.1
  180.1 3.0 copy-start.2
  183.1 2.5 copy-start.4
  185.8 3.2 collective-permute-start.2
  192.2 1.9 copy-start.3
  192.3 190.8 %reduce-scatter.5.cloned.1.call-start = ((), (), s32[]{:S(2)}) async-start(), calls=%async_computation.3 | async-start | bytes 4456448 | tf_op jit(solution)/shard_map/reduce_scatter | solution.py:80
  198.1 3.1 collective-permute-start.3
Sparse Core Ops, SparseCore 0:
  10.1 79.7 all-gather.5
  92.6 74.7 all-gather.7
  192.4 93.7 reduce-scatter.2
  288.3 94.7 reduce-scatter.4

commit v2 on v0

v2 whole, which is shorter than its diff:
```python
import jax
import jax.numpy as jnp
from jax import lax
from jax.sharding import PartitionSpec as P

BF16 = jnp.bfloat16
F32 = jnp.float32


def expert_rows(rows, gate_weight, up_weight, down_weight):
    gate = jnp.dot(rows, gate_weight, preferred_element_type=F32)
    upper = jnp.dot(rows, up_weight, preferred_element_type=F32)
    hidden = (jax.nn.silu(gate) * upper).astype(BF16)
    return jnp.dot(hidden, down_weight, preferred_element_type=F32).astype(BF16)


def per_device(tokens, router_weight, expert_ids, gate_weight, up_weight, down_weight):
    tok_rows, width = tokens.shape
    topk = expert_ids.shape[1]
    layers = lax.axis_size("expert")
    near = lax.axis_size("zero")
    experts = layers * near
    capacity = 5 * tok_rows * topk // (4 * experts)
    layer = lax.axis_index("expert")
    mine = layer * near + jnp.arange(near, dtype=jnp.int32)
    before = (jnp.arange(tok_rows)[None, :] < jnp.arange(tok_rows)[:, None]).astype(BF16)

    def along(array, d):
        return lax.ppermute(array, "expert", [(i, (i + d) % layers) for i in range(layers)])

    order = list(range(1, layers))
    order.sort(key=lambda d: min(d, layers - d))
    blocks, ids = {0: tokens}, {0: expert_ids}
    for d in order:
        ids[d] = along(expert_ids, d)
    for d in order:
        blocks[d] = along(tokens, d)

    def pick_of(block_ids):
        has = jnp.any(block_ids[:, :, None] == mine[None, None, :], axis=1)
        slot = jnp.dot(before, has.astype(BF16), preferred_element_type=F32)
        slot = jnp.where(has, slot, -1.0).T
        return slot[:, None, :] == jnp.arange(capacity, dtype=F32)[None, :, None]

    def exchange(slabs):
        return lax.all_to_all(slabs, "zero", split_axis=0, concat_axis=0, tiled=True)

    extra = -(-router_weight.size // width)
    extra_pad = -(-extra // 8) * 8
    ride = jnp.pad(router_weight.reshape(extra, width), ((0, extra_pad - extra), (0, 0)))

    picks, received = {}, {}
    for d in [0] + order:
        picks[d] = pick_of(ids[d])
        slabs = jnp.einsum("zst,td->zsd", picks[d].astype(BF16), blocks[d], preferred_element_type=F32).astype(BF16)
        if d == 0:
            slabs = jnp.concatenate([slabs, jnp.broadcast_to(ride[None], (near, extra_pad, width))], axis=1)
        received[d] = exchange(slabs)
    router = received[0][:, capacity : capacity + extra].reshape(width, experts)
    received[0] = received[0][:, :capacity]

    total = None
    for d in order + [0]:
        logits = jnp.dot(blocks[d], router, preferred_element_type=F32)
        chosen = jnp.any(ids[d][:, :, None] == jnp.arange(experts, dtype=jnp.int32)[None, None, :], axis=1)
        weights = jnp.where(chosen, jnp.exp(jnp.where(chosen, logits, 0.0)), 0.0)
        gates = weights / jnp.sum(weights, axis=1, keepdims=True)
        gates = lax.dynamic_slice_in_dim(gates, layer * near, near, axis=1).T
        mix = (picks[d] * gates[:, None, :]).astype(BF16)

        rows = received[d].reshape(near * capacity, width)
        result = expert_rows(rows, gate_weight[0], up_weight[0], down_weight[0])
        back = exchange(result.reshape(near, capacity, width))
        partial = jnp.einsum("zst,zsd->td", mix, back, preferred_element_type=F32)
        if d:
            partial = along(partial.astype(BF16), (layers - d) % layers).astype(F32)
        total = partial if total is None else total + partial
    return total.astype(BF16)


def solution(mesh):
    everything = ("expert", "zero")
    in_specs = (
        P(everything, None),
        P("zero", None),
        P(everything, None),
        P(everything, None, None),
        P(everything, None, None),
        P(everything, None, None),
    )
    return jax.shard_map(
        per_device, mesh=mesh, in_specs=in_specs, out_specs=P(everything, None), check_vma=False
    )
```

time: 335 us -> 237 us (0.71)
  blocking collectives: 162 us -> 0 us
  local copies, waits for them, and re-layouts: 67.1 us -> 6.41 us
  matrix products: 16.5 us -> 67.1 us
  waiting for transfers between devices: 69.5 us -> 113 us
  starting transfers between devices: 3.86 us -> 46.6 us
  other arithmetic: 15.4 us -> 2.17 us
    all_to_all x1 -> x0, blocking collectives: 123 us -> none  [per_device(): lax.all_to_all(buffer, ('expert', 'zero'), split_axis=0, concat_axis=0, t...]
    ppermute x0 -> x9, waiting for transfers between devices: none -> 78.7 us  [along(): lax.ppermute(array, 'expert', [(i, (i + d) % layers) for i in range(layer...]
    dot_general x4 -> x24, matrix products: 16.5 us -> 67.1 us  [the longest x4 24.8 us: expert_rows(): return jnp.dot(hidden, down_weight, preferred_element_type=F32).astype(BF16)]
    all_gather x1 -> x0, blocking collectives: 38.5 us -> none  [per_device(): lax.all_gather(router_weight, 'zero', axis=0, tiled=True)]
    all_to_all x1 -> x8, waiting for transfers between devices: 69.5 us -> 34.5 us  [exchange(): lax.all_to_all(slabs, 'zero', split_axis=0, concat_axis=0, tiled=True)]
    all_to_all x1 -> x8, starting transfers between devices: 3.86 us -> 34.3 us  [exchange(): lax.all_to_all(slabs, 'zero', split_axis=0, concat_axis=0, tiled=True)]
    scatter x1 -> x0, local copies, waits for them, and re-layouts: 23.9 us -> none  [per_device(): outgoing = outgoing.at[position].set(tokens[token_num])]
    slice x3 -> x2, local copies, waits for them, and re-layouts: 22.3 us -> 2.44 us  [the longest x1 1.46 us: per_device(): received[0] = received[0][:, :capacity]]
  transfers between devices with their start and end apart: 1 -> 17, of which waited for: 1 -> 14; matrix products, arithmetic and copies ran while one was open for 3% -> 28% of each run, Pallas kernels for 0% -> 0%
where the time goes in v2:
time: 237 us; the launch traced here: 236 us
  waiting for transfers between devices  113 us (48%)
  matrix products  67.1 us (28%)
  starting transfers between devices  46.6 us (20%)
  local copies, waits for them, and re-layouts  6.41 us (3%)
    ppermute x9, waiting for transfers between devices, along(): lax.ppermute(array, 'expert', [(i, (i + d) % layers) for i in range(layer...  78.7 us
    all_to_all x8, waiting for transfers between devices, exchange(): lax.all_to_all(slabs, 'zero', split_axis=0, concat_axis=0, tiled=True)  34.5 us
    all_to_all x8, starting transfers between devices, exchange(): lax.all_to_all(slabs, 'zero', split_axis=0, concat_axis=0, tiled=True)  34.3 us
    dot_general x4, matrix products, expert_rows(): return jnp.dot(hidden, down_weight, preferred_element_type=F32).astype(BF16)  24.8 us
    dot_general x4, matrix products, expert_rows(): gate = jnp.dot(rows, gate_weight, preferred_element_type=F32)  17.6 us
    ppermute x9, starting transfers between devices, along(): lax.ppermute(array, 'expert', [(i, (i + d) % layers) for i in range(layer...  12.3 us
    dot_general x4, matrix products, per_device(): partial = jnp.einsum('zst,zsd->td', mix, back, preferred_element_type=F32)  11 us
    dot_general x4, matrix products, per_device(): jnp.einsum('zst,td->zsd', picks[d].astype(BF16), blocks[d], preferred_ele...  8.38 us
  transfers between devices with their start and end apart: 17, of which 14 were waited for; matrix products, arithmetic and copies ran while one was open for 28% of the time, Pallas kernels for 0%

profile of v2, /device:TPU:0, one launch (start us, length us, event | category | flops | bytes accessed | tf_op | source)
XLA Modules:
  0.0 235.8 jit_solution(7616704417064143352)
XLA Ops:
  0.0 3.0 %collective-permute-start = (s32[128,8]{0,1:T(8,128)}, s32[128,8]{0,1:T(8,128)S(1)}, u32[]{:S(2)}, u32[]{:S(2)}) collective-permute-start(s32[128,8]{0,1:T(8,128)} %param.8), channel_id=1, source_target_pairs={{0,8},{8,16},{16,24},{24,0},{1,9},{9,17},{17,25},{25,1},{2,10},{10... | collective-permute-start | bytes 12296 | tf_op jit(solution)/shard_map/ppermute | solution.py:29
  7.1 2.8 %collective-permute-done.6 = s32[128,8]{0,1:T(8,128)S(1)} collective-permute-done((s32[128,8]{0,1:T(8,128)}, s32[128,8]{0,1:T(8,128)S(1)}, u32[]{:S(2)}, u32[]{:S(2)}) %collective-permute-start.6) | collective-permute-done | bytes 4128 | tf_op jit(solution)/shard_map/ppermute | solution.py:29
  13.6 4.3 %all-to-all-start = ((bf16[8,48,2048]{2,1,0:T(8,128)(2,1)}), bf16[8,48,2048]{2,1,0:T(8,128)(2,1)}, u32[]{:S(2)}, u32[]{:S(2)}) async-start(bf16[8,48,2048]{2,1,0:T(8,128)(2,1)} %pad_maximum_fusion), calls=%async_computation | async-start | bytes 3145728 | tf_op jit(solution)/shard_map/all_to_all | solution.py:46
  18.1 16.0 %collective-permute-done.1 = bf16[128,2048]{1,0:T(8,128)(2,1)S(1)} collective-permute-done((bf16[128,2048]{1,0:T(8,128)(2,1)}, bf16[128,2048]{1,0:T(8,128)(2,1)S(1)}, u32[]{:S(2)}, u32[]{:S(2)}) %collective-permute-start.1) | collective-permute-done | bytes 524320 | tf_op jit(solution)/shard_map/ppermute | solution.py:29
  38.9 4.3 %all-to-all-start.1 = ((bf16[8,40,2048]{2,1,0:T(8,128)(2,1)}), bf16[8,40,2048]{2,1,0:T(8,128)(2,1)}, u32[]{:S(2)}, u32[]{:S(2)}) async-start(bf16[8,40,2048]{2,1,0:T(8,128)(2,1)} %convolution_convert_fusion.2), calls=%async_computation.1 | async-start | bytes 2621440 | tf_op jit(solution)/shard_map/all_to_all | solution.py:46
  45.4 13.4 %collective-permute-done.4 = bf16[128,2048]{1,0:T(8,128)(2,1)} collective-permute-done((bf16[128,2048]{1,0:T(8,128)(2,1)}, bf16[128,2048]{1,0:T(8,128)(2,1)}, u32[]{:S(2)}, u32[]{:S(2)}) %collective-permute-start.4) | collective-permute-done | bytes 524320 | tf_op jit(solution)/shard_map/ppermute | solution.py:29
  61.4 4.3 %all-to-all-start.3 = ((bf16[8,40,2048]{2,1,0:T(8,128)(2,1)}), bf16[8,40,2048]{2,1,0:T(8,128)(2,1)}, u32[]{:S(2)}, u32[]{:S(2)}) async-start(bf16[8,40,2048]{2,1,0:T(8,128)(2,1)} %convolution_convert_fusion.1), calls=%async_computation.3 | async-start | bytes 2621440 | tf_op jit(solution)/shard_map/all_to_all | solution.py:46
  65.9 13.7 %collective-permute-done.7 = bf16[128,2048]{1,0:T(8,128)(2,1)} collective-permute-done((bf16[128,2048]{1,0:T(8,128)(2,1)}, bf16[128,2048]{1,0:T(8,128)(2,1)}, u32[]{:S(2)}, u32[]{:S(2)}) %collective-permute-start.7) | collective-permute-done | bytes 524320 | tf_op jit(solution)/shard_map/ppermute | solution.py:29
  79.6 2.6 %convolution_convert_fusion = bf16[8,40,2048]{2,1,0:T(8,128)(2,1)} fusion(bf16[128,2048]{1,0:T(8,128)(2,1)} %collective-permute-done.7, f32[8,128]{1,0:T(8,128)S(1)} %bitcast_select_fusion), kind=kOutput, calls=%fused_computation.24 | convolution fusion | flops 168468480 | bytes 1839104 | tf_op jit(solution)/shard_map/zst,td->zsd/dot_general | solution.py:55
  87.3 4.3 %all-to-all-start.5 = ((bf16[8,40,2048]{2,1,0:T(8,128)(2,1)}), bf16[8,40,2048]{2,1,0:T(8,128)(2,1)}, u32[]{:S(2)}, u32[]{:S(2)}) async-start(bf16[8,40,2048]{2,1,0:T(8,128)(2,1)} %convolution_convert_fusion), calls=%async_computation.5 | async-start | bytes 2621440 | tf_op jit(solution)/shard_map/all_to_all | solution.py:46
  93.1 4.5 %fusion.22 = f32[320,768]{1,0:T(8,128)} fusion(bf16[320,2048]{1,0:T(8,128)(2,1)} %bitcast.6, bf16[1,2048,768]{2,1,0:T(8,128)(2,1)} %param.9), kind=kOutput, calls=%fused_computation.22 | convolution fusion | flops 1006632960 | bytes 5439488 | tf_op jit(solution)/shard_map/dot_general | solution.py:11
  97.6 6.2 %fusion.24 = bf16[320,2048]{1,0:T(8,128)(2,1)} fusion(bf16[1,768,2048]{2,1,0:T(8,128)(2,1)S(1)} %copy-done, bf16[320,2048]{1,0:T(8,128)(2,1)} %bitcast.6, bf16[1,2048,768]{2,1,0:T(8,128)(2,1)} %param.10, f32[320,768]{1,0:T(8,128)} %fusion.22), kind=kOutput, calls=%fused_computation.28 | convolution fusion | flops 2015395840 | bytes 9895936 | tf_op jit(solution)/shard_map/dot_general | solution.py:14
  103.8 6.0 %all-to-all-done.5 = bf16[8,40,2048]{2,1,0:T(8,128)(2,1)} async-done(((bf16[8,40,2048]{2,1,0:T(8,128)(2,1)}), bf16[8,40,2048]{2,1,0:T(8,128)(2,1)}, u32[]{:S(2)}, u32[]{:S(2)}) %all-to-all-start.5) | async-done | bytes 1310752 | tf_op jit(solution)/shard_map/all_to_all | solution.py:46
  109.8 4.3 %all-to-all-start.2 = ((bf16[8,40,2048]{2,1,0:T(8,128)(2,1)}), bf16[8,40,2048]{2,1,0:T(8,128)(2,1)}, u32[]{:S(2)}, u32[]{:S(2)}) async-start(bf16[8,40,2048]{2,1,0:T(8,128)(2,1)} %bitcast.169), calls=%async_computation.2 | async-start | bytes 2621440 | tf_op jit(solution)/shard_map/all_to_all | solution.py:46
  114.1 4.5 %fusion.20 = f32[320,768]{1,0:T(8,128)} fusion(bf16[320,2048]{1,0:T(8,128)(2,1)} %bitcast.16, bf16[1,2048,768]{2,1,0:T(8,128)(2,1)} %param.9), kind=kOutput, calls=%fused_computation.20 | convolution fusion | flops 1006632960 | bytes 5439488 | tf_op jit(solution)/shard_map/dot_general | solution.py:11
  118.6 6.2 %fusion.27 = bf16[320,2048]{1,0:T(8,128)(2,1)} fusion(bf16[1,768,2048]{2,1,0:T(8,128)(2,1)S(1)} %copy-done, bf16[320,2048]{1,0:T(8,128)(2,1)} %bitcast.16, bf16[1,2048,768]{2,1,0:T(8,128)(2,1)} %param.10, f32[320,768]{1,0:T(8,128)} %fusion.20), kind=kOutput, calls=%fused_computation.29 | convolution fusion | flops 2015395840 | bytes 9895936 | tf_op jit(solution)/shard_map/dot_general | solution.py:14
  124.8 7.5 %all-to-all-done.2 = bf16[8,40,2048]{2,1,0:T(8,128)(2,1)} async-done(((bf16[8,40,2048]{2,1,0:T(8,128)(2,1)}), bf16[8,40,2048]{2,1,0:T(8,128)(2,1)}, u32[]{:S(2)}, u32[]{:S(2)}) %all-to-all-start.2) | async-done | bytes 1310752 | tf_op jit(solution)/shard_map/all_to_all | solution.py:46
  132.3 4.5 %all-to-all-start.4 = ((bf16[8,40,2048]{2,1,0:T(8,128)(2,1)}), bf16[8,40,2048]{2,1,0:T(8,128)(2,1)}, u32[]{:S(2)}, u32[]{:S(2)}) async-start(bf16[8,40,2048]{2,1,0:T(8,128)(2,1)} %bitcast.170), calls=%async_computation.4 | async-start | bytes 2621440 | tf_op jit(solution)/shard_map/all_to_all | solution.py:46
  136.8 4.5 %fusion.18 = f32[320,768]{1,0:T(8,128)} fusion(bf16[320,2048]{1,0:T(8,128)(2,1)} %bitcast.23, bf16[1,2048,768]{2,1,0:T(8,128)(2,1)} %param.9), kind=kOutput, calls=%fused_computation.18 | convolution fusion | flops 1006632960 | bytes 5439488 | tf_op jit(solution)/shard_map/dot_general | solution.py:11
  141.3 6.2 %fusion.30 = bf16[320,2048]{1,0:T(8,128)(2,1)} fusion(bf16[1,768,2048]{2,1,0:T(8,128)(2,1)S(1)} %copy-done, bf16[320,2048]{1,0:T(8,128)(2,1)} %bitcast.23, bf16[1,2048,768]{2,1,0:T(8,128)(2,1)} %param.10, f32[320,768]{1,0:T(8,128)} %fusion.18), kind=kOutput, calls=%fused_computation.30 | convolution fusion | flops 2015395840 | bytes 9895936 | tf_op jit(solution)/shard_map/dot_general | solution.py:14
  147.5 7.3 %all-to-all-done.4 = bf16[8,40,2048]{2,1,0:T(8,128)(2,1)} async-done(((bf16[8,40,2048]{2,1,0:T(8,128)(2,1)}), bf16[8,40,2048]{2,1,0:T(8,128)(2,1)}, u32[]{:S(2)}, u32[]{:S(2)}) %all-to-all-start.4) | async-done | bytes 1310752 | tf_op jit(solution)/shard_map/all_to_all | solution.py:46
  154.8 4.3 %all-to-all-start.6 = ((bf16[8,40,2048]{2,1,0:T(8,128)(2,1)}), bf16[8,40,2048]{2,1,0:T(8,128)(2,1)}, u32[]{:S(2)}, u32[]{:S(2)}) async-start(bf16[8,40,2048]{2,1,0:T(8,128)(2,1)} %bitcast.168), calls=%async_computation.6 | async-start | bytes 2621440 | tf_op jit(solution)/shard_map/all_to_all | solution.py:46
  161.7 4.1 %fusion.16 = f32[320,768]{1,0:T(8,128)} fusion(bf16[320,2048]{1,0:T(8,128)(2,1)S(1)} %bitcast.171, bf16[1,2048,768]{2,1,0:T(8,128)(2,1)} %param.9), kind=kOutput, calls=%fused_computation.16 | convolution fusion | flops 1006632960 | bytes 5439488 | tf_op jit(solution)/shard_map/dot_general | solution.py:11
  165.8 6.2 %fusion.33 = bf16[320,2048]{1,0:T(8,128)(2,1)} fusion(bf16[1,768,2048]{2,1,0:T(8,128)(2,1)S(1)} %copy-done, bf16[320,2048]{1,0:T(8,128)(2,1)} %bitcast.172, bf16[1,2048,768]{2,1,0:T(8,128)(2,1)} %param.10, f32[320,768]{1,0:T(8,128)} %fusion.16), kind=kOutput, calls=%fused_computation.31 | convolution fusion | flops 2015395840 | bytes 9895936 | tf_op jit(solution)/shard_map/dot_general | solution.py:14
  172.0 5.3 %all-to-all-done.6 = bf16[8,40,2048]{2,1,0:T(8,128)(2,1)} async-done(((bf16[8,40,2048]{2,1,0:T(8,128)(2,1)}), bf16[8,40,2048]{2,1,0:T(8,128)(2,1)}, u32[]{:S(2)}, u32[]{:S(2)}) %all-to-all-start.6) | async-done | bytes 1310752 | tf_op jit(solution)/shard_map/all_to_all | solution.py:46
  177.3 4.3 %all-to-all-start.7 = ((bf16[8,40,2048]{2,1,0:T(8,128)(2,1)}), bf16[8,40,2048]{2,1,0:T(8,128)(2,1)}, u32[]{:S(2)}, u32[]{:S(2)}) async-start(bf16[8,40,2048]{2,1,0:T(8,128)(2,1)} %bitcast.167), calls=%async_computation.7 | async-start | bytes 2621440 | tf_op jit(solution)/shard_map/all_to_all | solution.py:46
  184.2 3.7 %collective-permute-start.2 = (bf16[128,2048]{1,0:T(8,128)(2,1)}, bf16[128,2048]{1,0:T(8,128)(2,1)}, u32[]{:S(2)}, u32[]{:S(2)}) collective-permute-start(bf16[128,2048]{1,0:T(8,128)(2,1)} %fusion.36), channel_id=1, source_target_pairs={{0,24},{8,0},{16,8},{24,16},{1,25},{9,1},{17,9},{25,17},{2,26},{10... | collective-permute-start | bytes 1572872 | tf_op jit(solution)/shard_map/ppermute | solution.py:29
  190.5 2.7 %fusion.38 = bf16[128,2048]{1,0:T(8,128)(2,1)} fusion(bf16[8,40,2048]{2,1,0:T(8,128)(2,1)} %all-to-all-done.6, bf16[8,128]{1,0:T(8,128)(2,1)S(1)} %fusion.115, f32[8,128]{1,0:T(8,128)S(1)} %bitcast_select_fusion), kind=kOutput, calls=%fused_computation.38 | convolution fusion | flops 168116224 | bytes 1841152 | tf_op jit(solution)/shard_map/zst,zsd->td/dot_general | solution.py:74
  194.0 5.8 %all-to-all-done.7 = bf16[8,40,2048]{2,1,0:T(8,128)(2,1)} async-done(((bf16[8,40,2048]{2,1,0:T(8,128)(2,1)}), bf16[8,40,2048]{2,1,0:T(8,128)(2,1)}, u32[]{:S(2)}, u32[]{:S(2)}) %all-to-all-start.7) | async-done | bytes 1310752 | tf_op jit(solution)/shard_map/all_to_all | solution.py:46
  200.5 11.8 %collective-permute-done.5 = bf16[128,2048]{1,0:T(8,128)(2,1)} collective-permute-done((bf16[128,2048]{1,0:T(8,128)(2,1)}, bf16[128,2048]{1,0:T(8,128)(2,1)}, u32[]{:S(2)}, u32[]{:S(2)}) %collective-permute-start.5) | collective-permute-done | bytes 524320 | tf_op jit(solution)/shard_map/ppermute | solution.py:29
  212.3 20.4 %collective-permute-done.8 = bf16[128,2048]{1,0:T(8,128)(2,1)} collective-permute-done((bf16[128,2048]{1,0:T(8,128)(2,1)}, bf16[128,2048]{1,0:T(8,128)(2,1)}, u32[]{:S(2)}, u32[]{:S(2)}) %collective-permute-start.8) | collective-permute-done | bytes 524320 | tf_op jit(solution)/shard_map/ppermute | solution.py:29
  232.7 3.0 %add_convert_fusion = bf16[128,2048]{1,0:T(8,128)(2,1)} fusion(bf16[128,2048]{1,0:T(8,128)(2,1)} %collective-permute-done.8, bf16[128,2048]{1,0:T(8,128)(2,1)} %collective-permute-done.5, bf16[128,2048]{1,0:T(8,128)(2,1)} %collective-permute-done.2, bf16[8,40,2048]{2,1,0:T(8,128)(2,1)} %all-to-all-done.7, bf16[8,128]{1,0:T(8,128)(2,1)S(1)} %fusion.114, ...), kind=kOutput, calls=%fused_computation.65 | convolution fusion | flops 169689088 | bytes 3414016 | tf_op jit(solution)/shard_map/zst,zsd->td/dot_general | solution.py:74
  (56 shorter events, 33.7 us)
Async XLA Ops:
  0.0 97.6 %copy-start = (bf16[1,768,2048]{2,1,0:T(8,128)(2,1)S(1)}, bf16[1,768,2048]{2,1,0:T(8,128)(2,1)}, u32[]{:S(2)}) copy-start(bf16[1,768,2048]{2,1,0:T(8,128)(2,1)} %param.11) | copy-start | bytes 9437188
  0.0 7.0 %collective-permute-start = (s32[128,8]{0,1:T(8,128)}, s32[128,8]{0,1:T(8,128)S(1)}, u32[]{:S(2)}, u32[]{:S(2)}) collective-permute-start(s32[128,8]{0,1:T(8,128)} %param.8), channel_id=1, source_target_pairs={{0,8},{8,16},{16,24},{24,0},{1,9},{9,17},{17,25},{25,1},{2,10},{10... | collective-permute-start | bytes 12296 | tf_op jit(solution)/shard_map/ppermute | solution.py:29
  3.0 4.0 %collective-permute-start.3 = (s32[128,8]{0,1:T(8,128)}, s32[128,8]{0,1:T(8,128)S(1)}, u32[]{:S(2)}, u32[]{:S(2)}) collective-permute-start(s32[128,8]{0,1:T(8,128)} %param.8), channel_id=1, source_target_pairs={{0,24},{8,0},{16,8},{24,16},{1,25},{9,1},{17,9},{25,17},{2,26},{10... | collective-permute-start | bytes 12296 | tf_op jit(solution)/shard_map/ppermute | solution.py:29
  5.1 4.7 %collective-permute-start.6 = (s32[128,8]{0,1:T(8,128)}, s32[128,8]{0,1:T(8,128)S(1)}, u32[]{:S(2)}, u32[]{:S(2)}) collective-permute-start(s32[128,8]{0,1:T(8,128)} %param.8), channel_id=1, source_target_pairs={{0,16},{8,24},{16,0},{24,8},{1,17},{9,25},{17,1},{25,9},{2,18},{10... | collective-permute-start | bytes 12296 | tf_op jit(solution)/shard_map/ppermute | solution.py:29
  13.6 25.3 %all-to-all-start = ((bf16[8,48,2048]{2,1,0:T(8,128)(2,1)}), bf16[8,48,2048]{2,1,0:T(8,128)(2,1)}, u32[]{:S(2)}, u32[]{:S(2)}) async-start(bf16[8,48,2048]{2,1,0:T(8,128)(2,1)} %pad_maximum_fusion), calls=%async_computation | async-start | bytes 3145728 | tf_op jit(solution)/shard_map/all_to_all | solution.py:46
  17.9 16.2 %collective-permute-start.1 = (bf16[128,2048]{1,0:T(8,128)(2,1)}, bf16[128,2048]{1,0:T(8,128)(2,1)S(1)}, u32[]{:S(2)}, u32[]{:S(2)}) collective-permute-start(bf16[128,2048]{1,0:T(8,128)(2,1)} %param.6), channel_id=1, source_target_pairs={{0,8},{8,16},{16,24},{24,0},{1,9},{9,17},{17,25},{25,1},{2,10},{10... | collective-permute-start | bytes 1572872 | tf_op jit(solution)/shard_map/ppermute | solution.py:29
  34.1 0.8 copy-start.3
  38.9 22.5 %all-to-all-start.1 = ((bf16[8,40,2048]{2,1,0:T(8,128)(2,1)}), bf16[8,40,2048]{2,1,0:T(8,128)(2,1)}, u32[]{:S(2)}, u32[]{:S(2)}) async-start(bf16[8,40,2048]{2,1,0:T(8,128)(2,1)} %convolution_convert_fusion.2), calls=%async_computation.1 | async-start | bytes 2621440 | tf_op jit(solution)/shard_map/all_to_all | solution.py:46
  43.2 15.5 %collective-permute-start.4 = (bf16[128,2048]{1,0:T(8,128)(2,1)}, bf16[128,2048]{1,0:T(8,128)(2,1)}, u32[]{:S(2)}, u32[]{:S(2)}) collective-permute-start(bf16[128,2048]{1,0:T(8,128)(2,1)} %param.6), channel_id=1, source_target_pairs={{0,24},{8,0},{16,8},{24,16},{1,25},{9,1},{17,9},{25,17},{2,26},{10... | collective-permute-start | bytes 1572872 | tf_op jit(solution)/shard_map/ppermute | solution.py:29
  45.2 34.4 %collective-permute-start.7 = (bf16[128,2048]{1,0:T(8,128)(2,1)}, bf16[128,2048]{1,0:T(8,128)(2,1)}, u32[]{:S(2)}, u32[]{:S(2)}) collective-permute-start(bf16[128,2048]{1,0:T(8,128)(2,1)} %param.6), channel_id=1, source_target_pairs={{0,16},{8,24},{16,0},{24,8},{1,17},{9,25},{17,1},{25,9},{2,18},{10... | collective-permute-start | bytes 1572872 | tf_op jit(solution)/shard_map/ppermute | solution.py:29
  61.4 25.9 %all-to-all-start.3 = ((bf16[8,40,2048]{2,1,0:T(8,128)(2,1)}), bf16[8,40,2048]{2,1,0:T(8,128)(2,1)}, u32[]{:S(2)}, u32[]{:S(2)}) async-start(bf16[8,40,2048]{2,1,0:T(8,128)(2,1)} %convolution_convert_fusion.1), calls=%async_computation.3 | async-start | bytes 2621440 | tf_op jit(solution)/shard_map/all_to_all | solution.py:46
  87.3 22.5 %all-to-all-start.5 = ((bf16[8,40,2048]{2,1,0:T(8,128)(2,1)}), bf16[8,40,2048]{2,1,0:T(8,128)(2,1)}, u32[]{:S(2)}, u32[]{:S(2)}) async-start(bf16[8,40,2048]{2,1,0:T(8,128)(2,1)} %convolution_convert_fusion), calls=%async_computation.5 | async-start | bytes 2621440 | tf_op jit(solution)/shard_map/all_to_all | solution.py:46
  109.8 22.5 %all-to-all-start.2 = ((bf16[8,40,2048]{2,1,0:T(8,128)(2,1)}), bf16[8,40,2048]{2,1,0:T(8,128)(2,1)}, u32[]{:S(2)}, u32[]{:S(2)}) async-start(bf16[8,40,2048]{2,1,0:T(8,128)(2,1)} %bitcast.169), calls=%async_computation.2 | async-start | bytes 2621440 | tf_op jit(solution)/shard_map/all_to_all | solution.py:46
  132.3 22.5 %all-to-all-start.4 = ((bf16[8,40,2048]{2,1,0:T(8,128)(2,1)}), bf16[8,40,2048]{2,1,0:T(8,128)(2,1)}, u32[]{:S(2)}, u32[]{:S(2)}) async-start(bf16[8,40,2048]{2,1,0:T(8,128)(2,1)} %bitcast.170), calls=%async_computation.4 | async-start | bytes 2621440 | tf_op jit(solution)/shard_map/all_to_all | solution.py:46
  154.8 22.5 %all-to-all-start.6 = ((bf16[8,40,2048]{2,1,0:T(8,128)(2,1)}), bf16[8,40,2048]{2,1,0:T(8,128)(2,1)}, u32[]{:S(2)}, u32[]{:S(2)}) async-start(bf16[8,40,2048]{2,1,0:T(8,128)(2,1)} %bitcast.168), calls=%async_computation.6 | async-start | bytes 2621440 | tf_op jit(solution)/shard_map/all_to_all | solution.py:46
  160.6 1.1 copy-start.4
  177.3 22.5 %all-to-all-start.7 = ((bf16[8,40,2048]{2,1,0:T(8,128)(2,1)}), bf16[8,40,2048]{2,1,0:T(8,128)(2,1)}, u32[]{:S(2)}, u32[]{:S(2)}) async-start(bf16[8,40,2048]{2,1,0:T(8,128)(2,1)} %bitcast.167), calls=%async_computation.7 | async-start | bytes 2621440 | tf_op jit(solution)/shard_map/all_to_all | solution.py:46
  184.2 16.3 %collective-permute-start.2 = (bf16[128,2048]{1,0:T(8,128)(2,1)}, bf16[128,2048]{1,0:T(8,128)(2,1)}, u32[]{:S(2)}, u32[]{:S(2)}) collective-permute-start(bf16[128,2048]{1,0:T(8,128)(2,1)} %fusion.36), channel_id=1, source_target_pairs={{0,24},{8,0},{16,8},{24,16},{1,25},{9,1},{17,9},{25,17},{2,26},{10... | collective-permute-start | bytes 1572872 | tf_op jit(solution)/shard_map/ppermute | solution.py:29
  190.5 3.2 %copy-start.5 = (s32[128,8]{0,1:T(8,128)S(1)}, s32[128,8]{0,1:T(8,128)}, u32[]{:S(2)}) copy-start(s32[128,8]{0,1:T(8,128)} %param.8) | copy-start | bytes 12292
  190.5 3.2 %copy-start.1 = (bf16[2048,32]{1,0:T(8,128)(2,1)S(1)}, bf16[2048,32]{1,0:T(8,128)(2,1)}, u32[]{:S(2)}) copy-start(bf16[2048,32]{1,0:T(8,128)(2,1)} %reshape.52) | copy-start | bytes 393220
  190.5 3.2 %copy-start.2 = (bf16[128,2048]{1,0:T(8,128)(2,1)S(1)}, bf16[128,2048]{1,0:T(8,128)(2,1)}, u32[]{:S(2)}) copy-start(bf16[128,2048]{1,0:T(8,128)(2,1)} %param.6) | copy-start | bytes 1572868
  190.5 21.8 %collective-permute-start.5 = (bf16[128,2048]{1,0:T(8,128)(2,1)}, bf16[128,2048]{1,0:T(8,128)(2,1)}, u32[]{:S(2)}, u32[]{:S(2)}) collective-permute-start(bf16[128,2048]{1,0:T(8,128)(2,1)} %fusion.37), channel_id=1, source_target_pairs={{0,8},{8,16},{16,24},{24,0},{1,9},{9,17},{17,25},{25,1},{2,10},{10... | collective-permute-start | bytes 1572872 | tf_op jit(solution)/shard_map/ppermute | solution.py:29
  193.2 39.5 %collective-permute-start.8 = (bf16[128,2048]{1,0:T(8,128)(2,1)}, bf16[128,2048]{1,0:T(8,128)(2,1)}, u32[]{:S(2)}, u32[]{:S(2)}) collective-permute-start(bf16[128,2048]{1,0:T(8,128)(2,1)} %fusion.38), channel_id=1, source_target_pairs={{0,16},{8,24},{16,0},{24,8},{1,17},{9,25},{17,1},{25,9},{2,18},{10... | collective-permute-start | bytes 1572872 | tf_op jit(solution)/shard_map/ppermute | solution.py:29

commit v3 on v2

v3 whole, which is shorter than its diff:
```python
import functools

import jax
import jax.numpy as jnp
from jax import lax
from jax.experimental import pallas as pl
from jax.experimental.pallas import tpu as pltpu
from jax.sharding import PartitionSpec as P

BF16 = jnp.bfloat16
F32 = jnp.float32
VMEM_LIMIT = 40 * 1024 * 1024
STEPS = 4


def small_cost():
    return pl.CostEstimate(flops=1000, bytes_accessed=1000, transcendentals=0)


def params():
    return pltpu.CompilerParams(vmem_limit_bytes=VMEM_LIMIT)


def round_up(n, m):
    return -(-n // m) * m


def near_expert(near, offset):
    return lax.axis_index("expert") * near + lax.bitwise_xor(lax.axis_index("zero"), offset)


def slot_rows(ids_t, near, cap, cap_pad):
    toks = ids_t.shape[1]
    has = jnp.concatenate(
        [
            jnp.max((ids_t == near_expert(near, o)).astype(F32), axis=0, keepdims=True)
            for o in range(near)
        ],
        axis=0,
    )
    earlier = (
        lax.broadcasted_iota(jnp.int32, (toks, toks), 0)
        < lax.broadcasted_iota(jnp.int32, (toks, toks), 1)
    ).astype(F32).astype(BF16)
    slot = jnp.dot(has.astype(BF16), earlier, preferred_element_type=F32)
    slot = jnp.where(has > 0, slot, -1.0)
    row = lax.broadcasted_iota(jnp.int32, (cap_pad, toks), 0).astype(F32)
    return [jnp.where(row == slot[o : o + 1, :], 1.0, 0.0) for o in range(near)]


def pick_kernel(near, cap, cap_pad, ride, tokens_ref, ids_ref, *refs):
    if ride:
        router_ref, outs = refs[0], refs[1:]
    else:
        outs = refs
    picks = jnp.concatenate(slot_rows(ids_ref[...], near, cap, cap_pad), axis=0).astype(BF16)
    width = tokens_ref.shape[1]
    part = width // STEPS
    for c in range(STEPS):
        cols = slice(c * part, (c + 1) * part)
        rows = jnp.dot(picks, tokens_ref[:, cols], preferred_element_type=F32)
        for o in range(near):
            outs[o][0:cap_pad, cols] = rows[o * cap_pad : (o + 1) * cap_pad].astype(BF16)
    if ride:
        experts, depth = router_ref.shape
        per_row = width // depth
        for g in range(experts // 8):
            r, q = g // per_row, g % per_row
            piece = router_ref[8 * g : 8 * g + 8, :]
            for o in range(near):
                outs[o][cap_pad + 8 * r : cap_pad + 8 * r + 8, q * depth : (q + 1) * depth] = piece


def pick_rows(tokens, ids_t, near, cap, cap_pad, router_t=None):
    width = tokens.shape[1]
    extra = 0
    args = [tokens, ids_t]
    if router_t is not None:
        extra = round_up(router_t.shape[0] // 8 * router_t.shape[1], width) // width * 8
        args.append(router_t)
    vmem = pl.BlockSpec(memory_space=pltpu.VMEM)
    return pl.pallas_call(
        functools.partial(pick_kernel, near, cap, cap_pad, router_t is not None),
        out_shape=[jax.ShapeDtypeStruct((cap_pad + extra, width), BF16)] * near,
        in_specs=[vmem] * len(args),
        out_specs=[vmem] * near,
        compiler_params=params(),
        cost_estimate=small_cost(),
    )(*args)


def expert_kernel(near, rows_each, *refs):
    xs = refs[:near]
    gate_ref, up_ref, down_ref = refs[near : near + 3]
    outs = refs[near + 3 : 2 * near + 3]
    gate_sum, up_sum, hidden = refs[2 * near + 3 :]
    step = pl.program_id(0)

    @pl.when(step < STEPS)
    def _():
        x = jnp.concatenate([r[0:rows_each, :].astype(F32) for r in xs], axis=0).astype(BF16)
        gate = jnp.dot(x, gate_ref[...], preferred_element_type=F32)
        upper = jnp.dot(x, up_ref[...], preferred_element_type=F32)

        @pl.when(step == 0)
        def _():
            gate_sum[...] = gate
            up_sum[...] = upper

        @pl.when((step > 0) & (step < STEPS - 1))
        def _():
            gate_sum[...] += gate
            up_sum[...] += upper

        @pl.when(step == STEPS - 1)
        def _():
            v = gate_sum[...] + gate
            hidden[...] = (v / (1.0 + jnp.exp(-v)) * (up_sum[...] + upper)).astype(BF16)

    @pl.when(step >= STEPS)
    def _():
        y = jnp.dot(hidden[...], down_ref[...], preferred_element_type=F32)
        for o in range(near):
            outs[o][...] = y[o * rows_each : (o + 1) * rows_each].astype(BF16)


def run_expert(xs, gate_weight, up_weight, down_weight, rows_each):
    near = len(xs)
    width, ff = gate_weight.shape
    part = width // STEPS
    first = lambda i: jnp.minimum(i, STEPS - 1)
    second = lambda i: jnp.maximum(i - STEPS, 0)
    return pl.pallas_call(
        functools.partial(expert_kernel, near, rows_each),
        grid=(2 * STEPS,),
        out_shape=[jax.ShapeDtypeStruct((rows_each, width), BF16)] * near,
        in_specs=[pl.BlockSpec((x.shape[0], part), lambda i: (0, first(i))) for x in xs]
        + [pl.BlockSpec((part, ff), lambda i: (first(i), 0))] * 2
        + [pl.BlockSpec((ff, part), lambda i: (0, second(i)))],
        out_specs=[pl.BlockSpec((rows_each, part), lambda i: (0, second(i)))] * near,
        scratch_shapes=[
            pltpu.VMEM((near * rows_each, ff), F32),
            pltpu.VMEM((near * rows_each, ff), F32),
            pltpu.VMEM((near * rows_each, ff), BF16),
        ],
        compiler_params=params(),
        cost_estimate=small_cost(),
    )(*xs, gate_weight, up_weight, down_weight)


def mix_kernel(near, cap, cap_pad, depth, experts, tokens_ref, ids_ref, *refs):
    riders, backs, out = refs[:near], refs[near : 2 * near], refs[2 * near]
    ids_t = ids_ref[...]
    topk, toks = ids_t.shape
    width = tokens_ref.shape[1]
    per_row = width // depth
    logits = None
    for o in range(near):
        start = pl.multiple_of(lax.bitwise_xor(lax.axis_index("zero"), o) * depth, depth)
        pieces = []
        for g in range(experts // 8):
            r, q = g // per_row, g % per_row
            pieces.append(
                riders[o][cap_pad + 8 * r : cap_pad + 8 * r + 8, q * depth : (q + 1) * depth].astype(F32)
            )
        router_t = jnp.concatenate(pieces, axis=0).astype(BF16)
        term = lax.dot_general(
            router_t, tokens_ref[:, pl.ds(start, depth)], (((1,), (1,)), ((), ())), preferred_element_type=F32
        )
        logits = term if logits is None else logits + term
    number = lax.broadcasted_iota(jnp.int32, (experts, toks), 0)
    chosen = number == ids_t[0:1, :]
    for k in range(1, topk):
        chosen = chosen | (number == ids_t[k : k + 1, :])
    weights = jnp.where(chosen, jnp.exp(jnp.where(chosen, logits, 0.0)), 0.0)
    gates = weights / jnp.sum(weights, axis=0, keepdims=True)
    picks = slot_rows(ids_t, near, cap, cap_pad)
    mix = []
    for o in range(near):
        gate = jnp.sum(jnp.where(number == near_expert(near, o), gates, 0.0), axis=0, keepdims=True)
        mix.append(picks[o] * gate)
    mix = jnp.concatenate(mix, axis=0).astype(BF16)
    part = width // STEPS
    for c in range(STEPS):
        cols = slice(c * part, (c + 1) * part)
        y = jnp.concatenate([b[:, cols].astype(F32) for b in backs], axis=0).astype(BF16)
        out[:, cols] = lax.dot_general(
            mix, y, (((0,), (0,)), ((), ())), preferred_element_type=F32
        ).astype(BF16)


def mix_rows(tokens, ids_t, riders, backs, cap, cap_pad, depth, experts):
    near = len(backs)
    vmem = pl.BlockSpec(memory_space=pltpu.VMEM)
    return pl.pallas_call(
        functools.partial(mix_kernel, near, cap, cap_pad, depth, experts),
        out_shape=jax.ShapeDtypeStruct(tokens.shape, BF16),
        in_specs=[vmem] * (2 + 2 * near),
        out_specs=vmem,
        compiler_params=params(),
        cost_estimate=small_cost(),
    )(tokens, ids_t, *riders, *backs)


def per_device(tokens, router_weight, expert_ids, gate_weight, up_weight, down_weight):
    tok_rows, width = tokens.shape
    topk = expert_ids.shape[1]
    layers = lax.axis_size("expert")
    near = lax.axis_size("zero")
    experts = layers * near
    cap = 5 * tok_rows * topk // (4 * experts)
    cap_pad = round_up(cap, 8)
    depth = router_weight.shape[0]

    def along(array, d):
        return lax.ppermute(array, "expert", [(i, (i + d) % layers) for i in range(layers)])

    def across(array, o):
        return lax.ppermute(array, "zero", [(i, i ^ o) for i in range(near)]) if o else array

    order = sorted(range(1, layers), key=lambda d: -min(d, layers - d))
    blocks, ids = {0: tokens}, {0: expert_ids.T}
    for d in order:
        ids[d] = along(ids[0], d)
    source = tokens
    for d in order:
        blocks[d] = along(source, d)
        source, _ = lax.optimization_barrier((tokens, blocks[d]))

    received, results, partial = {}, {}, {}
    for d in [0] + order:
        router_t = None if d else router_weight.T
        slabs = pick_rows(blocks[d], ids[d], near, cap, cap_pad, router_t)
        received[d] = [across(s, o) for o, s in enumerate(slabs)]
    for d in [0] + order:
        results[d] = run_expert(received[d], gate_weight[0], up_weight[0], down_weight[0], cap_pad)
    for d in order + [0]:
        backs = [across(r, o) for o, r in enumerate(results[d])]
        mixed = mix_rows(blocks[d], ids[d], received[0], backs, cap, cap_pad, depth, experts)
        partial[d] = along(mixed, layers - d) if d else mixed
    total = partial[0].astype(F32)
    for d in order:
        total = total + partial[d].astype(F32)
    return total.astype(BF16)


def solution(mesh):
    everything = ("expert", "zero")
    in_specs = (
        P(everything, None),
        P("zero", None),
        P(everything, None),
        P(everything, None, None),
        P(everything, None, None),
        P(everything, None, None),
    )
    return jax.shard_map(
        per_device, mesh=mesh, in_specs=in_specs, out_specs=P(everything, None), check_vma=False
    )
```

time: 237 us -> 222 us (0.937)
  the two profiles are of different devices: /device:TPU:0 before, /device:TPU:8 now
where the time goes in v3:
time: 222 us; the launch traced here: 221 us
  waiting for transfers between devices  104 us (47%)
  starting transfers between devices  75.6 us (34%)
  Pallas kernels  31.8 us (14%)
  local copies, waits for them, and re-layouts  8.16 us (4%)
    ppermute x56, starting transfers between devices, across(): lax.ppermute(array, 'zero', [(i, i ^ o) for i in range(near)])  57.2 us
    ppermute x56, waiting for transfers between devices, across(): lax.ppermute(array, 'zero', [(i, i ^ o) for i in range(near)])  55.5 us
    ppermute x9, waiting for transfers between devices, along(): lax.ppermute(array, 'expert', [(i, (i + d) % layers) for i in range(layer...  48.9 us
    pallas_call x4, Pallas kernels, run_expert(): pl.pallas_call(functools.partial(expert_kernel, near, rows_each), grid=(2...  25.4 us
    ppermute x9, starting transfers between devices, along(): lax.ppermute(array, 'expert', [(i, (i + d) % layers) for i in range(layer...  18.5 us
    unnamed x18, local copies, waits for them, and re-layouts  8.16 us
  transfers between devices with their start and end apart: 65, of which 23 were waited for; matrix products, arithmetic and copies ran while one was open for 0% of the time, Pallas kernels for 14%

profile of v3, /device:TPU:8, one launch (start us, length us, event | category | flops | bytes accessed | tf_op | source)
XLA Modules:
  0.0 221.4 jit_solution(15639497938626405993)
XLA Ops:
  0.0 2.6 %collective-permute-start.14 = (bf16[128,2048]{1,0:T(8,128)(2,1)}, bf16[128,2048]{1,0:T(8,128)(2,1)S(1)}, u32[]{:S(2)}, u32[]{:S(2)}) collective-permute-start(bf16[128,2048]{1,0:T(8,128)(2,1)} %tokens_ref.3), channel_id=1, source_target_pairs={{0,16},{8,24},{16,0},{24,8},{1,17},{9,25},{17,1},{25,9},{2,18},{10... | collective-permute-start | bytes 1572872 | tf_op jit(solution)/shard_map/ppermute | solution.py:216
  2.6 22.6 %collective-permute-done.14.tokens_ref = bf16[128,2048]{1,0:T(8,128)(2,1)S(1)} collective-permute-done((bf16[128,2048]{1,0:T(8,128)(2,1)}, bf16[128,2048]{1,0:T(8,128)(2,1)S(1)}, u32[]{:S(2)}, u32[]{:S(2)}) %collective-permute-start.14) | collective-permute-done | bytes 524320 | tf_op jit(solution)/shard_map/ppermute | solution.py:216
  30.3 2.0 collective-permute-start.49
  32.3 4.1 %collective-permute-done.49.ids_ref = s32[8,128]{1,0:T(8,128)S(1)} collective-permute-done((s32[8,128]{1,0:T(8,128)}, s32[8,128]{1,0:T(8,128)S(1)}, u32[]{:S(2)}, u32[]{:S(2)}) %collective-permute-start.49) | collective-permute-done | bytes 4128 | tf_op jit(solution)/shard_map/ppermute | solution.py:216
  36.4 5.4 %collective-permute-start.15 = (s32[8,128]{1,0:T(8,128)}, s32[8,128]{1,0:T(8,128)S(1)}, u32[]{:S(2)}, u32[]{:S(2)}) collective-permute-start(s32[8,128]{1,0:T(8,128)} %bitcast.18), channel_id=1, source_target_pairs={{0,16},{8,24},{16,0},{24,8},{1,17},{9,25},{17,1},{25,9},{2,18},{10... | collective-permute-start | bytes 12296 | tf_op jit(solution)/shard_map/ppermute | solution.py:216
  43.6 2.6 %collective-permute-start.32 = (s32[8,128]{1,0:T(8,128)}, s32[8,128]{1,0:T(8,128)S(1)}, u32[]{:S(2)}, u32[]{:S(2)}) collective-permute-start(s32[8,128]{1,0:T(8,128)} %bitcast.19), channel_id=1, source_target_pairs={{0,8},{8,16},{16,24},{24,0},{1,9},{9,17},{17,25},{25,1},{2,10},{10... | collective-permute-start | bytes 12296 | tf_op jit(solution)/shard_map/ppermute | solution.py:216
  51.3 3.5 %collective-permute-done.17.refs_2_ = bf16[40,2048]{1,0:T(8,128)(2,1)S(1)} collective-permute-done((bf16[40,2048]{1,0:T(8,128)(2,1)S(1)}, bf16[40,2048]{1,0:T(8,128)(2,1)S(1)}, u32[]{:S(2)}, u32[]{:S(2)}) %collective-permute-start.17) | collective-permute-done | bytes 163872 | tf_op jit(solution)/shard_map/ppermute | solution.py:219
  54.7 2.4 %collective-permute-start.21 = (bf16[40,2048]{1,0:T(8,128)(2,1)S(1)}, bf16[40,2048]{1,0:T(8,128)(2,1)S(1)}, u32[]{:S(2)}, u32[]{:S(2)}) collective-permute-start(bf16[40,2048]{1,0:T(8,128)(2,1)S(1)} %get-tuple-element.93), channel_id=1, source_target_pairs={{0,6},{1,7},{2,4},{3,5},{4,2},{5,3},{6,0},{7,1},{8,14},{9,15},{10,... | collective-permute-start | bytes 491528 | tf_op jit(solution)/shard_map/ppermute | solution.py:219
  57.5 2.9 %collective-permute-start.22 = (bf16[40,2048]{1,0:T(8,128)(2,1)S(1)}, bf16[40,2048]{1,0:T(8,128)(2,1)S(1)}, u32[]{:S(2)}, u32[]{:S(2)}) collective-permute-start(bf16[40,2048]{1,0:T(8,128)(2,1)S(1)} %get-tuple-element.94), channel_id=1, source_target_pairs={{0,7},{1,6},{2,5},{3,4},{4,3},{5,2},{6,1},{7,0},{8,15},{9,14},{10,... | collective-permute-start | bytes 491528 | tf_op jit(solution)/shard_map/ppermute | solution.py:219
  61.4 4.8 %collective-permute-done.20.refs_5_ = bf16[40,2048]{1,0:T(8,128)(2,1)S(1)} collective-permute-done((bf16[40,2048]{1,0:T(8,128)(2,1)S(1)}, bf16[40,2048]{1,0:T(8,128)(2,1)S(1)}, u32[]{:S(2)}, u32[]{:S(2)}) %collective-permute-start.20) | collective-permute-done | bytes 163872 | tf_op jit(solution)/shard_map/ppermute | solution.py:219
  66.2 2.6 %collective-permute-start.48 = (bf16[128,2048]{1,0:T(8,128)(2,1)}, bf16[128,2048]{1,0:T(8,128)(2,1)S(1)}, u32[]{:S(2)}, u32[]{:S(2)}) collective-permute-start(bf16[128,2048]{1,0:T(8,128)(2,1)} %tokens_ref.3), channel_id=1, source_target_pairs={{0,24},{8,0},{16,8},{24,16},{1,25},{9,1},{17,9},{25,17},{2,26},{10... | collective-permute-start | bytes 1572872 | tf_op jit(solution)/shard_map/ppermute | solution.py:216
  68.8 2.1 collective-permute-start.5
  77.1 6.3 %shard_map.68 = (bf16[40,2048]{1,0:T(8,128)(2,1)S(1)}, bf16[40,2048]{1,0:T(8,128)(2,1)S(1)}, bf16[40,2048]{1,0:T(8,128)(2,1)S(1)}, bf16[40,2048]{1,0:T(8,128)(2,...) custom-call(bf16[40,2048]{1,0:T(8,128)(2,1)S(1)} %get-tuple-element., ...), custom_call_target="tpu_custom_call" | custom-call | flops 1000 | bytes 1000 | tf_op jit(solution)/shard_map/pallas_call | solution.py:133
  87.5 3.6 %collective-permute-done.24.refs_10_ = bf16[40,2048]{1,0:T(8,128)(2,1)S(1)} collective-permute-done((bf16[40,2048]{1,0:T(8,128)(2,1)S(1)}, bf16[40,2048]{1,0:T(8,128)(2,1)S(1)}, u32[]{:S(2)}, u32[]{:S(2)}) %collective-permute-start.24) | collective-permute-done | bytes 163872 | tf_op jit(solution)/shard_map/ppermute | solution.py:219
  91.1 2.2 collective-permute-start.28
  93.9 2.6 %collective-permute-start.29 = (bf16[40,2048]{1,0:T(8,128)(2,1)S(1)}, bf16[40,2048]{1,0:T(8,128)(2,1)S(1)}, u32[]{:S(2)}, u32[]{:S(2)}) collective-permute-start(bf16[40,2048]{1,0:T(8,128)(2,1)S(1)} %get-tuple-element.102), channel_id=1, source_target_pairs={{0,7},{1,6},{2,5},{3,4},{4,3},{5,2},{6,1},{7,0},{8,15},{9,14},{10,... | collective-permute-start | bytes 491528 | tf_op jit(solution)/shard_map/ppermute | solution.py:219
  96.5 6.0 %collective-permute-done.27.refs_13_ = bf16[40,2048]{1,0:T(8,128)(2,1)S(1)} collective-permute-done((bf16[40,2048]{1,0:T(8,128)(2,1)S(1)}, bf16[40,2048]{1,0:T(8,128)(2,1)S(1)}, u32[]{:S(2)}, u32[]{:S(2)}) %collective-permute-start.27) | collective-permute-done | bytes 163872 | tf_op jit(solution)/shard_map/ppermute | solution.py:219
  106.7 2.0 collective-permute-start.38
  114.7 6.2 %collective-permute-done.37.refs_5_ = bf16[40,2048]{1,0:T(8,128)(2,1)S(1)} collective-permute-done((bf16[40,2048]{1,0:T(8,128)(2,1)S(1)}, bf16[40,2048]{1,0:T(8,128)(2,1)S(1)}, u32[]{:S(2)}, u32[]{:S(2)}) %collective-permute-start.37) | collective-permute-done | bytes 163872 | tf_op jit(solution)/shard_map/ppermute | solution.py:219
  124.8 2.1 collective-permute-start.56
  127.0 6.3 %shard_map.71 = (bf16[40,2048]{1,0:T(8,128)(2,1)S(1)}, bf16[40,2048]{1,0:T(8,128)(2,1)S(1)}, bf16[40,2048]{1,0:T(8,128)(2,1)S(1)}, bf16[40,2048]{1,0:T(8,128)(2,...) custom-call(bf16[40,2048]{1,0:T(8,128)(2,1)S(1)} %get-tuple-element., ...), custom_call_target="tpu_custom_call" | custom-call | flops 1000 | bytes 1000 | tf_op jit(solution)/shard_map/pallas_call | solution.py:133
  133.5 3.2 %collective-permute-done.53.refs_4_ = bf16[40,2048]{1,0:T(8,128)(2,1)S(1)} collective-permute-done((bf16[40,2048]{1,0:T(8,128)(2,1)S(1)}, bf16[40,2048]{1,0:T(8,128)(2,1)S(1)}, u32[]{:S(2)}, u32[]{:S(2)}) %collective-permute-start.53) | collective-permute-done | bytes 163872 | tf_op jit(solution)/shard_map/ppermute | solution.py:219
  140.4 6.3 %shard_map.74 = (bf16[40,2048]{1,0:T(8,128)(2,1)S(1)}, bf16[40,2048]{1,0:T(8,128)(2,1)S(1)}, bf16[40,2048]{1,0:T(8,128)(2,1)S(1)}, bf16[40,2048]{1,0:T(8,128)(2,...) custom-call(bf16[40,2048]{1,0:T(8,128)(2,1)S(1)} %get-tuple-element., ...), custom_call_target="tpu_custom_call" | custom-call | flops 1000 | bytes 1000 | tf_op jit(solution)/shard_map/pallas_call | solution.py:133
  151.9 3.0 %collective-permute-done.45.refs_14_ = bf16[40,2048]{1,0:T(8,128)(2,1)S(1)} collective-permute-done((bf16[40,2048]{1,0:T(8,128)(2,1)S(1)}, bf16[40,2048]{1,0:T(8,128)(2,1)S(1)}, u32[]{:S(2)}, u32[]{:S(2)}) %collective-permute-start.45) | collective-permute-done | bytes 163872 | tf_op jit(solution)/shard_map/ppermute | solution.py:219
  155.7 2.5 %collective-permute-done.46.refs_15_ = bf16[40,2048]{1,0:T(8,128)(2,1)S(1)} collective-permute-done((bf16[40,2048]{1,0:T(8,128)(2,1)S(1)}, bf16[40,2048]{1,0:T(8,128)(2,1)S(1)}, u32[]{:S(2)}, u32[]{:S(2)}) %collective-permute-start.46) | collective-permute-done | bytes 163872 | tf_op jit(solution)/shard_map/ppermute | solution.py:219
  158.9 2.1 collective-permute-start.62
  163.0 6.4 %shard_map.65 = (bf16[40,2048]{1,0:T(8,128)(2,1)S(1)}, bf16[40,2048]{1,0:T(8,128)(2,1)S(1)}, bf16[40,2048]{1,0:T(8,128)(2,1)S(1)}, bf16[40,2048]{1,0:T(8,128)(2,...) custom-call(bf16[48,2048]{1,0:T(8,128)(2,1)S(1)} %get-tuple-element., ...), custom_call_target="tpu_custom_call" | custom-call | flops 1000 | bytes 1000 | tf_op jit(solution)/shard_map/pallas_call | solution.py:133
  176.9 6.4 %collective-permute-done.8.refs_10_ = bf16[40,2048]{1,0:T(8,128)(2,1)S(1)} collective-permute-done((bf16[40,2048]{1,0:T(8,128)(2,1)S(1)}, bf16[40,2048]{1,0:T(8,128)(2,1)S(1)}, u32[]{:S(2)}, u32[]{:S(2)}) %collective-permute-start.8) | collective-permute-done | bytes 163872 | tf_op jit(solution)/shard_map/ppermute | solution.py:219
  185.9 5.9 %collective-permute-done.10.refs_12_ = bf16[40,2048]{1,0:T(8,128)(2,1)S(1)} collective-permute-done((bf16[40,2048]{1,0:T(8,128)(2,1)S(1)}, bf16[40,2048]{1,0:T(8,128)(2,1)S(1)}, u32[]{:S(2)}, u32[]{:S(2)}) %collective-permute-start.10) | collective-permute-done | bytes 163872 | tf_op jit(solution)/shard_map/ppermute | solution.py:219
  194.1 5.7 %collective-permute-done.12.refs_14_ = bf16[40,2048]{1,0:T(8,128)(2,1)S(1)} collective-permute-done((bf16[40,2048]{1,0:T(8,128)(2,1)S(1)}, bf16[40,2048]{1,0:T(8,128)(2,1)S(1)}, u32[]{:S(2)}, u32[]{:S(2)}) %collective-permute-start.12) | collective-permute-done | bytes 163872 | tf_op jit(solution)/shard_map/ppermute | solution.py:219
  200.8 7.0 %collective-permute-done.30 = bf16[128,2048]{1,0:T(8,128)(2,1)S(1)} collective-permute-done((bf16[128,2048]{1,0:T(8,128)(2,1)S(1)}, bf16[128,2048]{1,0:T(8,128)(2,1)S(1)}, u32[]{:S(2)}, u32[]{:S(2)}) %collective-permute-start.30) | collective-permute-done | bytes 524320 | tf_op jit(solution)/shard_map/ppermute | solution.py:216
  207.8 12.5 %collective-permute-done.47 = bf16[128,2048]{1,0:T(8,128)(2,1)S(1)} collective-permute-done((bf16[128,2048]{1,0:T(8,128)(2,1)S(1)}, bf16[128,2048]{1,0:T(8,128)(2,1)S(1)}, u32[]{:S(2)}, u32[]{:S(2)}) %collective-permute-start.47) | collective-permute-done | bytes 524320 | tf_op jit(solution)/shard_map/ppermute | solution.py:216
  (129 shorter events, 65.1 us)
Async XLA Ops:
  0.0 25.2 %collective-permute-start.14 = (bf16[128,2048]{1,0:T(8,128)(2,1)}, bf16[128,2048]{1,0:T(8,128)(2,1)S(1)}, u32[]{:S(2)}, u32[]{:S(2)}) collective-permute-start(bf16[128,2048]{1,0:T(8,128)(2,1)} %tokens_ref.3), channel_id=1, source_target_pairs={{0,16},{8,24},{16,0},{24,8},{1,17},{9,25},{17,1},{25,9},{2,18},{10... | collective-permute-start | bytes 1572872 | tf_op jit(solution)/shard_map/ppermute | solution.py:216
  25.2 35.5 %collective-permute-start.31 = (bf16[128,2048]{1,0:T(8,128)(2,1)}, bf16[128,2048]{1,0:T(8,128)(2,1)S(1)}, u32[]{:S(2)}, u32[]{:S(2)}) collective-permute-start(bf16[128,2048]{1,0:T(8,128)(2,1)} %tokens_ref.3), channel_id=1, source_target_pairs={{0,8},{8,16},{16,24},{24,0},{1,9},{9,17},{17,25},{25,1},{2,10},{10... | collective-permute-start | bytes 1572872 | tf_op jit(solution)/shard_map/ppermute | solution.py:216
  28.3 19.4 %collective-permute-start = (bf16[48,2048]{1,0:T(8,128)(2,1)S(1)}, bf16[48,2048]{1,0:T(8,128)(2,1)S(1)}, u32[]{:S(2)}, u32[]{:S(2)}) collective-permute-start(bf16[48,2048]{1,0:T(8,128)(2,1)S(1)} %get-tuple-element.72), channel_id=1, source_target_pairs={{0,1},{1,0},{2,3},{3,2},{4,5},{5,4},{6,7},{7,6},{8,9},{9,8},{10,11... | collective-permute-start | bytes 589832 | tf_op jit(solution)/shard_map/ppermute | solution.py:219
  28.4 20.8 %collective-permute-start.1 = (bf16[48,2048]{1,0:T(8,128)(2,1)S(1)}, bf16[48,2048]{1,0:T(8,128)(2,1)S(1)}, u32[]{:S(2)}, u32[]{:S(2)}) collective-permute-start(bf16[48,2048]{1,0:T(8,128)(2,1)S(1)} %get-tuple-element.73), channel_id=1, source_target_pairs={{0,2},{1,3},{2,0},{3,1},{4,6},{5,7},{6,4},{7,5},{8,10},{9,11},{10,... | collective-permute-start | bytes 589832 | tf_op jit(solution)/shard_map/ppermute | solution.py:219
  29.9 19.7 %collective-permute-start.2 = (bf16[48,2048]{1,0:T(8,128)(2,1)S(1)}, bf16[48,2048]{1,0:T(8,128)(2,1)S(1)}, u32[]{:S(2)}, u32[]{:S(2)}) collective-permute-start(bf16[48,2048]{1,0:T(8,128)(2,1)S(1)} %get-tuple-element.74), channel_id=1, source_target_pairs={{0,3},{1,2},{2,1},{3,0},{4,7},{5,6},{6,5},{7,4},{8,11},{9,10},{10,... | collective-permute-start | bytes 589832 | tf_op jit(solution)/shard_map/ppermute | solution.py:219
  51.1 15.1 %collective-permute-start.20 = (bf16[40,2048]{1,0:T(8,128)(2,1)S(1)}, bf16[40,2048]{1,0:T(8,128)(2,1)S(1)}, u32[]{:S(2)}, u32[]{:S(2)}) collective-permute-start(bf16[40,2048]{1,0:T(8,128)(2,1)S(1)} %get-tuple-element.92), channel_id=1, source_target_pairs={{0,5},{1,4},{2,7},{3,6},{4,1},{5,0},{6,3},{7,2},{8,13},{9,12},{10,... | collective-permute-start | bytes 491528 | tf_op jit(solution)/shard_map/ppermute | solution.py:219
  54.7 14.1 %collective-permute-start.21 = (bf16[40,2048]{1,0:T(8,128)(2,1)S(1)}, bf16[40,2048]{1,0:T(8,128)(2,1)S(1)}, u32[]{:S(2)}, u32[]{:S(2)}) collective-permute-start(bf16[40,2048]{1,0:T(8,128)(2,1)S(1)} %get-tuple-element.93), channel_id=1, source_target_pairs={{0,6},{1,7},{2,4},{3,5},{4,2},{5,3},{6,0},{7,1},{8,14},{9,15},{10,... | collective-permute-start | bytes 491528 | tf_op jit(solution)/shard_map/ppermute | solution.py:219
  57.5 13.5 %collective-permute-start.22 = (bf16[40,2048]{1,0:T(8,128)(2,1)S(1)}, bf16[40,2048]{1,0:T(8,128)(2,1)S(1)}, u32[]{:S(2)}, u32[]{:S(2)}) collective-permute-start(bf16[40,2048]{1,0:T(8,128)(2,1)S(1)} %get-tuple-element.94), channel_id=1, source_target_pairs={{0,7},{1,6},{2,5},{3,4},{4,3},{5,2},{6,1},{7,0},{8,15},{9,14},{10,... | collective-permute-start | bytes 491528 | tf_op jit(solution)/shard_map/ppermute | solution.py:219
  60.4 23.1 %collective-permute-start.3 = (bf16[48,2048]{1,0:T(8,128)(2,1)S(1)}, bf16[48,2048]{1,0:T(8,128)(2,1)S(1)}, u32[]{:S(2)}, u32[]{:S(2)}) collective-permute-start(bf16[48,2048]{1,0:T(8,128)(2,1)S(1)} %get-tuple-element.75), channel_id=1, source_target_pairs={{0,4},{1,5},{2,6},{3,7},{4,0},{5,1},{6,2},{7,3},{8,12},{9,13},{10,... | collective-permute-start | bytes 589832 | tf_op jit(solution)/shard_map/ppermute | solution.py:219
  60.7 23.3 %collective-permute-start.4 = (bf16[48,2048]{1,0:T(8,128)(2,1)S(1)}, bf16[48,2048]{1,0:T(8,128)(2,1)S(1)}, u32[]{:S(2)}, u32[]{:S(2)}) collective-permute-start(bf16[48,2048]{1,0:T(8,128)(2,1)S(1)} %get-tuple-element.76), channel_id=1, source_target_pairs={{0,5},{1,4},{2,7},{3,6},{4,1},{5,0},{6,3},{7,2},{8,13},{9,12},{10,... | collective-permute-start | bytes 589832 | tf_op jit(solution)/shard_map/ppermute | solution.py:219
  66.2 37.8 %collective-permute-start.48 = (bf16[128,2048]{1,0:T(8,128)(2,1)}, bf16[128,2048]{1,0:T(8,128)(2,1)S(1)}, u32[]{:S(2)}, u32[]{:S(2)}) collective-permute-start(bf16[128,2048]{1,0:T(8,128)(2,1)} %tokens_ref.3), channel_id=1, source_target_pairs={{0,24},{8,0},{16,8},{24,16},{1,25},{9,1},{17,9},{25,17},{2,26},{10... | collective-permute-start | bytes 1572872 | tf_op jit(solution)/shard_map/ppermute | solution.py:216
  68.8 16.7 %collective-permute-start.5 = (bf16[48,2048]{1,0:T(8,128)(2,1)S(1)}, bf16[48,2048]{1,0:T(8,128)(2,1)S(1)}, u32[]{:S(2)}, u32[]{:S(2)}) collective-permute-start(bf16[48,2048]{1,0:T(8,128)(2,1)S(1)} %get-tuple-element.77), channel_id=1, source_target_pairs={{0,6},{1,7},{2,4},{3,5},{4,2},{5,3},{6,0},{7,1},{8,14},{9,15},{10,... | collective-permute-start | bytes 589832 | tf_op jit(solution)/shard_map/ppermute | solution.py:219
  71.0 14.5 %collective-permute-start.6 = (bf16[48,2048]{1,0:T(8,128)(2,1)S(1)}, bf16[48,2048]{1,0:T(8,128)(2,1)S(1)}, u32[]{:S(2)}, u32[]{:S(2)}) collective-permute-start(bf16[48,2048]{1,0:T(8,128)(2,1)S(1)} %get-tuple-element.78), channel_id=1, source_target_pairs={{0,7},{1,6},{2,5},{3,4},{4,3},{5,2},{6,1},{7,0},{8,15},{9,14},{10,... | collective-permute-start | bytes 589832 | tf_op jit(solution)/shard_map/ppermute | solution.py:219
  87.1 15.4 %collective-permute-start.27 = (bf16[40,2048]{1,0:T(8,128)(2,1)S(1)}, bf16[40,2048]{1,0:T(8,128)(2,1)S(1)}, u32[]{:S(2)}, u32[]{:S(2)}) collective-permute-start(bf16[40,2048]{1,0:T(8,128)(2,1)S(1)} %get-tuple-element.100), channel_id=1, source_target_pairs={{0,5},{1,4},{2,7},{3,6},{4,1},{5,0},{6,3},{7,2},{8,13},{9,12},{10,... | collective-permute-start | bytes 491528 | tf_op jit(solution)/shard_map/ppermute | solution.py:219
  91.1 13.0 %collective-permute-start.28 = (bf16[40,2048]{1,0:T(8,128)(2,1)S(1)}, bf16[40,2048]{1,0:T(8,128)(2,1)S(1)}, u32[]{:S(2)}, u32[]{:S(2)}) collective-permute-start(bf16[40,2048]{1,0:T(8,128)(2,1)S(1)} %get-tuple-element.101), channel_id=1, source_target_pairs={{0,6},{1,7},{2,4},{3,5},{4,2},{5,3},{6,0},{7,1},{8,14},{9,15},{10,... | collective-permute-start | bytes 491528 | tf_op jit(solution)/shard_map/ppermute | solution.py:219
  105.9 15.0 %collective-permute-start.37 = (bf16[40,2048]{1,0:T(8,128)(2,1)S(1)}, bf16[40,2048]{1,0:T(8,128)(2,1)S(1)}, u32[]{:S(2)}, u32[]{:S(2)}) collective-permute-start(bf16[40,2048]{1,0:T(8,128)(2,1)S(1)} %get-tuple-element.109), channel_id=1, source_target_pairs={{0,5},{1,4},{2,7},{3,6},{4,1},{5,0},{6,3},{7,2},{8,13},{9,12},{10,... | collective-permute-start | bytes 491528 | tf_op jit(solution)/shard_map/ppermute | solution.py:219
  106.7 15.9 %collective-permute-start.38 = (bf16[40,2048]{1,0:T(8,128)(2,1)S(1)}, bf16[40,2048]{1,0:T(8,128)(2,1)S(1)}, u32[]{:S(2)}, u32[]{:S(2)}) collective-permute-start(bf16[40,2048]{1,0:T(8,128)(2,1)S(1)} %get-tuple-element.110), channel_id=1, source_target_pairs={{0,6},{1,7},{2,4},{3,5},{4,2},{5,3},{6,0},{7,1},{8,14},{9,15},{10,... | collective-permute-start | bytes 491528 | tf_op jit(solution)/shard_map/ppermute | solution.py:219
  109.5 14.0 %collective-permute-start.39 = (bf16[40,2048]{1,0:T(8,128)(2,1)S(1)}, bf16[40,2048]{1,0:T(8,128)(2,1)S(1)}, u32[]{:S(2)}, u32[]{:S(2)}) collective-permute-start(bf16[40,2048]{1,0:T(8,128)(2,1)S(1)} %get-tuple-element.111), channel_id=1, source_target_pairs={{0,7},{1,6},{2,5},{3,4},{4,3},{5,2},{6,1},{7,0},{8,15},{9,14},{10,... | collective-permute-start | bytes 491528 | tf_op jit(solution)/shard_map/ppermute | solution.py:219
  120.9 12.4 %collective-permute-start.52 = (bf16[40,2048]{1,0:T(8,128)(2,1)S(1)}, bf16[40,2048]{1,0:T(8,128)(2,1)S(1)}, u32[]{:S(2)}, u32[]{:S(2)}) collective-permute-start(bf16[40,2048]{1,0:T(8,128)(2,1)S(1)} %get-tuple-element.124), channel_id=1, source_target_pairs={{0,3},{1,2},{2,1},{3,0},{4,7},{5,6},{6,5},{7,4},{8,11},{9,10},{10,... | collective-permute-start | bytes 491528 | tf_op jit(solution)/shard_map/ppermute | solution.py:219
  122.5 14.1 %collective-permute-start.53 = (bf16[40,2048]{1,0:T(8,128)(2,1)S(1)}, bf16[40,2048]{1,0:T(8,128)(2,1)S(1)}, u32[]{:S(2)}, u32[]{:S(2)}) collective-permute-start(bf16[40,2048]{1,0:T(8,128)(2,1)S(1)} %get-tuple-element.125), channel_id=1, source_target_pairs={{0,4},{1,5},{2,6},{3,7},{4,0},{5,1},{6,2},{7,3},{8,12},{9,13},{10,... | collective-permute-start | bytes 491528 | tf_op jit(solution)/shard_map/ppermute | solution.py:219
  123.6 14.8 %collective-permute-start.54 = (bf16[40,2048]{1,0:T(8,128)(2,1)S(1)}, bf16[40,2048]{1,0:T(8,128)(2,1)S(1)}, u32[]{:S(2)}, u32[]{:S(2)}) collective-permute-start(bf16[40,2048]{1,0:T(8,128)(2,1)S(1)} %get-tuple-element.126), channel_id=1, source_target_pairs={{0,5},{1,4},{2,7},{3,6},{4,1},{5,0},{6,3},{7,2},{8,13},{9,12},{10,... | collective-permute-start | bytes 491528 | tf_op jit(solution)/shard_map/ppermute | solution.py:219
  124.0 15.2 %collective-permute-start.55 = (bf16[40,2048]{1,0:T(8,128)(2,1)S(1)}, bf16[40,2048]{1,0:T(8,128)(2,1)S(1)}, u32[]{:S(2)}, u32[]{:S(2)}) collective-permute-start(bf16[40,2048]{1,0:T(8,128)(2,1)S(1)} %get-tuple-element.127), channel_id=1, source_target_pairs={{0,6},{1,7},{2,4},{3,5},{4,2},{5,3},{6,0},{7,1},{8,14},{9,15},{10,... | collective-permute-start | bytes 491528 | tf_op jit(solution)/shard_map/ppermute | solution.py:219
  124.8 15.3 %collective-permute-start.56 = (bf16[40,2048]{1,0:T(8,128)(2,1)S(1)}, bf16[40,2048]{1,0:T(8,128)(2,1)S(1)}, u32[]{:S(2)}, u32[]{:S(2)}) collective-permute-start(bf16[40,2048]{1,0:T(8,128)(2,1)S(1)} %get-tuple-element.128), channel_id=1, source_target_pairs={{0,7},{1,6},{2,5},{3,4},{4,3},{5,2},{6,1},{7,0},{8,15},{9,14},{10,... | collective-permute-start | bytes 491528 | tf_op jit(solution)/shard_map/ppermute | solution.py:219
  133.3 13.5 %collective-permute-start.40 = (bf16[40,2048]{1,0:T(8,128)(2,1)S(1)}, bf16[40,2048]{1,0:T(8,128)(2,1)S(1)}, u32[]{:S(2)}, u32[]{:S(2)}) collective-permute-start(bf16[40,2048]{1,0:T(8,128)(2,1)S(1)} %get-tuple-element.113), channel_id=1, source_target_pairs={{0,1},{1,0},{2,3},{3,2},{4,5},{5,4},{6,7},{7,6},{8,9},{9,8},{10,11... | collective-permute-start | bytes 491528 | tf_op jit(solution)/shard_map/ppermute | solution.py:219
  151.6 17.8 %collective-permute-start.59 = (bf16[40,2048]{1,0:T(8,128)(2,1)S(1)}, bf16[40,2048]{1,0:T(8,128)(2,1)S(1)}, u32[]{:S(2)}, u32[]{:S(2)}) collective-permute-start(bf16[40,2048]{1,0:T(8,128)(2,1)S(1)} %get-tuple-element.132), channel_id=1, source_target_pairs={{0,3},{1,2},{2,1},{3,0},{4,7},{5,6},{6,5},{7,4},{8,11},{9,10},{10,... | collective-permute-start | bytes 491528 | tf_op jit(solution)/shard_map/ppermute | solution.py:219
  154.8 17.0 %collective-permute-start.60 = (bf16[40,2048]{1,0:T(8,128)(2,1)S(1)}, bf16[40,2048]{1,0:T(8,128)(2,1)S(1)}, u32[]{:S(2)}, u32[]{:S(2)}) collective-permute-start(bf16[40,2048]{1,0:T(8,128)(2,1)S(1)} %get-tuple-element.133), channel_id=1, source_target_pairs={{0,4},{1,5},{2,6},{3,7},{4,0},{5,1},{6,2},{7,3},{8,12},{9,13},{10,... | collective-permute-start | bytes 491528 | tf_op jit(solution)/shard_map/ppermute | solution.py:219
  158.2 14.8 %collective-permute-start.61 = (bf16[40,2048]{1,0:T(8,128)(2,1)S(1)}, bf16[40,2048]{1,0:T(8,128)(2,1)S(1)}, u32[]{:S(2)}, u32[]{:S(2)}) collective-permute-start(bf16[40,2048]{1,0:T(8,128)(2,1)S(1)} %get-tuple-element.134), channel_id=1, source_target_pairs={{0,5},{1,4},{2,7},{3,6},{4,1},{5,0},{6,3},{7,2},{8,13},{9,12},{10,... | collective-permute-start | bytes 491528 | tf_op jit(solution)/shard_map/ppermute | solution.py:219
  158.9 15.3 %collective-permute-start.62 = (bf16[40,2048]{1,0:T(8,128)(2,1)S(1)}, bf16[40,2048]{1,0:T(8,128)(2,1)S(1)}, u32[]{:S(2)}, u32[]{:S(2)}) collective-permute-start(bf16[40,2048]{1,0:T(8,128)(2,1)S(1)} %get-tuple-element.135), channel_id=1, source_target_pairs={{0,6},{1,7},{2,4},{3,5},{4,2},{5,3},{6,0},{7,1},{8,14},{9,15},{10,... | collective-permute-start | bytes 491528 | tf_op jit(solution)/shard_map/ppermute | solution.py:219
  161.3 12.9 %collective-permute-start.63 = (bf16[40,2048]{1,0:T(8,128)(2,1)S(1)}, bf16[40,2048]{1,0:T(8,128)(2,1)S(1)}, u32[]{:S(2)}, u32[]{:S(2)}) collective-permute-start(bf16[40,2048]{1,0:T(8,128)(2,1)S(1)} %get-tuple-element.136), channel_id=1, source_target_pairs={{0,7},{1,6},{2,5},{3,4},{4,3},{5,2},{6,1},{7,0},{8,15},{9,14},{10,... | collective-permute-start | bytes 491528 | tf_op jit(solution)/shard_map/ppermute | solution.py:219
  171.9 35.9 %collective-permute-start.30 = (bf16[128,2048]{1,0:T(8,128)(2,1)S(1)}, bf16[128,2048]{1,0:T(8,128)(2,1)S(1)}, u32[]{:S(2)}, u32[]{:S(2)}) collective-permute-start(bf16[128,2048]{1,0:T(8,128)(2,1)S(1)} %shard_map.69), channel_id=1, source_target_pairs={{0,16},{8,24},{16,0},{24,8},{1,17},{9,25},{17,1},{25,9},{2,18},{10... | collective-permute-start | bytes 1572872 | tf_op jit(solution)/shard_map/ppermute | solution.py:216
  173.0 47.2 %collective-permute-start.47 = (bf16[128,2048]{1,0:T(8,128)(2,1)S(1)}, bf16[128,2048]{1,0:T(8,128)(2,1)S(1)}, u32[]{:S(2)}, u32[]{:S(2)}) collective-permute-start(bf16[128,2048]{1,0:T(8,128)(2,1)S(1)} %shard_map.72), channel_id=1, source_target_pairs={{0,24},{8,0},{16,8},{24,16},{1,25},{9,1},{17,9},{25,17},{2,26},{10... | collective-permute-start | bytes 1572872 | tf_op jit(solution)/shard_map/ppermute | solution.py:216
  175.1 45.1 %collective-permute-start.64 = (bf16[128,2048]{1,0:T(8,128)(2,1)S(1)}, bf16[128,2048]{1,0:T(8,128)(2,1)S(1)}, u32[]{:S(2)}, u32[]{:S(2)}) collective-permute-start(bf16[128,2048]{1,0:T(8,128)(2,1)S(1)} %shard_map.75), channel_id=1, source_target_pairs={{0,8},{8,16},{16,24},{24,0},{1,9},{9,17},{17,25},{25,1},{2,10},{10... | collective-permute-start | bytes 1572872 | tf_op jit(solution)/shard_map/ppermute | solution.py:216
  (42 other events, 400.5 us)

commit v4 on v2

v4 whole, which is shorter than its diff:
```python
import functools

import jax
import jax.numpy as jnp
from jax import lax
from jax.experimental import pallas as pl
from jax.experimental.pallas import tpu as pltpu
from jax.sharding import PartitionSpec as P

BF16 = jnp.bfloat16
F32 = jnp.float32
VMEM_LIMIT = 32 * 1024 * 1024
PARTS = 4
CORES = 2
VMEM = pl.BlockSpec(memory_space=pltpu.VMEM)


def call(body, out_shape, n_in, scratch=()):
    many = isinstance(out_shape, list)
    return pl.pallas_call(
        body,
        out_shape=out_shape,
        in_specs=[VMEM] * n_in,
        out_specs=[VMEM] * len(out_shape) if many else VMEM,
        scratch_shapes=list(scratch),
        compiler_params=pltpu.CompilerParams(vmem_limit_bytes=VMEM_LIMIT),
        cost_estimate=pl.CostEstimate(flops=1000, bytes_accessed=1000, transcendentals=0),
    )


def round_up(n, m):
    return -(-n // m) * m


class Sizes:
    def __init__(self, tokens, router_t, ids_t, near, layers):
        self.toks, self.width = tokens.shape
        self.experts, self.depth = router_t.shape
        self.topk = ids_t.shape[0]
        self.near, self.layers = near, layers
        self.chips = near // CORES
        self.cap = round_up(5 * self.toks * self.topk // (4 * self.experts), 8)
        self.tiles = self.width // self.depth
        self.extra = -(-(1 + self.experts // 8) // self.tiles) * 8

    def tile(self, g):
        r, q = g // self.tiles * 8, g % self.tiles * self.depth
        return slice(r, r + 8), slice(q, q + self.depth)


def pad_kernel(z, tokens_ref, ids_ref, router_ref, out):
    out[0 : z.toks, :] = tokens_ref[...]
    blank = jnp.zeros((z.extra, z.width), BF16)
    out[z.toks : z.toks + z.extra, :] = blank
    out[z.toks : z.toks + 8, 0 : z.toks] = ids_ref[...].astype(F32).astype(BF16)
    for g in range(z.experts // 8):
        rows, cols = z.tile(g + 1)
        out[z.toks + rows.start : z.toks + rows.stop, cols] = router_ref[8 * g : 8 * g + 8, :]


def served_expert(z, q):
    return lax.axis_index("expert") * z.near + lax.bitwise_xor(lax.axis_index("zero"), q * CORES)


def ids_of(z, block_ref):
    return block_ref[z.toks : z.toks + 8, 0 : z.toks].astype(F32).astype(jnp.int32)


def slot_marks(z, ids_t):
    has = jnp.concatenate(
        [
            jnp.max((ids_t == served_expert(z, q)).astype(F32), axis=0, keepdims=True)
            for q in range(z.chips)
        ]
        * 2,
        axis=0,
    )
    earlier = (
        lax.broadcasted_iota(jnp.int32, (z.toks, z.toks), 0)
        < lax.broadcasted_iota(jnp.int32, (z.toks, z.toks), 1)
    ).astype(F32).astype(BF16)
    slot = jnp.dot(has.astype(BF16), earlier, preferred_element_type=F32)
    slot = jnp.where(has > 0, slot, -1.0)
    row = lax.broadcasted_iota(jnp.int32, (z.cap, z.toks), 0).astype(F32)
    return [jnp.where(row == slot[q : q + 1, :], 1.0, 0.0) for q in range(z.chips)]


def pick_kernel(z, n, ride, *refs):
    blocks, outs = refs[:n], refs[n:]
    marks = [jnp.concatenate(slot_marks(z, ids_of(z, b)), axis=0).astype(BF16) for b in blocks]
    part = z.width // PARTS
    for c in range(PARTS):
        cols = slice(c * part, (c + 1) * part)
        rows = [jnp.dot(m, b[0 : z.toks, cols], preferred_element_type=F32) for m, b in zip(marks, blocks)]
        for q in range(z.chips):
            mine = [r[q * z.cap : (q + 1) * z.cap] for r in rows]
            outs[q][0 : n * z.cap, cols] = jnp.concatenate(mine, axis=0).astype(BF16)
    if ride:
        for q in range(z.chips):
            for r in range(CORES):
                start = n * z.cap + r * z.extra
                outs[q][start : start + z.extra, :] = blocks[r][z.toks : z.toks + z.extra, :]


def expert_kernel(z, rows, *refs):
    slabs, gate_ref, up_ref, down_ref = refs[: z.chips], *refs[z.chips : z.chips + 3]
    outs, (x, hidden) = refs[z.chips + 3 : 2 * z.chips + 3], refs[2 * z.chips + 3 :]
    for q in range(z.chips):
        x[q * rows : (q + 1) * rows, :] = slabs[q][0:rows, :]
    ff = gate_ref.shape[1]
    tile = 256
    for f in range(0, ff, tile):
        gate = jnp.dot(x[...], gate_ref[:, f : f + tile], preferred_element_type=F32)
        upper = jnp.dot(x[...], up_ref[:, f : f + tile], preferred_element_type=F32)
        hidden[:, f : f + tile] = (gate / (1.0 + jnp.exp(-gate)) * upper).astype(BF16)
    for c in range(0, z.width, tile):
        y = jnp.dot(hidden[...], down_ref[:, c : c + tile], preferred_element_type=F32)
        for q in range(z.chips):
            outs[q][:, c : c + tile] = y[q * rows : (q + 1) * rows].astype(BF16)


def mix_kernel(z, n, *refs):
    blocks, refs = refs[:n], refs[n:]
    riders, backs, outs = refs[: z.chips], refs[z.chips : 2 * z.chips], refs[2 * z.chips :]
    number = lax.broadcasted_iota(jnp.int32, (z.experts, z.toks), 0)
    routers = []
    for q in range(z.chips):
        for r in range(CORES):
            base = CORES * z.cap + r * z.extra
            pieces = []
            for g in range(z.experts // 8):
                rows, cols = z.tile(g + 1)
                pieces.append(riders[q][base + rows.start : base + rows.stop, cols].astype(F32))
            routers.append(jnp.concatenate(pieces, axis=0).astype(BF16))
    for b, block in enumerate(blocks):
        out, base = outs[b % CORES], b // CORES * z.toks
        ids_t = ids_of(z, block)
        logits = None
        for o in range(z.near):
            start = pl.multiple_of(lax.bitwise_xor(lax.axis_index("zero"), o) * z.depth, z.depth)
            term = lax.dot_general(
                routers[o],
                block[0 : z.toks, pl.ds(start, z.depth)],
                (((1,), (1,)), ((), ())),
                preferred_element_type=F32,
            )
            logits = term if logits is None else logits + term
        chosen = number == ids_t[0:1, :]
        for k in range(1, z.topk):
            chosen = chosen | (number == ids_t[k : k + 1, :])
        weights = jnp.where(chosen, jnp.exp(jnp.where(chosen, logits, 0.0)), 0.0)
        gates = weights / jnp.sum(weights, axis=0, keepdims=True)
        marks = slot_marks(z, ids_t)
        mix = []
        for q in range(z.chips):
            gate = jnp.sum(jnp.where(number == served_expert(z, q), gates, 0.0), axis=0, keepdims=True)
            mix.append(marks[q] * gate)
        mix = jnp.concatenate(mix, axis=0).astype(BF16)
        part = z.width // PARTS
        for c in range(PARTS):
            cols = slice(c * part, (c + 1) * part)
            own = slice(b * z.cap, (b + 1) * z.cap)
            y = jnp.concatenate([s[:, cols].astype(F32)[own] for s in backs], axis=0).astype(BF16)
            out[base : base + z.toks, cols] = lax.dot_general(
                mix, y, (((0,), (0,)), ((), ())), preferred_element_type=F32
            ).astype(BF16)


def per_device(tokens, router_weight, expert_ids, gate_weight, up_weight, down_weight):
    layers, near = lax.axis_size("expert"), lax.axis_size("zero")
    z = Sizes(tokens, router_weight.T, expert_ids.T, near, layers)

    def along(array, d):
        return lax.ppermute(array, "expert", [(i, (i + d) % layers) for i in range(layers)])

    def across(array, o):
        return lax.ppermute(array, "zero", [(i, i ^ o) for i in range(near)]) if o else array

    def after(arrays, *others):
        return list(lax.optimization_barrier((*arrays, *others))[: len(arrays)])

    def shape(rows):
        return jax.ShapeDtypeStruct((rows, z.width), BF16)

    def pick(blocks, ride):
        n = len(blocks)
        rows = n * z.cap + (CORES * z.extra if ride else 0)
        return call(functools.partial(pick_kernel, z, n, ride), [shape(rows)] * z.chips, n)(*blocks)

    def slabs_across(slabs):
        return [across(s, CORES * q) for q, s in enumerate(slabs)]

    def expert(slabs, n):
        rows = n * z.cap
        return call(
            functools.partial(expert_kernel, z, rows),
            [shape(rows)] * z.chips,
            z.chips + 3,
            [
                pltpu.VMEM((z.chips * rows, z.width), BF16),
                pltpu.VMEM((z.chips * rows, gate_weight.shape[2]), BF16),
            ],
        )(*slabs, gate_weight[0], up_weight[0], down_weight[0])

    def mix(blocks, backs):
        n = len(blocks)
        mine, other = call(
            functools.partial(mix_kernel, z, n), [shape(n // 2 * z.toks)] * 2, n + 2 * z.chips
        )(*blocks, *riders, *backs)
        other = across(other, 1)
        return [
            mine[i * z.toks : (i + 1) * z.toks].astype(F32) + other[i * z.toks : (i + 1) * z.toks].astype(F32)
            for i in range(n // 2)
        ]

    half = layers // 2
    groups = [sorted({d, layers - d}) for d in range(1, half + 1)]

    own = call(functools.partial(pad_kernel, z), shape(z.toks + z.extra), 3)(
        tokens, expert_ids.T, router_weight.T
    )
    pairs, slots, results = {}, {}, {}
    coming = [along(own, d) for d in groups[0]]
    pairs[0] = [own, across(own, 1)]
    slots[0] = slabs_across(pick(pairs[0], True))
    riders = slots[0]
    for g in range(1, len(groups) + 1):
        blocks = coming
        if g < len(groups):
            source = after([own], *blocks, *slots[g - 1])[0]
            coming = [along(source, d) for d in groups[g]]
        pairs[g] = [b for block in blocks for b in (block, across(block, 1))]
        slabs = after(pick(pairs[g], False), *slots[g - 1])
        slots[g] = slabs_across(slabs)
        results[g - 1] = expert(after(slots[g - 1], slabs[1]), len(pairs[g - 1]))
    results[g] = expert(slots[g], len(pairs[g]))
    turns = list(range(1, len(groups) + 1)) + [0]
    backs, leaving, home = [], [], {}
    for g, later in zip(turns, turns[1:] + turns[:1]):
        rows = after(results[g], *backs) if backs else results[g]
        backs = slabs_across(rows)
        if g:
            ready = after(backs, results[later][1], *leaving)
            sums = mix(pairs[g], ready)
            leaving = [part.astype(BF16) for part in sums]
            for d, part in zip(groups[g - 1], leaving):
                home[d] = along(part, layers - d)
        else:
            early = [home[d] for group in groups[:-1] for d in group]
            total = mix(pairs[0], after(backs, *early))[0]
    for d in home:
        total = total + home[d].astype(F32)
    return total.astype(BF16)


def solution(mesh):
    everything = ("expert", "zero")
    in_specs = (
        P(everything, None),
        P("zero", None),
        P(everything, None),
        P(everything, None, None),
        P(everything, None, None),
        P(everything, None, None),
    )
    return jax.shard_map(
        per_device, mesh=mesh, in_specs=in_specs, out_specs=P(everything, None), check_vma=False
    )
```

time: 237 us -> 204 us (0.86)
  matrix products: 67.1 us -> 0 us
  waiting for transfers between devices: 113 us -> 142 us
  Pallas kernels: 0 us -> 20.5 us
  starting transfers between devices: 46.6 us -> 32.2 us
    ppermute x0 -> x25, waiting for transfers between devices: none -> 72 us  [across(): lax.ppermute(array, 'zero', [(i, i ^ o) for i in range(near)])]
    dot_general x24 -> x0, matrix products: 67.1 us -> none  [the longest x4 24.8 us: expert_rows(): return jnp.dot(hidden, down_weight, preferred_element_type=F32).astype(BF16)]
    all_to_all x8 -> x0, waiting for transfers between devices: 34.5 us -> none  [exchange(): lax.all_to_all(slabs, 'zero', split_axis=0, concat_axis=0, tiled=True)]
    all_to_all x8 -> x0, starting transfers between devices: 34.3 us -> none  [exchange(): lax.all_to_all(slabs, 'zero', split_axis=0, concat_axis=0, tiled=True)]
    ppermute x0 -> x25, starting transfers between devices: none -> 21.8 us  [across(): lax.ppermute(array, 'zero', [(i, i ^ o) for i in range(near)])]
    pallas_call x0 -> x10, Pallas kernels: none -> 20.5 us  [the longest x3 12.9 us: expert(): call(functools.partial(expert_kernel, z, rows), [shape(rows)] * z.chips,...]
    ppermute x9 -> x6, waiting for transfers between devices: 78.7 us -> 70.3 us  [along(): lax.ppermute(array, 'expert', [(i, (i + d) % layers) for i in range(layer...]
    unnamed x13 -> x16, local copies, waits for them, and re-layouts: 2.74 us -> 6.39 us
  transfers between devices with their start and end apart: 17 -> 31, of which waited for: 14 -> 16; matrix products, arithmetic and copies ran while one was open for 28% -> 0% of each run, Pallas kernels for 0% -> 9%
where the time goes in v4:
time: 204 us; the launch traced here: 203 us
  waiting for transfers between devices  142 us (70%)
  starting transfers between devices  32.2 us (16%)
  Pallas kernels  20.5 us (10%)
  local copies, waits for them, and re-layouts  6.39 us (3%)
    ppermute x25, waiting for transfers between devices, across(): lax.ppermute(array, 'zero', [(i, i ^ o) for i in range(near)])  72 us
    ppermute x6, waiting for transfers between devices, along(): lax.ppermute(array, 'expert', [(i, (i + d) % layers) for i in range(layer...  70.3 us
    ppermute x25, starting transfers between devices, across(): lax.ppermute(array, 'zero', [(i, i ^ o) for i in range(near)])  21.8 us
    pallas_call x3, Pallas kernels, expert(): call(functools.partial(expert_kernel, z, rows), [shape(rows)] * z.chips,...  12.9 us
    ppermute x6, starting transfers between devices, along(): lax.ppermute(array, 'expert', [(i, (i + d) % layers) for i in range(layer...  10.5 us
    unnamed x16, local copies, waits for them, and re-layouts  6.39 us
    pallas_call x3, Pallas kernels, mix(): call(functools.partial(mix_kernel, z, n), [shape(n // 2 * z.toks)] * 2, n...  5.44 us
  transfers between devices with their start and end apart: 31, of which 16 were waited for; matrix products, arithmetic and copies ran while one was open for 0% of the time, Pallas kernels for 9%

profile of v4, /device:TPU:0, one launch (start us, length us, event | category | flops | bytes accessed | tf_op | source)
XLA Modules:
  0.0 203.4 jit_solution(16966886822375393661)
XLA Ops:
  3.2 4.7 %collective-permute-start.6 = (bf16[136,2048]{1,0:T(8,128)(2,1)S(1)}, bf16[136,2048]{1,0:T(8,128)(2,1)S(1)}, u32[]{:S(2)}, u32[]{:S(2)}) collective-permute-start(bf16[136,2048]{1,0:T(8,128)(2,1)S(1)} %shard_map.64.refs_0_), channel_id=1, source_target_pairs={{0,24},{8,0},{16,8},{24,16},{1,25},{9,1},{17,9},{25,17},{2,26},{10... | collective-permute-start | bytes 1671176 | tf_op jit(solution)/shard_map/ppermute | solution.py:174
  8.4 1.6 collective-permute-start.1
  10.0 1.5 collective-permute-start.2
  12.0 8.8 %collective-permute-done.6.refs_2_ = bf16[136,2048]{1,0:T(8,128)(2,1)S(1)} collective-permute-done((bf16[136,2048]{1,0:T(8,128)(2,1)S(1)}, bf16[136,2048]{1,0:T(8,128)(2,1)S(1)}, u32[]{:S(2)}, u32[]{:S(2)}) %collective-permute-start.6) | collective-permute-done | bytes 557088 | tf_op jit(solution)/shard_map/ppermute | solution.py:174
  20.8 12.3 %collective-permute-done.4.refs_0_ = bf16[136,2048]{1,0:T(8,128)(2,1)S(1)} collective-permute-done((bf16[136,2048]{1,0:T(8,128)(2,1)S(1)}, bf16[136,2048]{1,0:T(8,128)(2,1)S(1)}, u32[]{:S(2)}, u32[]{:S(2)}) %collective-permute-start.4) | collective-permute-done | bytes 557088 | tf_op jit(solution)/shard_map/ppermute | solution.py:174
  36.1 1.6 collective-permute-start.11
  39.6 21.5 %collective-permute-done.8.refs_0_ = bf16[136,2048]{1,0:T(8,128)(2,1)S(1)} collective-permute-done((bf16[136,2048]{1,0:T(8,128)(2,1)S(1)}, bf16[136,2048]{1,0:T(8,128)(2,1)S(1)}, u32[]{:S(2)}, u32[]{:S(2)}) %collective-permute-start.8) | collective-permute-done | bytes 557088 | tf_op jit(solution)/shard_map/ppermute | solution.py:174
  61.1 2.0 collective-permute-done.9.refs_1_
  63.7 3.3 %collective-permute-done.11.refs_2_ = bf16[160,2048]{1,0:T(8,128)(2,1)S(1)} collective-permute-done((bf16[160,2048]{1,0:T(8,128)(2,1)S(1)}, bf16[160,2048]{1,0:T(8,128)(2,1)S(1)}, u32[]{:S(2)}, u32[]{:S(2)}) %collective-permute-start.11) | collective-permute-done | bytes 655392 | tf_op jit(solution)/shard_map/ppermute | solution.py:177
  68.2 1.5 collective-permute-start.14
  69.7 1.9 copy-done.1
  71.6 1.9 copy-done.3
  73.5 6.3 %shard_map.70 = (bf16[160,2048]{1,0:T(8,128)(2,1)S(1)}, bf16[160,2048]{1,0:T(8,128)(2,1)S(1)}, bf16[160,2048]{1,0:T(8,128)(2,1)S(1)}, bf16[160,2048]{1,0:T(8,128)(2,1)S(1)}) custom-call(bf16[160,2048]{1,0:T(8,128)(2,1)S(1)} %get-tuple-element.105.refs_0_, bf16[160,2048]{1,0:T(8,128)(2,1)S(1)} %collective-permute-done.10.refs_1_, ...), custom_call_target="tpu_custom_call" | custom-call | flops 1000 | bytes 1000 | tf_op jit(solution)/shard_map/pallas_call | solution.py:195
  79.7 1.6 collective-permute-start.16
  81.8 1.5 collective-permute-start.18
  83.3 1.4 collective-permute-start.15
  85.3 33.2 %collective-permute-done.15.refs_3_ = bf16[80,2048]{1,0:T(8,128)(2,1)S(1)} collective-permute-done((bf16[80,2048]{1,0:T(8,128)(2,1)S(1)}, bf16[80,2048]{1,0:T(8,128)(2,1)S(1)}, u32[]{:S(2)}, u32[]{:S(2)}) %collective-permute-start.15) | collective-permute-done | bytes 327712 | tf_op jit(solution)/shard_map/ppermute | solution.py:177
  118.5 4.8 %collective-permute-done.13.refs_1_ = bf16[80,2048]{1,0:T(8,128)(2,1)S(1)} collective-permute-done((bf16[80,2048]{1,0:T(8,128)(2,1)S(1)}, bf16[80,2048]{1,0:T(8,128)(2,1)S(1)}, u32[]{:S(2)}, u32[]{:S(2)}) %collective-permute-start.13) | collective-permute-done | bytes 327712 | tf_op jit(solution)/shard_map/ppermute | solution.py:177
  123.3 3.2 %shard_map.69 = (bf16[80,2048]{1,0:T(8,128)(2,1)S(1)}, bf16[80,2048]{1,0:T(8,128)(2,1)S(1)}, bf16[80,2048]{1,0:T(8,128)(2,1)S(1)}, bf16[80,2048]{1,0:T(8,128)(2,1)S(1)}) custom-call(bf16[80,2048]{1,0:T(8,128)(2,1)S(1)} %get-tuple-element.97.refs_0_, bf16[80,2048]{1,0:T(8,128)(2,1)S(1)} %collective-permute-done.13.refs_1_, ...), custom_call_target="tpu_custom_call" | custom-call | flops 1000 | bytes 1000 | tf_op jit(solution)/shard_map/pallas_call | solution.py:195
  126.6 2.8 %shard_map.71 = (bf16[256,2048]{1,0:T(8,128)(2,1)S(1)}, bf16[256,2048]{1,0:T(8,128)(2,1)S(1)}) custom-call(bf16[136,2048]{1,0:T(8,128)(2,1)S(1)} %collective-permute-done.4.refs_0_, bf16[136,2048]{1,0:T(8,128)(2,1)S(1)} %collective-permute-done.5.refs_1_, bf16[136,2048]{1,0:T(8,128)(2,1)S(1)} %collective-permute-done.6.refs_2_, ...), custom_call_target="tpu_custom_call" | custom-call | flops 1000 | bytes 1000 | tf_op jit(solution)/shard_map/pallas_call | solution.py:207
  129.4 1.5 collective-permute-start.19
  131.6 1.4 collective-permute-start.21
  133.0 3.4 %shard_map.67 = (bf16[80,2048]{1,0:T(8,128)(2,1)S(1)}, bf16[80,2048]{1,0:T(8,128)(2,1)S(1)}, bf16[80,2048]{1,0:T(8,128)(2,1)S(1)}, bf16[80,2048]{1,0:T(8,128)(2,1)S(1)}) custom-call(bf16[96,2048]{1,0:T(8,128)(2,1)S(1)} %get-tuple-element.81.refs_0_.refs_4_.refs_2_, bf16[96,2048]{1,0:T(8,128)(2,1)S(1)} %collective-permute-done.1.refs_1_.refs_5_.refs_3_, ...), custom_call_target="tpu_custom_call" | custom-call | flops 1000 | bytes 1000 | tf_op jit(solution)/shard_map/pallas_call | solution.py:195
  136.4 3.6 %collective-permute-done.19.refs_7_ = bf16[80,2048]{1,0:T(8,128)(2,1)S(1)} collective-permute-done((bf16[80,2048]{1,0:T(8,128)(2,1)S(1)}, bf16[80,2048]{1,0:T(8,128)(2,1)S(1)}, u32[]{:S(2)}, u32[]{:S(2)}) %collective-permute-start.19) | collective-permute-done | bytes 327712 | tf_op jit(solution)/shard_map/ppermute | solution.py:177
  140.0 7.8 %collective-permute-done.20.refs_8_ = bf16[80,2048]{1,0:T(8,128)(2,1)S(1)} collective-permute-done((bf16[80,2048]{1,0:T(8,128)(2,1)S(1)}, bf16[80,2048]{1,0:T(8,128)(2,1)S(1)}, u32[]{:S(2)}, u32[]{:S(2)}) %collective-permute-start.20) | collective-permute-done | bytes 327712 | tf_op jit(solution)/shard_map/ppermute | solution.py:177
  148.7 1.7 collective-permute-start.27
  150.5 2.2 %collective-permute-start.26 = (bf16[128,2048]{1,0:T(8,128)(2,1)S(1)}, bf16[128,2048]{1,0:T(8,128)(2,1)S(1)}, u32[]{:S(2)}, u32[]{:S(2)}) collective-permute-start(bf16[128,2048]{1,0:T(8,128)(2,1)S(1)} %get-tuple-element.140), channel_id=1, source_target_pairs={{0,24},{8,0},{16,8},{24,16},{1,25},{9,1},{17,9},{25,17},{2,26},{10... | collective-permute-start | bytes 1572872 | tf_op jit(solution)/shard_map/ppermute | solution.py:174
  155.3 1.5 collective-permute-done.22.refs_7_
  156.8 1.5 collective-permute-start.24
  158.3 12.9 %collective-permute-done.23.refs_8_ = bf16[80,2048]{1,0:T(8,128)(2,1)S(1)} collective-permute-done((bf16[80,2048]{1,0:T(8,128)(2,1)S(1)}, bf16[80,2048]{1,0:T(8,128)(2,1)S(1)}, u32[]{:S(2)}, u32[]{:S(2)}) %collective-permute-start.23) | collective-permute-done | bytes 327712 | tf_op jit(solution)/shard_map/ppermute | solution.py:177
  171.2 3.1 %collective-permute-done.26 = bf16[128,2048]{1,0:T(8,128)(2,1)S(1)} collective-permute-done((bf16[128,2048]{1,0:T(8,128)(2,1)S(1)}, bf16[128,2048]{1,0:T(8,128)(2,1)S(1)}, u32[]{:S(2)}, u32[]{:S(2)}) %collective-permute-start.26) | collective-permute-done | bytes 524320 | tf_op jit(solution)/shard_map/ppermute | solution.py:174
  177.7 24.5 %collective-permute-done.30 = bf16[128,2048]{1,0:T(8,128)(2,1)S(1)} collective-permute-done((bf16[128,2048]{1,0:T(8,128)(2,1)S(1)}, bf16[128,2048]{1,0:T(8,128)(2,1)S(1)}, u32[]{:S(2)}, u32[]{:S(2)}) %collective-permute-start.30) | collective-permute-done | bytes 524320 | tf_op jit(solution)/shard_map/ppermute | solution.py:174
  (59 shorter events, 20.8 us)
Async XLA Ops:
  0.0 69.7 %copy-start = (bf16[1,2048,768]{2,1,0:T(8,128)(2,1)S(1)}, bf16[1,2048,768]{2,1,0:T(8,128)(2,1)}, u32[]{:S(2)}) copy-start(bf16[1,2048,768]{2,1,0:T(8,128)(2,1)} %param.9) | copy-start | bytes 9437188
  2.6 5.2 %collective-permute-start = (bf16[136,2048]{1,0:T(8,128)(2,1)S(1)}, bf16[136,2048]{1,0:T(8,128)(2,1)S(1)}, u32[]{:S(2)}, u32[]{:S(2)}) collective-permute-start(bf16[136,2048]{1,0:T(8,128)(2,1)S(1)} %shard_map.64.refs_0_), channel_id=1, source_target_pairs={{0,1},{1,0},{2,3},{3,2},{4,5},{5,4},{6,7},{7,6},{8,9},{9,8},{10,11... | collective-permute-start | bytes 1671176 | tf_op jit(solution)/shard_map/ppermute | solution.py:177
  3.2 17.7 %collective-permute-start.6 = (bf16[136,2048]{1,0:T(8,128)(2,1)S(1)}, bf16[136,2048]{1,0:T(8,128)(2,1)S(1)}, u32[]{:S(2)}, u32[]{:S(2)}) collective-permute-start(bf16[136,2048]{1,0:T(8,128)(2,1)S(1)} %shard_map.64.refs_0_), channel_id=1, source_target_pairs={{0,24},{8,0},{16,8},{24,16},{1,25},{9,1},{17,9},{25,17},{2,26},{10... | collective-permute-start | bytes 1671176 | tf_op jit(solution)/shard_map/ppermute | solution.py:174
  7.8 25.3 %collective-permute-start.4 = (bf16[136,2048]{1,0:T(8,128)(2,1)S(1)}, bf16[136,2048]{1,0:T(8,128)(2,1)S(1)}, u32[]{:S(2)}, u32[]{:S(2)}) collective-permute-start(bf16[136,2048]{1,0:T(8,128)(2,1)S(1)} %shard_map.64.refs_0_), channel_id=1, source_target_pairs={{0,8},{8,16},{16,24},{24,0},{1,9},{9,17},{17,25},{25,1},{2,10},{10... | collective-permute-start | bytes 1671176 | tf_op jit(solution)/shard_map/ppermute | solution.py:174
  8.4 24.7 %collective-permute-start.1 = (bf16[96,2048]{1,0:T(8,128)(2,1)S(1)}, bf16[96,2048]{1,0:T(8,128)(2,1)S(1)}, u32[]{:S(2)}, u32[]{:S(2)}) collective-permute-start(bf16[96,2048]{1,0:T(8,128)(2,1)S(1)} %get-tuple-element.73), channel_id=1, source_target_pairs={{0,2},{1,3},{2,0},{3,1},{4,6},{5,7},{6,4},{7,5},{8,10},{9,11},{10,... | collective-permute-start | bytes 1179656 | tf_op jit(solution)/shard_map/ppermute | solution.py:177
  10.0 23.2 %collective-permute-start.2 = (bf16[96,2048]{1,0:T(8,128)(2,1)S(1)}, bf16[96,2048]{1,0:T(8,128)(2,1)S(1)}, u32[]{:S(2)}, u32[]{:S(2)}) collective-permute-start(bf16[96,2048]{1,0:T(8,128)(2,1)S(1)} %get-tuple-element.74), channel_id=1, source_target_pairs={{0,4},{1,5},{2,6},{3,7},{4,0},{5,1},{6,2},{7,3},{8,12},{9,13},{10,... | collective-permute-start | bytes 1179656 | tf_op jit(solution)/shard_map/ppermute | solution.py:177
  11.5 21.7 %collective-permute-start.3 = (bf16[96,2048]{1,0:T(8,128)(2,1)S(1)}, bf16[96,2048]{1,0:T(8,128)(2,1)S(1)}, u32[]{:S(2)}, u32[]{:S(2)}) collective-permute-start(bf16[96,2048]{1,0:T(8,128)(2,1)S(1)} %get-tuple-element.75), channel_id=1, source_target_pairs={{0,6},{1,7},{2,4},{3,5},{4,2},{5,3},{6,0},{7,1},{8,14},{9,15},{10,... | collective-permute-start | bytes 1179656 | tf_op jit(solution)/shard_map/ppermute | solution.py:177
  20.8 13.2 %collective-permute-start.7 = (bf16[136,2048]{1,0:T(8,128)(2,1)S(1)}, bf16[136,2048]{1,0:T(8,128)(2,1)S(1)}, u32[]{:S(2)}, u32[]{:S(2)}) collective-permute-start(bf16[136,2048]{1,0:T(8,128)(2,1)S(1)} %collective-permute-done.6.refs_2_), channel_id=1, source_target_pairs={{0,1},{1,0},{2,3},{3,2},{4,5},{5,4},{6,7},{7,6},{8,9},{9,8},{10,11... | collective-permute-start | bytes 1671176 | tf_op jit(solution)/shard_map/ppermute | solution.py:177
  33.2 2.0 collective-permute-start.5
  33.2 27.9 %collective-permute-start.8 = (bf16[136,2048]{1,0:T(8,128)(2,1)S(1)}, bf16[136,2048]{1,0:T(8,128)(2,1)S(1)}, u32[]{:S(2)}, u32[]{:S(2)}) collective-permute-start(bf16[136,2048]{1,0:T(8,128)(2,1)S(1)} %shard_map.64.refs_0_), channel_id=1, source_target_pairs={{0,16},{8,24},{16,0},{24,8},{1,17},{9,25},{17,1},{25,9},{2,18},{10... | collective-permute-start | bytes 1671176 | tf_op jit(solution)/shard_map/ppermute | solution.py:174
  36.1 30.9 %collective-permute-start.11 = (bf16[160,2048]{1,0:T(8,128)(2,1)S(1)}, bf16[160,2048]{1,0:T(8,128)(2,1)S(1)}, u32[]{:S(2)}, u32[]{:S(2)}) collective-permute-start(bf16[160,2048]{1,0:T(8,128)(2,1)S(1)} %get-tuple-element.95), channel_id=1, source_target_pairs={{0,4},{1,5},{2,6},{3,7},{4,0},{5,1},{6,2},{7,3},{8,12},{9,13},{10,... | collective-permute-start | bytes 1966088 | tf_op jit(solution)/shard_map/ppermute | solution.py:177
  37.7 29.3 %collective-permute-start.12 = (bf16[160,2048]{1,0:T(8,128)(2,1)S(1)}, bf16[160,2048]{1,0:T(8,128)(2,1)S(1)}, u32[]{:S(2)}, u32[]{:S(2)}) collective-permute-start(bf16[160,2048]{1,0:T(8,128)(2,1)S(1)} %get-tuple-element.96), channel_id=1, source_target_pairs={{0,6},{1,7},{2,4},{3,5},{4,2},{5,3},{6,0},{7,1},{8,14},{9,15},{10,... | collective-permute-start | bytes 1966088 | tf_op jit(solution)/shard_map/ppermute | solution.py:177
  39.1 29.1 %collective-permute-start.10 = (bf16[160,2048]{1,0:T(8,128)(2,1)S(1)}, bf16[160,2048]{1,0:T(8,128)(2,1)S(1)}, u32[]{:S(2)}, u32[]{:S(2)}) collective-permute-start(bf16[160,2048]{1,0:T(8,128)(2,1)S(1)} %get-tuple-element.80), channel_id=1, source_target_pairs={{0,2},{1,3},{2,0},{3,1},{4,6},{5,7},{6,4},{7,5},{8,10},{9,11},{10,... | collective-permute-start | bytes 1966088 | tf_op jit(solution)/shard_map/ppermute | solution.py:177
  61.1 2.0 collective-permute-start.9
  68.2 16.6 %collective-permute-start.14 = (bf16[80,2048]{1,0:T(8,128)(2,1)S(1)}, bf16[80,2048]{1,0:T(8,128)(2,1)S(1)}, u32[]{:S(2)}, u32[]{:S(2)}) collective-permute-start(bf16[80,2048]{1,0:T(8,128)(2,1)S(1)} %get-tuple-element.99), channel_id=1, source_target_pairs={{0,4},{1,5},{2,6},{3,7},{4,0},{5,1},{6,2},{7,3},{8,12},{9,13},{10,... | collective-permute-start | bytes 983048 | tf_op jit(solution)/shard_map/ppermute | solution.py:177
  79.7 46.8 %collective-permute-start.16 = (bf16[160,2048]{1,0:T(8,128)(2,1)S(1)}, bf16[160,2048]{1,0:T(8,128)(2,1)S(1)}, u32[]{:S(2)}, u32[]{:S(2)}) collective-permute-start(bf16[160,2048]{1,0:T(8,128)(2,1)S(1)} %get-tuple-element.110), channel_id=1, source_target_pairs={{0,2},{1,3},{2,0},{3,1},{4,6},{5,7},{6,4},{7,5},{8,10},{9,11},{10,... | collective-permute-start | bytes 1966088 | tf_op jit(solution)/shard_map/ppermute | solution.py:177
  81.3 45.2 %collective-permute-start.17 = (bf16[160,2048]{1,0:T(8,128)(2,1)S(1)}, bf16[160,2048]{1,0:T(8,128)(2,1)S(1)}, u32[]{:S(2)}, u32[]{:S(2)}) collective-permute-start(bf16[160,2048]{1,0:T(8,128)(2,1)S(1)} %get-tuple-element.111), channel_id=1, source_target_pairs={{0,4},{1,5},{2,6},{3,7},{4,0},{5,1},{6,2},{7,3},{8,12},{9,13},{10,... | collective-permute-start | bytes 1966088 | tf_op jit(solution)/shard_map/ppermute | solution.py:177
  81.8 44.8 %collective-permute-start.18 = (bf16[160,2048]{1,0:T(8,128)(2,1)S(1)}, bf16[160,2048]{1,0:T(8,128)(2,1)S(1)}, u32[]{:S(2)}, u32[]{:S(2)}) collective-permute-start(bf16[160,2048]{1,0:T(8,128)(2,1)S(1)} %get-tuple-element.112), channel_id=1, source_target_pairs={{0,6},{1,7},{2,4},{3,5},{4,2},{5,3},{6,0},{7,1},{8,14},{9,15},{10,... | collective-permute-start | bytes 1966088 | tf_op jit(solution)/shard_map/ppermute | solution.py:177
  83.3 35.2 %collective-permute-start.15 = (bf16[80,2048]{1,0:T(8,128)(2,1)S(1)}, bf16[80,2048]{1,0:T(8,128)(2,1)S(1)}, u32[]{:S(2)}, u32[]{:S(2)}) collective-permute-start(bf16[80,2048]{1,0:T(8,128)(2,1)S(1)} %get-tuple-element.100), channel_id=1, source_target_pairs={{0,6},{1,7},{2,4},{3,5},{4,2},{5,3},{6,0},{7,1},{8,14},{9,15},{10,... | collective-permute-start | bytes 983048 | tf_op jit(solution)/shard_map/ppermute | solution.py:177
  84.8 38.6 %collective-permute-start.13 = (bf16[80,2048]{1,0:T(8,128)(2,1)S(1)}, bf16[80,2048]{1,0:T(8,128)(2,1)S(1)}, u32[]{:S(2)}, u32[]{:S(2)}) collective-permute-start(bf16[80,2048]{1,0:T(8,128)(2,1)S(1)} %get-tuple-element.98), channel_id=1, source_target_pairs={{0,2},{1,3},{2,0},{3,1},{4,6},{5,7},{6,4},{7,5},{8,10},{9,11},{10,... | collective-permute-start | bytes 983048 | tf_op jit(solution)/shard_map/ppermute | solution.py:177
  129.4 19.0 %collective-permute-start.25 = (bf16[256,2048]{1,0:T(8,128)(2,1)S(1)}, bf16[256,2048]{1,0:T(8,128)(2,1)S(1)}, u32[]{:S(2)}, u32[]{:S(2)}) collective-permute-start(bf16[256,2048]{1,0:T(8,128)(2,1)S(1)} %get-tuple-element.126), channel_id=1, source_target_pairs={{0,1},{1,0},{2,3},{3,2},{4,5},{5,4},{6,7},{7,6},{8,9},{9,8},{10,11... | collective-permute-start | bytes 3145736 | tf_op jit(solution)/shard_map/ppermute | solution.py:177
  129.4 10.6 %collective-permute-start.19 = (bf16[80,2048]{1,0:T(8,128)(2,1)S(1)}, bf16[80,2048]{1,0:T(8,128)(2,1)S(1)}, u32[]{:S(2)}, u32[]{:S(2)}) collective-permute-start(bf16[80,2048]{1,0:T(8,128)(2,1)S(1)} %get-tuple-element.114), channel_id=1, source_target_pairs={{0,2},{1,3},{2,0},{3,1},{4,6},{5,7},{6,4},{7,5},{8,10},{9,11},{10,... | collective-permute-start | bytes 983048 | tf_op jit(solution)/shard_map/ppermute | solution.py:177
  131.0 16.8 %collective-permute-start.20 = (bf16[80,2048]{1,0:T(8,128)(2,1)S(1)}, bf16[80,2048]{1,0:T(8,128)(2,1)S(1)}, u32[]{:S(2)}, u32[]{:S(2)}) collective-permute-start(bf16[80,2048]{1,0:T(8,128)(2,1)S(1)} %get-tuple-element.115), channel_id=1, source_target_pairs={{0,4},{1,5},{2,6},{3,7},{4,0},{5,1},{6,2},{7,3},{8,12},{9,13},{10,... | collective-permute-start | bytes 983048 | tf_op jit(solution)/shard_map/ppermute | solution.py:177
  131.6 16.2 %collective-permute-start.21 = (bf16[80,2048]{1,0:T(8,128)(2,1)S(1)}, bf16[80,2048]{1,0:T(8,128)(2,1)S(1)}, u32[]{:S(2)}, u32[]{:S(2)}) collective-permute-start(bf16[80,2048]{1,0:T(8,128)(2,1)S(1)} %get-tuple-element.116), channel_id=1, source_target_pairs={{0,6},{1,7},{2,4},{3,5},{4,2},{5,3},{6,0},{7,1},{8,14},{9,15},{10,... | collective-permute-start | bytes 983048 | tf_op jit(solution)/shard_map/ppermute | solution.py:177
  147.8 9.0 %collective-permute-start.22 = (bf16[80,2048]{1,0:T(8,128)(2,1)S(1)}, bf16[80,2048]{1,0:T(8,128)(2,1)S(1)}, u32[]{:S(2)}, u32[]{:S(2)}) collective-permute-start(bf16[80,2048]{1,0:T(8,128)(2,1)S(1)} %get-tuple-element.118), channel_id=1, source_target_pairs={{0,2},{1,3},{2,0},{3,1},{4,6},{5,7},{6,4},{7,5},{8,10},{9,11},{10,... | collective-permute-start | bytes 983048 | tf_op jit(solution)/shard_map/ppermute | solution.py:177
  148.7 22.5 %collective-permute-start.27 = (bf16[128,2048]{1,0:T(8,128)(2,1)S(1)}, bf16[128,2048]{1,0:T(8,128)(2,1)S(1)}, u32[]{:S(2)}, u32[]{:S(2)}) collective-permute-start(bf16[128,2048]{1,0:T(8,128)(2,1)S(1)} %get-tuple-element.139), channel_id=1, source_target_pairs={{0,8},{8,16},{16,24},{24,0},{1,9},{9,17},{17,25},{25,1},{2,10},{10... | collective-permute-start | bytes 1572872 | tf_op jit(solution)/shard_map/ppermute | solution.py:174
  150.5 23.9 %collective-permute-start.26 = (bf16[128,2048]{1,0:T(8,128)(2,1)S(1)}, bf16[128,2048]{1,0:T(8,128)(2,1)S(1)}, u32[]{:S(2)}, u32[]{:S(2)}) collective-permute-start(bf16[128,2048]{1,0:T(8,128)(2,1)S(1)} %get-tuple-element.140), channel_id=1, source_target_pairs={{0,24},{8,0},{16,8},{24,16},{1,25},{9,1},{17,9},{25,17},{2,26},{10... | collective-permute-start | bytes 1572872 | tf_op jit(solution)/shard_map/ppermute | solution.py:174
  154.0 21.8 %collective-permute-start.29 = (bf16[128,2048]{1,0:T(8,128)(2,1)S(1)}, bf16[128,2048]{1,0:T(8,128)(2,1)S(1)}, u32[]{:S(2)}, u32[]{:S(2)}) collective-permute-start(bf16[128,2048]{1,0:T(8,128)(2,1)S(1)} %get-tuple-element.138), channel_id=1, source_target_pairs={{0,1},{1,0},{2,3},{3,2},{4,5},{5,4},{6,7},{7,6},{8,9},{9,8},{10,11... | collective-permute-start | bytes 1572872 | tf_op jit(solution)/shard_map/ppermute | solution.py:177
  154.0 17.1 %collective-permute-start.23 = (bf16[80,2048]{1,0:T(8,128)(2,1)S(1)}, bf16[80,2048]{1,0:T(8,128)(2,1)S(1)}, u32[]{:S(2)}, u32[]{:S(2)}) collective-permute-start(bf16[80,2048]{1,0:T(8,128)(2,1)S(1)} %get-tuple-element.119), channel_id=1, source_target_pairs={{0,4},{1,5},{2,6},{3,7},{4,0},{5,1},{6,2},{7,3},{8,12},{9,13},{10,... | collective-permute-start | bytes 983048 | tf_op jit(solution)/shard_map/ppermute | solution.py:177
  156.8 14.4 %collective-permute-start.24 = (bf16[80,2048]{1,0:T(8,128)(2,1)S(1)}, bf16[80,2048]{1,0:T(8,128)(2,1)S(1)}, u32[]{:S(2)}, u32[]{:S(2)}) collective-permute-start(bf16[80,2048]{1,0:T(8,128)(2,1)S(1)} %get-tuple-element.120), channel_id=1, source_target_pairs={{0,6},{1,7},{2,4},{3,5},{4,2},{5,3},{6,0},{7,1},{8,14},{9,15},{10,... | collective-permute-start | bytes 983048 | tf_op jit(solution)/shard_map/ppermute | solution.py:177
  175.7 2.0 collective-permute-start.28
  175.9 26.3 %collective-permute-start.30 = (bf16[128,2048]{1,0:T(8,128)(2,1)S(1)}, bf16[128,2048]{1,0:T(8,128)(2,1)S(1)}, u32[]{:S(2)}, u32[]{:S(2)}) collective-permute-start(bf16[128,2048]{1,0:T(8,128)(2,1)S(1)} %add_convert_fusion.1), channel_id=1, source_target_pairs={{0,16},{8,24},{16,0},{24,8},{1,17},{9,25},{17,1},{25,9},{2,18},{10... | collective-permute-start | bytes 1572872 | tf_op jit(solution)/shard_map/ppermute | solution.py:174
  (7 other events, 62.6 us)

commit v5 on v4

--- a/solution.py
+++ b/solution.py
@@ -213,42 +213,49 @@
             for i in range(n // 2)
         ]
 
-    half = layers // 2
-    groups = [sorted({d, layers - d}) for d in range(1, half + 1)]
+    far = layers // 2
+    out_turns = list(range(layers))
+    back_turns = [far] + [d for d in out_turns if d not in (0, far)] + [0]
 
     own = call(functools.partial(pad_kernel, z), shape(z.toks + z.extra), 3)(
         tokens, expert_ids.T, router_weight.T
     )
-    pairs, slots, results = {}, {}, {}
-    coming = [along(own, d) for d in groups[0]]
-    pairs[0] = [own, across(own, 1)]
-    slots[0] = slabs_across(pick(pairs[0], True))
-    riders = slots[0]
-    for g in range(1, len(groups) + 1):
-        blocks = coming
-        if g < len(groups):
-            source = after([own], *blocks, *slots[g - 1])[0]
-            coming = [along(source, d) for d in groups[g]]
-        pairs[g] = [b for block in blocks for b in (block, across(block, 1))]
-        slabs = after(pick(pairs[g], False), *slots[g - 1])
-        slots[g] = slabs_across(slabs)
-        results[g - 1] = expert(after(slots[g - 1], slabs[1]), len(pairs[g - 1]))
-    results[g] = expert(slots[g], len(pairs[g]))
-    turns = list(range(1, len(groups) + 1)) + [0]
-    backs, leaving, home = [], [], {}
-    for g, later in zip(turns, turns[1:] + turns[:1]):
-        rows = after(results[g], *backs) if backs else results[g]
+
+    blocks, pairs, slots, results = {0: own}, {}, {}, {}
+    for d in out_turns:
+        if d:
+            gone = slots[d - 2] if d > 1 else []
+            blocks[d] = along(after([blocks[d - 1]], *gone)[0], 1)
+        pairs[d] = [blocks[d], across(blocks[d], 1)]
+        slabs = pick(pairs[d], d == 1)
+        if d:
+            done = results[d - 2][:1] if d > 1 else []
+            ready = [after([s], b, *done)[0] for s, b in zip(slabs, slots[d - 1])]
+            results[d - 1] = expert(after(slots[d - 1], slabs[0]), 2)
+        else:
+            ready = slabs
+        slots[d] = slabs_across(ready)
+    riders = slots[1]
+    results[d] = expert(after(slots[d], results[d - 1][0]), 2)
+
+    backs, home, leaving = slots[d], {}, {}
+    for i, d in enumerate(back_turns):
+        first = [leaving[back_turns[i - 2]]] if i > 1 else [results[layers - 2 + i][0]]
+        if d == 0:
+            first = first + [home[far]]
+        rows = [after([r], b, *first)[0] for r, b in zip(results[d], backs)]
         backs = slabs_across(rows)
-        if g:
-            ready = after(backs, results[later][1], *leaving)
-            sums = mix(pairs[g], ready)
-            leaving = [part.astype(BF16) for part in sums]
-            for d, part in zip(groups[g - 1], leaving):
-                home[d] = along(part, layers - d)
-        else:
-            early = [home[d] for group in groups[:-1] for d in group]
-            total = mix(pairs[0], after(backs, *early))[0]
-    for d in home:
+        last = leaving[back_turns[i - 1]] if i else results[layers - 1][0]
+        if d:
+            part = mix(pairs[d], after(backs, last))[0]
+            leaving[d] = part.astype(BF16)
+            way = layers - d
+            if d == far:
+                home[d] = along(along(leaving[d], way // 2), way - way // 2)
+            else:
+                home[d] = along(leaving[d], way)
+    total = mix(pairs[0], after(backs, last))[0]
+    for d in out_turns[1:]:
         total = total + home[d].astype(F32)
     return total.astype(BF16)
 

time: 204 us -> 198 us (0.971)
  waiting for transfers between devices: 142 us -> 134 us
  starting transfers between devices: 32.2 us -> 35 us
    ppermute x6 -> x7, waiting for transfers between devices: 70.3 us -> 46.9 us  [along(): lax.ppermute(array, 'expert', [(i, (i + d) % layers) for i in range(layer...]
    ppermute x25 -> x32, waiting for transfers between devices: 72 us -> 87.1 us  [across(): lax.ppermute(array, 'zero', [(i, i ^ o) for i in range(near)])]
    ppermute x25 -> x32, starting transfers between devices: 21.8 us -> 28.5 us  [across(): lax.ppermute(array, 'zero', [(i, i ^ o) for i in range(near)])]
    ppermute x6 -> x7, starting transfers between devices: 10.5 us -> 6.46 us  [along(): lax.ppermute(array, 'expert', [(i, (i + d) % layers) for i in range(layer...]
    pallas_call x3 -> x4, Pallas kernels: 5.44 us -> 5.36 us  [mix(): call(functools.partial(mix_kernel, z, n), [shape(n // 2 * z.toks)] * 2, n...]
    pallas_call x3 -> x4, Pallas kernels: 12.9 us -> 12.9 us  [expert(): call(functools.partial(expert_kernel, z, rows), [shape(rows)] * z.chips,...]
    unnamed x16 -> x14, local copies, waits for them, and re-layouts: 6.39 us -> 6.38 us
  transfers between devices with their start and end apart: 31 -> 39, of which waited for: 16 -> 19; matrix products, arithmetic and copies ran while one was open for 0% -> 0% of each run, Pallas kernels for 9% -> 10%
where the time goes in v5:
time: 198 us
  waiting for transfers between devices  134 us (68%)
  starting transfers between devices  35 us (18%)
  Pallas kernels  20.7 us (10%)
  local copies, waits for them, and re-layouts  6.38 us (3%)
    ppermute x32, waiting for transfers between devices, across(): lax.ppermute(array, 'zero', [(i, i ^ o) for i in range(near)])  87.1 us
    ppermute x7, waiting for transfers between devices, along(): lax.ppermute(array, 'expert', [(i, (i + d) % layers) for i in range(layer...  46.9 us
    ppermute x32, starting transfers between devices, across(): lax.ppermute(array, 'zero', [(i, i ^ o) for i in range(near)])  28.5 us
    pallas_call x4, Pallas kernels, expert(): call(functools.partial(expert_kernel, z, rows), [shape(rows)] * z.chips,...  12.9 us
    ppermute x7, starting transfers between devices, along(): lax.ppermute(array, 'expert', [(i, (i + d) % layers) for i in range(layer...  6.46 us
    unnamed x14, local copies, waits for them, and re-layouts  6.38 us
    pallas_call x4, Pallas kernels, mix(): call(functools.partial(mix_kernel, z, n), [shape(n // 2 * z.toks)] * 2, n...  5.36 us
  transfers between devices with their start and end apart: 39, of which 19 were waited for; matrix products, arithmetic and copies ran while one was open for 0% of the time, Pallas kernels for 10%

profile of v5, /device:TPU:0, one launch (start us, length us, event | category | flops | bytes accessed | tf_op | source)
XLA Modules:
  0.0 197.8 jit_solution(7514354208888630976)
XLA Ops:
  2.6 3.1 %collective-permute-start.1 = (bf16[136,2048]{1,0:T(8,128)(2,1)S(1)}, bf16[136,2048]{1,0:T(8,128)(2,1)S(1)}, u32[]{:S(2)}, u32[]{:S(2)}) collective-permute-start(bf16[136,2048]{1,0:T(8,128)(2,1)S(1)} %shard_map.64.refs_0_), channel_id=1, source_target_pairs={{0,8},{8,16},{16,24},{24,0},{1,9},{9,17},{17,25},{25,1},{2,10},{10... | collective-permute-start | bytes 1671176 | tf_op jit(solution)/shard_map/ppermute | solution.py:174
  5.7 14.6 %collective-permute-done.1.refs_0_ = bf16[136,2048]{1,0:T(8,128)(2,1)S(1)} collective-permute-done((bf16[136,2048]{1,0:T(8,128)(2,1)S(1)}, bf16[136,2048]{1,0:T(8,128)(2,1)S(1)}, u32[]{:S(2)}, u32[]{:S(2)}) %collective-permute-start.1) | collective-permute-done | bytes 557088 | tf_op jit(solution)/shard_map/ppermute | solution.py:174
  21.0 1.6 collective-permute-start.3
  24.5 7.0 %collective-permute-done.3.refs_1_ = bf16[80,2048]{1,0:T(8,128)(2,1)S(1)} collective-permute-done((bf16[80,2048]{1,0:T(8,128)(2,1)S(1)}, bf16[80,2048]{1,0:T(8,128)(2,1)S(1)}, u32[]{:S(2)}, u32[]{:S(2)}) %collective-permute-start.3) | collective-permute-done | bytes 327712 | tf_op jit(solution)/shard_map/ppermute | solution.py:177
  31.6 7.8 %collective-permute-done.5.refs_2_ = bf16[80,2048]{1,0:T(8,128)(2,1)S(1)} collective-permute-done((bf16[80,2048]{1,0:T(8,128)(2,1)S(1)}, bf16[80,2048]{1,0:T(8,128)(2,1)S(1)}, u32[]{:S(2)}, u32[]{:S(2)}) %collective-permute-start.5) | collective-permute-done | bytes 327712 | tf_op jit(solution)/shard_map/ppermute | solution.py:177
  40.0 1.6 collective-permute-start.8
  43.6 11.7 %collective-permute-done.9.refs_0_ = bf16[136,2048]{1,0:T(8,128)(2,1)S(1)} collective-permute-done((bf16[136,2048]{1,0:T(8,128)(2,1)S(1)}, bf16[136,2048]{1,0:T(8,128)(2,1)S(1)}, u32[]{:S(2)}, u32[]{:S(2)}) %collective-permute-start.9) | collective-permute-done | bytes 557088 | tf_op jit(solution)/shard_map/ppermute | solution.py:174
  55.3 4.7 %collective-permute-done.6.refs_2_.refs_4_ = bf16[96,2048]{1,0:T(8,128)(2,1)S(1)} collective-permute-done((bf16[96,2048]{1,0:T(8,128)(2,1)S(1)}, bf16[96,2048]{1,0:T(8,128)(2,1)S(1)}, u32[]{:S(2)}, u32[]{:S(2)}) %collective-permute-start.6) | collective-permute-done | bytes 393248 | tf_op jit(solution)/shard_map/ppermute | solution.py:177
  61.0 15.3 %collective-permute-done.10.refs_0_ = bf16[136,2048]{1,0:T(8,128)(2,1)S(1)} collective-permute-done((bf16[136,2048]{1,0:T(8,128)(2,1)S(1)}, bf16[136,2048]{1,0:T(8,128)(2,1)S(1)}, u32[]{:S(2)}, u32[]{:S(2)}) %collective-permute-start.10) | collective-permute-done | bytes 557088 | tf_op jit(solution)/shard_map/ppermute | solution.py:174
  76.3 1.9 copy-done.1
  78.2 1.9 copy-done.3
  80.1 3.2 %shard_map.67 = (bf16[80,2048]{1,0:T(8,128)(2,1)S(1)}, bf16[80,2048]{1,0:T(8,128)(2,1)S(1)}, bf16[80,2048]{1,0:T(8,128)(2,1)S(1)}, bf16[80,2048]{1,0:T(8,128)(2,1)S(1)}) custom-call(bf16[80,2048]{1,0:T(8,128)(2,1)S(1)} %get-tuple-element.119.refs_0_, bf16[80,2048]{1,0:T(8,128)(2,1)S(1)} %collective-permute-done.3.refs_1_, ...), custom_call_target="tpu_custom_call" | custom-call | flops 1000 | bytes 1000 | tf_op jit(solution)/shard_map/pallas_call | solution.py:195
  87.5 3.2 %shard_map.70 = (bf16[80,2048]{1,0:T(8,128)(2,1)S(1)}, bf16[80,2048]{1,0:T(8,128)(2,1)S(1)}, bf16[80,2048]{1,0:T(8,128)(2,1)S(1)}, bf16[80,2048]{1,0:T(8,128)(2,1)S(1)}) custom-call(bf16[96,2048]{1,0:T(8,128)(2,1)S(1)} %get-tuple-element.129.refs_0_.refs_2_, bf16[96,2048]{1,0:T(8,128)(2,1)S(1)} %collective-permute-done.4.refs_1_.refs_3_, ...), custom_call_target="tpu_custom_call" | custom-call | flops 1000 | bytes 1000 | tf_op jit(solution)/shard_map/pallas_call | solution.py:195
  91.4 3.2 %collective-permute-done.13.refs_1_ = bf16[80,2048]{1,0:T(8,128)(2,1)S(1)} collective-permute-done((bf16[80,2048]{1,0:T(8,128)(2,1)S(1)}, bf16[80,2048]{1,0:T(8,128)(2,1)S(1)}, u32[]{:S(2)}, u32[]{:S(2)}) %collective-permute-start.13) | collective-permute-done | bytes 327712 | tf_op jit(solution)/shard_map/ppermute | solution.py:177
  95.9 6.5 %collective-permute-done.15.refs_2_ = bf16[80,2048]{1,0:T(8,128)(2,1)S(1)} collective-permute-done((bf16[80,2048]{1,0:T(8,128)(2,1)S(1)}, bf16[80,2048]{1,0:T(8,128)(2,1)S(1)}, u32[]{:S(2)}, u32[]{:S(2)}) %collective-permute-start.15) | collective-permute-done | bytes 327712 | tf_op jit(solution)/shard_map/ppermute | solution.py:177
  102.9 1.7 collective-permute-start.18
  104.5 3.2 %shard_map.71 = (bf16[80,2048]{1,0:T(8,128)(2,1)S(1)}, bf16[80,2048]{1,0:T(8,128)(2,1)S(1)}, bf16[80,2048]{1,0:T(8,128)(2,1)S(1)}, bf16[80,2048]{1,0:T(8,128)(2,1)S(1)}) custom-call(bf16[80,2048]{1,0:T(8,128)(2,1)S(1)} %get-tuple-element.147.refs_0_, bf16[80,2048]{1,0:T(8,128)(2,1)S(1)} %collective-permute-done.13.refs_1_, ...), custom_call_target="tpu_custom_call" | custom-call | flops 1000 | bytes 1000 | tf_op jit(solution)/shard_map/pallas_call | solution.py:195
  110.0 6.8 %collective-permute-done.16.refs_2_ = bf16[80,2048]{1,0:T(8,128)(2,1)S(1)} collective-permute-done((bf16[80,2048]{1,0:T(8,128)(2,1)S(1)}, bf16[80,2048]{1,0:T(8,128)(2,1)S(1)}, u32[]{:S(2)}, u32[]{:S(2)}) %collective-permute-start.16) | collective-permute-done | bytes 327712 | tf_op jit(solution)/shard_map/ppermute | solution.py:177
  116.9 2.0 %collective-permute-start.21 = (bf16[80,2048]{1,0:T(8,128)(2,1)S(1)}, bf16[80,2048]{1,0:T(8,128)(2,1)S(1)}, u32[]{:S(2)}, u32[]{:S(2)}) collective-permute-start(bf16[80,2048]{1,0:T(8,128)(2,1)S(1)} %get-tuple-element.164), channel_id=1, source_target_pairs={{0,6},{1,7},{2,4},{3,5},{4,2},{5,3},{6,0},{7,1},{8,14},{9,15},{10,... | collective-permute-start | bytes 983048 | tf_op jit(solution)/shard_map/ppermute | solution.py:177
  118.9 3.2 %shard_map.72 = (bf16[80,2048]{1,0:T(8,128)(2,1)S(1)}, bf16[80,2048]{1,0:T(8,128)(2,1)S(1)}, bf16[80,2048]{1,0:T(8,128)(2,1)S(1)}, bf16[80,2048]{1,0:T(8,128)(2,1)S(1)}) custom-call(bf16[80,2048]{1,0:T(8,128)(2,1)S(1)} %get-tuple-element.152.refs_0_, bf16[80,2048]{1,0:T(8,128)(2,1)S(1)} %collective-permute-done.14.refs_1_, ...), custom_call_target="tpu_custom_call" | custom-call | flops 1000 | bytes 1000 | tf_op jit(solution)/shard_map/pallas_call | solution.py:195
  122.7 8.2 %collective-permute-done.20.refs_8_ = bf16[80,2048]{1,0:T(8,128)(2,1)S(1)} collective-permute-done((bf16[80,2048]{1,0:T(8,128)(2,1)S(1)}, bf16[80,2048]{1,0:T(8,128)(2,1)S(1)}, u32[]{:S(2)}, u32[]{:S(2)}) %collective-permute-start.20) | collective-permute-done | bytes 327712 | tf_op jit(solution)/shard_map/ppermute | solution.py:177
  133.9 2.0 %collective-permute-start.25 = (bf16[80,2048]{1,0:T(8,128)(2,1)S(1)}, bf16[80,2048]{1,0:T(8,128)(2,1)S(1)}, u32[]{:S(2)}, u32[]{:S(2)}) collective-permute-start(bf16[80,2048]{1,0:T(8,128)(2,1)S(1)} %get-tuple-element.177), channel_id=1, source_target_pairs={{0,6},{1,7},{2,4},{3,5},{4,2},{5,3},{6,0},{7,1},{8,14},{9,15},{10,... | collective-permute-start | bytes 983048 | tf_op jit(solution)/shard_map/ppermute | solution.py:177
  136.3 6.6 %collective-permute-done.23.refs_7_ = bf16[80,2048]{1,0:T(8,128)(2,1)S(1)} collective-permute-done((bf16[80,2048]{1,0:T(8,128)(2,1)S(1)}, bf16[80,2048]{1,0:T(8,128)(2,1)S(1)}, u32[]{:S(2)}, u32[]{:S(2)}) %collective-permute-start.23) | collective-permute-done | bytes 327712 | tf_op jit(solution)/shard_map/ppermute | solution.py:177
  143.0 6.9 %collective-permute-done.24.refs_8_ = bf16[80,2048]{1,0:T(8,128)(2,1)S(1)} collective-permute-done((bf16[80,2048]{1,0:T(8,128)(2,1)S(1)}, bf16[80,2048]{1,0:T(8,128)(2,1)S(1)}, u32[]{:S(2)}, u32[]{:S(2)}) %collective-permute-start.24) | collective-permute-done | bytes 327712 | tf_op jit(solution)/shard_map/ppermute | solution.py:177
  153.1 1.8 collective-permute-start.33
  155.0 6.9 %collective-permute-done.29.refs_7_ = bf16[80,2048]{1,0:T(8,128)(2,1)S(1)} collective-permute-done((bf16[80,2048]{1,0:T(8,128)(2,1)S(1)}, bf16[80,2048]{1,0:T(8,128)(2,1)S(1)}, u32[]{:S(2)}, u32[]{:S(2)}) %collective-permute-start.29) | collective-permute-done | bytes 327712 | tf_op jit(solution)/shard_map/ppermute | solution.py:177
  161.8 7.7 %collective-permute-done.31.refs_8_ = bf16[80,2048]{1,0:T(8,128)(2,1)S(1)} collective-permute-done((bf16[80,2048]{1,0:T(8,128)(2,1)S(1)}, bf16[80,2048]{1,0:T(8,128)(2,1)S(1)}, u32[]{:S(2)}, u32[]{:S(2)}) %collective-permute-start.31) | collective-permute-done | bytes 327712 | tf_op jit(solution)/shard_map/ppermute | solution.py:177
  171.0 1.8 collective-permute-start.37
  174.5 1.8 collective-permute-start.34
  176.8 6.6 %collective-permute-done.30.refs_7_ = bf16[80,2048]{1,0:T(8,128)(2,1)S(1)} collective-permute-done((bf16[80,2048]{1,0:T(8,128)(2,1)S(1)}, bf16[80,2048]{1,0:T(8,128)(2,1)S(1)}, u32[]{:S(2)}, u32[]{:S(2)}) %collective-permute-start.30) | collective-permute-done | bytes 327712 | tf_op jit(solution)/shard_map/ppermute | solution.py:177
  183.3 6.6 %collective-permute-done.32.refs_8_ = bf16[80,2048]{1,0:T(8,128)(2,1)S(1)} collective-permute-done((bf16[80,2048]{1,0:T(8,128)(2,1)S(1)}, bf16[80,2048]{1,0:T(8,128)(2,1)S(1)}, u32[]{:S(2)}, u32[]{:S(2)}) %collective-permute-start.32) | collective-permute-done | bytes 327712 | tf_op jit(solution)/shard_map/ppermute | solution.py:177
  191.4 5.2 %collective-permute-done.38 = bf16[128,2048]{1,0:T(8,128)(2,1)S(1)} collective-permute-done((bf16[128,2048]{1,0:T(8,128)(2,1)S(1)}, bf16[128,2048]{1,0:T(8,128)(2,1)S(1)}, u32[]{:S(2)}, u32[]{:S(2)}) %collective-permute-start.38) | collective-permute-done | bytes 524320 | tf_op jit(solution)/shard_map/ppermute | solution.py:174
  (77 shorter events, 31.3 us)
Async XLA Ops:
  2.6 17.7 %collective-permute-start.1 = (bf16[136,2048]{1,0:T(8,128)(2,1)S(1)}, bf16[136,2048]{1,0:T(8,128)(2,1)S(1)}, u32[]{:S(2)}, u32[]{:S(2)}) collective-permute-start(bf16[136,2048]{1,0:T(8,128)(2,1)S(1)} %shard_map.64.refs_0_), channel_id=1, source_target_pairs={{0,8},{8,16},{16,24},{24,0},{1,9},{9,17},{17,25},{25,1},{2,10},{10... | collective-permute-start | bytes 1671176 | tf_op jit(solution)/shard_map/ppermute | solution.py:174
  5.7 14.7 %collective-permute-start = (bf16[136,2048]{1,0:T(8,128)(2,1)S(1)}, bf16[136,2048]{1,0:T(8,128)(2,1)S(1)}, u32[]{:S(2)}, u32[]{:S(2)}) collective-permute-start(bf16[136,2048]{1,0:T(8,128)(2,1)S(1)} %shard_map.64.refs_0_), channel_id=1, source_target_pairs={{0,1},{1,0},{2,3},{3,2},{4,5},{5,4},{6,7},{7,6},{8,9},{9,8},{10,11... | collective-permute-start | bytes 1671176 | tf_op jit(solution)/shard_map/ppermute | solution.py:177
  20.4 19.0 %collective-permute-start.2 = (bf16[136,2048]{1,0:T(8,128)(2,1)S(1)}, bf16[136,2048]{1,0:T(8,128)(2,1)S(1)}, u32[]{:S(2)}, u32[]{:S(2)}) collective-permute-start(bf16[136,2048]{1,0:T(8,128)(2,1)S(1)} %collective-permute-done.1.refs_0_), channel_id=1, source_target_pairs={{0,1},{1,0},{2,3},{3,2},{4,5},{5,4},{6,7},{7,6},{8,9},{9,8},{10,11... | collective-permute-start | bytes 1671176 | tf_op jit(solution)/shard_map/ppermute | solution.py:177
  22.5 16.9 %collective-permute-start.5 = (bf16[80,2048]{1,0:T(8,128)(2,1)S(1)}, bf16[80,2048]{1,0:T(8,128)(2,1)S(1)}, u32[]{:S(2)}, u32[]{:S(2)}) collective-permute-start(bf16[80,2048]{1,0:T(8,128)(2,1)S(1)} %get-tuple-element.114), channel_id=1, source_target_pairs={{0,4},{1,5},{2,6},{3,7},{4,0},{5,1},{6,2},{7,3},{8,12},{9,13},{10,... | collective-permute-start | bytes 983048 | tf_op jit(solution)/shard_map/ppermute | solution.py:177
  24.1 15.3 %collective-permute-start.7 = (bf16[80,2048]{1,0:T(8,128)(2,1)S(1)}, bf16[80,2048]{1,0:T(8,128)(2,1)S(1)}, u32[]{:S(2)}, u32[]{:S(2)}) collective-permute-start(bf16[80,2048]{1,0:T(8,128)(2,1)S(1)} %get-tuple-element.117), channel_id=1, source_target_pairs={{0,6},{1,7},{2,4},{3,5},{4,2},{5,3},{6,0},{7,1},{8,14},{9,15},{10,... | collective-permute-start | bytes 983048 | tf_op jit(solution)/shard_map/ppermute | solution.py:177
  39.4 15.8 %collective-permute-start.9 = (bf16[136,2048]{1,0:T(8,128)(2,1)S(1)}, bf16[136,2048]{1,0:T(8,128)(2,1)S(1)}, u32[]{:S(2)}, u32[]{:S(2)}) collective-permute-start(bf16[136,2048]{1,0:T(8,128)(2,1)S(1)} %collective-permute-done.1.refs_0_), channel_id=1, source_target_pairs={{0,8},{8,16},{16,24},{24,0},{1,9},{9,17},{17,25},{25,1},{2,10},{10... | collective-permute-start | bytes 1671176 | tf_op jit(solution)/shard_map/ppermute | solution.py:174
  40.0 15.2 %collective-permute-start.8 = (bf16[96,2048]{1,0:T(8,128)(2,1)S(1)}, bf16[96,2048]{1,0:T(8,128)(2,1)S(1)}, u32[]{:S(2)}, u32[]{:S(2)}) collective-permute-start(bf16[96,2048]{1,0:T(8,128)(2,1)S(1)} %get-tuple-element.118), channel_id=1, source_target_pairs={{0,6},{1,7},{2,4},{3,5},{4,2},{5,3},{6,0},{7,1},{8,14},{9,15},{10,... | collective-permute-start | bytes 1179656 | tf_op jit(solution)/shard_map/ppermute | solution.py:177
  41.6 18.4 %collective-permute-start.6 = (bf16[96,2048]{1,0:T(8,128)(2,1)S(1)}, bf16[96,2048]{1,0:T(8,128)(2,1)S(1)}, u32[]{:S(2)}, u32[]{:S(2)}) collective-permute-start(bf16[96,2048]{1,0:T(8,128)(2,1)S(1)} %get-tuple-element.115), channel_id=1, source_target_pairs={{0,4},{1,5},{2,6},{3,7},{4,0},{5,1},{6,2},{7,3},{8,12},{9,13},{10,... | collective-permute-start | bytes 1179656 | tf_op jit(solution)/shard_map/ppermute | solution.py:177
  42.8 17.2 %collective-permute-start.4 = (bf16[96,2048]{1,0:T(8,128)(2,1)S(1)}, bf16[96,2048]{1,0:T(8,128)(2,1)S(1)}, u32[]{:S(2)}, u32[]{:S(2)}) collective-permute-start(bf16[96,2048]{1,0:T(8,128)(2,1)S(1)} %get-tuple-element.112), channel_id=1, source_target_pairs={{0,2},{1,3},{2,0},{3,1},{4,6},{5,7},{6,4},{7,5},{8,10},{9,11},{10,... | collective-permute-start | bytes 1179656 | tf_op jit(solution)/shard_map/ppermute | solution.py:177
  60.0 16.4 %collective-permute-start.10 = (bf16[136,2048]{1,0:T(8,128)(2,1)S(1)}, bf16[136,2048]{1,0:T(8,128)(2,1)S(1)}, u32[]{:S(2)}, u32[]{:S(2)}) collective-permute-start(bf16[136,2048]{1,0:T(8,128)(2,1)S(1)} %collective-permute-done.9.refs_0_), channel_id=1, source_target_pairs={{0,8},{8,16},{16,24},{24,0},{1,9},{9,17},{17,25},{25,1},{2,10},{10... | collective-permute-start | bytes 1671176 | tf_op jit(solution)/shard_map/ppermute | solution.py:174
  61.0 22.4 %collective-permute-start.12 = (bf16[136,2048]{1,0:T(8,128)(2,1)S(1)}, bf16[136,2048]{1,0:T(8,128)(2,1)S(1)}, u32[]{:S(2)}, u32[]{:S(2)}) collective-permute-start(bf16[136,2048]{1,0:T(8,128)(2,1)S(1)} %collective-permute-done.9.refs_0_), channel_id=1, source_target_pairs={{0,1},{1,0},{2,3},{3,2},{4,5},{5,4},{6,7},{7,6},{8,9},{9,8},{10,11... | collective-permute-start | bytes 1671176 | tf_op jit(solution)/shard_map/ppermute | solution.py:177
  76.3 14.4 %collective-permute-start.11 = (bf16[136,2048]{1,0:T(8,128)(2,1)S(1)}, bf16[136,2048]{1,0:T(8,128)(2,1)S(1)}, u32[]{:S(2)}, u32[]{:S(2)}) collective-permute-start(bf16[136,2048]{1,0:T(8,128)(2,1)S(1)} %collective-permute-done.10.refs_0_), channel_id=1, source_target_pairs={{0,1},{1,0},{2,3},{3,2},{4,5},{5,4},{6,7},{7,6},{8,9},{9,8},{10,11... | collective-permute-start | bytes 1671176 | tf_op jit(solution)/shard_map/ppermute | solution.py:177
  85.4 17.0 %collective-permute-start.15 = (bf16[80,2048]{1,0:T(8,128)(2,1)S(1)}, bf16[80,2048]{1,0:T(8,128)(2,1)S(1)}, u32[]{:S(2)}, u32[]{:S(2)}) collective-permute-start(bf16[80,2048]{1,0:T(8,128)(2,1)S(1)} %get-tuple-element.141), channel_id=1, source_target_pairs={{0,4},{1,5},{2,6},{3,7},{4,0},{5,1},{6,2},{7,3},{8,12},{9,13},{10,... | collective-permute-start | bytes 983048 | tf_op jit(solution)/shard_map/ppermute | solution.py:177
  86.0 16.9 %collective-permute-start.17 = (bf16[80,2048]{1,0:T(8,128)(2,1)S(1)}, bf16[80,2048]{1,0:T(8,128)(2,1)S(1)}, u32[]{:S(2)}, u32[]{:S(2)}) collective-permute-start(bf16[80,2048]{1,0:T(8,128)(2,1)S(1)} %get-tuple-element.145), channel_id=1, source_target_pairs={{0,6},{1,7},{2,4},{3,5},{4,2},{5,3},{6,0},{7,1},{8,14},{9,15},{10,... | collective-permute-start | bytes 983048 | tf_op jit(solution)/shard_map/ppermute | solution.py:177
  94.5 14.1 %collective-permute-start.14 = (bf16[80,2048]{1,0:T(8,128)(2,1)S(1)}, bf16[80,2048]{1,0:T(8,128)(2,1)S(1)}, u32[]{:S(2)}, u32[]{:S(2)}) collective-permute-start(bf16[80,2048]{1,0:T(8,128)(2,1)S(1)} %get-tuple-element.138), channel_id=1, source_target_pairs={{0,2},{1,3},{2,0},{3,1},{4,6},{5,7},{6,4},{7,5},{8,10},{9,11},{10,... | collective-permute-start | bytes 983048 | tf_op jit(solution)/shard_map/ppermute | solution.py:177
  102.5 14.4 %collective-permute-start.16 = (bf16[80,2048]{1,0:T(8,128)(2,1)S(1)}, bf16[80,2048]{1,0:T(8,128)(2,1)S(1)}, u32[]{:S(2)}, u32[]{:S(2)}) collective-permute-start(bf16[80,2048]{1,0:T(8,128)(2,1)S(1)} %get-tuple-element.142), channel_id=1, source_target_pairs={{0,4},{1,5},{2,6},{3,7},{4,0},{5,1},{6,2},{7,3},{8,12},{9,13},{10,... | collective-permute-start | bytes 983048 | tf_op jit(solution)/shard_map/ppermute | solution.py:177
  102.9 14.1 %collective-permute-start.18 = (bf16[80,2048]{1,0:T(8,128)(2,1)S(1)}, bf16[80,2048]{1,0:T(8,128)(2,1)S(1)}, u32[]{:S(2)}, u32[]{:S(2)}) collective-permute-start(bf16[80,2048]{1,0:T(8,128)(2,1)S(1)} %get-tuple-element.146), channel_id=1, source_target_pairs={{0,6},{1,7},{2,4},{3,5},{4,2},{5,3},{6,0},{7,1},{8,14},{9,15},{10,... | collective-permute-start | bytes 983048 | tf_op jit(solution)/shard_map/ppermute | solution.py:177
  108.6 14.1 %collective-permute-start.19 = (bf16[80,2048]{1,0:T(8,128)(2,1)S(1)}, bf16[80,2048]{1,0:T(8,128)(2,1)S(1)}, u32[]{:S(2)}, u32[]{:S(2)}) collective-permute-start(bf16[80,2048]{1,0:T(8,128)(2,1)S(1)} %get-tuple-element.160), channel_id=1, source_target_pairs={{0,2},{1,3},{2,0},{3,1},{4,6},{5,7},{6,4},{7,5},{8,10},{9,11},{10,... | collective-permute-start | bytes 983048 | tf_op jit(solution)/shard_map/ppermute | solution.py:177
  116.9 14.1 %collective-permute-start.20 = (bf16[80,2048]{1,0:T(8,128)(2,1)S(1)}, bf16[80,2048]{1,0:T(8,128)(2,1)S(1)}, u32[]{:S(2)}, u32[]{:S(2)}) collective-permute-start(bf16[80,2048]{1,0:T(8,128)(2,1)S(1)} %get-tuple-element.162), channel_id=1, source_target_pairs={{0,4},{1,5},{2,6},{3,7},{4,0},{5,1},{6,2},{7,3},{8,12},{9,13},{10,... | collective-permute-start | bytes 983048 | tf_op jit(solution)/shard_map/ppermute | solution.py:177
  116.9 14.0 %collective-permute-start.21 = (bf16[80,2048]{1,0:T(8,128)(2,1)S(1)}, bf16[80,2048]{1,0:T(8,128)(2,1)S(1)}, u32[]{:S(2)}, u32[]{:S(2)}) collective-permute-start(bf16[80,2048]{1,0:T(8,128)(2,1)S(1)} %get-tuple-element.164), channel_id=1, source_target_pairs={{0,6},{1,7},{2,4},{3,5},{4,2},{5,3},{6,0},{7,1},{8,14},{9,15},{10,... | collective-permute-start | bytes 983048 | tf_op jit(solution)/shard_map/ppermute | solution.py:177
  132.4 10.6 %collective-permute-start.23 = (bf16[80,2048]{1,0:T(8,128)(2,1)S(1)}, bf16[80,2048]{1,0:T(8,128)(2,1)S(1)}, u32[]{:S(2)}, u32[]{:S(2)}) collective-permute-start(bf16[80,2048]{1,0:T(8,128)(2,1)S(1)} %get-tuple-element.173), channel_id=1, source_target_pairs={{0,2},{1,3},{2,0},{3,1},{4,6},{5,7},{6,4},{7,5},{8,10},{9,11},{10,... | collective-permute-start | bytes 983048 | tf_op jit(solution)/shard_map/ppermute | solution.py:177
  133.0 16.8 %collective-permute-start.24 = (bf16[80,2048]{1,0:T(8,128)(2,1)S(1)}, bf16[80,2048]{1,0:T(8,128)(2,1)S(1)}, u32[]{:S(2)}, u32[]{:S(2)}) collective-permute-start(bf16[80,2048]{1,0:T(8,128)(2,1)S(1)} %get-tuple-element.175), channel_id=1, source_target_pairs={{0,4},{1,5},{2,6},{3,7},{4,0},{5,1},{6,2},{7,3},{8,12},{9,13},{10,... | collective-permute-start | bytes 983048 | tf_op jit(solution)/shard_map/ppermute | solution.py:177
  133.9 15.9 %collective-permute-start.25 = (bf16[80,2048]{1,0:T(8,128)(2,1)S(1)}, bf16[80,2048]{1,0:T(8,128)(2,1)S(1)}, u32[]{:S(2)}, u32[]{:S(2)}) collective-permute-start(bf16[80,2048]{1,0:T(8,128)(2,1)S(1)} %get-tuple-element.177), channel_id=1, source_target_pairs={{0,6},{1,7},{2,4},{3,5},{4,2},{5,3},{6,0},{7,1},{8,14},{9,15},{10,... | collective-permute-start | bytes 983048 | tf_op jit(solution)/shard_map/ppermute | solution.py:177
  136.1 18.8 %collective-permute-start.27 = (bf16[128,2048]{1,0:T(8,128)(2,1)S(1)}, bf16[128,2048]{1,0:T(8,128)(2,1)S(1)}, u32[]{:S(2)}, u32[]{:S(2)}) collective-permute-start(bf16[128,2048]{1,0:T(8,128)(2,1)S(1)} %add_convert_fusion.3), channel_id=1, source_target_pairs={{0,8},{8,16},{16,24},{24,0},{1,9},{9,17},{17,25},{25,1},{2,10},{10... | collective-permute-start | bytes 1572872 | tf_op jit(solution)/shard_map/ppermute | solution.py:174
  151.3 10.6 %collective-permute-start.29 = (bf16[80,2048]{1,0:T(8,128)(2,1)S(1)}, bf16[80,2048]{1,0:T(8,128)(2,1)S(1)}, u32[]{:S(2)}, u32[]{:S(2)}) collective-permute-start(bf16[80,2048]{1,0:T(8,128)(2,1)S(1)} %get-tuple-element.187), channel_id=1, source_target_pairs={{0,2},{1,3},{2,0},{3,1},{4,6},{5,7},{6,4},{7,5},{8,10},{9,11},{10,... | collective-permute-start | bytes 983048 | tf_op jit(solution)/shard_map/ppermute | solution.py:177
  152.8 16.8 %collective-permute-start.31 = (bf16[80,2048]{1,0:T(8,128)(2,1)S(1)}, bf16[80,2048]{1,0:T(8,128)(2,1)S(1)}, u32[]{:S(2)}, u32[]{:S(2)}) collective-permute-start(bf16[80,2048]{1,0:T(8,128)(2,1)S(1)} %get-tuple-element.191), channel_id=1, source_target_pairs={{0,4},{1,5},{2,6},{3,7},{4,0},{5,1},{6,2},{7,3},{8,12},{9,13},{10,... | collective-permute-start | bytes 983048 | tf_op jit(solution)/shard_map/ppermute | solution.py:177
  153.1 16.5 %collective-permute-start.33 = (bf16[80,2048]{1,0:T(8,128)(2,1)S(1)}, bf16[80,2048]{1,0:T(8,128)(2,1)S(1)}, u32[]{:S(2)}, u32[]{:S(2)}) collective-permute-start(bf16[80,2048]{1,0:T(8,128)(2,1)S(1)} %get-tuple-element.195), channel_id=1, source_target_pairs={{0,6},{1,7},{2,4},{3,5},{4,2},{5,3},{6,0},{7,1},{8,14},{9,15},{10,... | collective-permute-start | bytes 983048 | tf_op jit(solution)/shard_map/ppermute | solution.py:177
  154.8 18.0 %collective-permute-start.28 = (bf16[128,2048]{1,0:T(8,128)(2,1)S(1)}, bf16[128,2048]{1,0:T(8,128)(2,1)S(1)}, u32[]{:S(2)}, u32[]{:S(2)}) collective-permute-start(bf16[128,2048]{1,0:T(8,128)(2,1)S(1)} %collective-permute-done.27), channel_id=1, source_target_pairs={{0,8},{8,16},{16,24},{24,0},{1,9},{9,17},{17,25},{25,1},{2,10},{10... | collective-permute-start | bytes 1572872 | tf_op jit(solution)/shard_map/ppermute | solution.py:174
  171.0 20.4 %collective-permute-start.37 = (bf16[128,2048]{1,0:T(8,128)(2,1)S(1)}, bf16[128,2048]{1,0:T(8,128)(2,1)S(1)}, u32[]{:S(2)}, u32[]{:S(2)}) collective-permute-start(bf16[128,2048]{1,0:T(8,128)(2,1)S(1)} %add_convert_fusion.2), channel_id=1, source_target_pairs={{0,24},{8,0},{16,8},{24,16},{1,25},{9,1},{17,9},{25,17},{2,26},{10... | collective-permute-start | bytes 1572872 | tf_op jit(solution)/shard_map/ppermute | solution.py:174
  173.4 16.5 %collective-permute-start.32 = (bf16[80,2048]{1,0:T(8,128)(2,1)S(1)}, bf16[80,2048]{1,0:T(8,128)(2,1)S(1)}, u32[]{:S(2)}, u32[]{:S(2)}) collective-permute-start(bf16[80,2048]{1,0:T(8,128)(2,1)S(1)} %get-tuple-element.192), channel_id=1, source_target_pairs={{0,4},{1,5},{2,6},{3,7},{4,0},{5,1},{6,2},{7,3},{8,12},{9,13},{10,... | collective-permute-start | bytes 983048 | tf_op jit(solution)/shard_map/ppermute | solution.py:177
  174.5 15.4 %collective-permute-start.34 = (bf16[80,2048]{1,0:T(8,128)(2,1)S(1)}, bf16[80,2048]{1,0:T(8,128)(2,1)S(1)}, u32[]{:S(2)}, u32[]{:S(2)}) collective-permute-start(bf16[80,2048]{1,0:T(8,128)(2,1)S(1)} %get-tuple-element.196), channel_id=1, source_target_pairs={{0,6},{1,7},{2,4},{3,5},{4,2},{5,3},{6,0},{7,1},{8,14},{9,15},{10,... | collective-permute-start | bytes 983048 | tf_op jit(solution)/shard_map/ppermute | solution.py:177
  176.4 20.1 %collective-permute-start.38 = (bf16[128,2048]{1,0:T(8,128)(2,1)S(1)}, bf16[128,2048]{1,0:T(8,128)(2,1)S(1)}, u32[]{:S(2)}, u32[]{:S(2)}) collective-permute-start(bf16[128,2048]{1,0:T(8,128)(2,1)S(1)} %add_convert_fusion.1), channel_id=1, source_target_pairs={{0,8},{8,16},{16,24},{24,0},{1,9},{9,17},{17,25},{25,1},{2,10},{10... | collective-permute-start | bytes 1572872 | tf_op jit(solution)/shard_map/ppermute | solution.py:174
  (14 other events, 139.7 us)

commit v6 on v5

--- a/solution.py
+++ b/solution.py
@@ -12,10 +12,11 @@
 VMEM_LIMIT = 32 * 1024 * 1024
 PARTS = 4
 CORES = 2
+PHASE_FLOPS = 50_000_000_000
 VMEM = pl.BlockSpec(memory_space=pltpu.VMEM)
 
 
-def call(body, out_shape, n_in, scratch=()):
+def call(body, out_shape, n_in, scratch=(), flops=1000):
     many = isinstance(out_shape, list)
     return pl.pallas_call(
         body,
@@ -24,8 +25,15 @@
         out_specs=[VMEM] * len(out_shape) if many else VMEM,
         scratch_shapes=list(scratch),
         compiler_params=pltpu.CompilerParams(vmem_limit_bytes=VMEM_LIMIT),
-        cost_estimate=pl.CostEstimate(flops=1000, bytes_accessed=1000, transcendentals=0),
-    )
+        cost_estimate=pl.CostEstimate(flops=flops, bytes_accessed=1000, transcendentals=0),
+    )
+
+
+def arrived_kernel(*refs):
+    total = refs[0][0:8, 0:128]
+    for ref in refs[1:-1]:
+        total = total + ref[0:8, 0:128]
+    refs[-1][...] = total
 
 
 def round_up(n, m):
@@ -187,6 +195,10 @@
         rows = n * z.cap + (CORES * z.extra if ride else 0)
         return call(functools.partial(pick_kernel, z, n, ride), [shape(rows)] * z.chips, n)(*blocks)
 
+    def arrived(arrays):
+        out = jax.ShapeDtypeStruct((8, 128), BF16)
+        return call(arrived_kernel, out, len(arrays), flops=PHASE_FLOPS)(*arrays)
+
     def slabs_across(slabs):
         return [across(s, CORES * q) for q, s in enumerate(slabs)]
 
@@ -222,15 +234,16 @@
     )
 
     blocks, pairs, slots, results = {0: own}, {}, {}, {}
+    gate = None
     for d in out_turns:
         if d:
-            gone = slots[d - 2] if d > 1 else []
-            blocks[d] = along(after([blocks[d - 1]], *gone)[0], 1)
+            blocks[d] = after([along(blocks[d - 1], 1)], slots[d - 1][1])[0]
         pairs[d] = [blocks[d], across(blocks[d], 1)]
         slabs = pick(pairs[d], d == 1)
         if d:
-            done = results[d - 2][:1] if d > 1 else []
-            ready = [after([s], b, *done)[0] for s, b in zip(slabs, slots[d - 1])]
+            seen = slots[d - 1][1:] + ([results[d - 2][0]] if d > 1 else [])
+            gate = arrived(seen)
+            ready = [after([s], gate)[0] for s in slabs]
             results[d - 1] = expert(after(slots[d - 1], slabs[0]), 2)
         else:
             ready = slabs

time: 198 us -> 161 us (0.81)
  waiting for transfers between devices: 134 us -> 89.1 us
  starting transfers between devices: 35 us -> 42.4 us
    ppermute x7, waiting for transfers between devices: 46.9 us -> 18.3 us  [along(): lax.ppermute(array, 'expert', [(i, (i + d) % layers) for i in range(layer...]
    ppermute x32, waiting for transfers between devices: 87.1 us -> 70.8 us  [across(): lax.ppermute(array, 'zero', [(i, i ^ o) for i in range(near)])]
    ppermute x7, starting transfers between devices: 6.46 us -> 11.5 us  [along(): lax.ppermute(array, 'expert', [(i, (i + d) % layers) for i in range(layer...]
    ppermute x32, starting transfers between devices: 28.5 us -> 30.9 us  [across(): lax.ppermute(array, 'zero', [(i, i ^ o) for i in range(near)])]
  transfers between devices with their start and end apart: 39 -> 39, of which waited for: 19 -> 23; matrix products, arithmetic and copies ran while one was open for 0% -> 0% of each run, Pallas kernels for 10% -> 12%
where the time goes in v6:
time: 161 us; the launch traced here: 160 us
  waiting for transfers between devices  89.1 us (55%)
  starting transfers between devices  42.4 us (26%)
  Pallas kernels  20.7 us (13%)
  local copies, waits for them, and re-layouts  6.38 us (4%)
    ppermute x32, waiting for transfers between devices, across(): lax.ppermute(array, 'zero', [(i, i ^ o) for i in range(near)])  70.8 us
    ppermute x32, starting transfers between devices, across(): lax.ppermute(array, 'zero', [(i, i ^ o) for i in range(near)])  30.9 us
    ppermute x7, waiting for transfers between devices, along(): lax.ppermute(array, 'expert', [(i, (i + d) % layers) for i in range(layer...  18.3 us
    pallas_call x4, Pallas kernels, expert(): call(functools.partial(expert_kernel, z, rows), [shape(rows)] * z.chips,...  12.9 us
    ppermute x7, starting transfers between devices, along(): lax.ppermute(array, 'expert', [(i, (i + d) % layers) for i in range(layer...  11.5 us
    unnamed x14, local copies, waits for them, and re-layouts  6.38 us
    pallas_call x4, Pallas kernels, mix(): call(functools.partial(mix_kernel, z, n), [shape(n // 2 * z.toks)] * 2, n...  5.36 us
  transfers between devices with their start and end apart: 39, of which 23 were waited for; matrix products, arithmetic and copies ran while one was open for 0% of the time, Pallas kernels for 12%

profile of v6, /device:TPU:0, one launch (start us, length us, event | category | flops | bytes accessed | tf_op | source)
XLA Modules:
  0.0 160.3 jit_solution(12840153598806234555)
XLA Ops:
  3.2 2.6 %collective-permute-start.1 = (bf16[136,2048]{1,0:T(8,128)(2,1)S(1)}, bf16[136,2048]{1,0:T(8,128)(2,1)S(1)}, u32[]{:S(2)}, u32[]{:S(2)}) collective-permute-start(bf16[136,2048]{1,0:T(8,128)(2,1)S(1)} %shard_map.64.refs_0_), channel_id=1, source_target_pairs={{0,8},{8,16},{16,24},{24,0},{1,9},{9,17},{17,25},{25,1},{2,10},{10... | collective-permute-start | bytes 1671176 | tf_op jit(solution)/shard_map/ppermute | solution.py:182
  6.4 1.9 %collective-permute-start.2 = (bf16[80,2048]{1,0:T(8,128)(2,1)S(1)}, bf16[80,2048]{1,0:T(8,128)(2,1)S(1)}, u32[]{:S(2)}, u32[]{:S(2)}) collective-permute-start(bf16[80,2048]{1,0:T(8,128)(2,1)S(1)} %get-tuple-element.108), channel_id=1, source_target_pairs={{0,2},{1,3},{2,0},{3,1},{4,6},{5,7},{6,4},{7,5},{8,10},{9,11},{10,... | collective-permute-start | bytes 983048 | tf_op jit(solution)/shard_map/ppermute | solution.py:185
  10.0 11.1 %collective-permute-done.1.refs_0_ = bf16[136,2048]{1,0:T(8,128)(2,1)S(1)} collective-permute-done((bf16[136,2048]{1,0:T(8,128)(2,1)S(1)}, bf16[136,2048]{1,0:T(8,128)(2,1)S(1)}, u32[]{:S(2)}, u32[]{:S(2)}) %collective-permute-start.1) | collective-permute-done | bytes 557088 | tf_op jit(solution)/shard_map/ppermute | solution.py:182
  21.1 3.7 %collective-permute-done.4.refs_2_ = bf16[80,2048]{1,0:T(8,128)(2,1)S(1)} collective-permute-done((bf16[80,2048]{1,0:T(8,128)(2,1)S(1)}, bf16[80,2048]{1,0:T(8,128)(2,1)S(1)}, u32[]{:S(2)}, u32[]{:S(2)}) %collective-permute-start.4) | collective-permute-done | bytes 327712 | tf_op jit(solution)/shard_map/ppermute | solution.py:185
  26.7 1.8 %collective-permute-start.8 = (bf16[96,2048]{1,0:T(8,128)(2,1)S(1)}, bf16[96,2048]{1,0:T(8,128)(2,1)S(1)}, u32[]{:S(2)}, u32[]{:S(2)}) collective-permute-start(bf16[96,2048]{1,0:T(8,128)(2,1)S(1)} %get-tuple-element.119), channel_id=1, source_target_pairs={{0,6},{1,7},{2,4},{3,5},{4,2},{5,3},{6,0},{7,1},{8,14},{9,15},{10,... | collective-permute-start | bytes 1179656 | tf_op jit(solution)/shard_map/ppermute | solution.py:185
  28.9 1.9 %copy-done.1 = bf16[1,2048,768]{2,1,0:T(8,128)(2,1)S(1)} copy-done((bf16[1,2048,768]{2,1,0:T(8,128)(2,1)S(1)}, bf16[1,2048,768]{2,1,0:T(8,128)(2,1)}, u32[]{:S(2)}) %copy-start.1) | copy-done | bytes 3145752
  30.8 1.9 %copy-done.3 = bf16[1,768,2048]{2,1,0:T(8,128)(2,1)S(1)} copy-done((bf16[1,768,2048]{2,1,0:T(8,128)(2,1)S(1)}, bf16[1,768,2048]{2,1,0:T(8,128)(2,1)}, u32[]{:S(2)}) %copy-start.3) | copy-done | bytes 3145752
  32.7 3.2 %shard_map.67 = (bf16[80,2048]{1,0:T(8,128)(2,1)S(1)}, bf16[80,2048]{1,0:T(8,128)(2,1)S(1)}, bf16[80,2048]{1,0:T(8,128)(2,1)S(1)}, bf16[80,2048]{1,0:T(8,128)(2,1)S(1)}) custom-call(bf16[80,2048]{1,0:T(8,128)(2,1)S(1)} %get-tuple-element.121.refs_0_, bf16[80,2048]{1,0:T(8,128)(2,1)S(1)} %collective-permute-done.2.refs_1_, ...), custom_call_target="tpu_custom_call" | custom-call | flops 1000 | bytes 1000 | tf_op jit(solution)/shard_map/pallas_call | solution.py:207
  39.1 5.8 %collective-permute-done.8.refs_3_.refs_5_ = bf16[96,2048]{1,0:T(8,128)(2,1)S(1)} collective-permute-done((bf16[96,2048]{1,0:T(8,128)(2,1)S(1)}, bf16[96,2048]{1,0:T(8,128)(2,1)S(1)}, u32[]{:S(2)}, u32[]{:S(2)}) %collective-permute-start.8) | collective-permute-done | bytes 393248 | tf_op jit(solution)/shard_map/ppermute | solution.py:185
  50.5 3.2 %shard_map.70 = (bf16[80,2048]{1,0:T(8,128)(2,1)S(1)}, bf16[80,2048]{1,0:T(8,128)(2,1)S(1)}, bf16[80,2048]{1,0:T(8,128)(2,1)S(1)}, bf16[80,2048]{1,0:T(8,128)(2,1)S(1)}) custom-call(bf16[96,2048]{1,0:T(8,128)(2,1)S(1)} %get-tuple-element.136.refs_0_.refs_2_, bf16[96,2048]{1,0:T(8,128)(2,1)S(1)} %collective-permute-done.6.refs_1_.refs_3_, ...), custom_call_target="tpu_custom_call" | custom-call | flops 1000 | bytes 1000 | tf_op jit(solution)/shard_map/pallas_call | solution.py:207
  54.4 2.3 %collective-permute-done.12.refs_1_ = bf16[80,2048]{1,0:T(8,128)(2,1)S(1)} collective-permute-done((bf16[80,2048]{1,0:T(8,128)(2,1)S(1)}, bf16[80,2048]{1,0:T(8,128)(2,1)S(1)}, u32[]{:S(2)}, u32[]{:S(2)}) %collective-permute-start.12) | collective-permute-done | bytes 327712 | tf_op jit(solution)/shard_map/ppermute | solution.py:185
  56.7 3.8 %collective-permute-done.15.refs_3_ = bf16[80,2048]{1,0:T(8,128)(2,1)S(1)} collective-permute-done((bf16[80,2048]{1,0:T(8,128)(2,1)S(1)}, bf16[80,2048]{1,0:T(8,128)(2,1)S(1)}, u32[]{:S(2)}, u32[]{:S(2)}) %collective-permute-start.15) | collective-permute-done | bytes 327712 | tf_op jit(solution)/shard_map/ppermute | solution.py:185
  62.5 1.7 %collective-permute-start.16 = (bf16[80,2048]{1,0:T(8,128)(2,1)S(1)}, bf16[80,2048]{1,0:T(8,128)(2,1)S(1)}, u32[]{:S(2)}, u32[]{:S(2)}) collective-permute-start(bf16[80,2048]{1,0:T(8,128)(2,1)S(1)} %get-tuple-element.143), channel_id=1, source_target_pairs={{0,2},{1,3},{2,0},{3,1},{4,6},{5,7},{6,4},{7,5},{8,10},{9,11},{10,... | collective-permute-start | bytes 983048 | tf_op jit(solution)/shard_map/ppermute | solution.py:185
  66.1 3.2 %shard_map.71 = (bf16[80,2048]{1,0:T(8,128)(2,1)S(1)}, bf16[80,2048]{1,0:T(8,128)(2,1)S(1)}, bf16[80,2048]{1,0:T(8,128)(2,1)S(1)}, bf16[80,2048]{1,0:T(8,128)(2,1)S(1)}) custom-call(bf16[80,2048]{1,0:T(8,128)(2,1)S(1)} %get-tuple-element.149.refs_0_, bf16[80,2048]{1,0:T(8,128)(2,1)S(1)} %collective-permute-done.12.refs_1_, ...), custom_call_target="tpu_custom_call" | custom-call | flops 1000 | bytes 1000 | tf_op jit(solution)/shard_map/pallas_call | solution.py:207
  69.3 3.9 %collective-permute-done.16.refs_1_ = bf16[80,2048]{1,0:T(8,128)(2,1)S(1)} collective-permute-done((bf16[80,2048]{1,0:T(8,128)(2,1)S(1)}, bf16[80,2048]{1,0:T(8,128)(2,1)S(1)}, u32[]{:S(2)}, u32[]{:S(2)}) %collective-permute-start.16) | collective-permute-done | bytes 327712 | tf_op jit(solution)/shard_map/ppermute | solution.py:185
  73.2 1.6 %collective-permute-start.19 = (bf16[80,2048]{1,0:T(8,128)(2,1)S(1)}, bf16[80,2048]{1,0:T(8,128)(2,1)S(1)}, u32[]{:S(2)}, u32[]{:S(2)}) collective-permute-start(bf16[80,2048]{1,0:T(8,128)(2,1)S(1)} %get-tuple-element.162), channel_id=1, source_target_pairs={{0,2},{1,3},{2,0},{3,1},{4,6},{5,7},{6,4},{7,5},{8,10},{9,11},{10,... | collective-permute-start | bytes 983048 | tf_op jit(solution)/shard_map/ppermute | solution.py:185
  74.9 2.1 %collective-permute-done.17.refs_2_ = bf16[80,2048]{1,0:T(8,128)(2,1)S(1)} collective-permute-done((bf16[80,2048]{1,0:T(8,128)(2,1)S(1)}, bf16[80,2048]{1,0:T(8,128)(2,1)S(1)}, u32[]{:S(2)}, u32[]{:S(2)}) %collective-permute-start.17) | collective-permute-done | bytes 327712 | tf_op jit(solution)/shard_map/ppermute | solution.py:185
  76.9 1.8 %collective-permute-start.20 = (bf16[80,2048]{1,0:T(8,128)(2,1)S(1)}, bf16[80,2048]{1,0:T(8,128)(2,1)S(1)}, u32[]{:S(2)}, u32[]{:S(2)}) collective-permute-start(bf16[80,2048]{1,0:T(8,128)(2,1)S(1)} %get-tuple-element.164), channel_id=1, source_target_pairs={{0,4},{1,5},{2,6},{3,7},{4,0},{5,1},{6,2},{7,3},{8,12},{9,13},{10,... | collective-permute-start | bytes 983048 | tf_op jit(solution)/shard_map/ppermute | solution.py:185
  78.8 2.3 %collective-permute-done.18.refs_3_ = bf16[80,2048]{1,0:T(8,128)(2,1)S(1)} collective-permute-done((bf16[80,2048]{1,0:T(8,128)(2,1)S(1)}, bf16[80,2048]{1,0:T(8,128)(2,1)S(1)}, u32[]{:S(2)}, u32[]{:S(2)}) %collective-permute-start.18) | collective-permute-done | bytes 327712 | tf_op jit(solution)/shard_map/ppermute | solution.py:185
  81.1 1.8 %collective-permute-start.21 = (bf16[80,2048]{1,0:T(8,128)(2,1)S(1)}, bf16[80,2048]{1,0:T(8,128)(2,1)S(1)}, u32[]{:S(2)}, u32[]{:S(2)}) collective-permute-start(bf16[80,2048]{1,0:T(8,128)(2,1)S(1)} %get-tuple-element.166), channel_id=1, source_target_pairs={{0,6},{1,7},{2,4},{3,5},{4,2},{5,3},{6,0},{7,1},{8,14},{9,15},{10,... | collective-permute-start | bytes 983048 | tf_op jit(solution)/shard_map/ppermute | solution.py:185
  82.9 3.2 %shard_map.72 = (bf16[80,2048]{1,0:T(8,128)(2,1)S(1)}, bf16[80,2048]{1,0:T(8,128)(2,1)S(1)}, bf16[80,2048]{1,0:T(8,128)(2,1)S(1)}, bf16[80,2048]{1,0:T(8,128)(2,1)S(1)}) custom-call(bf16[80,2048]{1,0:T(8,128)(2,1)S(1)} %get-tuple-element.154.refs_0_, bf16[80,2048]{1,0:T(8,128)(2,1)S(1)} %collective-permute-done.16.refs_1_, ...), custom_call_target="tpu_custom_call" | custom-call | flops 1000 | bytes 1000 | tf_op jit(solution)/shard_map/pallas_call | solution.py:207
  86.7 4.4 %collective-permute-done.20.refs_8_ = bf16[80,2048]{1,0:T(8,128)(2,1)S(1)} collective-permute-done((bf16[80,2048]{1,0:T(8,128)(2,1)S(1)}, bf16[80,2048]{1,0:T(8,128)(2,1)S(1)}, u32[]{:S(2)}, u32[]{:S(2)}) %collective-permute-start.20) | collective-permute-done | bytes 327712 | tf_op jit(solution)/shard_map/ppermute | solution.py:185
  97.6 5.5 %collective-permute-done.23.refs_7_ = bf16[80,2048]{1,0:T(8,128)(2,1)S(1)} collective-permute-done((bf16[80,2048]{1,0:T(8,128)(2,1)S(1)}, bf16[80,2048]{1,0:T(8,128)(2,1)S(1)}, u32[]{:S(2)}, u32[]{:S(2)}) %collective-permute-start.23) | collective-permute-done | bytes 327712 | tf_op jit(solution)/shard_map/ppermute | solution.py:185
  103.2 7.3 %collective-permute-done.24.refs_8_ = bf16[80,2048]{1,0:T(8,128)(2,1)S(1)} collective-permute-done((bf16[80,2048]{1,0:T(8,128)(2,1)S(1)}, bf16[80,2048]{1,0:T(8,128)(2,1)S(1)}, u32[]{:S(2)}, u32[]{:S(2)}) %collective-permute-start.24) | collective-permute-done | bytes 327712 | tf_op jit(solution)/shard_map/ppermute | solution.py:185
  115.5 1.7 %collective-permute-start.28 = (bf16[128,2048]{1,0:T(8,128)(2,1)S(1)}, bf16[128,2048]{1,0:T(8,128)(2,1)S(1)}, u32[]{:S(2)}, u32[]{:S(2)}) collective-permute-start(bf16[128,2048]{1,0:T(8,128)(2,1)S(1)} %collective-permute-done.27), channel_id=1, source_target_pairs={{0,8},{8,16},{16,24},{24,0},{1,9},{9,17},{17,25},{25,1},{2,10},{10... | collective-permute-start | bytes 1572872 | tf_op jit(solution)/shard_map/ppermute | solution.py:182
  117.3 5.1 %collective-permute-done.29.refs_7_ = bf16[80,2048]{1,0:T(8,128)(2,1)S(1)} collective-permute-done((bf16[80,2048]{1,0:T(8,128)(2,1)S(1)}, bf16[80,2048]{1,0:T(8,128)(2,1)S(1)}, u32[]{:S(2)}, u32[]{:S(2)}) %collective-permute-start.29) | collective-permute-done | bytes 327712 | tf_op jit(solution)/shard_map/ppermute | solution.py:185
  122.5 7.3 %collective-permute-done.31.refs_8_ = bf16[80,2048]{1,0:T(8,128)(2,1)S(1)} collective-permute-done((bf16[80,2048]{1,0:T(8,128)(2,1)S(1)}, bf16[80,2048]{1,0:T(8,128)(2,1)S(1)}, u32[]{:S(2)}, u32[]{:S(2)}) %collective-permute-start.31) | collective-permute-done | bytes 327712 | tf_op jit(solution)/shard_map/ppermute | solution.py:185
  131.2 4.1 %collective-permute-start.37 = (bf16[128,2048]{1,0:T(8,128)(2,1)S(1)}, bf16[128,2048]{1,0:T(8,128)(2,1)S(1)}, u32[]{:S(2)}, u32[]{:S(2)}) collective-permute-start(bf16[128,2048]{1,0:T(8,128)(2,1)S(1)} %add_convert_fusion.2), channel_id=1, source_target_pairs={{0,24},{8,0},{16,8},{24,16},{1,25},{9,1},{17,9},{25,17},{2,26},{10... | collective-permute-start | bytes 1572872 | tf_op jit(solution)/shard_map/ppermute | solution.py:182
  135.9 1.7 %collective-permute-start.32 = (bf16[80,2048]{1,0:T(8,128)(2,1)S(1)}, bf16[80,2048]{1,0:T(8,128)(2,1)S(1)}, u32[]{:S(2)}, u32[]{:S(2)}) collective-permute-start(bf16[80,2048]{1,0:T(8,128)(2,1)S(1)} %get-tuple-element.194), channel_id=1, source_target_pairs={{0,4},{1,5},{2,6},{3,7},{4,0},{5,1},{6,2},{7,3},{8,12},{9,13},{10,... | collective-permute-start | bytes 983048 | tf_op jit(solution)/shard_map/ppermute | solution.py:185
  139.0 6.9 %collective-permute-done.30.refs_7_ = bf16[80,2048]{1,0:T(8,128)(2,1)S(1)} collective-permute-done((bf16[80,2048]{1,0:T(8,128)(2,1)S(1)}, bf16[80,2048]{1,0:T(8,128)(2,1)S(1)}, u32[]{:S(2)}, u32[]{:S(2)}) %collective-permute-start.30) | collective-permute-done | bytes 327712 | tf_op jit(solution)/shard_map/ppermute | solution.py:185
  145.9 5.8 %collective-permute-done.32.refs_8_ = bf16[80,2048]{1,0:T(8,128)(2,1)S(1)} collective-permute-done((bf16[80,2048]{1,0:T(8,128)(2,1)S(1)}, bf16[80,2048]{1,0:T(8,128)(2,1)S(1)}, u32[]{:S(2)}, u32[]{:S(2)}) %collective-permute-start.32) | collective-permute-done | bytes 327712 | tf_op jit(solution)/shard_map/ppermute | solution.py:185
  153.9 5.2 %collective-permute-done.38 = bf16[128,2048]{1,0:T(8,128)(2,1)S(1)} collective-permute-done((bf16[128,2048]{1,0:T(8,128)(2,1)S(1)}, bf16[128,2048]{1,0:T(8,128)(2,1)S(1)}, u32[]{:S(2)}, u32[]{:S(2)}) %collective-permute-start.38) | collective-permute-done | bytes 524320 | tf_op jit(solution)/shard_map/ppermute | solution.py:182
  (77 shorter events, 40.0 us)
Async XLA Ops:
  3.2 17.9 %collective-permute-start.1 = (bf16[136,2048]{1,0:T(8,128)(2,1)S(1)}, bf16[136,2048]{1,0:T(8,128)(2,1)S(1)}, u32[]{:S(2)}, u32[]{:S(2)}) collective-permute-start(bf16[136,2048]{1,0:T(8,128)(2,1)S(1)} %shard_map.64.refs_0_), channel_id=1, source_target_pairs={{0,8},{8,16},{16,24},{24,0},{1,9},{9,17},{17,25},{25,1},{2,10},{10... | collective-permute-start | bytes 1671176 | tf_op jit(solution)/shard_map/ppermute | solution.py:182
  6.4 14.7 %collective-permute-start.2 = (bf16[80,2048]{1,0:T(8,128)(2,1)S(1)}, bf16[80,2048]{1,0:T(8,128)(2,1)S(1)}, u32[]{:S(2)}, u32[]{:S(2)}) collective-permute-start(bf16[80,2048]{1,0:T(8,128)(2,1)S(1)} %get-tuple-element.108), channel_id=1, source_target_pairs={{0,2},{1,3},{2,0},{3,1},{4,6},{5,7},{6,4},{7,5},{8,10},{9,11},{10,... | collective-permute-start | bytes 983048 | tf_op jit(solution)/shard_map/ppermute | solution.py:185
  8.3 16.5 %collective-permute-start.4 = (bf16[80,2048]{1,0:T(8,128)(2,1)S(1)}, bf16[80,2048]{1,0:T(8,128)(2,1)S(1)}, u32[]{:S(2)}, u32[]{:S(2)}) collective-permute-start(bf16[80,2048]{1,0:T(8,128)(2,1)S(1)} %get-tuple-element.111), channel_id=1, source_target_pairs={{0,4},{1,5},{2,6},{3,7},{4,0},{5,1},{6,2},{7,3},{8,12},{9,13},{10,... | collective-permute-start | bytes 983048 | tf_op jit(solution)/shard_map/ppermute | solution.py:185
  9.8 15.0 %collective-permute-start.5 = (bf16[80,2048]{1,0:T(8,128)(2,1)S(1)}, bf16[80,2048]{1,0:T(8,128)(2,1)S(1)}, u32[]{:S(2)}, u32[]{:S(2)}) collective-permute-start(bf16[80,2048]{1,0:T(8,128)(2,1)S(1)} %get-tuple-element.112), channel_id=1, source_target_pairs={{0,6},{1,7},{2,4},{3,5},{4,2},{5,3},{6,0},{7,1},{8,14},{9,15},{10,... | collective-permute-start | bytes 983048 | tf_op jit(solution)/shard_map/ppermute | solution.py:185
  21.1 16.2 %collective-permute-start.9 = (bf16[136,2048]{1,0:T(8,128)(2,1)S(1)}, bf16[136,2048]{1,0:T(8,128)(2,1)S(1)}, u32[]{:S(2)}, u32[]{:S(2)}) collective-permute-start(bf16[136,2048]{1,0:T(8,128)(2,1)S(1)} %collective-permute-done.1.refs_0_), channel_id=1, source_target_pairs={{0,8},{8,16},{16,24},{24,0},{1,9},{9,17},{17,25},{25,1},{2,10},{10... | collective-permute-start | bytes 1671176 | tf_op jit(solution)/shard_map/ppermute | solution.py:182
  25.4 12.1 %collective-permute-start.6 = (bf16[96,2048]{1,0:T(8,128)(2,1)S(1)}, bf16[96,2048]{1,0:T(8,128)(2,1)S(1)}, u32[]{:S(2)}, u32[]{:S(2)}) collective-permute-start(bf16[96,2048]{1,0:T(8,128)(2,1)S(1)} %get-tuple-element.115), channel_id=1, source_target_pairs={{0,2},{1,3},{2,0},{3,1},{4,6},{5,7},{6,4},{7,5},{8,10},{9,11},{10,... | collective-permute-start | bytes 1179656 | tf_op jit(solution)/shard_map/ppermute | solution.py:185
  26.7 18.3 %collective-permute-start.8 = (bf16[96,2048]{1,0:T(8,128)(2,1)S(1)}, bf16[96,2048]{1,0:T(8,128)(2,1)S(1)}, u32[]{:S(2)}, u32[]{:S(2)}) collective-permute-start(bf16[96,2048]{1,0:T(8,128)(2,1)S(1)} %get-tuple-element.119), channel_id=1, source_target_pairs={{0,6},{1,7},{2,4},{3,5},{4,2},{5,3},{6,0},{7,1},{8,14},{9,15},{10,... | collective-permute-start | bytes 1179656 | tf_op jit(solution)/shard_map/ppermute | solution.py:185
  28.4 17.9 %collective-permute-start.7 = (bf16[96,2048]{1,0:T(8,128)(2,1)S(1)}, bf16[96,2048]{1,0:T(8,128)(2,1)S(1)}, u32[]{:S(2)}, u32[]{:S(2)}) collective-permute-start(bf16[96,2048]{1,0:T(8,128)(2,1)S(1)} %get-tuple-element.117), channel_id=1, source_target_pairs={{0,4},{1,5},{2,6},{3,7},{4,0},{5,1},{6,2},{7,3},{8,12},{9,13},{10,... | collective-permute-start | bytes 1179656 | tf_op jit(solution)/shard_map/ppermute | solution.py:185
  37.5 8.8 %collective-permute-start.11 = (bf16[136,2048]{1,0:T(8,128)(2,1)S(1)}, bf16[136,2048]{1,0:T(8,128)(2,1)S(1)}, u32[]{:S(2)}, u32[]{:S(2)}) collective-permute-start(bf16[136,2048]{1,0:T(8,128)(2,1)S(1)} %collective-permute-done.9.refs_0_), channel_id=1, source_target_pairs={{0,1},{1,0},{2,3},{3,2},{4,5},{5,4},{6,7},{7,6},{8,9},{9,8},{10,11... | collective-permute-start | bytes 1671176 | tf_op jit(solution)/shard_map/ppermute | solution.py:185
  37.5 16.9 %collective-permute-start.10 = (bf16[136,2048]{1,0:T(8,128)(2,1)S(1)}, bf16[136,2048]{1,0:T(8,128)(2,1)S(1)}, u32[]{:S(2)}, u32[]{:S(2)}) collective-permute-start(bf16[136,2048]{1,0:T(8,128)(2,1)S(1)} %collective-permute-done.9.refs_0_), channel_id=1, source_target_pairs={{0,8},{8,16},{16,24},{24,0},{1,9},{9,17},{17,25},{25,1},{2,10},{10... | collective-permute-start | bytes 1671176 | tf_op jit(solution)/shard_map/ppermute | solution.py:182
  46.9 9.8 %collective-permute-start.12 = (bf16[80,2048]{1,0:T(8,128)(2,1)S(1)}, bf16[80,2048]{1,0:T(8,128)(2,1)S(1)}, u32[]{:S(2)}, u32[]{:S(2)}) collective-permute-start(bf16[80,2048]{1,0:T(8,128)(2,1)S(1)} %get-tuple-element.128), channel_id=1, source_target_pairs={{0,2},{1,3},{2,0},{3,1},{4,6},{5,7},{6,4},{7,5},{8,10},{9,11},{10,... | collective-permute-start | bytes 983048 | tf_op jit(solution)/shard_map/ppermute | solution.py:185
  47.9 12.7 %collective-permute-start.15 = (bf16[80,2048]{1,0:T(8,128)(2,1)S(1)}, bf16[80,2048]{1,0:T(8,128)(2,1)S(1)}, u32[]{:S(2)}, u32[]{:S(2)}) collective-permute-start(bf16[80,2048]{1,0:T(8,128)(2,1)S(1)} %get-tuple-element.134), channel_id=1, source_target_pairs={{0,6},{1,7},{2,4},{3,5},{4,2},{5,3},{6,0},{7,1},{8,14},{9,15},{10,... | collective-permute-start | bytes 983048 | tf_op jit(solution)/shard_map/ppermute | solution.py:185
  49.1 12.8 %collective-permute-start.14 = (bf16[80,2048]{1,0:T(8,128)(2,1)S(1)}, bf16[80,2048]{1,0:T(8,128)(2,1)S(1)}, u32[]{:S(2)}, u32[]{:S(2)}) collective-permute-start(bf16[80,2048]{1,0:T(8,128)(2,1)S(1)} %get-tuple-element.132), channel_id=1, source_target_pairs={{0,4},{1,5},{2,6},{3,7},{4,0},{5,1},{6,2},{7,3},{8,12},{9,13},{10,... | collective-permute-start | bytes 983048 | tf_op jit(solution)/shard_map/ppermute | solution.py:185
  62.5 10.7 %collective-permute-start.16 = (bf16[80,2048]{1,0:T(8,128)(2,1)S(1)}, bf16[80,2048]{1,0:T(8,128)(2,1)S(1)}, u32[]{:S(2)}, u32[]{:S(2)}) collective-permute-start(bf16[80,2048]{1,0:T(8,128)(2,1)S(1)} %get-tuple-element.143), channel_id=1, source_target_pairs={{0,2},{1,3},{2,0},{3,1},{4,6},{5,7},{6,4},{7,5},{8,10},{9,11},{10,... | collective-permute-start | bytes 983048 | tf_op jit(solution)/shard_map/ppermute | solution.py:185
  64.2 12.7 %collective-permute-start.17 = (bf16[80,2048]{1,0:T(8,128)(2,1)S(1)}, bf16[80,2048]{1,0:T(8,128)(2,1)S(1)}, u32[]{:S(2)}, u32[]{:S(2)}) collective-permute-start(bf16[80,2048]{1,0:T(8,128)(2,1)S(1)} %get-tuple-element.145), channel_id=1, source_target_pairs={{0,4},{1,5},{2,6},{3,7},{4,0},{5,1},{6,2},{7,3},{8,12},{9,13},{10,... | collective-permute-start | bytes 983048 | tf_op jit(solution)/shard_map/ppermute | solution.py:185
  65.1 16.0 %collective-permute-start.18 = (bf16[80,2048]{1,0:T(8,128)(2,1)S(1)}, bf16[80,2048]{1,0:T(8,128)(2,1)S(1)}, u32[]{:S(2)}, u32[]{:S(2)}) collective-permute-start(bf16[80,2048]{1,0:T(8,128)(2,1)S(1)} %get-tuple-element.147), channel_id=1, source_target_pairs={{0,6},{1,7},{2,4},{3,5},{4,2},{5,3},{6,0},{7,1},{8,14},{9,15},{10,... | collective-permute-start | bytes 983048 | tf_op jit(solution)/shard_map/ppermute | solution.py:185
  73.2 13.5 %collective-permute-start.19 = (bf16[80,2048]{1,0:T(8,128)(2,1)S(1)}, bf16[80,2048]{1,0:T(8,128)(2,1)S(1)}, u32[]{:S(2)}, u32[]{:S(2)}) collective-permute-start(bf16[80,2048]{1,0:T(8,128)(2,1)S(1)} %get-tuple-element.162), channel_id=1, source_target_pairs={{0,2},{1,3},{2,0},{3,1},{4,6},{5,7},{6,4},{7,5},{8,10},{9,11},{10,... | collective-permute-start | bytes 983048 | tf_op jit(solution)/shard_map/ppermute | solution.py:185
  76.9 14.2 %collective-permute-start.20 = (bf16[80,2048]{1,0:T(8,128)(2,1)S(1)}, bf16[80,2048]{1,0:T(8,128)(2,1)S(1)}, u32[]{:S(2)}, u32[]{:S(2)}) collective-permute-start(bf16[80,2048]{1,0:T(8,128)(2,1)S(1)} %get-tuple-element.164), channel_id=1, source_target_pairs={{0,4},{1,5},{2,6},{3,7},{4,0},{5,1},{6,2},{7,3},{8,12},{9,13},{10,... | collective-permute-start | bytes 983048 | tf_op jit(solution)/shard_map/ppermute | solution.py:185
  81.1 10.1 %collective-permute-start.21 = (bf16[80,2048]{1,0:T(8,128)(2,1)S(1)}, bf16[80,2048]{1,0:T(8,128)(2,1)S(1)}, u32[]{:S(2)}, u32[]{:S(2)}) collective-permute-start(bf16[80,2048]{1,0:T(8,128)(2,1)S(1)} %get-tuple-element.166), channel_id=1, source_target_pairs={{0,6},{1,7},{2,4},{3,5},{4,2},{5,3},{6,0},{7,1},{8,14},{9,15},{10,... | collective-permute-start | bytes 983048 | tf_op jit(solution)/shard_map/ppermute | solution.py:185
  92.6 10.6 %collective-permute-start.23 = (bf16[80,2048]{1,0:T(8,128)(2,1)S(1)}, bf16[80,2048]{1,0:T(8,128)(2,1)S(1)}, u32[]{:S(2)}, u32[]{:S(2)}) collective-permute-start(bf16[80,2048]{1,0:T(8,128)(2,1)S(1)} %get-tuple-element.175), channel_id=1, source_target_pairs={{0,2},{1,3},{2,0},{3,1},{4,6},{5,7},{6,4},{7,5},{8,10},{9,11},{10,... | collective-permute-start | bytes 983048 | tf_op jit(solution)/shard_map/ppermute | solution.py:185
  93.7 16.8 %collective-permute-start.24 = (bf16[80,2048]{1,0:T(8,128)(2,1)S(1)}, bf16[80,2048]{1,0:T(8,128)(2,1)S(1)}, u32[]{:S(2)}, u32[]{:S(2)}) collective-permute-start(bf16[80,2048]{1,0:T(8,128)(2,1)S(1)} %get-tuple-element.177), channel_id=1, source_target_pairs={{0,4},{1,5},{2,6},{3,7},{4,0},{5,1},{6,2},{7,3},{8,12},{9,13},{10,... | collective-permute-start | bytes 983048 | tf_op jit(solution)/shard_map/ppermute | solution.py:185
  94.7 15.8 %collective-permute-start.25 = (bf16[80,2048]{1,0:T(8,128)(2,1)S(1)}, bf16[80,2048]{1,0:T(8,128)(2,1)S(1)}, u32[]{:S(2)}, u32[]{:S(2)}) collective-permute-start(bf16[80,2048]{1,0:T(8,128)(2,1)S(1)} %get-tuple-element.179), channel_id=1, source_target_pairs={{0,6},{1,7},{2,4},{3,5},{4,2},{5,3},{6,0},{7,1},{8,14},{9,15},{10,... | collective-permute-start | bytes 983048 | tf_op jit(solution)/shard_map/ppermute | solution.py:185
  96.3 19.2 %collective-permute-start.27 = (bf16[128,2048]{1,0:T(8,128)(2,1)S(1)}, bf16[128,2048]{1,0:T(8,128)(2,1)S(1)}, u32[]{:S(2)}, u32[]{:S(2)}) collective-permute-start(bf16[128,2048]{1,0:T(8,128)(2,1)S(1)} %add_convert_fusion.3), channel_id=1, source_target_pairs={{0,8},{8,16},{16,24},{24,0},{1,9},{9,17},{17,25},{25,1},{2,10},{10... | collective-permute-start | bytes 1572872 | tf_op jit(solution)/shard_map/ppermute | solution.py:182
  111.9 10.6 %collective-permute-start.29 = (bf16[80,2048]{1,0:T(8,128)(2,1)S(1)}, bf16[80,2048]{1,0:T(8,128)(2,1)S(1)}, u32[]{:S(2)}, u32[]{:S(2)}) collective-permute-start(bf16[80,2048]{1,0:T(8,128)(2,1)S(1)} %get-tuple-element.189), channel_id=1, source_target_pairs={{0,2},{1,3},{2,0},{3,1},{4,6},{5,7},{6,4},{7,5},{8,10},{9,11},{10,... | collective-permute-start | bytes 983048 | tf_op jit(solution)/shard_map/ppermute | solution.py:185
  113.0 16.8 %collective-permute-start.31 = (bf16[80,2048]{1,0:T(8,128)(2,1)S(1)}, bf16[80,2048]{1,0:T(8,128)(2,1)S(1)}, u32[]{:S(2)}, u32[]{:S(2)}) collective-permute-start(bf16[80,2048]{1,0:T(8,128)(2,1)S(1)} %get-tuple-element.193), channel_id=1, source_target_pairs={{0,4},{1,5},{2,6},{3,7},{4,0},{5,1},{6,2},{7,3},{8,12},{9,13},{10,... | collective-permute-start | bytes 983048 | tf_op jit(solution)/shard_map/ppermute | solution.py:185
  114.1 15.7 %collective-permute-start.33 = (bf16[80,2048]{1,0:T(8,128)(2,1)S(1)}, bf16[80,2048]{1,0:T(8,128)(2,1)S(1)}, u32[]{:S(2)}, u32[]{:S(2)}) collective-permute-start(bf16[80,2048]{1,0:T(8,128)(2,1)S(1)} %get-tuple-element.197), channel_id=1, source_target_pairs={{0,6},{1,7},{2,4},{3,5},{4,2},{5,3},{6,0},{7,1},{8,14},{9,15},{10,... | collective-permute-start | bytes 983048 | tf_op jit(solution)/shard_map/ppermute | solution.py:185
  115.5 19.9 %collective-permute-start.28 = (bf16[128,2048]{1,0:T(8,128)(2,1)S(1)}, bf16[128,2048]{1,0:T(8,128)(2,1)S(1)}, u32[]{:S(2)}, u32[]{:S(2)}) collective-permute-start(bf16[128,2048]{1,0:T(8,128)(2,1)S(1)} %collective-permute-done.27), channel_id=1, source_target_pairs={{0,8},{8,16},{16,24},{24,0},{1,9},{9,17},{17,25},{25,1},{2,10},{10... | collective-permute-start | bytes 1572872 | tf_op jit(solution)/shard_map/ppermute | solution.py:182
  131.2 22.7 %collective-permute-start.37 = (bf16[128,2048]{1,0:T(8,128)(2,1)S(1)}, bf16[128,2048]{1,0:T(8,128)(2,1)S(1)}, u32[]{:S(2)}, u32[]{:S(2)}) collective-permute-start(bf16[128,2048]{1,0:T(8,128)(2,1)S(1)} %add_convert_fusion.2), channel_id=1, source_target_pairs={{0,24},{8,0},{16,8},{24,16},{1,25},{9,1},{17,9},{25,17},{2,26},{10... | collective-permute-start | bytes 1572872 | tf_op jit(solution)/shard_map/ppermute | solution.py:182
  135.3 10.6 %collective-permute-start.30 = (bf16[80,2048]{1,0:T(8,128)(2,1)S(1)}, bf16[80,2048]{1,0:T(8,128)(2,1)S(1)}, u32[]{:S(2)}, u32[]{:S(2)}) collective-permute-start(bf16[80,2048]{1,0:T(8,128)(2,1)S(1)} %get-tuple-element.190), channel_id=1, source_target_pairs={{0,2},{1,3},{2,0},{3,1},{4,6},{5,7},{6,4},{7,5},{8,10},{9,11},{10,... | collective-permute-start | bytes 983048 | tf_op jit(solution)/shard_map/ppermute | solution.py:185
  135.9 15.8 %collective-permute-start.32 = (bf16[80,2048]{1,0:T(8,128)(2,1)S(1)}, bf16[80,2048]{1,0:T(8,128)(2,1)S(1)}, u32[]{:S(2)}, u32[]{:S(2)}) collective-permute-start(bf16[80,2048]{1,0:T(8,128)(2,1)S(1)} %get-tuple-element.194), channel_id=1, source_target_pairs={{0,4},{1,5},{2,6},{3,7},{4,0},{5,1},{6,2},{7,3},{8,12},{9,13},{10,... | collective-permute-start | bytes 983048 | tf_op jit(solution)/shard_map/ppermute | solution.py:185
  137.6 14.8 %collective-permute-start.34 = (bf16[80,2048]{1,0:T(8,128)(2,1)S(1)}, bf16[80,2048]{1,0:T(8,128)(2,1)S(1)}, u32[]{:S(2)}, u32[]{:S(2)}) collective-permute-start(bf16[80,2048]{1,0:T(8,128)(2,1)S(1)} %get-tuple-element.198), channel_id=1, source_target_pairs={{0,6},{1,7},{2,4},{3,5},{4,2},{5,3},{6,0},{7,1},{8,14},{9,15},{10,... | collective-permute-start | bytes 983048 | tf_op jit(solution)/shard_map/ppermute | solution.py:185
  139.0 20.1 %collective-permute-start.38 = (bf16[128,2048]{1,0:T(8,128)(2,1)S(1)}, bf16[128,2048]{1,0:T(8,128)(2,1)S(1)}, u32[]{:S(2)}, u32[]{:S(2)}) collective-permute-start(bf16[128,2048]{1,0:T(8,128)(2,1)S(1)} %add_convert_fusion.1), channel_id=1, source_target_pairs={{0,8},{8,16},{16,24},{24,0},{1,9},{9,17},{17,25},{25,1},{2,10},{10... | collective-permute-start | bytes 1572872 | tf_op jit(solution)/shard_map/ppermute | solution.py:182
  (14 other events, 87.1 us)

commit v7 on v6

--- a/solution.py
+++ b/solution.py
@@ -50,6 +50,7 @@
         self.cap = round_up(5 * self.toks * self.topk // (4 * self.experts), 8)
         self.tiles = self.width // self.depth
         self.extra = -(-(1 + self.experts // 8) // self.tiles) * 8
+        self.ride = -(-(CORES * self.experts // 8) // self.tiles) * 8
 
     def tile(self, g):
         r, q = g // self.tiles * 8, g % self.tiles * self.depth
@@ -104,10 +105,13 @@
             mine = [r[q * z.cap : (q + 1) * z.cap] for r in rows]
             outs[q][0 : n * z.cap, cols] = jnp.concatenate(mine, axis=0).astype(BF16)
     if ride:
-        for q in range(z.chips):
-            for r in range(CORES):
-                start = n * z.cap + r * z.extra
-                outs[q][start : start + z.extra, :] = blocks[r][z.toks : z.toks + z.extra, :]
+        for r in range(CORES):
+            for g in range(z.experts // 8):
+                rows, cols = z.tile(g + 1)
+                piece = blocks[r][z.toks + rows.start : z.toks + rows.stop, cols]
+                rows, cols = z.tile(r * (z.experts // 8) + g)
+                for q in range(z.chips):
+                    outs[q][n * z.cap + rows.start : n * z.cap + rows.stop, cols] = piece
 
 
 def expert_kernel(z, rows, *refs):
@@ -134,14 +138,13 @@
     routers = []
     for q in range(z.chips):
         for r in range(CORES):
-            base = CORES * z.cap + r * z.extra
+            base = CORES * z.cap
             pieces = []
             for g in range(z.experts // 8):
-                rows, cols = z.tile(g + 1)
+                rows, cols = z.tile(r * (z.experts // 8) + g)
                 pieces.append(riders[q][base + rows.start : base + rows.stop, cols].astype(F32))
             routers.append(jnp.concatenate(pieces, axis=0).astype(BF16))
     for b, block in enumerate(blocks):
-        out, base = outs[b % CORES], b // CORES * z.toks
         ids_t = ids_of(z, block)
         logits = None
         for o in range(z.near):
@@ -169,9 +172,24 @@
             cols = slice(c * part, (c + 1) * part)
             own = slice(b * z.cap, (b + 1) * z.cap)
             y = jnp.concatenate([s[:, cols].astype(F32)[own] for s in backs], axis=0).astype(BF16)
-            out[base : base + z.toks, cols] = lax.dot_general(
-                mix, y, (((0,), (0,)), ((), ())), preferred_element_type=F32
-            ).astype(BF16)
+            mixed = lax.dot_general(mix, y, (((0,), (0,)), ((), ())), preferred_element_type=F32).astype(BF16)
+            if b == 0:
+                outs[0][:, cols] = mixed
+            else:
+                half = z.toks // 2
+                outs[1][:, cols] = mixed[0:half]
+                outs[2][:, cols] = mixed[half:]
+
+
+def join_kernel(*refs):
+    out = refs[-1]
+    half = out.shape[0] // 2
+    for i in range(2):
+        rows = slice(i * half, (i + 1) * half)
+        total = refs[0][rows, :].astype(F32) + refs[1 + i][...].astype(F32)
+        for ref in refs[3:-1]:
+            total = total + ref[rows, :].astype(F32)
+        out[rows, :] = total.astype(BF16)
 
 
 def per_device(tokens, router_weight, expert_ids, gate_weight, up_weight, down_weight):
@@ -192,7 +210,7 @@
 
     def pick(blocks, ride):
         n = len(blocks)
-        rows = n * z.cap + (CORES * z.extra if ride else 0)
+        rows = n * z.cap + (z.ride if ride else 0)
         return call(functools.partial(pick_kernel, z, n, ride), [shape(rows)] * z.chips, n)(*blocks)
 
     def arrived(arrays):
@@ -215,15 +233,16 @@
         )(*slabs, gate_weight[0], up_weight[0], down_weight[0])
 
     def mix(blocks, backs):
-        n = len(blocks)
-        mine, other = call(
-            functools.partial(mix_kernel, z, n), [shape(n // 2 * z.toks)] * 2, n + 2 * z.chips
+        mine, *other = call(
+            functools.partial(mix_kernel, z, CORES),
+            [shape(z.toks), shape(z.toks // 2), shape(z.toks // 2)],
+            CORES + 2 * z.chips,
+            flops=PHASE_FLOPS,
         )(*blocks, *riders, *backs)
-        other = across(other, 1)
-        return [
-            mine[i * z.toks : (i + 1) * z.toks].astype(F32) + other[i * z.toks : (i + 1) * z.toks].astype(F32)
-            for i in range(n // 2)
-        ]
+        return [mine] + [across(part, 1) for part in other]
+
+    def join(parts):
+        return call(join_kernel, shape(z.toks), len(parts))(*parts)
 
     far = layers // 2
     out_turns = list(range(layers))
@@ -234,19 +253,16 @@
     )
 
     blocks, pairs, slots, results = {0: own}, {}, {}, {}
-    gate = None
     for d in out_turns:
         if d:
             blocks[d] = after([along(blocks[d - 1], 1)], slots[d - 1][1])[0]
         pairs[d] = [blocks[d], across(blocks[d], 1)]
         slabs = pick(pairs[d], d == 1)
+        ready = slabs
         if d:
-            seen = slots[d - 1][1:] + ([results[d - 2][0]] if d > 1 else [])
-            gate = arrived(seen)
+            gate = arrived(slots[d - 1][1:] + ([results[d - 2][0]] if d > 1 else []))
             ready = [after([s], gate)[0] for s in slabs]
             results[d - 1] = expert(after(slots[d - 1], slabs[0]), 2)
-        else:
-            ready = slabs
         slots[d] = slabs_across(ready)
     riders = slots[1]
     results[d] = expert(after(slots[d], results[d - 1][0]), 2)
@@ -259,18 +275,15 @@
         rows = [after([r], b, *first)[0] for r, b in zip(results[d], backs)]
         backs = slabs_across(rows)
         last = leaving[back_turns[i - 1]] if i else results[layers - 1][0]
+        sums = mix(pairs[d], after(backs, last))
         if d:
-            part = mix(pairs[d], after(backs, last))[0]
-            leaving[d] = part.astype(BF16)
+            leaving[d] = join(sums)
             way = layers - d
             if d == far:
                 home[d] = along(along(leaving[d], way // 2), way - way // 2)
             else:
                 home[d] = along(leaving[d], way)
-    total = mix(pairs[0], after(backs, last))[0]
-    for d in out_turns[1:]:
-        total = total + home[d].astype(F32)
-    return total.astype(BF16)
+    return join(sums + [home[d] for d in out_turns[1:]])
 
 
 def solution(mesh):

time: 161 us -> 170 us (1.056)
  waiting for transfers between devices: 89.1 us -> 97.4 us
    ppermute x7, waiting for transfers between devices: 18.3 us -> 39.4 us  [along(): lax.ppermute(array, 'expert', [(i, (i + d) % layers) for i in range(layer...]
    ppermute x32 -> x36, waiting for transfers between devices: 70.8 us -> 58 us  [across(): lax.ppermute(array, 'zero', [(i, i ^ o) for i in range(near)])]
    ppermute x32 -> x36, starting transfers between devices: 30.9 us -> 33 us  [across(): lax.ppermute(array, 'zero', [(i, i ^ o) for i in range(near)])]
    ppermute x7, starting transfers between devices: 11.5 us -> 9.58 us  [along(): lax.ppermute(array, 'expert', [(i, (i + d) % layers) for i in range(layer...]
    pallas_call x4 -> x8, Pallas kernels: 5.36 us -> 6.83 us  [the longest x4 5.35 us: mix(): call(functools.partial(mix_kernel, z, CORES), [shape(z.toks), shape(z.tok...]
    unnamed x14 -> x22, local copies, waits for them, and re-layouts: 6.38 us -> 7.19 us
  transfers between devices with their start and end apart: 39 -> 43, of which waited for: 23 -> 27; matrix products, arithmetic and copies ran while one was open for 0% -> 0% of each run, Pallas kernels for 12% -> 12%
where the time goes in v7:
time: 170 us
  waiting for transfers between devices  97.4 us (57%)
  starting transfers between devices  42.6 us (25%)
  Pallas kernels  22.2 us (13%)
  local copies, waits for them, and re-layouts  7.19 us (4%)
    ppermute x36, waiting for transfers between devices, across(): lax.ppermute(array, 'zero', [(i, i ^ o) for i in range(near)])  58 us
    ppermute x7, waiting for transfers between devices, along(): lax.ppermute(array, 'expert', [(i, (i + d) % layers) for i in range(layer...  39.4 us
    ppermute x36, starting transfers between devices, across(): lax.ppermute(array, 'zero', [(i, i ^ o) for i in range(near)])  33 us
    pallas_call x4, Pallas kernels, expert(): call(functools.partial(expert_kernel, z, rows), [shape(rows)] * z.chips,...  12.9 us
    ppermute x7, starting transfers between devices, along(): lax.ppermute(array, 'expert', [(i, (i + d) % layers) for i in range(layer...  9.58 us
    unnamed x22, local copies, waits for them, and re-layouts  7.19 us
    pallas_call x4, Pallas kernels, mix(): call(functools.partial(mix_kernel, z, CORES), [shape(z.toks), shape(z.tok...  5.35 us
  transfers between devices with their start and end apart: 43, of which 27 were waited for; matrix products, arithmetic and copies ran while one was open for 0% of the time, Pallas kernels for 12%

profile of v7, /device:TPU:0, one launch (start us, length us, event | category | flops | bytes accessed | tf_op | source)
XLA Modules:
  0.0 169.5 jit_solution(17611686043702093201)
XLA Ops:
  3.2 2.6 %collective-permute-start.1 = (bf16[136,2048]{1,0:T(8,128)(2,1)S(1)}, bf16[136,2048]{1,0:T(8,128)(2,1)S(1)}, u32[]{:S(2)}, u32[]{:S(2)}) collective-permute-start(bf16[136,2048]{1,0:T(8,128)(2,1)S(1)} %shard_map.64.refs_0_), channel_id=1, source_target_pairs={{0,8},{8,16},{16,24},{24,0},{1,9},{9,17},{17,25},{25,1},{2,10},{10... | collective-permute-start | bytes 1671176 | tf_op jit(solution)/shard_map/ppermute | solution.py:200
  7.2 1.8 %collective-permute-start.2 = (bf16[80,2048]{1,0:T(8,128)(2,1)S(1)}, bf16[80,2048]{1,0:T(8,128)(2,1)S(1)}, u32[]{:S(2)}, u32[]{:S(2)}) collective-permute-start(bf16[80,2048]{1,0:T(8,128)(2,1)S(1)} %get-tuple-element.112), channel_id=1, source_target_pairs={{0,2},{1,3},{2,0},{3,1},{4,6},{5,7},{6,4},{7,5},{8,10},{9,11},{10,... | collective-permute-start | bytes 983048 | tf_op jit(solution)/shard_map/ppermute | solution.py:203
  10.7 10.3 %collective-permute-done.1.refs_0_ = bf16[136,2048]{1,0:T(8,128)(2,1)S(1)} collective-permute-done((bf16[136,2048]{1,0:T(8,128)(2,1)S(1)}, bf16[136,2048]{1,0:T(8,128)(2,1)S(1)}, u32[]{:S(2)}, u32[]{:S(2)}) %collective-permute-start.1) | collective-permute-done | bytes 557088 | tf_op jit(solution)/shard_map/ppermute | solution.py:200
  21.1 4.4 %collective-permute-done.4.refs_2_ = bf16[80,2048]{1,0:T(8,128)(2,1)S(1)} collective-permute-done((bf16[80,2048]{1,0:T(8,128)(2,1)S(1)}, bf16[80,2048]{1,0:T(8,128)(2,1)S(1)}, u32[]{:S(2)}, u32[]{:S(2)}) %collective-permute-start.4) | collective-permute-done | bytes 327712 | tf_op jit(solution)/shard_map/ppermute | solution.py:203
  27.4 1.8 %collective-permute-start.8 = (bf16[88,2048]{1,0:T(8,128)(2,1)S(1)}, bf16[88,2048]{1,0:T(8,128)(2,1)S(1)}, u32[]{:S(2)}, u32[]{:S(2)}) collective-permute-start(bf16[88,2048]{1,0:T(8,128)(2,1)S(1)} %get-tuple-element.123), channel_id=1, source_target_pairs={{0,6},{1,7},{2,4},{3,5},{4,2},{5,3},{6,0},{7,1},{8,14},{9,15},{10,... | collective-permute-start | bytes 1081352 | tf_op jit(solution)/shard_map/ppermute | solution.py:203
  29.7 1.9 %copy-done.1 = bf16[1,2048,768]{2,1,0:T(8,128)(2,1)S(1)} copy-done((bf16[1,2048,768]{2,1,0:T(8,128)(2,1)S(1)}, bf16[1,2048,768]{2,1,0:T(8,128)(2,1)}, u32[]{:S(2)}) %copy-start.1) | copy-done | bytes 3145752
  31.6 1.9 %copy-done.3 = bf16[1,768,2048]{2,1,0:T(8,128)(2,1)S(1)} copy-done((bf16[1,768,2048]{2,1,0:T(8,128)(2,1)S(1)}, bf16[1,768,2048]{2,1,0:T(8,128)(2,1)}, u32[]{:S(2)}) %copy-start.3) | copy-done | bytes 3145752
  33.5 3.2 %shard_map.67 = (bf16[80,2048]{1,0:T(8,128)(2,1)S(1)}, bf16[80,2048]{1,0:T(8,128)(2,1)S(1)}, bf16[80,2048]{1,0:T(8,128)(2,1)S(1)}, bf16[80,2048]{1,0:T(8,128)(2,1)S(1)}) custom-call(bf16[80,2048]{1,0:T(8,128)(2,1)S(1)} %get-tuple-element.125.refs_0_, bf16[80,2048]{1,0:T(8,128)(2,1)S(1)} %collective-permute-done.2.refs_1_, ...), custom_call_target="tpu_custom_call" | custom-call | flops 1000 | bytes 1000 | tf_op jit(solution)/shard_map/pallas_call | solution.py:225
  37.5 1.6 collective-permute-start.10
  39.1 5.1 %collective-permute-done.8.refs_3_.refs_5_ = bf16[88,2048]{1,0:T(8,128)(2,1)S(1)} collective-permute-done((bf16[88,2048]{1,0:T(8,128)(2,1)S(1)}, bf16[88,2048]{1,0:T(8,128)(2,1)S(1)}, u32[]{:S(2)}, u32[]{:S(2)}) %collective-permute-start.8) | collective-permute-done | bytes 360480 | tf_op jit(solution)/shard_map/ppermute | solution.py:203
  49.8 3.2 %shard_map.70 = (bf16[80,2048]{1,0:T(8,128)(2,1)S(1)}, bf16[80,2048]{1,0:T(8,128)(2,1)S(1)}, bf16[80,2048]{1,0:T(8,128)(2,1)S(1)}, bf16[80,2048]{1,0:T(8,128)(2,1)S(1)}) custom-call(bf16[88,2048]{1,0:T(8,128)(2,1)S(1)} %get-tuple-element.140.refs_0_.refs_2_, bf16[88,2048]{1,0:T(8,128)(2,1)S(1)} %collective-permute-done.6.refs_1_.refs_3_, ...), custom_call_target="tpu_custom_call" | custom-call | flops 1000 | bytes 1000 | tf_op jit(solution)/shard_map/pallas_call | solution.py:225
  54.5 1.6 collective-permute-done.12.refs_1_
  56.1 3.8 %collective-permute-done.15.refs_3_ = bf16[80,2048]{1,0:T(8,128)(2,1)S(1)} collective-permute-done((bf16[80,2048]{1,0:T(8,128)(2,1)S(1)}, bf16[80,2048]{1,0:T(8,128)(2,1)S(1)}, u32[]{:S(2)}, u32[]{:S(2)}) %collective-permute-start.15) | collective-permute-done | bytes 327712 | tf_op jit(solution)/shard_map/ppermute | solution.py:203
  61.8 1.7 collective-permute-start.17
  65.7 3.2 %shard_map.71 = (bf16[80,2048]{1,0:T(8,128)(2,1)S(1)}, bf16[80,2048]{1,0:T(8,128)(2,1)S(1)}, bf16[80,2048]{1,0:T(8,128)(2,1)S(1)}, bf16[80,2048]{1,0:T(8,128)(2,1)S(1)}) custom-call(bf16[80,2048]{1,0:T(8,128)(2,1)S(1)} %get-tuple-element.153.refs_0_, bf16[80,2048]{1,0:T(8,128)(2,1)S(1)} %collective-permute-done.12.refs_1_, ...), custom_call_target="tpu_custom_call" | custom-call | flops 1000 | bytes 1000 | tf_op jit(solution)/shard_map/pallas_call | solution.py:225
  69.0 7.0 %collective-permute-done.17.refs_2_ = bf16[80,2048]{1,0:T(8,128)(2,1)S(1)} collective-permute-done((bf16[80,2048]{1,0:T(8,128)(2,1)S(1)}, bf16[80,2048]{1,0:T(8,128)(2,1)S(1)}, u32[]{:S(2)}, u32[]{:S(2)}) %collective-permute-start.17) | collective-permute-done | bytes 327712 | tf_op jit(solution)/shard_map/ppermute | solution.py:203
  76.0 3.0 %collective-permute-start.20 = (bf16[80,2048]{1,0:T(8,128)(2,1)S(1)}, bf16[80,2048]{1,0:T(8,128)(2,1)S(1)}, u32[]{:S(2)}, u32[]{:S(2)}) collective-permute-start(bf16[80,2048]{1,0:T(8,128)(2,1)S(1)} %get-tuple-element.168), channel_id=1, source_target_pairs={{0,4},{1,5},{2,6},{3,7},{4,0},{5,1},{6,2},{7,3},{8,12},{9,13},{10,... | collective-permute-start | bytes 983048 | tf_op jit(solution)/shard_map/ppermute | solution.py:203
  79.0 2.5 %collective-permute-done.18.refs_3_ = bf16[80,2048]{1,0:T(8,128)(2,1)S(1)} collective-permute-done((bf16[80,2048]{1,0:T(8,128)(2,1)S(1)}, bf16[80,2048]{1,0:T(8,128)(2,1)S(1)}, u32[]{:S(2)}, u32[]{:S(2)}) %collective-permute-start.18) | collective-permute-done | bytes 327712 | tf_op jit(solution)/shard_map/ppermute | solution.py:203
  83.0 3.2 %shard_map.72 = (bf16[80,2048]{1,0:T(8,128)(2,1)S(1)}, bf16[80,2048]{1,0:T(8,128)(2,1)S(1)}, bf16[80,2048]{1,0:T(8,128)(2,1)S(1)}, bf16[80,2048]{1,0:T(8,128)(2,1)S(1)}) custom-call(bf16[80,2048]{1,0:T(8,128)(2,1)S(1)} %get-tuple-element.158.refs_0_, bf16[80,2048]{1,0:T(8,128)(2,1)S(1)} %collective-permute-done.16.refs_1_, ...), custom_call_target="tpu_custom_call" | custom-call | flops 1000 | bytes 1000 | tf_op jit(solution)/shard_map/pallas_call | solution.py:225
  86.3 5.6 %collective-permute-done.20.refs_8_ = bf16[80,2048]{1,0:T(8,128)(2,1)S(1)} collective-permute-done((bf16[80,2048]{1,0:T(8,128)(2,1)S(1)}, bf16[80,2048]{1,0:T(8,128)(2,1)S(1)}, u32[]{:S(2)}, u32[]{:S(2)}) %collective-permute-start.20) | collective-permute-done | bytes 327712 | tf_op jit(solution)/shard_map/ppermute | solution.py:203
  92.2 2.7 %collective-permute-start.25 = (bf16[80,2048]{1,0:T(8,128)(2,1)S(1)}, bf16[80,2048]{1,0:T(8,128)(2,1)S(1)}, u32[]{:S(2)}, u32[]{:S(2)}) collective-permute-start(bf16[80,2048]{1,0:T(8,128)(2,1)S(1)} %get-tuple-element.182), channel_id=1, source_target_pairs={{0,4},{1,5},{2,6},{3,7},{4,0},{5,1},{6,2},{7,3},{8,12},{9,13},{10,... | collective-permute-start | bytes 983048 | tf_op jit(solution)/shard_map/ppermute | solution.py:203
  101.0 1.8 %collective-permute-start.29 = (bf16[128,2048]{1,0:T(8,128)(2,1)S(1)}, bf16[128,2048]{1,0:T(8,128)(2,1)S(1)}, u32[]{:S(2)}, u32[]{:S(2)}) collective-permute-start(bf16[128,2048]{1,0:T(8,128)(2,1)S(1)} %shard_map.74), channel_id=1, source_target_pairs={{0,8},{8,16},{16,24},{24,0},{1,9},{9,17},{17,25},{25,1},{2,10},{10... | collective-permute-start | bytes 1572872 | tf_op jit(solution)/shard_map/ppermute | solution.py:200
  102.7 2.3 %collective-permute-done.25.refs_8_ = bf16[80,2048]{1,0:T(8,128)(2,1)S(1)} collective-permute-done((bf16[80,2048]{1,0:T(8,128)(2,1)S(1)}, bf16[80,2048]{1,0:T(8,128)(2,1)S(1)}, u32[]{:S(2)}, u32[]{:S(2)}) %collective-permute-start.25) | collective-permute-done | bytes 327712 | tf_op jit(solution)/shard_map/ppermute | solution.py:203
  106.4 10.6 %collective-permute-done.29 = bf16[128,2048]{1,0:T(8,128)(2,1)S(1)} collective-permute-done((bf16[128,2048]{1,0:T(8,128)(2,1)S(1)}, bf16[128,2048]{1,0:T(8,128)(2,1)S(1)}, u32[]{:S(2)}, u32[]{:S(2)}) %collective-permute-start.29) | collective-permute-done | bytes 524320 | tf_op jit(solution)/shard_map/ppermute | solution.py:200
  117.0 2.0 %collective-permute-start.31 = (bf16[80,2048]{1,0:T(8,128)(2,1)S(1)}, bf16[80,2048]{1,0:T(8,128)(2,1)S(1)}, u32[]{:S(2)}, u32[]{:S(2)}) collective-permute-start(bf16[80,2048]{1,0:T(8,128)(2,1)S(1)} %get-tuple-element.195), channel_id=1, source_target_pairs={{0,2},{1,3},{2,0},{3,1},{4,6},{5,7},{6,4},{7,5},{8,10},{9,11},{10,... | collective-permute-start | bytes 983048 | tf_op jit(solution)/shard_map/ppermute | solution.py:203
  122.1 5.4 %collective-permute-done.31.refs_7_ = bf16[80,2048]{1,0:T(8,128)(2,1)S(1)} collective-permute-done((bf16[80,2048]{1,0:T(8,128)(2,1)S(1)}, bf16[80,2048]{1,0:T(8,128)(2,1)S(1)}, u32[]{:S(2)}, u32[]{:S(2)}) %collective-permute-start.31) | collective-permute-done | bytes 327712 | tf_op jit(solution)/shard_map/ppermute | solution.py:203
  127.6 7.3 %collective-permute-done.33.refs_8_ = bf16[80,2048]{1,0:T(8,128)(2,1)S(1)} collective-permute-done((bf16[80,2048]{1,0:T(8,128)(2,1)S(1)}, bf16[80,2048]{1,0:T(8,128)(2,1)S(1)}, u32[]{:S(2)}, u32[]{:S(2)}) %collective-permute-start.33) | collective-permute-done | bytes 327712 | tf_op jit(solution)/shard_map/ppermute | solution.py:203
  136.7 1.8 %collective-permute-start.36 = (bf16[80,2048]{1,0:T(8,128)(2,1)S(1)}, bf16[80,2048]{1,0:T(8,128)(2,1)S(1)}, u32[]{:S(2)}, u32[]{:S(2)}) collective-permute-start(bf16[80,2048]{1,0:T(8,128)(2,1)S(1)} %get-tuple-element.204), channel_id=1, source_target_pairs={{0,6},{1,7},{2,4},{3,5},{4,2},{5,3},{6,0},{7,1},{8,14},{9,15},{10,... | collective-permute-start | bytes 983048 | tf_op jit(solution)/shard_map/ppermute | solution.py:203
  141.4 3.5 %collective-permute-start.41 = (bf16[128,2048]{1,0:T(8,128)(2,1)S(1)}, bf16[128,2048]{1,0:T(8,128)(2,1)S(1)}, u32[]{:S(2)}, u32[]{:S(2)}) collective-permute-start(bf16[128,2048]{1,0:T(8,128)(2,1)S(1)} %shard_map.76), channel_id=1, source_target_pairs={{0,24},{8,0},{16,8},{24,16},{1,25},{9,1},{17,9},{25,17},{2,26},{10... | collective-permute-start | bytes 1572872 | tf_op jit(solution)/shard_map/ppermute | solution.py:200
  145.4 3.8 %collective-permute-done.34.refs_8_ = bf16[80,2048]{1,0:T(8,128)(2,1)S(1)} collective-permute-done((bf16[80,2048]{1,0:T(8,128)(2,1)S(1)}, bf16[80,2048]{1,0:T(8,128)(2,1)S(1)}, u32[]{:S(2)}, u32[]{:S(2)}) %collective-permute-start.34) | collective-permute-done | bytes 327712 | tf_op jit(solution)/shard_map/ppermute | solution.py:203
  151.9 5.4 %collective-permute-done.41.refs_3_ = bf16[128,2048]{1,0:T(8,128)(2,1)S(1)} collective-permute-done((bf16[128,2048]{1,0:T(8,128)(2,1)S(1)}, bf16[128,2048]{1,0:T(8,128)(2,1)S(1)}, u32[]{:S(2)}, u32[]{:S(2)}) %collective-permute-start.41) | collective-permute-done | bytes 524320 | tf_op jit(solution)/shard_map/ppermute | solution.py:200
  157.3 11.1 %collective-permute-done.42.refs_5_ = bf16[128,2048]{1,0:T(8,128)(2,1)S(1)} collective-permute-done((bf16[128,2048]{1,0:T(8,128)(2,1)S(1)}, bf16[128,2048]{1,0:T(8,128)(2,1)S(1)}, u32[]{:S(2)}, u32[]{:S(2)}) %collective-permute-start.42) | collective-permute-done | bytes 524320 | tf_op jit(solution)/shard_map/ppermute | solution.py:200
  (93 shorter events, 42.2 us)
Async XLA Ops:
  3.2 17.9 %collective-permute-start.1 = (bf16[136,2048]{1,0:T(8,128)(2,1)S(1)}, bf16[136,2048]{1,0:T(8,128)(2,1)S(1)}, u32[]{:S(2)}, u32[]{:S(2)}) collective-permute-start(bf16[136,2048]{1,0:T(8,128)(2,1)S(1)} %shard_map.64.refs_0_), channel_id=1, source_target_pairs={{0,8},{8,16},{16,24},{24,0},{1,9},{9,17},{17,25},{25,1},{2,10},{10... | collective-permute-start | bytes 1671176 | tf_op jit(solution)/shard_map/ppermute | solution.py:200
  7.2 13.8 %collective-permute-start.2 = (bf16[80,2048]{1,0:T(8,128)(2,1)S(1)}, bf16[80,2048]{1,0:T(8,128)(2,1)S(1)}, u32[]{:S(2)}, u32[]{:S(2)}) collective-permute-start(bf16[80,2048]{1,0:T(8,128)(2,1)S(1)} %get-tuple-element.112), channel_id=1, source_target_pairs={{0,2},{1,3},{2,0},{3,1},{4,6},{5,7},{6,4},{7,5},{8,10},{9,11},{10,... | collective-permute-start | bytes 983048 | tf_op jit(solution)/shard_map/ppermute | solution.py:203
  9.0 16.5 %collective-permute-start.4 = (bf16[80,2048]{1,0:T(8,128)(2,1)S(1)}, bf16[80,2048]{1,0:T(8,128)(2,1)S(1)}, u32[]{:S(2)}, u32[]{:S(2)}) collective-permute-start(bf16[80,2048]{1,0:T(8,128)(2,1)S(1)} %get-tuple-element.115), channel_id=1, source_target_pairs={{0,4},{1,5},{2,6},{3,7},{4,0},{5,1},{6,2},{7,3},{8,12},{9,13},{10,... | collective-permute-start | bytes 983048 | tf_op jit(solution)/shard_map/ppermute | solution.py:203
  10.5 15.0 %collective-permute-start.5 = (bf16[80,2048]{1,0:T(8,128)(2,1)S(1)}, bf16[80,2048]{1,0:T(8,128)(2,1)S(1)}, u32[]{:S(2)}, u32[]{:S(2)}) collective-permute-start(bf16[80,2048]{1,0:T(8,128)(2,1)S(1)} %get-tuple-element.116), channel_id=1, source_target_pairs={{0,6},{1,7},{2,4},{3,5},{4,2},{5,3},{6,0},{7,1},{8,14},{9,15},{10,... | collective-permute-start | bytes 983048 | tf_op jit(solution)/shard_map/ppermute | solution.py:203
  21.1 16.2 %collective-permute-start.9 = (bf16[136,2048]{1,0:T(8,128)(2,1)S(1)}, bf16[136,2048]{1,0:T(8,128)(2,1)S(1)}, u32[]{:S(2)}, u32[]{:S(2)}) collective-permute-start(bf16[136,2048]{1,0:T(8,128)(2,1)S(1)} %collective-permute-done.1.refs_0_), channel_id=1, source_target_pairs={{0,8},{8,16},{16,24},{24,0},{1,9},{9,17},{17,25},{25,1},{2,10},{10... | collective-permute-start | bytes 1671176 | tf_op jit(solution)/shard_map/ppermute | solution.py:200
  26.1 11.4 %collective-permute-start.6 = (bf16[88,2048]{1,0:T(8,128)(2,1)S(1)}, bf16[88,2048]{1,0:T(8,128)(2,1)S(1)}, u32[]{:S(2)}, u32[]{:S(2)}) collective-permute-start(bf16[88,2048]{1,0:T(8,128)(2,1)S(1)} %get-tuple-element.119), channel_id=1, source_target_pairs={{0,2},{1,3},{2,0},{3,1},{4,6},{5,7},{6,4},{7,5},{8,10},{9,11},{10,... | collective-permute-start | bytes 1081352 | tf_op jit(solution)/shard_map/ppermute | solution.py:203
  27.4 16.9 %collective-permute-start.8 = (bf16[88,2048]{1,0:T(8,128)(2,1)S(1)}, bf16[88,2048]{1,0:T(8,128)(2,1)S(1)}, u32[]{:S(2)}, u32[]{:S(2)}) collective-permute-start(bf16[88,2048]{1,0:T(8,128)(2,1)S(1)} %get-tuple-element.123), channel_id=1, source_target_pairs={{0,6},{1,7},{2,4},{3,5},{4,2},{5,3},{6,0},{7,1},{8,14},{9,15},{10,... | collective-permute-start | bytes 1081352 | tf_op jit(solution)/shard_map/ppermute | solution.py:203
  29.2 16.5 %collective-permute-start.7 = (bf16[88,2048]{1,0:T(8,128)(2,1)S(1)}, bf16[88,2048]{1,0:T(8,128)(2,1)S(1)}, u32[]{:S(2)}, u32[]{:S(2)}) collective-permute-start(bf16[88,2048]{1,0:T(8,128)(2,1)S(1)} %get-tuple-element.121), channel_id=1, source_target_pairs={{0,4},{1,5},{2,6},{3,7},{4,0},{5,1},{6,2},{7,3},{8,12},{9,13},{10,... | collective-permute-start | bytes 1081352 | tf_op jit(solution)/shard_map/ppermute | solution.py:203
  37.5 16.9 %collective-permute-start.10 = (bf16[136,2048]{1,0:T(8,128)(2,1)S(1)}, bf16[136,2048]{1,0:T(8,128)(2,1)S(1)}, u32[]{:S(2)}, u32[]{:S(2)}) collective-permute-start(bf16[136,2048]{1,0:T(8,128)(2,1)S(1)} %collective-permute-done.9.refs_0_), channel_id=1, source_target_pairs={{0,8},{8,16},{16,24},{24,0},{1,9},{9,17},{17,25},{25,1},{2,10},{10... | collective-permute-start | bytes 1671176 | tf_op jit(solution)/shard_map/ppermute | solution.py:200
  46.9 12.9 %collective-permute-start.15 = (bf16[80,2048]{1,0:T(8,128)(2,1)S(1)}, bf16[80,2048]{1,0:T(8,128)(2,1)S(1)}, u32[]{:S(2)}, u32[]{:S(2)}) collective-permute-start(bf16[80,2048]{1,0:T(8,128)(2,1)S(1)} %get-tuple-element.138), channel_id=1, source_target_pairs={{0,6},{1,7},{2,4},{3,5},{4,2},{5,3},{6,0},{7,1},{8,14},{9,15},{10,... | collective-permute-start | bytes 983048 | tf_op jit(solution)/shard_map/ppermute | solution.py:203
  48.4 12.8 %collective-permute-start.14 = (bf16[80,2048]{1,0:T(8,128)(2,1)S(1)}, bf16[80,2048]{1,0:T(8,128)(2,1)S(1)}, u32[]{:S(2)}, u32[]{:S(2)}) collective-permute-start(bf16[80,2048]{1,0:T(8,128)(2,1)S(1)} %get-tuple-element.136), channel_id=1, source_target_pairs={{0,4},{1,5},{2,6},{3,7},{4,0},{5,1},{6,2},{7,3},{8,12},{9,13},{10,... | collective-permute-start | bytes 983048 | tf_op jit(solution)/shard_map/ppermute | solution.py:203
  61.8 14.2 %collective-permute-start.17 = (bf16[80,2048]{1,0:T(8,128)(2,1)S(1)}, bf16[80,2048]{1,0:T(8,128)(2,1)S(1)}, u32[]{:S(2)}, u32[]{:S(2)}) collective-permute-start(bf16[80,2048]{1,0:T(8,128)(2,1)S(1)} %get-tuple-element.149), channel_id=1, source_target_pairs={{0,4},{1,5},{2,6},{3,7},{4,0},{5,1},{6,2},{7,3},{8,12},{9,13},{10,... | collective-permute-start | bytes 983048 | tf_op jit(solution)/shard_map/ppermute | solution.py:203
  63.5 15.5 %collective-permute-start.16 = (bf16[80,2048]{1,0:T(8,128)(2,1)S(1)}, bf16[80,2048]{1,0:T(8,128)(2,1)S(1)}, u32[]{:S(2)}, u32[]{:S(2)}) collective-permute-start(bf16[80,2048]{1,0:T(8,128)(2,1)S(1)} %get-tuple-element.147), channel_id=1, source_target_pairs={{0,2},{1,3},{2,0},{3,1},{4,6},{5,7},{6,4},{7,5},{8,10},{9,11},{10,... | collective-permute-start | bytes 983048 | tf_op jit(solution)/shard_map/ppermute | solution.py:203
  64.4 17.1 %collective-permute-start.18 = (bf16[80,2048]{1,0:T(8,128)(2,1)S(1)}, bf16[80,2048]{1,0:T(8,128)(2,1)S(1)}, u32[]{:S(2)}, u32[]{:S(2)}) collective-permute-start(bf16[80,2048]{1,0:T(8,128)(2,1)S(1)} %get-tuple-element.151), channel_id=1, source_target_pairs={{0,6},{1,7},{2,4},{3,5},{4,2},{5,3},{6,0},{7,1},{8,14},{9,15},{10,... | collective-permute-start | bytes 983048 | tf_op jit(solution)/shard_map/ppermute | solution.py:203
  76.0 15.9 %collective-permute-start.20 = (bf16[80,2048]{1,0:T(8,128)(2,1)S(1)}, bf16[80,2048]{1,0:T(8,128)(2,1)S(1)}, u32[]{:S(2)}, u32[]{:S(2)}) collective-permute-start(bf16[80,2048]{1,0:T(8,128)(2,1)S(1)} %get-tuple-element.168), channel_id=1, source_target_pairs={{0,4},{1,5},{2,6},{3,7},{4,0},{5,1},{6,2},{7,3},{8,12},{9,13},{10,... | collective-permute-start | bytes 983048 | tf_op jit(solution)/shard_map/ppermute | solution.py:203
  79.0 12.9 %collective-permute-start.19 = (bf16[80,2048]{1,0:T(8,128)(2,1)S(1)}, bf16[80,2048]{1,0:T(8,128)(2,1)S(1)}, u32[]{:S(2)}, u32[]{:S(2)}) collective-permute-start(bf16[80,2048]{1,0:T(8,128)(2,1)S(1)} %get-tuple-element.166), channel_id=1, source_target_pairs={{0,2},{1,3},{2,0},{3,1},{4,6},{5,7},{6,4},{7,5},{8,10},{9,11},{10,... | collective-permute-start | bytes 983048 | tf_op jit(solution)/shard_map/ppermute | solution.py:203
  81.5 14.6 %collective-permute-start.21 = (bf16[80,2048]{1,0:T(8,128)(2,1)S(1)}, bf16[80,2048]{1,0:T(8,128)(2,1)S(1)}, u32[]{:S(2)}, u32[]{:S(2)}) collective-permute-start(bf16[80,2048]{1,0:T(8,128)(2,1)S(1)} %get-tuple-element.170), channel_id=1, source_target_pairs={{0,6},{1,7},{2,4},{3,5},{4,2},{5,3},{6,0},{7,1},{8,14},{9,15},{10,... | collective-permute-start | bytes 983048 | tf_op jit(solution)/shard_map/ppermute | solution.py:203
  91.9 10.9 %collective-permute-start.24 = (bf16[80,2048]{1,0:T(8,128)(2,1)S(1)}, bf16[80,2048]{1,0:T(8,128)(2,1)S(1)}, u32[]{:S(2)}, u32[]{:S(2)}) collective-permute-start(bf16[80,2048]{1,0:T(8,128)(2,1)S(1)} %get-tuple-element.180), channel_id=1, source_target_pairs={{0,2},{1,3},{2,0},{3,1},{4,6},{5,7},{6,4},{7,5},{8,10},{9,11},{10,... | collective-permute-start | bytes 983048 | tf_op jit(solution)/shard_map/ppermute | solution.py:203
  92.2 12.8 %collective-permute-start.25 = (bf16[80,2048]{1,0:T(8,128)(2,1)S(1)}, bf16[80,2048]{1,0:T(8,128)(2,1)S(1)}, u32[]{:S(2)}, u32[]{:S(2)}) collective-permute-start(bf16[80,2048]{1,0:T(8,128)(2,1)S(1)} %get-tuple-element.182), channel_id=1, source_target_pairs={{0,4},{1,5},{2,6},{3,7},{4,0},{5,1},{6,2},{7,3},{8,12},{9,13},{10,... | collective-permute-start | bytes 983048 | tf_op jit(solution)/shard_map/ppermute | solution.py:203
  101.0 16.0 %collective-permute-start.29 = (bf16[128,2048]{1,0:T(8,128)(2,1)S(1)}, bf16[128,2048]{1,0:T(8,128)(2,1)S(1)}, u32[]{:S(2)}, u32[]{:S(2)}) collective-permute-start(bf16[128,2048]{1,0:T(8,128)(2,1)S(1)} %shard_map.74), channel_id=1, source_target_pairs={{0,8},{8,16},{16,24},{24,0},{1,9},{9,17},{17,25},{25,1},{2,10},{10... | collective-permute-start | bytes 1572872 | tf_op jit(solution)/shard_map/ppermute | solution.py:200
  106.3 14.1 %collective-permute-start.27 = (bf16[64,2048]{1,0:T(8,128)(2,1)S(1)}, bf16[64,2048]{1,0:T(8,128)(2,1)S(1)}, u32[]{:S(2)}, u32[]{:S(2)}) collective-permute-start(bf16[64,2048]{1,0:T(8,128)(2,1)S(1)} %get-tuple-element.190), channel_id=1, source_target_pairs={{0,1},{1,0},{2,3},{3,2},{4,5},{5,4},{6,7},{7,6},{8,9},{9,8},{10,11... | collective-permute-start | bytes 786440 | tf_op jit(solution)/shard_map/ppermute | solution.py:203
  117.0 17.9 %collective-permute-start.30 = (bf16[128,2048]{1,0:T(8,128)(2,1)S(1)}, bf16[128,2048]{1,0:T(8,128)(2,1)S(1)}, u32[]{:S(2)}, u32[]{:S(2)}) collective-permute-start(bf16[128,2048]{1,0:T(8,128)(2,1)S(1)} %collective-permute-done.29), channel_id=1, source_target_pairs={{0,8},{8,16},{16,24},{24,0},{1,9},{9,17},{17,25},{25,1},{2,10},{10... | collective-permute-start | bytes 1572872 | tf_op jit(solution)/shard_map/ppermute | solution.py:200
  117.0 10.6 %collective-permute-start.31 = (bf16[80,2048]{1,0:T(8,128)(2,1)S(1)}, bf16[80,2048]{1,0:T(8,128)(2,1)S(1)}, u32[]{:S(2)}, u32[]{:S(2)}) collective-permute-start(bf16[80,2048]{1,0:T(8,128)(2,1)S(1)} %get-tuple-element.195), channel_id=1, source_target_pairs={{0,2},{1,3},{2,0},{3,1},{4,6},{5,7},{6,4},{7,5},{8,10},{9,11},{10,... | collective-permute-start | bytes 983048 | tf_op jit(solution)/shard_map/ppermute | solution.py:203
  119.0 15.9 %collective-permute-start.33 = (bf16[80,2048]{1,0:T(8,128)(2,1)S(1)}, bf16[80,2048]{1,0:T(8,128)(2,1)S(1)}, u32[]{:S(2)}, u32[]{:S(2)}) collective-permute-start(bf16[80,2048]{1,0:T(8,128)(2,1)S(1)} %get-tuple-element.199), channel_id=1, source_target_pairs={{0,4},{1,5},{2,6},{3,7},{4,0},{5,1},{6,2},{7,3},{8,12},{9,13},{10,... | collective-permute-start | bytes 983048 | tf_op jit(solution)/shard_map/ppermute | solution.py:203
  119.0 15.9 %collective-permute-start.35 = (bf16[80,2048]{1,0:T(8,128)(2,1)S(1)}, bf16[80,2048]{1,0:T(8,128)(2,1)S(1)}, u32[]{:S(2)}, u32[]{:S(2)}) collective-permute-start(bf16[80,2048]{1,0:T(8,128)(2,1)S(1)} %get-tuple-element.203), channel_id=1, source_target_pairs={{0,6},{1,7},{2,4},{3,5},{4,2},{5,3},{6,0},{7,1},{8,14},{9,15},{10,... | collective-permute-start | bytes 983048 | tf_op jit(solution)/shard_map/ppermute | solution.py:203
  134.9 10.5 %collective-permute-start.32 = (bf16[80,2048]{1,0:T(8,128)(2,1)S(1)}, bf16[80,2048]{1,0:T(8,128)(2,1)S(1)}, u32[]{:S(2)}, u32[]{:S(2)}) collective-permute-start(bf16[80,2048]{1,0:T(8,128)(2,1)S(1)} %get-tuple-element.196), channel_id=1, source_target_pairs={{0,2},{1,3},{2,0},{3,1},{4,6},{5,7},{6,4},{7,5},{8,10},{9,11},{10,... | collective-permute-start | bytes 983048 | tf_op jit(solution)/shard_map/ppermute | solution.py:203
  135.2 13.9 %collective-permute-start.34 = (bf16[80,2048]{1,0:T(8,128)(2,1)S(1)}, bf16[80,2048]{1,0:T(8,128)(2,1)S(1)}, u32[]{:S(2)}, u32[]{:S(2)}) collective-permute-start(bf16[80,2048]{1,0:T(8,128)(2,1)S(1)} %get-tuple-element.200), channel_id=1, source_target_pairs={{0,4},{1,5},{2,6},{3,7},{4,0},{5,1},{6,2},{7,3},{8,12},{9,13},{10,... | collective-permute-start | bytes 983048 | tf_op jit(solution)/shard_map/ppermute | solution.py:203
  136.7 13.3 %collective-permute-start.36 = (bf16[80,2048]{1,0:T(8,128)(2,1)S(1)}, bf16[80,2048]{1,0:T(8,128)(2,1)S(1)}, u32[]{:S(2)}, u32[]{:S(2)}) collective-permute-start(bf16[80,2048]{1,0:T(8,128)(2,1)S(1)} %get-tuple-element.204), channel_id=1, source_target_pairs={{0,6},{1,7},{2,4},{3,5},{4,2},{5,3},{6,0},{7,1},{8,14},{9,15},{10,... | collective-permute-start | bytes 983048 | tf_op jit(solution)/shard_map/ppermute | solution.py:203
  141.4 15.9 %collective-permute-start.41 = (bf16[128,2048]{1,0:T(8,128)(2,1)S(1)}, bf16[128,2048]{1,0:T(8,128)(2,1)S(1)}, u32[]{:S(2)}, u32[]{:S(2)}) collective-permute-start(bf16[128,2048]{1,0:T(8,128)(2,1)S(1)} %shard_map.76), channel_id=1, source_target_pairs={{0,24},{8,0},{16,8},{24,16},{1,25},{9,1},{17,9},{25,17},{2,26},{10... | collective-permute-start | bytes 1572872 | tf_op jit(solution)/shard_map/ppermute | solution.py:200
  145.1 23.3 %collective-permute-start.42 = (bf16[128,2048]{1,0:T(8,128)(2,1)S(1)}, bf16[128,2048]{1,0:T(8,128)(2,1)S(1)}, u32[]{:S(2)}, u32[]{:S(2)}) collective-permute-start(bf16[128,2048]{1,0:T(8,128)(2,1)S(1)} %shard_map.78), channel_id=1, source_target_pairs={{0,8},{8,16},{16,24},{24,0},{1,9},{9,17},{17,25},{25,1},{2,10},{10... | collective-permute-start | bytes 1572872 | tf_op jit(solution)/shard_map/ppermute | solution.py:200
  151.3 17.1 %collective-permute-start.39 = (bf16[64,2048]{1,0:T(8,128)(2,1)S(1)}, bf16[64,2048]{1,0:T(8,128)(2,1)S(1)}, u32[]{:S(2)}, u32[]{:S(2)}) collective-permute-start(bf16[64,2048]{1,0:T(8,128)(2,1)S(1)} %get-tuple-element.217), channel_id=1, source_target_pairs={{0,1},{1,0},{2,3},{3,2},{4,5},{5,4},{6,7},{7,6},{8,9},{9,8},{10,11... | collective-permute-start | bytes 786440 | tf_op jit(solution)/shard_map/ppermute | solution.py:203
  151.4 17.0 %collective-permute-start.40 = (bf16[64,2048]{1,0:T(8,128)(2,1)S(1)}, bf16[64,2048]{1,0:T(8,128)(2,1)S(1)}, u32[]{:S(2)}, u32[]{:S(2)}) collective-permute-start(bf16[64,2048]{1,0:T(8,128)(2,1)S(1)} %get-tuple-element.218), channel_id=1, source_target_pairs={{0,1},{1,0},{2,3},{3,2},{4,5},{5,4},{6,7},{7,6},{8,9},{9,8},{10,11... | collective-permute-start | bytes 786440 | tf_op jit(solution)/shard_map/ppermute | solution.py:203
  (22 other events, 149.9 us)

commit v8 on v7

--- a/solution.py
+++ b/solution.py
@@ -208,10 +208,11 @@
     def shape(rows):
         return jax.ShapeDtypeStruct((rows, z.width), BF16)
 
-    def pick(blocks, ride):
+    def pick(blocks, ride, flops=1000):
         n = len(blocks)
         rows = n * z.cap + (z.ride if ride else 0)
-        return call(functools.partial(pick_kernel, z, n, ride), [shape(rows)] * z.chips, n)(*blocks)
+        body = functools.partial(pick_kernel, z, n, ride)
+        return call(body, [shape(rows)] * z.chips, n, flops=flops)(*blocks)
 
     def arrived(arrays):
         out = jax.ShapeDtypeStruct((8, 128), BF16)
@@ -220,7 +221,7 @@
     def slabs_across(slabs):
         return [across(s, CORES * q) for q, s in enumerate(slabs)]
 
-    def expert(slabs, n):
+    def expert(slabs, n, flops=1000):
         rows = n * z.cap
         return call(
             functools.partial(expert_kernel, z, rows),
@@ -230,9 +231,11 @@
                 pltpu.VMEM((z.chips * rows, z.width), BF16),
                 pltpu.VMEM((z.chips * rows, gate_weight.shape[2]), BF16),
             ],
+            flops,
         )(*slabs, gate_weight[0], up_weight[0], down_weight[0])
 
     def mix(blocks, backs):
+        riders = slots[1]
         mine, *other = call(
             functools.partial(mix_kernel, z, CORES),
             [shape(z.toks), shape(z.toks // 2), shape(z.toks // 2)],
@@ -244,46 +247,43 @@
     def join(parts):
         return call(join_kernel, shape(z.toks), len(parts))(*parts)
 
-    far = layers // 2
-    out_turns = list(range(layers))
-    back_turns = [far] + [d for d in out_turns if d not in (0, far)] + [0]
-
     own = call(functools.partial(pad_kernel, z), shape(z.toks + z.extra), 3)(
         tokens, expert_ids.T, router_weight.T
     )
 
+    end = layers - 1
+    turns = [(d, True) for d in range(end)] + [(d, False) for d in range(1, end)]
+    turns += [(end, True), (end, False), (0, False)]
     blocks, pairs, slots, results = {0: own}, {}, {}, {}
-    for d in out_turns:
-        if d:
-            blocks[d] = after([along(blocks[d - 1], 1)], slots[d - 1][1])[0]
-        pairs[d] = [blocks[d], across(blocks[d], 1)]
-        slabs = pick(pairs[d], d == 1)
-        ready = slabs
-        if d:
-            gate = arrived(slots[d - 1][1:] + ([results[d - 2][0]] if d > 1 else []))
-            ready = [after([s], gate)[0] for s in slabs]
-            results[d - 1] = expert(after(slots[d - 1], slabs[0]), 2)
-        slots[d] = slabs_across(ready)
-    riders = slots[1]
-    results[d] = expert(after(slots[d], results[d - 1][0]), 2)
-
-    backs, home, leaving = slots[d], {}, {}
-    for i, d in enumerate(back_turns):
-        first = [leaving[back_turns[i - 2]]] if i > 1 else [results[layers - 2 + i][0]]
-        if d == 0:
-            first = first + [home[far]]
-        rows = [after([r], b, *first)[0] for r, b in zip(results[d], backs)]
-        backs = slabs_across(rows)
-        last = leaving[back_turns[i - 1]] if i else results[layers - 1][0]
-        sums = mix(pairs[d], after(backs, last))
-        if d:
-            leaving[d] = join(sums)
-            way = layers - d
-            if d == far:
-                home[d] = along(along(leaving[d], way // 2), way - way // 2)
-            else:
-                home[d] = along(leaving[d], way)
-    return join(sums + [home[d] for d in out_turns[1:]])
+    leaving, home, seen, waiting = {}, {}, None, None
+    for d, outward in turns:
+        if outward:
+            if d:
+                blocks[d] = after([along(blocks[d - 1], 1)], slots[d - 1][1])[0]
+            pairs[d] = [blocks[d], across(blocks[d], 1)]
+            rows = slabs = pick(pairs[d], d == 1, PHASE_FLOPS if d == end else 1000)
+            if 0 < d < end:
+                gate = arrived(slots[d - 1][1:] + ([results[d - 2][0]] if d > 1 else []))
+                rows = [after([s], gate)[0] for s in slabs]
+                results[d - 1] = expert(after(slots[d - 1], slabs[0]), 2)
+            if d == end:
+                rows = [after([r], b)[0] for r, b in zip(slabs, seen)]
+            seen = slots[d] = slabs_across(rows)
+            if d == end - 1:
+                results[d] = expert(slots[d], 2)
+            if d == end:
+                first = [leaving[e] for e in range(1, end)]
+                results[d] = expert(after(slots[d], *first), 2, PHASE_FLOPS)
+        else:
+            rows = [after([r], b)[0] for r, b in zip(results[d], seen)]
+            seen = backs = slabs_across(rows)
+            first = [(home if d else leaving)[waiting]] if waiting else [results[end - 1][0]]
+            sums = mix(pairs[d], after(backs, *first))
+            if d:
+                leaving[d] = join(sums)
+                home[d] = along(leaving[d], layers - d)
+                waiting = d
+    return join(sums + [home[d] for d in range(1, layers)])
 
 
 def solution(mesh):

time: 170 us -> 153 us (0.900)
  waiting for transfers between devices: 97.4 us -> 77.6 us
  starting transfers between devices: 42.6 us -> 44.7 us
    ppermute x7 -> x6, waiting for transfers between devices: 39.4 us -> 16.7 us  [along(): lax.ppermute(array, 'expert', [(i, (i + d) % layers) for i in range(layer...]
    ppermute x36, waiting for transfers between devices: 58 us -> 61 us  [across(): lax.ppermute(array, 'zero', [(i, i ^ o) for i in range(near)])]
    ppermute x7 -> x6, starting transfers between devices: 9.58 us -> 12.4 us  [along(): lax.ppermute(array, 'expert', [(i, (i + d) % layers) for i in range(layer...]
    unnamed x22 -> x28, local copies, waits for them, and re-layouts: 7.19 us -> 7.99 us
  transfers between devices with their start and end apart: 43 -> 42, of which waited for: 27 -> 21; matrix products, arithmetic and copies ran while one was open for 0% -> 0% of each run, Pallas kernels for 12% -> 13%
where the time goes in v8:
time: 153 us
  waiting for transfers between devices  77.6 us (51%)
  starting transfers between devices  44.7 us (29%)
  Pallas kernels  22.2 us (15%)
  local copies, waits for them, and re-layouts  7.99 us (5%)
    ppermute x36, waiting for transfers between devices, across(): lax.ppermute(array, 'zero', [(i, i ^ o) for i in range(near)])  61 us
    ppermute x36, starting transfers between devices, across(): lax.ppermute(array, 'zero', [(i, i ^ o) for i in range(near)])  32.4 us
    ppermute x6, waiting for transfers between devices, along(): lax.ppermute(array, 'expert', [(i, (i + d) % layers) for i in range(layer...  16.7 us
    pallas_call x4, Pallas kernels, expert(): call(functools.partial(expert_kernel, z, rows), [shape(rows)] * z.chips,...  12.9 us
    ppermute x6, starting transfers between devices, along(): lax.ppermute(array, 'expert', [(i, (i + d) % layers) for i in range(layer...  12.4 us
    unnamed x28, local copies, waits for them, and re-layouts  7.99 us
    pallas_call x4, Pallas kernels, mix(): call(functools.partial(mix_kernel, z, CORES), [shape(z.toks), shape(z.tok...  5.36 us
  transfers between devices with their start and end apart: 42, of which 21 were waited for; matrix products, arithmetic and copies ran while one was open for 0% of the time, Pallas kernels for 13%

profile of v8, /device:TPU:0, one launch (start us, length us, event | category | flops | bytes accessed | tf_op | source)
XLA Modules:
  0.0 152.7 jit_solution(1356670341910439410)
XLA Ops:
  3.2 2.6 %collective-permute-start.1 = (bf16[136,2048]{1,0:T(8,128)(2,1)S(1)}, bf16[136,2048]{1,0:T(8,128)(2,1)S(1)}, u32[]{:S(2)}, u32[]{:S(2)}) collective-permute-start(bf16[136,2048]{1,0:T(8,128)(2,1)S(1)} %shard_map.64.refs_0_), channel_id=1, source_target_pairs={{0,8},{8,16},{16,24},{24,0},{1,9},{9,17},{17,25},{25,1},{2,10},{10... | collective-permute-start | bytes 1671176 | tf_op jit(solution)/shard_map/ppermute | solution.py:200
  7.2 1.8 %collective-permute-start.2 = (bf16[80,2048]{1,0:T(8,128)(2,1)S(1)}, bf16[80,2048]{1,0:T(8,128)(2,1)S(1)}, u32[]{:S(2)}, u32[]{:S(2)}) collective-permute-start(bf16[80,2048]{1,0:T(8,128)(2,1)S(1)} %get-tuple-element.108), channel_id=1, source_target_pairs={{0,2},{1,3},{2,0},{3,1},{4,6},{5,7},{6,4},{7,5},{8,10},{9,11},{10,... | collective-permute-start | bytes 983048 | tf_op jit(solution)/shard_map/ppermute | solution.py:203
  10.7 10.3 %collective-permute-done.1.refs_0_ = bf16[136,2048]{1,0:T(8,128)(2,1)S(1)} collective-permute-done((bf16[136,2048]{1,0:T(8,128)(2,1)S(1)}, bf16[136,2048]{1,0:T(8,128)(2,1)S(1)}, u32[]{:S(2)}, u32[]{:S(2)}) %collective-permute-start.1) | collective-permute-done | bytes 557088 | tf_op jit(solution)/shard_map/ppermute | solution.py:200
  21.1 4.4 %collective-permute-done.4.refs_2_ = bf16[80,2048]{1,0:T(8,128)(2,1)S(1)} collective-permute-done((bf16[80,2048]{1,0:T(8,128)(2,1)S(1)}, bf16[80,2048]{1,0:T(8,128)(2,1)S(1)}, u32[]{:S(2)}, u32[]{:S(2)}) %collective-permute-start.4) | collective-permute-done | bytes 327712 | tf_op jit(solution)/shard_map/ppermute | solution.py:203
  27.4 1.7 %collective-permute-start.8 = (bf16[88,2048]{1,0:T(8,128)(2,1)S(1)}, bf16[88,2048]{1,0:T(8,128)(2,1)S(1)}, u32[]{:S(2)}, u32[]{:S(2)}) collective-permute-start(bf16[88,2048]{1,0:T(8,128)(2,1)S(1)} %get-tuple-element.119), channel_id=1, source_target_pairs={{0,6},{1,7},{2,4},{3,5},{4,2},{5,3},{6,0},{7,1},{8,14},{9,15},{10,... | collective-permute-start | bytes 1081352 | tf_op jit(solution)/shard_map/ppermute | solution.py:203
  29.7 1.9 %copy-done.1 = bf16[1,2048,768]{2,1,0:T(8,128)(2,1)S(1)} copy-done((bf16[1,2048,768]{2,1,0:T(8,128)(2,1)S(1)}, bf16[1,2048,768]{2,1,0:T(8,128)(2,1)}, u32[]{:S(2)}) %copy-start.1) | copy-done | bytes 3145752
  31.6 1.9 %copy-done.3 = bf16[1,768,2048]{2,1,0:T(8,128)(2,1)S(1)} copy-done((bf16[1,768,2048]{2,1,0:T(8,128)(2,1)S(1)}, bf16[1,768,2048]{2,1,0:T(8,128)(2,1)}, u32[]{:S(2)}) %copy-start.3) | copy-done | bytes 3145752
  33.5 3.2 %shard_map.67 = (bf16[80,2048]{1,0:T(8,128)(2,1)S(1)}, bf16[80,2048]{1,0:T(8,128)(2,1)S(1)}, bf16[80,2048]{1,0:T(8,128)(2,1)S(1)}, bf16[80,2048]{1,0:T(8,128)(2,1)S(1)}) custom-call(bf16[80,2048]{1,0:T(8,128)(2,1)S(1)} %get-tuple-element.121.refs_0_, bf16[80,2048]{1,0:T(8,128)(2,1)S(1)} %collective-permute-done.2.refs_1_, ...), custom_call_target="tpu_custom_call" | custom-call | flops 1000 | bytes 1000 | tf_op jit(solution)/shard_map/pallas_call | solution.py:226
  37.9 6.4 %collective-permute-done.8.refs_3_.refs_5_ = bf16[88,2048]{1,0:T(8,128)(2,1)S(1)} collective-permute-done((bf16[88,2048]{1,0:T(8,128)(2,1)S(1)}, bf16[88,2048]{1,0:T(8,128)(2,1)S(1)}, u32[]{:S(2)}, u32[]{:S(2)}) %collective-permute-start.8) | collective-permute-done | bytes 360480 | tf_op jit(solution)/shard_map/ppermute | solution.py:203
  49.8 1.6 %collective-permute-start.10 = (bf16[136,2048]{1,0:T(8,128)(2,1)S(1)}, bf16[136,2048]{1,0:T(8,128)(2,1)S(1)}, u32[]{:S(2)}, u32[]{:S(2)}) collective-permute-start(bf16[136,2048]{1,0:T(8,128)(2,1)S(1)} %collective-permute-done.9.refs_0_), channel_id=1, source_target_pairs={{0,8},{8,16},{16,24},{24,0},{1,9},{9,17},{17,25},{25,1},{2,10},{10... | collective-permute-start | bytes 1671176 | tf_op jit(solution)/shard_map/ppermute | solution.py:200
  51.4 3.2 %shard_map.71 = (bf16[80,2048]{1,0:T(8,128)(2,1)S(1)}, bf16[80,2048]{1,0:T(8,128)(2,1)S(1)}, bf16[80,2048]{1,0:T(8,128)(2,1)S(1)}, bf16[80,2048]{1,0:T(8,128)(2,1)S(1)}) custom-call(bf16[88,2048]{1,0:T(8,128)(2,1)S(1)} %get-tuple-element.138.refs_0_.refs_2_, bf16[88,2048]{1,0:T(8,128)(2,1)S(1)} %collective-permute-done.6.refs_1_.refs_3_, ...), custom_call_target="tpu_custom_call" | custom-call | flops 1000 | bytes 1000 | tf_op jit(solution)/shard_map/pallas_call | solution.py:226
  54.6 3.3 %collective-permute-done.15.refs_3_ = bf16[80,2048]{1,0:T(8,128)(2,1)S(1)} collective-permute-done((bf16[80,2048]{1,0:T(8,128)(2,1)S(1)}, bf16[80,2048]{1,0:T(8,128)(2,1)S(1)}, u32[]{:S(2)}, u32[]{:S(2)}) %collective-permute-start.15) | collective-permute-done | bytes 327712 | tf_op jit(solution)/shard_map/ppermute | solution.py:203
  59.5 4.6 %collective-permute-done.14.refs_2_ = bf16[80,2048]{1,0:T(8,128)(2,1)S(1)} collective-permute-done((bf16[80,2048]{1,0:T(8,128)(2,1)S(1)}, bf16[80,2048]{1,0:T(8,128)(2,1)S(1)}, u32[]{:S(2)}, u32[]{:S(2)}) %collective-permute-start.14) | collective-permute-done | bytes 327712 | tf_op jit(solution)/shard_map/ppermute | solution.py:203
  64.7 1.6 %collective-permute-start.16 = (bf16[80,2048]{1,0:T(8,128)(2,1)S(1)}, bf16[80,2048]{1,0:T(8,128)(2,1)S(1)}, u32[]{:S(2)}, u32[]{:S(2)}) collective-permute-start(bf16[80,2048]{1,0:T(8,128)(2,1)S(1)} %get-tuple-element.149), channel_id=1, source_target_pairs={{0,2},{1,3},{2,0},{3,1},{4,6},{5,7},{6,4},{7,5},{8,10},{9,11},{10,... | collective-permute-start | bytes 983048 | tf_op jit(solution)/shard_map/ppermute | solution.py:203
  66.3 3.2 %shard_map.70 = (bf16[80,2048]{1,0:T(8,128)(2,1)S(1)}, bf16[80,2048]{1,0:T(8,128)(2,1)S(1)}, bf16[80,2048]{1,0:T(8,128)(2,1)S(1)}, bf16[80,2048]{1,0:T(8,128)(2,1)S(1)}) custom-call(bf16[80,2048]{1,0:T(8,128)(2,1)S(1)} %get-tuple-element.132.refs_0_, bf16[80,2048]{1,0:T(8,128)(2,1)S(1)} %collective-permute-done.12.refs_1_, ...), custom_call_target="tpu_custom_call" | custom-call | flops 1000 | bytes 1000 | tf_op jit(solution)/shard_map/pallas_call | solution.py:226
  69.6 5.1 %collective-permute-done.19.refs_8_ = bf16[80,2048]{1,0:T(8,128)(2,1)S(1)} collective-permute-done((bf16[80,2048]{1,0:T(8,128)(2,1)S(1)}, bf16[80,2048]{1,0:T(8,128)(2,1)S(1)}, u32[]{:S(2)}, u32[]{:S(2)}) %collective-permute-start.19) | collective-permute-done | bytes 327712 | tf_op jit(solution)/shard_map/ppermute | solution.py:203
  76.5 1.8 %collective-permute-start.23 = (bf16[80,2048]{1,0:T(8,128)(2,1)S(1)}, bf16[80,2048]{1,0:T(8,128)(2,1)S(1)}, u32[]{:S(2)}, u32[]{:S(2)}) collective-permute-start(bf16[80,2048]{1,0:T(8,128)(2,1)S(1)} %get-tuple-element.162), channel_id=1, source_target_pairs={{0,6},{1,7},{2,4},{3,5},{4,2},{5,3},{6,0},{7,1},{8,14},{9,15},{10,... | collective-permute-start | bytes 983048 | tf_op jit(solution)/shard_map/ppermute | solution.py:203
  80.2 3.9 %collective-permute-start.27 = (bf16[128,2048]{1,0:T(8,128)(2,1)S(1)}, bf16[128,2048]{1,0:T(8,128)(2,1)S(1)}, u32[]{:S(2)}, u32[]{:S(2)}) collective-permute-start(bf16[128,2048]{1,0:T(8,128)(2,1)S(1)} %shard_map.73), channel_id=1, source_target_pairs={{0,24},{8,0},{16,8},{24,16},{1,25},{9,1},{17,9},{25,17},{2,26},{10... | collective-permute-start | bytes 1572872 | tf_op jit(solution)/shard_map/ppermute | solution.py:200
  84.7 3.4 %collective-permute-done.23.refs_9_ = bf16[80,2048]{1,0:T(8,128)(2,1)S(1)} collective-permute-done((bf16[80,2048]{1,0:T(8,128)(2,1)S(1)}, bf16[80,2048]{1,0:T(8,128)(2,1)S(1)}, u32[]{:S(2)}, u32[]{:S(2)}) %collective-permute-start.23) | collective-permute-done | bytes 327712 | tf_op jit(solution)/shard_map/ppermute | solution.py:203
  88.1 1.8 %collective-permute-start.24 = (bf16[80,2048]{1,0:T(8,128)(2,1)S(1)}, bf16[80,2048]{1,0:T(8,128)(2,1)S(1)}, u32[]{:S(2)}, u32[]{:S(2)}) collective-permute-start(bf16[80,2048]{1,0:T(8,128)(2,1)S(1)} %get-tuple-element.163), channel_id=1, source_target_pairs={{0,6},{1,7},{2,4},{3,5},{4,2},{5,3},{6,0},{7,1},{8,14},{9,15},{10,... | collective-permute-start | bytes 983048 | tf_op jit(solution)/shard_map/ppermute | solution.py:203
  89.9 5.1 %collective-permute-done.20.refs_8_ = bf16[80,2048]{1,0:T(8,128)(2,1)S(1)} collective-permute-done((bf16[80,2048]{1,0:T(8,128)(2,1)S(1)}, bf16[80,2048]{1,0:T(8,128)(2,1)S(1)}, u32[]{:S(2)}, u32[]{:S(2)}) %collective-permute-start.20) | collective-permute-done | bytes 327712 | tf_op jit(solution)/shard_map/ppermute | solution.py:203
  95.7 1.6 %collective-permute-start.18 = (bf16[80,2048]{1,0:T(8,128)(2,1)S(1)}, bf16[80,2048]{1,0:T(8,128)(2,1)S(1)}, u32[]{:S(2)}, u32[]{:S(2)}) collective-permute-start(bf16[80,2048]{1,0:T(8,128)(2,1)S(1)} %get-tuple-element.151), channel_id=1, source_target_pairs={{0,2},{1,3},{2,0},{3,1},{4,6},{5,7},{6,4},{7,5},{8,10},{9,11},{10,... | collective-permute-start | bytes 983048 | tf_op jit(solution)/shard_map/ppermute | solution.py:203
  101.5 2.6 %collective-permute-start.36 = (bf16[128,2048]{1,0:T(8,128)(2,1)S(1)}, bf16[128,2048]{1,0:T(8,128)(2,1)S(1)}, u32[]{:S(2)}, u32[]{:S(2)}) collective-permute-start(bf16[128,2048]{1,0:T(8,128)(2,1)S(1)} %shard_map.75), channel_id=1, source_target_pairs={{0,16},{8,24},{16,0},{24,8},{1,17},{9,25},{17,1},{25,9},{2,18},{10... | collective-permute-start | bytes 1572872 | tf_op jit(solution)/shard_map/ppermute | solution.py:200
  104.1 4.1 %collective-permute-done.21.refs_2_ = bf16[80,2048]{1,0:T(8,128)(2,1)S(1)} collective-permute-done((bf16[80,2048]{1,0:T(8,128)(2,1)S(1)}, bf16[80,2048]{1,0:T(8,128)(2,1)S(1)}, u32[]{:S(2)}, u32[]{:S(2)}) %collective-permute-start.21) | collective-permute-done | bytes 327712 | tf_op jit(solution)/shard_map/ppermute | solution.py:203
  108.3 3.2 %shard_map.76 = (bf16[80,2048]{1,0:T(8,128)(2,1)S(1)}, bf16[80,2048]{1,0:T(8,128)(2,1)S(1)}, bf16[80,2048]{1,0:T(8,128)(2,1)S(1)}, bf16[80,2048]{1,0:T(8,128)(2,1)S(1)}) custom-call(bf16[80,2048]{1,0:T(8,128)(2,1)S(1)} %get-tuple-element.178.refs_0_, bf16[80,2048]{1,0:T(8,128)(2,1)S(1)} %collective-permute-done.18.refs_1_, ...), custom_call_target="tpu_custom_call" | custom-call | flops 49999998976 | bytes 1000 | tf_op jit(solution)/shard_map/pallas_call | solution.py:226
  111.5 1.9 %collective-permute-start.34 = (bf16[80,2048]{1,0:T(8,128)(2,1)S(1)}, bf16[80,2048]{1,0:T(8,128)(2,1)S(1)}, u32[]{:S(2)}, u32[]{:S(2)}) collective-permute-start(bf16[80,2048]{1,0:T(8,128)(2,1)S(1)} %get-tuple-element.195), channel_id=1, source_target_pairs={{0,6},{1,7},{2,4},{3,5},{4,2},{5,3},{6,0},{7,1},{8,14},{9,15},{10,... | collective-permute-start | bytes 983048 | tf_op jit(solution)/shard_map/ppermute | solution.py:203
  115.0 8.0 %collective-permute-done.34.refs_9_ = bf16[80,2048]{1,0:T(8,128)(2,1)S(1)} collective-permute-done((bf16[80,2048]{1,0:T(8,128)(2,1)S(1)}, bf16[80,2048]{1,0:T(8,128)(2,1)S(1)}, u32[]{:S(2)}, u32[]{:S(2)}) %collective-permute-start.34) | collective-permute-done | bytes 327712 | tf_op jit(solution)/shard_map/ppermute | solution.py:203
  123.1 1.8 %collective-permute-start.35 = (bf16[80,2048]{1,0:T(8,128)(2,1)S(1)}, bf16[80,2048]{1,0:T(8,128)(2,1)S(1)}, u32[]{:S(2)}, u32[]{:S(2)}) collective-permute-start(bf16[80,2048]{1,0:T(8,128)(2,1)S(1)} %get-tuple-element.196), channel_id=1, source_target_pairs={{0,6},{1,7},{2,4},{3,5},{4,2},{5,3},{6,0},{7,1},{8,14},{9,15},{10,... | collective-permute-start | bytes 983048 | tf_op jit(solution)/shard_map/ppermute | solution.py:203
  124.9 5.1 %collective-permute-done.32.refs_8_ = bf16[80,2048]{1,0:T(8,128)(2,1)S(1)} collective-permute-done((bf16[80,2048]{1,0:T(8,128)(2,1)S(1)}, bf16[80,2048]{1,0:T(8,128)(2,1)S(1)}, u32[]{:S(2)}, u32[]{:S(2)}) %collective-permute-start.32) | collective-permute-done | bytes 327712 | tf_op jit(solution)/shard_map/ppermute | solution.py:203
  135.7 1.6 %collective-permute-start.41 = (bf16[128,2048]{1,0:T(8,128)(2,1)S(1)}, bf16[128,2048]{1,0:T(8,128)(2,1)S(1)}, u32[]{:S(2)}, u32[]{:S(2)}) collective-permute-start(bf16[128,2048]{1,0:T(8,128)(2,1)S(1)} %shard_map.78), channel_id=1, source_target_pairs={{0,8},{8,16},{16,24},{24,0},{1,9},{9,17},{17,25},{25,1},{2,10},{10... | collective-permute-start | bytes 1572872 | tf_op jit(solution)/shard_map/ppermute | solution.py:200
  137.3 5.9 %collective-permute-done.33.refs_8_ = bf16[80,2048]{1,0:T(8,128)(2,1)S(1)} collective-permute-done((bf16[80,2048]{1,0:T(8,128)(2,1)S(1)}, bf16[80,2048]{1,0:T(8,128)(2,1)S(1)}, u32[]{:S(2)}, u32[]{:S(2)}) %collective-permute-start.33) | collective-permute-done | bytes 327712 | tf_op jit(solution)/shard_map/ppermute | solution.py:203
  146.5 5.1 %collective-permute-done.41.refs_5_ = bf16[128,2048]{1,0:T(8,128)(2,1)S(1)} collective-permute-done((bf16[128,2048]{1,0:T(8,128)(2,1)S(1)}, bf16[128,2048]{1,0:T(8,128)(2,1)S(1)}, u32[]{:S(2)}, u32[]{:S(2)}) %collective-permute-start.41) | collective-permute-done | bytes 524320 | tf_op jit(solution)/shard_map/ppermute | solution.py:200
  (97 shorter events, 38.8 us)
Async XLA Ops:
  3.2 17.9 %collective-permute-start.1 = (bf16[136,2048]{1,0:T(8,128)(2,1)S(1)}, bf16[136,2048]{1,0:T(8,128)(2,1)S(1)}, u32[]{:S(2)}, u32[]{:S(2)}) collective-permute-start(bf16[136,2048]{1,0:T(8,128)(2,1)S(1)} %shard_map.64.refs_0_), channel_id=1, source_target_pairs={{0,8},{8,16},{16,24},{24,0},{1,9},{9,17},{17,25},{25,1},{2,10},{10... | collective-permute-start | bytes 1671176 | tf_op jit(solution)/shard_map/ppermute | solution.py:200
  7.2 13.8 %collective-permute-start.2 = (bf16[80,2048]{1,0:T(8,128)(2,1)S(1)}, bf16[80,2048]{1,0:T(8,128)(2,1)S(1)}, u32[]{:S(2)}, u32[]{:S(2)}) collective-permute-start(bf16[80,2048]{1,0:T(8,128)(2,1)S(1)} %get-tuple-element.108), channel_id=1, source_target_pairs={{0,2},{1,3},{2,0},{3,1},{4,6},{5,7},{6,4},{7,5},{8,10},{9,11},{10,... | collective-permute-start | bytes 983048 | tf_op jit(solution)/shard_map/ppermute | solution.py:203
  9.0 16.5 %collective-permute-start.4 = (bf16[80,2048]{1,0:T(8,128)(2,1)S(1)}, bf16[80,2048]{1,0:T(8,128)(2,1)S(1)}, u32[]{:S(2)}, u32[]{:S(2)}) collective-permute-start(bf16[80,2048]{1,0:T(8,128)(2,1)S(1)} %get-tuple-element.111), channel_id=1, source_target_pairs={{0,4},{1,5},{2,6},{3,7},{4,0},{5,1},{6,2},{7,3},{8,12},{9,13},{10,... | collective-permute-start | bytes 983048 | tf_op jit(solution)/shard_map/ppermute | solution.py:203
  10.5 15.0 %collective-permute-start.5 = (bf16[80,2048]{1,0:T(8,128)(2,1)S(1)}, bf16[80,2048]{1,0:T(8,128)(2,1)S(1)}, u32[]{:S(2)}, u32[]{:S(2)}) collective-permute-start(bf16[80,2048]{1,0:T(8,128)(2,1)S(1)} %get-tuple-element.112), channel_id=1, source_target_pairs={{0,6},{1,7},{2,4},{3,5},{4,2},{5,3},{6,0},{7,1},{8,14},{9,15},{10,... | collective-permute-start | bytes 983048 | tf_op jit(solution)/shard_map/ppermute | solution.py:203
  21.1 16.8 %collective-permute-start.9 = (bf16[136,2048]{1,0:T(8,128)(2,1)S(1)}, bf16[136,2048]{1,0:T(8,128)(2,1)S(1)}, u32[]{:S(2)}, u32[]{:S(2)}) collective-permute-start(bf16[136,2048]{1,0:T(8,128)(2,1)S(1)} %collective-permute-done.1.refs_0_), channel_id=1, source_target_pairs={{0,8},{8,16},{16,24},{24,0},{1,9},{9,17},{17,25},{25,1},{2,10},{10... | collective-permute-start | bytes 1671176 | tf_op jit(solution)/shard_map/ppermute | solution.py:200
  26.1 11.8 %collective-permute-start.6 = (bf16[88,2048]{1,0:T(8,128)(2,1)S(1)}, bf16[88,2048]{1,0:T(8,128)(2,1)S(1)}, u32[]{:S(2)}, u32[]{:S(2)}) collective-permute-start(bf16[88,2048]{1,0:T(8,128)(2,1)S(1)} %get-tuple-element.115), channel_id=1, source_target_pairs={{0,2},{1,3},{2,0},{3,1},{4,6},{5,7},{6,4},{7,5},{8,10},{9,11},{10,... | collective-permute-start | bytes 1081352 | tf_op jit(solution)/shard_map/ppermute | solution.py:203
  27.4 16.8 %collective-permute-start.8 = (bf16[88,2048]{1,0:T(8,128)(2,1)S(1)}, bf16[88,2048]{1,0:T(8,128)(2,1)S(1)}, u32[]{:S(2)}, u32[]{:S(2)}) collective-permute-start(bf16[88,2048]{1,0:T(8,128)(2,1)S(1)} %get-tuple-element.119), channel_id=1, source_target_pairs={{0,6},{1,7},{2,4},{3,5},{4,2},{5,3},{6,0},{7,1},{8,14},{9,15},{10,... | collective-permute-start | bytes 1081352 | tf_op jit(solution)/shard_map/ppermute | solution.py:203
  29.2 16.5 %collective-permute-start.7 = (bf16[88,2048]{1,0:T(8,128)(2,1)S(1)}, bf16[88,2048]{1,0:T(8,128)(2,1)S(1)}, u32[]{:S(2)}, u32[]{:S(2)}) collective-permute-start(bf16[88,2048]{1,0:T(8,128)(2,1)S(1)} %get-tuple-element.117), channel_id=1, source_target_pairs={{0,4},{1,5},{2,6},{3,7},{4,0},{5,1},{6,2},{7,3},{8,12},{9,13},{10,... | collective-permute-start | bytes 1081352 | tf_op jit(solution)/shard_map/ppermute | solution.py:203
  37.9 7.7 %collective-permute-start.11 = (bf16[136,2048]{1,0:T(8,128)(2,1)S(1)}, bf16[136,2048]{1,0:T(8,128)(2,1)S(1)}, u32[]{:S(2)}, u32[]{:S(2)}) collective-permute-start(bf16[136,2048]{1,0:T(8,128)(2,1)S(1)} %collective-permute-done.9.refs_0_), channel_id=1, source_target_pairs={{0,1},{1,0},{2,3},{3,2},{4,5},{5,4},{6,7},{7,6},{8,9},{9,8},{10,11... | collective-permute-start | bytes 1671176 | tf_op jit(solution)/shard_map/ppermute | solution.py:203
  46.2 11.7 %collective-permute-start.15 = (bf16[80,2048]{1,0:T(8,128)(2,1)S(1)}, bf16[80,2048]{1,0:T(8,128)(2,1)S(1)}, u32[]{:S(2)}, u32[]{:S(2)}) collective-permute-start(bf16[80,2048]{1,0:T(8,128)(2,1)S(1)} %get-tuple-element.136), channel_id=1, source_target_pairs={{0,6},{1,7},{2,4},{3,5},{4,2},{5,3},{6,0},{7,1},{8,14},{9,15},{10,... | collective-permute-start | bytes 983048 | tf_op jit(solution)/shard_map/ppermute | solution.py:203
  47.8 16.2 %collective-permute-start.14 = (bf16[80,2048]{1,0:T(8,128)(2,1)S(1)}, bf16[80,2048]{1,0:T(8,128)(2,1)S(1)}, u32[]{:S(2)}, u32[]{:S(2)}) collective-permute-start(bf16[80,2048]{1,0:T(8,128)(2,1)S(1)} %get-tuple-element.134), channel_id=1, source_target_pairs={{0,4},{1,5},{2,6},{3,7},{4,0},{5,1},{6,2},{7,3},{8,12},{9,13},{10,... | collective-permute-start | bytes 983048 | tf_op jit(solution)/shard_map/ppermute | solution.py:203
  48.4 16.4 %collective-permute-start.12 = (bf16[80,2048]{1,0:T(8,128)(2,1)S(1)}, bf16[80,2048]{1,0:T(8,128)(2,1)S(1)}, u32[]{:S(2)}, u32[]{:S(2)}) collective-permute-start(bf16[80,2048]{1,0:T(8,128)(2,1)S(1)} %get-tuple-element.128), channel_id=1, source_target_pairs={{0,2},{1,3},{2,0},{3,1},{4,6},{5,7},{6,4},{7,5},{8,10},{9,11},{10,... | collective-permute-start | bytes 983048 | tf_op jit(solution)/shard_map/ppermute | solution.py:203
  49.8 16.5 %collective-permute-start.10 = (bf16[136,2048]{1,0:T(8,128)(2,1)S(1)}, bf16[136,2048]{1,0:T(8,128)(2,1)S(1)}, u32[]{:S(2)}, u32[]{:S(2)}) collective-permute-start(bf16[136,2048]{1,0:T(8,128)(2,1)S(1)} %collective-permute-done.9.refs_0_), channel_id=1, source_target_pairs={{0,8},{8,16},{16,24},{24,0},{1,9},{9,17},{17,25},{25,1},{2,10},{10... | collective-permute-start | bytes 1671176 | tf_op jit(solution)/shard_map/ppermute | solution.py:200
  58.0 11.6 %collective-permute-start.22 = (bf16[80,2048]{1,0:T(8,128)(2,1)S(1)}, bf16[80,2048]{1,0:T(8,128)(2,1)S(1)}, u32[]{:S(2)}, u32[]{:S(2)}) collective-permute-start(bf16[80,2048]{1,0:T(8,128)(2,1)S(1)} %get-tuple-element.161), channel_id=1, source_target_pairs={{0,6},{1,7},{2,4},{3,5},{4,2},{5,3},{6,0},{7,1},{8,14},{9,15},{10,... | collective-permute-start | bytes 983048 | tf_op jit(solution)/shard_map/ppermute | solution.py:203
  64.0 10.6 %collective-permute-start.19 = (bf16[80,2048]{1,0:T(8,128)(2,1)S(1)}, bf16[80,2048]{1,0:T(8,128)(2,1)S(1)}, u32[]{:S(2)}, u32[]{:S(2)}) collective-permute-start(bf16[80,2048]{1,0:T(8,128)(2,1)S(1)} %get-tuple-element.155), channel_id=1, source_target_pairs={{0,4},{1,5},{2,6},{3,7},{4,0},{5,1},{6,2},{7,3},{8,12},{9,13},{10,... | collective-permute-start | bytes 983048 | tf_op jit(solution)/shard_map/ppermute | solution.py:203
  64.7 9.9 %collective-permute-start.16 = (bf16[80,2048]{1,0:T(8,128)(2,1)S(1)}, bf16[80,2048]{1,0:T(8,128)(2,1)S(1)}, u32[]{:S(2)}, u32[]{:S(2)}) collective-permute-start(bf16[80,2048]{1,0:T(8,128)(2,1)S(1)} %get-tuple-element.149), channel_id=1, source_target_pairs={{0,2},{1,3},{2,0},{3,1},{4,6},{5,7},{6,4},{7,5},{8,10},{9,11},{10,... | collective-permute-start | bytes 983048 | tf_op jit(solution)/shard_map/ppermute | solution.py:203
  66.3 17.7 %collective-permute-start.13 = (bf16[136,2048]{1,0:T(8,128)(2,1)S(1)}, bf16[136,2048]{1,0:T(8,128)(2,1)S(1)}, u32[]{:S(2)}, u32[]{:S(2)}) collective-permute-start(bf16[136,2048]{1,0:T(8,128)(2,1)S(1)} %collective-permute-done.10.refs_0_), channel_id=1, source_target_pairs={{0,1},{1,0},{2,3},{3,2},{4,5},{5,4},{6,7},{7,6},{8,9},{9,8},{10,11... | collective-permute-start | bytes 1671176 | tf_op jit(solution)/shard_map/ppermute | solution.py:203
  76.5 11.5 %collective-permute-start.23 = (bf16[80,2048]{1,0:T(8,128)(2,1)S(1)}, bf16[80,2048]{1,0:T(8,128)(2,1)S(1)}, u32[]{:S(2)}, u32[]{:S(2)}) collective-permute-start(bf16[80,2048]{1,0:T(8,128)(2,1)S(1)} %get-tuple-element.162), channel_id=1, source_target_pairs={{0,6},{1,7},{2,4},{3,5},{4,2},{5,3},{6,0},{7,1},{8,14},{9,15},{10,... | collective-permute-start | bytes 983048 | tf_op jit(solution)/shard_map/ppermute | solution.py:203
  78.3 16.6 %collective-permute-start.20 = (bf16[80,2048]{1,0:T(8,128)(2,1)S(1)}, bf16[80,2048]{1,0:T(8,128)(2,1)S(1)}, u32[]{:S(2)}, u32[]{:S(2)}) collective-permute-start(bf16[80,2048]{1,0:T(8,128)(2,1)S(1)} %get-tuple-element.156), channel_id=1, source_target_pairs={{0,4},{1,5},{2,6},{3,7},{4,0},{5,1},{6,2},{7,3},{8,12},{9,13},{10,... | collective-permute-start | bytes 983048 | tf_op jit(solution)/shard_map/ppermute | solution.py:203
  78.9 16.8 %collective-permute-start.17 = (bf16[80,2048]{1,0:T(8,128)(2,1)S(1)}, bf16[80,2048]{1,0:T(8,128)(2,1)S(1)}, u32[]{:S(2)}, u32[]{:S(2)}) collective-permute-start(bf16[80,2048]{1,0:T(8,128)(2,1)S(1)} %get-tuple-element.150), channel_id=1, source_target_pairs={{0,2},{1,3},{2,0},{3,1},{4,6},{5,7},{6,4},{7,5},{8,10},{9,11},{10,... | collective-permute-start | bytes 983048 | tf_op jit(solution)/shard_map/ppermute | solution.py:203
  80.2 17.1 %collective-permute-start.27 = (bf16[128,2048]{1,0:T(8,128)(2,1)S(1)}, bf16[128,2048]{1,0:T(8,128)(2,1)S(1)}, u32[]{:S(2)}, u32[]{:S(2)}) collective-permute-start(bf16[128,2048]{1,0:T(8,128)(2,1)S(1)} %shard_map.73), channel_id=1, source_target_pairs={{0,24},{8,0},{16,8},{24,16},{1,25},{9,1},{17,9},{25,17},{2,26},{10... | collective-permute-start | bytes 1572872 | tf_op jit(solution)/shard_map/ppermute | solution.py:200
  88.1 16.1 %collective-permute-start.24 = (bf16[80,2048]{1,0:T(8,128)(2,1)S(1)}, bf16[80,2048]{1,0:T(8,128)(2,1)S(1)}, u32[]{:S(2)}, u32[]{:S(2)}) collective-permute-start(bf16[80,2048]{1,0:T(8,128)(2,1)S(1)} %get-tuple-element.163), channel_id=1, source_target_pairs={{0,6},{1,7},{2,4},{3,5},{4,2},{5,3},{6,0},{7,1},{8,14},{9,15},{10,... | collective-permute-start | bytes 983048 | tf_op jit(solution)/shard_map/ppermute | solution.py:203
  95.0 13.3 %collective-permute-start.21 = (bf16[80,2048]{1,0:T(8,128)(2,1)S(1)}, bf16[80,2048]{1,0:T(8,128)(2,1)S(1)}, u32[]{:S(2)}, u32[]{:S(2)}) collective-permute-start(bf16[80,2048]{1,0:T(8,128)(2,1)S(1)} %get-tuple-element.157), channel_id=1, source_target_pairs={{0,4},{1,5},{2,6},{3,7},{4,0},{5,1},{6,2},{7,3},{8,12},{9,13},{10,... | collective-permute-start | bytes 983048 | tf_op jit(solution)/shard_map/ppermute | solution.py:203
  95.7 12.6 %collective-permute-start.18 = (bf16[80,2048]{1,0:T(8,128)(2,1)S(1)}, bf16[80,2048]{1,0:T(8,128)(2,1)S(1)}, u32[]{:S(2)}, u32[]{:S(2)}) collective-permute-start(bf16[80,2048]{1,0:T(8,128)(2,1)S(1)} %get-tuple-element.151), channel_id=1, source_target_pairs={{0,2},{1,3},{2,0},{3,1},{4,6},{5,7},{6,4},{7,5},{8,10},{9,11},{10,... | collective-permute-start | bytes 983048 | tf_op jit(solution)/shard_map/ppermute | solution.py:203
  101.5 30.8 %collective-permute-start.36 = (bf16[128,2048]{1,0:T(8,128)(2,1)S(1)}, bf16[128,2048]{1,0:T(8,128)(2,1)S(1)}, u32[]{:S(2)}, u32[]{:S(2)}) collective-permute-start(bf16[128,2048]{1,0:T(8,128)(2,1)S(1)} %shard_map.75), channel_id=1, source_target_pairs={{0,16},{8,24},{16,0},{24,8},{1,17},{9,25},{17,1},{25,9},{2,18},{10... | collective-permute-start | bytes 1572872 | tf_op jit(solution)/shard_map/ppermute | solution.py:200
  111.5 11.6 %collective-permute-start.34 = (bf16[80,2048]{1,0:T(8,128)(2,1)S(1)}, bf16[80,2048]{1,0:T(8,128)(2,1)S(1)}, u32[]{:S(2)}, u32[]{:S(2)}) collective-permute-start(bf16[80,2048]{1,0:T(8,128)(2,1)S(1)} %get-tuple-element.195), channel_id=1, source_target_pairs={{0,6},{1,7},{2,4},{3,5},{4,2},{5,3},{6,0},{7,1},{8,14},{9,15},{10,... | collective-permute-start | bytes 983048 | tf_op jit(solution)/shard_map/ppermute | solution.py:203
  113.4 16.6 %collective-permute-start.32 = (bf16[80,2048]{1,0:T(8,128)(2,1)S(1)}, bf16[80,2048]{1,0:T(8,128)(2,1)S(1)}, u32[]{:S(2)}, u32[]{:S(2)}) collective-permute-start(bf16[80,2048]{1,0:T(8,128)(2,1)S(1)} %get-tuple-element.191), channel_id=1, source_target_pairs={{0,4},{1,5},{2,6},{3,7},{4,0},{5,1},{6,2},{7,3},{8,12},{9,13},{10,... | collective-permute-start | bytes 983048 | tf_op jit(solution)/shard_map/ppermute | solution.py:203
  114.0 16.7 %collective-permute-start.30 = (bf16[80,2048]{1,0:T(8,128)(2,1)S(1)}, bf16[80,2048]{1,0:T(8,128)(2,1)S(1)}, u32[]{:S(2)}, u32[]{:S(2)}) collective-permute-start(bf16[80,2048]{1,0:T(8,128)(2,1)S(1)} %get-tuple-element.187), channel_id=1, source_target_pairs={{0,2},{1,3},{2,0},{3,1},{4,6},{5,7},{6,4},{7,5},{8,10},{9,11},{10,... | collective-permute-start | bytes 983048 | tf_op jit(solution)/shard_map/ppermute | solution.py:203
  123.1 14.3 %collective-permute-start.35 = (bf16[80,2048]{1,0:T(8,128)(2,1)S(1)}, bf16[80,2048]{1,0:T(8,128)(2,1)S(1)}, u32[]{:S(2)}, u32[]{:S(2)}) collective-permute-start(bf16[80,2048]{1,0:T(8,128)(2,1)S(1)} %get-tuple-element.196), channel_id=1, source_target_pairs={{0,6},{1,7},{2,4},{3,5},{4,2},{5,3},{6,0},{7,1},{8,14},{9,15},{10,... | collective-permute-start | bytes 983048 | tf_op jit(solution)/shard_map/ppermute | solution.py:203
  130.0 13.2 %collective-permute-start.33 = (bf16[80,2048]{1,0:T(8,128)(2,1)S(1)}, bf16[80,2048]{1,0:T(8,128)(2,1)S(1)}, u32[]{:S(2)}, u32[]{:S(2)}) collective-permute-start(bf16[80,2048]{1,0:T(8,128)(2,1)S(1)} %get-tuple-element.192), channel_id=1, source_target_pairs={{0,4},{1,5},{2,6},{3,7},{4,0},{5,1},{6,2},{7,3},{8,12},{9,13},{10,... | collective-permute-start | bytes 983048 | tf_op jit(solution)/shard_map/ppermute | solution.py:203
  130.7 12.5 %collective-permute-start.31 = (bf16[80,2048]{1,0:T(8,128)(2,1)S(1)}, bf16[80,2048]{1,0:T(8,128)(2,1)S(1)}, u32[]{:S(2)}, u32[]{:S(2)}) collective-permute-start(bf16[80,2048]{1,0:T(8,128)(2,1)S(1)} %get-tuple-element.188), channel_id=1, source_target_pairs={{0,2},{1,3},{2,0},{3,1},{4,6},{5,7},{6,4},{7,5},{8,10},{9,11},{10,... | collective-permute-start | bytes 983048 | tf_op jit(solution)/shard_map/ppermute | solution.py:203
  135.7 15.9 %collective-permute-start.41 = (bf16[128,2048]{1,0:T(8,128)(2,1)S(1)}, bf16[128,2048]{1,0:T(8,128)(2,1)S(1)}, u32[]{:S(2)}, u32[]{:S(2)}) collective-permute-start(bf16[128,2048]{1,0:T(8,128)(2,1)S(1)} %shard_map.78), channel_id=1, source_target_pairs={{0,8},{8,16},{16,24},{24,0},{1,9},{9,17},{17,25},{25,1},{2,10},{10... | collective-permute-start | bytes 1572872 | tf_op jit(solution)/shard_map/ppermute | solution.py:200
  (24 other events, 149.3 us)

commit v9 on v8

--- a/solution.py
+++ b/solution.py
@@ -10,21 +10,22 @@
 BF16 = jnp.bfloat16
 F32 = jnp.float32
 VMEM_LIMIT = 32 * 1024 * 1024
+PAD_VMEM_LIMIT = 60 * 1024 * 1024
 PARTS = 4
 CORES = 2
 PHASE_FLOPS = 50_000_000_000
 VMEM = pl.BlockSpec(memory_space=pltpu.VMEM)
 
 
-def call(body, out_shape, n_in, scratch=(), flops=1000):
+def call(body, out_shape, n_in, scratch=(), flops=1000, spec=VMEM, limit=VMEM_LIMIT):
     many = isinstance(out_shape, list)
     return pl.pallas_call(
         body,
         out_shape=out_shape,
-        in_specs=[VMEM] * n_in,
+        in_specs=[spec] * n_in,
         out_specs=[VMEM] * len(out_shape) if many else VMEM,
         scratch_shapes=list(scratch),
-        compiler_params=pltpu.CompilerParams(vmem_limit_bytes=VMEM_LIMIT),
+        compiler_params=pltpu.CompilerParams(vmem_limit_bytes=limit),
         cost_estimate=pl.CostEstimate(flops=flops, bytes_accessed=1000, transcendentals=0),
     )
 
@@ -47,6 +48,7 @@
         self.topk = ids_t.shape[0]
         self.near, self.layers = near, layers
         self.chips = near // CORES
+        self.offsets = sorted(range(self.chips), key=lambda q: (q == 2, q))
         self.cap = round_up(5 * self.toks * self.topk // (4 * self.experts), 8)
         self.tiles = self.width // self.depth
         self.extra = -(-(1 + self.experts // 8) // self.tiles) * 8
@@ -57,14 +59,22 @@
         return slice(r, r + 8), slice(q, q + self.depth)
 
 
-def pad_kernel(z, tokens_ref, ids_ref, router_ref, out):
-    out[0 : z.toks, :] = tokens_ref[...]
-    blank = jnp.zeros((z.extra, z.width), BF16)
-    out[z.toks : z.toks + z.extra, :] = blank
-    out[z.toks : z.toks + 8, 0 : z.toks] = ids_ref[...].astype(F32).astype(BF16)
+def pad_kernel(z, tokens_ref, ids_ref, router_ref, out, ids, router, sems):
+    copies = [
+        pltpu.make_async_copy(tokens_ref, out.at[0 : z.toks, :], sems.at[0]),
+        pltpu.make_async_copy(ids_ref, ids, sems.at[1]),
+        pltpu.make_async_copy(router_ref, router, sems.at[2]),
+    ]
+    for copy in copies:
+        copy.start()
+    out[z.toks : z.toks + z.extra, :] = jnp.zeros((z.extra, z.width), BF16)
+    for copy in copies[1:]:
+        copy.wait()
+    out[z.toks : z.toks + 8, 0 : z.toks] = ids[...].astype(F32).astype(BF16)
     for g in range(z.experts // 8):
         rows, cols = z.tile(g + 1)
-        out[z.toks + rows.start : z.toks + rows.stop, cols] = router_ref[8 * g : 8 * g + 8, :]
+        out[z.toks + rows.start : z.toks + rows.stop, cols] = router[8 * g : 8 * g + 8, :]
+    copies[0].wait()
 
 
 def served_expert(z, q):
@@ -79,7 +89,7 @@
     has = jnp.concatenate(
         [
             jnp.max((ids_t == served_expert(z, q)).astype(F32), axis=0, keepdims=True)
-            for q in range(z.chips)
+            for q in z.offsets
         ]
         * 2,
         axis=0,
@@ -135,15 +145,15 @@
     blocks, refs = refs[:n], refs[n:]
     riders, backs, outs = refs[: z.chips], refs[z.chips : 2 * z.chips], refs[2 * z.chips :]
     number = lax.broadcasted_iota(jnp.int32, (z.experts, z.toks), 0)
-    routers = []
-    for q in range(z.chips):
+    routers = {}
+    for i, q in enumerate(z.offsets):
         for r in range(CORES):
             base = CORES * z.cap
             pieces = []
             for g in range(z.experts // 8):
                 rows, cols = z.tile(r * (z.experts // 8) + g)
-                pieces.append(riders[q][base + rows.start : base + rows.stop, cols].astype(F32))
-            routers.append(jnp.concatenate(pieces, axis=0).astype(BF16))
+                pieces.append(riders[i][base + rows.start : base + rows.stop, cols].astype(F32))
+            routers[CORES * q + r] = jnp.concatenate(pieces, axis=0).astype(BF16)
     for b, block in enumerate(blocks):
         ids_t = ids_of(z, block)
         logits = None
@@ -163,9 +173,9 @@
         gates = weights / jnp.sum(weights, axis=0, keepdims=True)
         marks = slot_marks(z, ids_t)
         mix = []
-        for q in range(z.chips):
+        for i, q in enumerate(z.offsets):
             gate = jnp.sum(jnp.where(number == served_expert(z, q), gates, 0.0), axis=0, keepdims=True)
-            mix.append(marks[q] * gate)
+            mix.append(marks[i] * gate)
         mix = jnp.concatenate(mix, axis=0).astype(BF16)
         part = z.width // PARTS
         for c in range(PARTS):
@@ -219,7 +229,7 @@
         return call(arrived_kernel, out, len(arrays), flops=PHASE_FLOPS)(*arrays)
 
     def slabs_across(slabs):
-        return [across(s, CORES * q) for q, s in enumerate(slabs)]
+        return [across(s, CORES * q) for q, s in zip(z.offsets, slabs)]
 
     def expert(slabs, n, flops=1000):
         rows = n * z.cap
@@ -247,9 +257,18 @@
     def join(parts):
         return call(join_kernel, shape(z.toks), len(parts))(*parts)
 
-    own = call(functools.partial(pad_kernel, z), shape(z.toks + z.extra), 3)(
-        tokens, expert_ids.T, router_weight.T
-    )
+    own = call(
+        functools.partial(pad_kernel, z),
+        shape(z.toks + z.extra),
+        3,
+        [
+            pltpu.VMEM((z.topk, z.toks), jnp.int32),
+            pltpu.VMEM((z.experts, z.depth), BF16),
+            pltpu.SemaphoreType.DMA((3,)),
+        ],
+        spec=pl.BlockSpec(memory_space=pl.ANY),
+        limit=PAD_VMEM_LIMIT,
+    )(tokens, expert_ids.T, router_weight.T)
 
     end = layers - 1
     turns = [(d, True) for d in range(end)] + [(d, False) for d in range(1, end)]

time: 153 us -> 154 us (level)
  waiting for transfers between devices: 77.6 us -> 85.1 us
  starting transfers between devices: 44.7 us -> 39.6 us
  local copies, waits for them, and re-layouts: 7.99 us -> 5.08 us
  Pallas kernels: 22.2 us -> 24.2 us
    ppermute x36, waiting for transfers between devices: 61 us -> 72.4 us  [across(): lax.ppermute(array, 'zero', [(i, i ^ o) for i in range(near)])]
    ppermute x6, waiting for transfers between devices: 16.7 us -> 12.7 us  [along(): lax.ppermute(array, 'expert', [(i, (i + d) % layers) for i in range(layer...]
    ppermute x6, starting transfers between devices: 12.4 us -> 9.14 us  [along(): lax.ppermute(array, 'expert', [(i, (i + d) % layers) for i in range(layer...]
    unnamed x28 -> x22, local copies, waits for them, and re-layouts: 7.99 us -> 5.08 us
    pallas_call x1, Pallas kernels: 0.04 us -> 2.03 us  [per_device(): call(functools.partial(pad_kernel, z), shape(z.toks + z.extra), 3, [pltpu...]
    ppermute x36, starting transfers between devices: 32.4 us -> 30.5 us  [across(): lax.ppermute(array, 'zero', [(i, i ^ o) for i in range(near)])]
  transfers between devices with their start and end apart: 42 -> 42, of which waited for: 21 -> 23; matrix products, arithmetic and copies ran while one was open for 0% -> 0% of each run, Pallas kernels for 13% -> 13%
where the time goes in v9:
time: 154 us
  waiting for transfers between devices  85.1 us (55%)
  starting transfers between devices  39.6 us (26%)
  Pallas kernels  24.2 us (16%)
  local copies, waits for them, and re-layouts  5.08 us (3%)
    ppermute x36, waiting for transfers between devices, across(): lax.ppermute(array, 'zero', [(i, i ^ o) for i in range(near)])  72.4 us
    ppermute x36, starting transfers between devices, across(): lax.ppermute(array, 'zero', [(i, i ^ o) for i in range(near)])  30.5 us
    pallas_call x4, Pallas kernels, expert(): call(functools.partial(expert_kernel, z, rows), [shape(rows)] * z.chips,...  12.9 us
    ppermute x6, waiting for transfers between devices, along(): lax.ppermute(array, 'expert', [(i, (i + d) % layers) for i in range(layer...  12.7 us
    ppermute x6, starting transfers between devices, along(): lax.ppermute(array, 'expert', [(i, (i + d) % layers) for i in range(layer...  9.14 us
    pallas_call x4, Pallas kernels, mix(): call(functools.partial(mix_kernel, z, CORES), [shape(z.toks), shape(z.tok...  5.35 us
    unnamed x22, local copies, waits for them, and re-layouts  5.08 us
  transfers between devices with their start and end apart: 42, of which 23 were waited for; matrix products, arithmetic and copies ran while one was open for 0% of the time, Pallas kernels for 13%

profile of v9, /device:TPU:0, one launch (start us, length us, event | category | flops | bytes accessed | tf_op | source)
XLA Modules:
  0.0 154.2 jit_solution(776137490792306720)
XLA Ops:
  0.0 2.0 %shard_map.64.refs_0_ = bf16[136,2048]{1,0:T(8,128)(2,1)} custom-call(bf16[128,2048]{1,0:T(8,128)(2,1)} %tokens_ref.1, s32[8,128]{1,0:T(8,128)} %bitcast.18, bf16[32,256]{1,0:T(8,128)(2,1)} %bitcast.17), custom_call_target="tpu_custom_call" | custom-call | flops 1000 | bytes 1000 | tf_op jit(solution)/shard_map/pallas_call | solution.py:260
  2.6 2.6 %collective-permute-start.1 = (bf16[136,2048]{1,0:T(8,128)(2,1)}, bf16[136,2048]{1,0:T(8,128)(2,1)S(1)}, u32[]{:S(2)}, u32[]{:S(2)}) collective-permute-start(bf16[136,2048]{1,0:T(8,128)(2,1)} %shard_map.64.refs_0_), channel_id=1, source_target_pairs={{0,8},{8,16},{16,24},{24,0},{1,9},{9,17},{17,25},{25,1},{2,10},{10... | collective-permute-start | bytes 1671176 | tf_op jit(solution)/shard_map/ppermute | solution.py:210
  7.1 2.0 %collective-permute-start.2 = (bf16[80,2048]{1,0:T(8,128)(2,1)S(1)}, bf16[80,2048]{1,0:T(8,128)(2,1)S(1)}, u32[]{:S(2)}, u32[]{:S(2)}) collective-permute-start(bf16[80,2048]{1,0:T(8,128)(2,1)S(1)} %get-tuple-element.108), channel_id=1, source_target_pairs={{0,2},{1,3},{2,0},{3,1},{4,6},{5,7},{6,4},{7,5},{8,10},{9,11},{10,... | collective-permute-start | bytes 983048 | tf_op jit(solution)/shard_map/ppermute | solution.py:213
  9.1 1.5 collective-permute-start.4
  10.6 10.1 %collective-permute-done.1.refs_0_ = bf16[136,2048]{1,0:T(8,128)(2,1)S(1)} collective-permute-done((bf16[136,2048]{1,0:T(8,128)(2,1)}, bf16[136,2048]{1,0:T(8,128)(2,1)S(1)}, u32[]{:S(2)}, u32[]{:S(2)}) %collective-permute-start.1) | collective-permute-done | bytes 557088 | tf_op jit(solution)/shard_map/ppermute | solution.py:210
  20.7 4.7 %collective-permute-done.4.refs_2_ = bf16[80,2048]{1,0:T(8,128)(2,1)S(1)} collective-permute-done((bf16[80,2048]{1,0:T(8,128)(2,1)S(1)}, bf16[80,2048]{1,0:T(8,128)(2,1)S(1)}, u32[]{:S(2)}, u32[]{:S(2)}) %collective-permute-start.4) | collective-permute-done | bytes 327712 | tf_op jit(solution)/shard_map/ppermute | solution.py:213
  27.4 1.6 %collective-permute-start.6 = (bf16[88,2048]{1,0:T(8,128)(2,1)S(1)}, bf16[88,2048]{1,0:T(8,128)(2,1)S(1)}, u32[]{:S(2)}, u32[]{:S(2)}) collective-permute-start(bf16[88,2048]{1,0:T(8,128)(2,1)S(1)} %get-tuple-element.115), channel_id=1, source_target_pairs={{0,2},{1,3},{2,0},{3,1},{4,6},{5,7},{6,4},{7,5},{8,10},{9,11},{10,... | collective-permute-start | bytes 1081352 | tf_op jit(solution)/shard_map/ppermute | solution.py:213
  29.4 1.5 collective-permute-start.7
  30.9 1.9 %copy-done.1 = bf16[1,2048,768]{2,1,0:T(8,128)(2,1)S(1)} copy-done((bf16[1,2048,768]{2,1,0:T(8,128)(2,1)S(1)}, bf16[1,2048,768]{2,1,0:T(8,128)(2,1)}, u32[]{:S(2)}) %copy-start.1) | copy-done | bytes 3145752
  32.8 1.9 %copy-done.3 = bf16[1,768,2048]{2,1,0:T(8,128)(2,1)S(1)} copy-done((bf16[1,768,2048]{2,1,0:T(8,128)(2,1)S(1)}, bf16[1,768,2048]{2,1,0:T(8,128)(2,1)}, u32[]{:S(2)}) %copy-start.3) | copy-done | bytes 3145752
  34.7 3.2 %shard_map.67 = (bf16[80,2048]{1,0:T(8,128)(2,1)S(1)}, bf16[80,2048]{1,0:T(8,128)(2,1)S(1)}, bf16[80,2048]{1,0:T(8,128)(2,1)S(1)}, bf16[80,2048]{1,0:T(8,128)(2,1)S(1)}) custom-call(bf16[80,2048]{1,0:T(8,128)(2,1)S(1)} %get-tuple-element.121.refs_0_, bf16[80,2048]{1,0:T(8,128)(2,1)S(1)} %collective-permute-done.2.refs_1_, ...), custom_call_target="tpu_custom_call" | custom-call | flops 1000 | bytes 1000 | tf_op jit(solution)/shard_map/pallas_call | solution.py:236
  38.8 5.8 %collective-permute-done.8.refs_3_.refs_5_ = bf16[88,2048]{1,0:T(8,128)(2,1)S(1)} collective-permute-done((bf16[88,2048]{1,0:T(8,128)(2,1)S(1)}, bf16[88,2048]{1,0:T(8,128)(2,1)S(1)}, u32[]{:S(2)}, u32[]{:S(2)}) %collective-permute-start.8) | collective-permute-done | bytes 360480 | tf_op jit(solution)/shard_map/ppermute | solution.py:213
  45.8 1.5 collective-permute-start.14
  47.3 1.5 collective-permute-start.12
  48.8 1.9 %collective-permute-start.10 = (bf16[136,2048]{1,0:T(8,128)(2,1)S(1)}, bf16[136,2048]{1,0:T(8,128)(2,1)S(1)}, u32[]{:S(2)}, u32[]{:S(2)}) collective-permute-start(bf16[136,2048]{1,0:T(8,128)(2,1)S(1)} %collective-permute-done.9.refs_0_), channel_id=1, source_target_pairs={{0,8},{8,16},{16,24},{24,0},{1,9},{9,17},{17,25},{25,1},{2,10},{10... | collective-permute-start | bytes 1671176 | tf_op jit(solution)/shard_map/ppermute | solution.py:210
  50.7 3.2 %shard_map.71 = (bf16[80,2048]{1,0:T(8,128)(2,1)S(1)}, bf16[80,2048]{1,0:T(8,128)(2,1)S(1)}, bf16[80,2048]{1,0:T(8,128)(2,1)S(1)}, bf16[80,2048]{1,0:T(8,128)(2,1)S(1)}) custom-call(bf16[88,2048]{1,0:T(8,128)(2,1)S(1)} %get-tuple-element.138.refs_0_.refs_2_, bf16[88,2048]{1,0:T(8,128)(2,1)S(1)} %collective-permute-done.6.refs_1_.refs_3_, ...), custom_call_target="tpu_custom_call" | custom-call | flops 1000 | bytes 1000 | tf_op jit(solution)/shard_map/pallas_call | solution.py:236
  54.0 5.7 %collective-permute-done.15.refs_3_ = bf16[80,2048]{1,0:T(8,128)(2,1)S(1)} collective-permute-done((bf16[80,2048]{1,0:T(8,128)(2,1)S(1)}, bf16[80,2048]{1,0:T(8,128)(2,1)S(1)}, u32[]{:S(2)}, u32[]{:S(2)}) %collective-permute-start.15) | collective-permute-done | bytes 327712 | tf_op jit(solution)/shard_map/ppermute | solution.py:213
  61.2 2.0 %collective-permute-start.16 = (bf16[80,2048]{1,0:T(8,128)(2,1)S(1)}, bf16[80,2048]{1,0:T(8,128)(2,1)S(1)}, u32[]{:S(2)}, u32[]{:S(2)}) collective-permute-start(bf16[80,2048]{1,0:T(8,128)(2,1)S(1)} %get-tuple-element.149), channel_id=1, source_target_pairs={{0,2},{1,3},{2,0},{3,1},{4,6},{5,7},{6,4},{7,5},{8,10},{9,11},{10,... | collective-permute-start | bytes 983048 | tf_op jit(solution)/shard_map/ppermute | solution.py:213
  63.2 3.2 %shard_map.70 = (bf16[80,2048]{1,0:T(8,128)(2,1)S(1)}, bf16[80,2048]{1,0:T(8,128)(2,1)S(1)}, bf16[80,2048]{1,0:T(8,128)(2,1)S(1)}, bf16[80,2048]{1,0:T(8,128)(2,1)S(1)}) custom-call(bf16[80,2048]{1,0:T(8,128)(2,1)S(1)} %get-tuple-element.132.refs_0_, bf16[80,2048]{1,0:T(8,128)(2,1)S(1)} %collective-permute-done.12.refs_1_, ...), custom_call_target="tpu_custom_call" | custom-call | flops 1000 | bytes 1000 | tf_op jit(solution)/shard_map/pallas_call | solution.py:236
  66.4 8.9 %collective-permute-done.22.refs_9_ = bf16[80,2048]{1,0:T(8,128)(2,1)S(1)} collective-permute-done((bf16[80,2048]{1,0:T(8,128)(2,1)S(1)}, bf16[80,2048]{1,0:T(8,128)(2,1)S(1)}, u32[]{:S(2)}, u32[]{:S(2)}) %collective-permute-start.22) | collective-permute-done | bytes 327712 | tf_op jit(solution)/shard_map/ppermute | solution.py:213
  79.4 2.5 %collective-permute-start.17 = (bf16[80,2048]{1,0:T(8,128)(2,1)S(1)}, bf16[80,2048]{1,0:T(8,128)(2,1)S(1)}, u32[]{:S(2)}, u32[]{:S(2)}) collective-permute-start(bf16[80,2048]{1,0:T(8,128)(2,1)S(1)} %get-tuple-element.150), channel_id=1, source_target_pairs={{0,2},{1,3},{2,0},{3,1},{4,6},{5,7},{6,4},{7,5},{8,10},{9,11},{10,... | collective-permute-start | bytes 983048 | tf_op jit(solution)/shard_map/ppermute | solution.py:213
  82.0 2.6 %collective-permute-start.27 = (bf16[128,2048]{1,0:T(8,128)(2,1)S(1)}, bf16[128,2048]{1,0:T(8,128)(2,1)S(1)}, u32[]{:S(2)}, u32[]{:S(2)}) collective-permute-start(bf16[128,2048]{1,0:T(8,128)(2,1)S(1)} %shard_map.73), channel_id=1, source_target_pairs={{0,24},{8,0},{16,8},{24,16},{1,25},{9,1},{17,9},{25,17},{2,26},{10... | collective-permute-start | bytes 1572872 | tf_op jit(solution)/shard_map/ppermute | solution.py:210
  85.3 9.8 %collective-permute-done.23.refs_9_ = bf16[80,2048]{1,0:T(8,128)(2,1)S(1)} collective-permute-done((bf16[80,2048]{1,0:T(8,128)(2,1)S(1)}, bf16[80,2048]{1,0:T(8,128)(2,1)S(1)}, u32[]{:S(2)}, u32[]{:S(2)}) %collective-permute-start.23) | collective-permute-done | bytes 327712 | tf_op jit(solution)/shard_map/ppermute | solution.py:213
  96.4 2.3 %collective-permute-start.18 = (bf16[80,2048]{1,0:T(8,128)(2,1)S(1)}, bf16[80,2048]{1,0:T(8,128)(2,1)S(1)}, u32[]{:S(2)}, u32[]{:S(2)}) collective-permute-start(bf16[80,2048]{1,0:T(8,128)(2,1)S(1)} %get-tuple-element.151), channel_id=1, source_target_pairs={{0,2},{1,3},{2,0},{3,1},{4,6},{5,7},{6,4},{7,5},{8,10},{9,11},{10,... | collective-permute-start | bytes 983048 | tf_op jit(solution)/shard_map/ppermute | solution.py:213
  102.1 1.5 collective-permute-start.36
  103.5 7.5 %collective-permute-done.24.refs_3_ = bf16[80,2048]{1,0:T(8,128)(2,1)S(1)} collective-permute-done((bf16[80,2048]{1,0:T(8,128)(2,1)S(1)}, bf16[80,2048]{1,0:T(8,128)(2,1)S(1)}, u32[]{:S(2)}, u32[]{:S(2)}) %collective-permute-start.24) | collective-permute-done | bytes 327712 | tf_op jit(solution)/shard_map/ppermute | solution.py:213
  112.2 3.2 %shard_map.76 = (bf16[80,2048]{1,0:T(8,128)(2,1)S(1)}, bf16[80,2048]{1,0:T(8,128)(2,1)S(1)}, bf16[80,2048]{1,0:T(8,128)(2,1)S(1)}, bf16[80,2048]{1,0:T(8,128)(2,1)S(1)}) custom-call(bf16[80,2048]{1,0:T(8,128)(2,1)S(1)} %get-tuple-element.178.refs_0_, bf16[80,2048]{1,0:T(8,128)(2,1)S(1)} %collective-permute-done.18.refs_1_, ...), custom_call_target="tpu_custom_call" | custom-call | flops 49999998976 | bytes 1000 | tf_op jit(solution)/shard_map/pallas_call | solution.py:236
  116.5 2.5 %collective-permute-start.30 = (bf16[80,2048]{1,0:T(8,128)(2,1)S(1)}, bf16[80,2048]{1,0:T(8,128)(2,1)S(1)}, u32[]{:S(2)}, u32[]{:S(2)}) collective-permute-start(bf16[80,2048]{1,0:T(8,128)(2,1)S(1)} %get-tuple-element.187), channel_id=1, source_target_pairs={{0,2},{1,3},{2,0},{3,1},{4,6},{5,7},{6,4},{7,5},{8,10},{9,11},{10,... | collective-permute-start | bytes 983048 | tf_op jit(solution)/shard_map/ppermute | solution.py:213
  119.0 11.2 %collective-permute-done.34.refs_9_ = bf16[80,2048]{1,0:T(8,128)(2,1)S(1)} collective-permute-done((bf16[80,2048]{1,0:T(8,128)(2,1)S(1)}, bf16[80,2048]{1,0:T(8,128)(2,1)S(1)}, u32[]{:S(2)}, u32[]{:S(2)}) %collective-permute-start.34) | collective-permute-done | bytes 327712 | tf_op jit(solution)/shard_map/ppermute | solution.py:213
  131.5 2.3 %collective-permute-start.31 = (bf16[80,2048]{1,0:T(8,128)(2,1)S(1)}, bf16[80,2048]{1,0:T(8,128)(2,1)S(1)}, u32[]{:S(2)}, u32[]{:S(2)}) collective-permute-start(bf16[80,2048]{1,0:T(8,128)(2,1)S(1)} %get-tuple-element.188), channel_id=1, source_target_pairs={{0,2},{1,3},{2,0},{3,1},{4,6},{5,7},{6,4},{7,5},{8,10},{9,11},{10,... | collective-permute-start | bytes 983048 | tf_op jit(solution)/shard_map/ppermute | solution.py:213
  137.7 8.2 %collective-permute-done.35.refs_9_ = bf16[80,2048]{1,0:T(8,128)(2,1)S(1)} collective-permute-done((bf16[80,2048]{1,0:T(8,128)(2,1)S(1)}, bf16[80,2048]{1,0:T(8,128)(2,1)S(1)}, u32[]{:S(2)}, u32[]{:S(2)}) %collective-permute-start.35) | collective-permute-done | bytes 327712 | tf_op jit(solution)/shard_map/ppermute | solution.py:213
  150.4 2.6 %collective-permute-done.41.refs_5_ = bf16[128,2048]{1,0:T(8,128)(2,1)S(1)} collective-permute-done((bf16[128,2048]{1,0:T(8,128)(2,1)S(1)}, bf16[128,2048]{1,0:T(8,128)(2,1)S(1)}, u32[]{:S(2)}, u32[]{:S(2)}) %collective-permute-start.41) | collective-permute-done | bytes 524320 | tf_op jit(solution)/shard_map/ppermute | solution.py:210
  (91 shorter events, 31.1 us)
Async XLA Ops:
  2.6 18.1 %collective-permute-start.1 = (bf16[136,2048]{1,0:T(8,128)(2,1)}, bf16[136,2048]{1,0:T(8,128)(2,1)S(1)}, u32[]{:S(2)}, u32[]{:S(2)}) collective-permute-start(bf16[136,2048]{1,0:T(8,128)(2,1)} %shard_map.64.refs_0_), channel_id=1, source_target_pairs={{0,8},{8,16},{16,24},{24,0},{1,9},{9,17},{17,25},{25,1},{2,10},{10... | collective-permute-start | bytes 1671176 | tf_op jit(solution)/shard_map/ppermute | solution.py:210
  7.1 13.6 %collective-permute-start.2 = (bf16[80,2048]{1,0:T(8,128)(2,1)S(1)}, bf16[80,2048]{1,0:T(8,128)(2,1)S(1)}, u32[]{:S(2)}, u32[]{:S(2)}) collective-permute-start(bf16[80,2048]{1,0:T(8,128)(2,1)S(1)} %get-tuple-element.108), channel_id=1, source_target_pairs={{0,2},{1,3},{2,0},{3,1},{4,6},{5,7},{6,4},{7,5},{8,10},{9,11},{10,... | collective-permute-start | bytes 983048 | tf_op jit(solution)/shard_map/ppermute | solution.py:213
  9.1 16.3 %collective-permute-start.4 = (bf16[80,2048]{1,0:T(8,128)(2,1)S(1)}, bf16[80,2048]{1,0:T(8,128)(2,1)S(1)}, u32[]{:S(2)}, u32[]{:S(2)}) collective-permute-start(bf16[80,2048]{1,0:T(8,128)(2,1)S(1)} %get-tuple-element.111), channel_id=1, source_target_pairs={{0,6},{1,7},{2,4},{3,5},{4,2},{5,3},{6,0},{7,1},{8,14},{9,15},{10,... | collective-permute-start | bytes 983048 | tf_op jit(solution)/shard_map/ppermute | solution.py:213
  10.6 16.2 %collective-permute-start.5 = (bf16[80,2048]{1,0:T(8,128)(2,1)S(1)}, bf16[80,2048]{1,0:T(8,128)(2,1)S(1)}, u32[]{:S(2)}, u32[]{:S(2)}) collective-permute-start(bf16[80,2048]{1,0:T(8,128)(2,1)S(1)} %get-tuple-element.112), channel_id=1, source_target_pairs={{0,4},{1,5},{2,6},{3,7},{4,0},{5,1},{6,2},{7,3},{8,12},{9,13},{10,... | collective-permute-start | bytes 983048 | tf_op jit(solution)/shard_map/ppermute | solution.py:213
  20.7 6.1 %collective-permute-start.3 = (bf16[136,2048]{1,0:T(8,128)(2,1)S(1)}, bf16[136,2048]{1,0:T(8,128)(2,1)S(1)}, u32[]{:S(2)}, u32[]{:S(2)}) collective-permute-start(bf16[136,2048]{1,0:T(8,128)(2,1)S(1)} %collective-permute-done.1.refs_0_), channel_id=1, source_target_pairs={{0,1},{1,0},{2,3},{3,2},{4,5},{5,4},{6,7},{7,6},{8,9},{9,8},{10,11... | collective-permute-start | bytes 1671176 | tf_op jit(solution)/shard_map/ppermute | solution.py:213
  20.7 17.3 %collective-permute-start.9 = (bf16[136,2048]{1,0:T(8,128)(2,1)S(1)}, bf16[136,2048]{1,0:T(8,128)(2,1)S(1)}, u32[]{:S(2)}, u32[]{:S(2)}) collective-permute-start(bf16[136,2048]{1,0:T(8,128)(2,1)S(1)} %collective-permute-done.1.refs_0_), channel_id=1, source_target_pairs={{0,8},{8,16},{16,24},{24,0},{1,9},{9,17},{17,25},{25,1},{2,10},{10... | collective-permute-start | bytes 1671176 | tf_op jit(solution)/shard_map/ppermute | solution.py:210
  27.4 11.4 %collective-permute-start.6 = (bf16[88,2048]{1,0:T(8,128)(2,1)S(1)}, bf16[88,2048]{1,0:T(8,128)(2,1)S(1)}, u32[]{:S(2)}, u32[]{:S(2)}) collective-permute-start(bf16[88,2048]{1,0:T(8,128)(2,1)S(1)} %get-tuple-element.115), channel_id=1, source_target_pairs={{0,2},{1,3},{2,0},{3,1},{4,6},{5,7},{6,4},{7,5},{8,10},{9,11},{10,... | collective-permute-start | bytes 1081352 | tf_op jit(solution)/shard_map/ppermute | solution.py:213
  29.0 15.7 %collective-permute-start.8 = (bf16[88,2048]{1,0:T(8,128)(2,1)S(1)}, bf16[88,2048]{1,0:T(8,128)(2,1)S(1)}, u32[]{:S(2)}, u32[]{:S(2)}) collective-permute-start(bf16[88,2048]{1,0:T(8,128)(2,1)S(1)} %get-tuple-element.119), channel_id=1, source_target_pairs={{0,4},{1,5},{2,6},{3,7},{4,0},{5,1},{6,2},{7,3},{8,12},{9,13},{10,... | collective-permute-start | bytes 1081352 | tf_op jit(solution)/shard_map/ppermute | solution.py:213
  29.4 15.2 %collective-permute-start.7 = (bf16[88,2048]{1,0:T(8,128)(2,1)S(1)}, bf16[88,2048]{1,0:T(8,128)(2,1)S(1)}, u32[]{:S(2)}, u32[]{:S(2)}) collective-permute-start(bf16[88,2048]{1,0:T(8,128)(2,1)S(1)} %get-tuple-element.117), channel_id=1, source_target_pairs={{0,6},{1,7},{2,4},{3,5},{4,2},{5,3},{6,0},{7,1},{8,14},{9,15},{10,... | collective-permute-start | bytes 1081352 | tf_op jit(solution)/shard_map/ppermute | solution.py:213
  45.2 14.4 %collective-permute-start.15 = (bf16[80,2048]{1,0:T(8,128)(2,1)S(1)}, bf16[80,2048]{1,0:T(8,128)(2,1)S(1)}, u32[]{:S(2)}, u32[]{:S(2)}) collective-permute-start(bf16[80,2048]{1,0:T(8,128)(2,1)S(1)} %get-tuple-element.136), channel_id=1, source_target_pairs={{0,4},{1,5},{2,6},{3,7},{4,0},{5,1},{6,2},{7,3},{8,12},{9,13},{10,... | collective-permute-start | bytes 983048 | tf_op jit(solution)/shard_map/ppermute | solution.py:213
  45.8 14.2 %collective-permute-start.14 = (bf16[80,2048]{1,0:T(8,128)(2,1)S(1)}, bf16[80,2048]{1,0:T(8,128)(2,1)S(1)}, u32[]{:S(2)}, u32[]{:S(2)}) collective-permute-start(bf16[80,2048]{1,0:T(8,128)(2,1)S(1)} %get-tuple-element.134), channel_id=1, source_target_pairs={{0,6},{1,7},{2,4},{3,5},{4,2},{5,3},{6,0},{7,1},{8,14},{9,15},{10,... | collective-permute-start | bytes 983048 | tf_op jit(solution)/shard_map/ppermute | solution.py:213
  47.3 13.9 %collective-permute-start.12 = (bf16[80,2048]{1,0:T(8,128)(2,1)S(1)}, bf16[80,2048]{1,0:T(8,128)(2,1)S(1)}, u32[]{:S(2)}, u32[]{:S(2)}) collective-permute-start(bf16[80,2048]{1,0:T(8,128)(2,1)S(1)} %get-tuple-element.128), channel_id=1, source_target_pairs={{0,2},{1,3},{2,0},{3,1},{4,6},{5,7},{6,4},{7,5},{8,10},{9,11},{10,... | collective-permute-start | bytes 983048 | tf_op jit(solution)/shard_map/ppermute | solution.py:213
  48.8 14.4 %collective-permute-start.10 = (bf16[136,2048]{1,0:T(8,128)(2,1)S(1)}, bf16[136,2048]{1,0:T(8,128)(2,1)S(1)}, u32[]{:S(2)}, u32[]{:S(2)}) collective-permute-start(bf16[136,2048]{1,0:T(8,128)(2,1)S(1)} %collective-permute-done.9.refs_0_), channel_id=1, source_target_pairs={{0,8},{8,16},{16,24},{24,0},{1,9},{9,17},{17,25},{25,1},{2,10},{10... | collective-permute-start | bytes 1671176 | tf_op jit(solution)/shard_map/ppermute | solution.py:210
  59.7 15.6 %collective-permute-start.22 = (bf16[80,2048]{1,0:T(8,128)(2,1)S(1)}, bf16[80,2048]{1,0:T(8,128)(2,1)S(1)}, u32[]{:S(2)}, u32[]{:S(2)}) collective-permute-start(bf16[80,2048]{1,0:T(8,128)(2,1)S(1)} %get-tuple-element.161), channel_id=1, source_target_pairs={{0,4},{1,5},{2,6},{3,7},{4,0},{5,1},{6,2},{7,3},{8,12},{9,13},{10,... | collective-permute-start | bytes 983048 | tf_op jit(solution)/shard_map/ppermute | solution.py:213
  59.9 15.3 %collective-permute-start.19 = (bf16[80,2048]{1,0:T(8,128)(2,1)S(1)}, bf16[80,2048]{1,0:T(8,128)(2,1)S(1)}, u32[]{:S(2)}, u32[]{:S(2)}) collective-permute-start(bf16[80,2048]{1,0:T(8,128)(2,1)S(1)} %get-tuple-element.155), channel_id=1, source_target_pairs={{0,6},{1,7},{2,4},{3,5},{4,2},{5,3},{6,0},{7,1},{8,14},{9,15},{10,... | collective-permute-start | bytes 983048 | tf_op jit(solution)/shard_map/ppermute | solution.py:213
  61.2 15.3 %collective-permute-start.16 = (bf16[80,2048]{1,0:T(8,128)(2,1)S(1)}, bf16[80,2048]{1,0:T(8,128)(2,1)S(1)}, u32[]{:S(2)}, u32[]{:S(2)}) collective-permute-start(bf16[80,2048]{1,0:T(8,128)(2,1)S(1)} %get-tuple-element.149), channel_id=1, source_target_pairs={{0,2},{1,3},{2,0},{3,1},{4,6},{5,7},{6,4},{7,5},{8,10},{9,11},{10,... | collective-permute-start | bytes 983048 | tf_op jit(solution)/shard_map/ppermute | solution.py:213
  63.2 21.5 %collective-permute-start.13 = (bf16[136,2048]{1,0:T(8,128)(2,1)S(1)}, bf16[136,2048]{1,0:T(8,128)(2,1)S(1)}, u32[]{:S(2)}, u32[]{:S(2)}) collective-permute-start(bf16[136,2048]{1,0:T(8,128)(2,1)S(1)} %collective-permute-done.10.refs_0_), channel_id=1, source_target_pairs={{0,1},{1,0},{2,3},{3,2},{4,5},{5,4},{6,7},{7,6},{8,9},{9,8},{10,11... | collective-permute-start | bytes 1671176 | tf_op jit(solution)/shard_map/ppermute | solution.py:213
  78.4 16.7 %collective-permute-start.23 = (bf16[80,2048]{1,0:T(8,128)(2,1)S(1)}, bf16[80,2048]{1,0:T(8,128)(2,1)S(1)}, u32[]{:S(2)}, u32[]{:S(2)}) collective-permute-start(bf16[80,2048]{1,0:T(8,128)(2,1)S(1)} %get-tuple-element.162), channel_id=1, source_target_pairs={{0,4},{1,5},{2,6},{3,7},{4,0},{5,1},{6,2},{7,3},{8,12},{9,13},{10,... | collective-permute-start | bytes 983048 | tf_op jit(solution)/shard_map/ppermute | solution.py:213
  78.7 16.7 %collective-permute-start.20 = (bf16[80,2048]{1,0:T(8,128)(2,1)S(1)}, bf16[80,2048]{1,0:T(8,128)(2,1)S(1)}, u32[]{:S(2)}, u32[]{:S(2)}) collective-permute-start(bf16[80,2048]{1,0:T(8,128)(2,1)S(1)} %get-tuple-element.156), channel_id=1, source_target_pairs={{0,6},{1,7},{2,4},{3,5},{4,2},{5,3},{6,0},{7,1},{8,14},{9,15},{10,... | collective-permute-start | bytes 983048 | tf_op jit(solution)/shard_map/ppermute | solution.py:213
  79.4 16.9 %collective-permute-start.17 = (bf16[80,2048]{1,0:T(8,128)(2,1)S(1)}, bf16[80,2048]{1,0:T(8,128)(2,1)S(1)}, u32[]{:S(2)}, u32[]{:S(2)}) collective-permute-start(bf16[80,2048]{1,0:T(8,128)(2,1)S(1)} %get-tuple-element.150), channel_id=1, source_target_pairs={{0,2},{1,3},{2,0},{3,1},{4,6},{5,7},{6,4},{7,5},{8,10},{9,11},{10,... | collective-permute-start | bytes 983048 | tf_op jit(solution)/shard_map/ppermute | solution.py:213
  82.0 16.6 %collective-permute-start.27 = (bf16[128,2048]{1,0:T(8,128)(2,1)S(1)}, bf16[128,2048]{1,0:T(8,128)(2,1)S(1)}, u32[]{:S(2)}, u32[]{:S(2)}) collective-permute-start(bf16[128,2048]{1,0:T(8,128)(2,1)S(1)} %shard_map.73), channel_id=1, source_target_pairs={{0,24},{8,0},{16,8},{24,16},{1,25},{9,1},{17,9},{25,17},{2,26},{10... | collective-permute-start | bytes 1572872 | tf_op jit(solution)/shard_map/ppermute | solution.py:210
  95.1 15.9 %collective-permute-start.24 = (bf16[80,2048]{1,0:T(8,128)(2,1)S(1)}, bf16[80,2048]{1,0:T(8,128)(2,1)S(1)}, u32[]{:S(2)}, u32[]{:S(2)}) collective-permute-start(bf16[80,2048]{1,0:T(8,128)(2,1)S(1)} %get-tuple-element.163), channel_id=1, source_target_pairs={{0,4},{1,5},{2,6},{3,7},{4,0},{5,1},{6,2},{7,3},{8,12},{9,13},{10,... | collective-permute-start | bytes 983048 | tf_op jit(solution)/shard_map/ppermute | solution.py:213
  95.4 15.6 %collective-permute-start.21 = (bf16[80,2048]{1,0:T(8,128)(2,1)S(1)}, bf16[80,2048]{1,0:T(8,128)(2,1)S(1)}, u32[]{:S(2)}, u32[]{:S(2)}) collective-permute-start(bf16[80,2048]{1,0:T(8,128)(2,1)S(1)} %get-tuple-element.157), channel_id=1, source_target_pairs={{0,6},{1,7},{2,4},{3,5},{4,2},{5,3},{6,0},{7,1},{8,14},{9,15},{10,... | collective-permute-start | bytes 983048 | tf_op jit(solution)/shard_map/ppermute | solution.py:213
  96.4 15.9 %collective-permute-start.18 = (bf16[80,2048]{1,0:T(8,128)(2,1)S(1)}, bf16[80,2048]{1,0:T(8,128)(2,1)S(1)}, u32[]{:S(2)}, u32[]{:S(2)}) collective-permute-start(bf16[80,2048]{1,0:T(8,128)(2,1)S(1)} %get-tuple-element.151), channel_id=1, source_target_pairs={{0,2},{1,3},{2,0},{3,1},{4,6},{5,7},{6,4},{7,5},{8,10},{9,11},{10,... | collective-permute-start | bytes 983048 | tf_op jit(solution)/shard_map/ppermute | solution.py:213
  102.1 31.7 %collective-permute-start.36 = (bf16[128,2048]{1,0:T(8,128)(2,1)S(1)}, bf16[128,2048]{1,0:T(8,128)(2,1)S(1)}, u32[]{:S(2)}, u32[]{:S(2)}) collective-permute-start(bf16[128,2048]{1,0:T(8,128)(2,1)S(1)} %shard_map.75), channel_id=1, source_target_pairs={{0,16},{8,24},{16,0},{24,8},{1,17},{9,25},{17,1},{25,9},{2,18},{10... | collective-permute-start | bytes 1572872 | tf_op jit(solution)/shard_map/ppermute | solution.py:210
  115.5 14.8 %collective-permute-start.34 = (bf16[80,2048]{1,0:T(8,128)(2,1)S(1)}, bf16[80,2048]{1,0:T(8,128)(2,1)S(1)}, u32[]{:S(2)}, u32[]{:S(2)}) collective-permute-start(bf16[80,2048]{1,0:T(8,128)(2,1)S(1)} %get-tuple-element.195), channel_id=1, source_target_pairs={{0,4},{1,5},{2,6},{3,7},{4,0},{5,1},{6,2},{7,3},{8,12},{9,13},{10,... | collective-permute-start | bytes 983048 | tf_op jit(solution)/shard_map/ppermute | solution.py:213
  115.8 14.7 %collective-permute-start.32 = (bf16[80,2048]{1,0:T(8,128)(2,1)S(1)}, bf16[80,2048]{1,0:T(8,128)(2,1)S(1)}, u32[]{:S(2)}, u32[]{:S(2)}) collective-permute-start(bf16[80,2048]{1,0:T(8,128)(2,1)S(1)} %get-tuple-element.191), channel_id=1, source_target_pairs={{0,6},{1,7},{2,4},{3,5},{4,2},{5,3},{6,0},{7,1},{8,14},{9,15},{10,... | collective-permute-start | bytes 983048 | tf_op jit(solution)/shard_map/ppermute | solution.py:213
  116.5 14.9 %collective-permute-start.30 = (bf16[80,2048]{1,0:T(8,128)(2,1)S(1)}, bf16[80,2048]{1,0:T(8,128)(2,1)S(1)}, u32[]{:S(2)}, u32[]{:S(2)}) collective-permute-start(bf16[80,2048]{1,0:T(8,128)(2,1)S(1)} %get-tuple-element.187), channel_id=1, source_target_pairs={{0,2},{1,3},{2,0},{3,1},{4,6},{5,7},{6,4},{7,5},{8,10},{9,11},{10,... | collective-permute-start | bytes 983048 | tf_op jit(solution)/shard_map/ppermute | solution.py:213
  130.3 15.6 %collective-permute-start.35 = (bf16[80,2048]{1,0:T(8,128)(2,1)S(1)}, bf16[80,2048]{1,0:T(8,128)(2,1)S(1)}, u32[]{:S(2)}, u32[]{:S(2)}) collective-permute-start(bf16[80,2048]{1,0:T(8,128)(2,1)S(1)} %get-tuple-element.196), channel_id=1, source_target_pairs={{0,4},{1,5},{2,6},{3,7},{4,0},{5,1},{6,2},{7,3},{8,12},{9,13},{10,... | collective-permute-start | bytes 983048 | tf_op jit(solution)/shard_map/ppermute | solution.py:213
  130.5 15.3 %collective-permute-start.33 = (bf16[80,2048]{1,0:T(8,128)(2,1)S(1)}, bf16[80,2048]{1,0:T(8,128)(2,1)S(1)}, u32[]{:S(2)}, u32[]{:S(2)}) collective-permute-start(bf16[80,2048]{1,0:T(8,128)(2,1)S(1)} %get-tuple-element.192), channel_id=1, source_target_pairs={{0,6},{1,7},{2,4},{3,5},{4,2},{5,3},{6,0},{7,1},{8,14},{9,15},{10,... | collective-permute-start | bytes 983048 | tf_op jit(solution)/shard_map/ppermute | solution.py:213
  131.5 15.6 %collective-permute-start.31 = (bf16[80,2048]{1,0:T(8,128)(2,1)S(1)}, bf16[80,2048]{1,0:T(8,128)(2,1)S(1)}, u32[]{:S(2)}, u32[]{:S(2)}) collective-permute-start(bf16[80,2048]{1,0:T(8,128)(2,1)S(1)} %get-tuple-element.188), channel_id=1, source_target_pairs={{0,2},{1,3},{2,0},{3,1},{4,6},{5,7},{6,4},{7,5},{8,10},{9,11},{10,... | collective-permute-start | bytes 983048 | tf_op jit(solution)/shard_map/ppermute | solution.py:213
  137.2 15.8 %collective-permute-start.41 = (bf16[128,2048]{1,0:T(8,128)(2,1)S(1)}, bf16[128,2048]{1,0:T(8,128)(2,1)S(1)}, u32[]{:S(2)}, u32[]{:S(2)}) collective-permute-start(bf16[128,2048]{1,0:T(8,128)(2,1)S(1)} %shard_map.78), channel_id=1, source_target_pairs={{0,8},{8,16},{16,24},{24,0},{1,9},{9,17},{17,25},{25,1},{2,10},{10... | collective-permute-start | bytes 1572872 | tf_op jit(solution)/shard_map/ppermute | solution.py:210
  (21 other events, 141.9 us)

commit v10 on v9

--- a/solution.py
+++ b/solution.py
@@ -48,7 +48,7 @@
         self.topk = ids_t.shape[0]
         self.near, self.layers = near, layers
         self.chips = near // CORES
-        self.offsets = sorted(range(self.chips), key=lambda q: (q == 2, q))
+        self.offsets = list(range(self.chips))
         self.cap = round_up(5 * self.toks * self.topk // (4 * self.experts), 8)
         self.tiles = self.width // self.depth
         self.extra = -(-(1 + self.experts // 8) // self.tiles) * 8
@@ -141,8 +141,10 @@
             outs[q][:, c : c + tile] = y[q * rows : (q + 1) * rows].astype(BF16)
 
 
-def mix_kernel(z, n, *refs):
+def mix_kernel(z, n, own, *refs):
     blocks, refs = refs[:n], refs[n:]
+    if own:
+        own_ids, refs = refs[0], refs[1:]
     riders, backs, outs = refs[: z.chips], refs[z.chips : 2 * z.chips], refs[2 * z.chips :]
     number = lax.broadcasted_iota(jnp.int32, (z.experts, z.toks), 0)
     routers = {}
@@ -155,7 +157,7 @@
                 pieces.append(riders[i][base + rows.start : base + rows.stop, cols].astype(F32))
             routers[CORES * q + r] = jnp.concatenate(pieces, axis=0).astype(BF16)
     for b, block in enumerate(blocks):
-        ids_t = ids_of(z, block)
+        ids_t = own_ids[...] if own and b == 0 else ids_of(z, block)
         logits = None
         for o in range(z.near):
             start = pl.multiple_of(lax.bitwise_xor(lax.axis_index("zero"), o) * z.depth, z.depth)
@@ -244,14 +246,15 @@
             flops,
         )(*slabs, gate_weight[0], up_weight[0], down_weight[0])
 
-    def mix(blocks, backs):
-        riders = slots[1]
+    def mix(blocks, backs, own):
+        ids = [expert_ids.T] if own else []
+        args = [*blocks, *ids, *slots[1], *backs]
         mine, *other = call(
-            functools.partial(mix_kernel, z, CORES),
+            functools.partial(mix_kernel, z, CORES, own),
             [shape(z.toks), shape(z.toks // 2), shape(z.toks // 2)],
-            CORES + 2 * z.chips,
+            len(args),
             flops=PHASE_FLOPS,
-        )(*blocks, *riders, *backs)
+        )(*args)
         return [mine] + [across(part, 1) for part in other]
 
     def join(parts):
@@ -275,12 +278,18 @@
     turns += [(end, True), (end, False), (0, False)]
     blocks, pairs, slots, results = {0: own}, {}, {}, {}
     leaving, home, seen, waiting = {}, {}, None, None
+
+    def bring(d):
+        if d:
+            blocks[d] = after([along(blocks[d - 1], 1)], slots[d - 1][1])[0]
+        pairs[d] = [blocks[d], across(blocks[d], 1)]
+
     for d, outward in turns:
         if outward:
-            if d:
-                blocks[d] = after([along(blocks[d - 1], 1)], slots[d - 1][1])[0]
-            pairs[d] = [blocks[d], across(blocks[d], 1)]
-            rows = slabs = pick(pairs[d], d == 1, PHASE_FLOPS if d == end else 1000)
+            if d < end:
+                bring(d)
+            members = after(pairs[d], leaving[d - 2]) if d == end and d > 2 else pairs[d]
+            rows = slabs = pick(members, d == 1, PHASE_FLOPS if d == end else 1000)
             if 0 < d < end:
                 gate = arrived(slots[d - 1][1:] + ([results[d - 2][0]] if d > 1 else []))
                 rows = [after([s], gate)[0] for s in slabs]
@@ -289,7 +298,8 @@
                 rows = [after([r], b)[0] for r, b in zip(slabs, seen)]
             seen = slots[d] = slabs_across(rows)
             if d == end - 1:
-                results[d] = expert(slots[d], 2)
+                bring(end)
+                results[d] = expert(after(slots[d], pairs[end][1]), 2)
             if d == end:
                 first = [leaving[e] for e in range(1, end)]
                 results[d] = expert(after(slots[d], *first), 2, PHASE_FLOPS)
@@ -297,7 +307,8 @@
             rows = [after([r], b)[0] for r, b in zip(results[d], seen)]
             seen = backs = slabs_across(rows)
             first = [(home if d else leaving)[waiting]] if waiting else [results[end - 1][0]]
-            sums = mix(pairs[d], after(backs, *first))
+            members = pairs[d] if d else [tokens, pairs[0][1]]
+            sums = mix(members, after(backs, *first), d == 0)
             if d:
                 leaving[d] = join(sums)
                 home[d] = along(leaving[d], layers - d)

time: 154 us -> 159 us (1.032)
  starting transfers between devices: 39.6 us -> 43.9 us
    ppermute x36, waiting for transfers between devices: 72.4 us -> 65 us  [across(): lax.ppermute(array, 'zero', [(i, i ^ o) for i in range(near)])]
    ppermute x6, waiting for transfers between devices: 12.7 us -> 20 us  [along(): lax.ppermute(array, 'expert', [(i, (i + d) % layers) for i in range(layer...]
    ppermute x6, starting transfers between devices: 9.14 us -> 12.4 us  [along(): lax.ppermute(array, 'expert', [(i, (i + d) % layers) for i in range(layer...]
    unnamed x22 -> x24, local copies, waits for them, and re-layouts: 5.08 us -> 5.88 us
  transfers between devices with their start and end apart: 42 -> 42, of which waited for: 23 -> 25; matrix products, arithmetic and copies ran while one was open for 0% -> 0% of each run, Pallas kernels for 13% -> 12%
where the time goes in v10:
time: 159 us
  waiting for transfers between devices  85 us (53%)
  starting transfers between devices  43.9 us (28%)
  Pallas kernels  24.2 us (15%)
  local copies, waits for them, and re-layouts  5.88 us (4%)
    ppermute x36, waiting for transfers between devices, across(): lax.ppermute(array, 'zero', [(i, i ^ o) for i in range(near)])  65 us
    ppermute x36, starting transfers between devices, across(): lax.ppermute(array, 'zero', [(i, i ^ o) for i in range(near)])  31.6 us
    ppermute x6, waiting for transfers between devices, along(): lax.ppermute(array, 'expert', [(i, (i + d) % layers) for i in range(layer...  20 us
    pallas_call x4, Pallas kernels, expert(): call(functools.partial(expert_kernel, z, rows), [shape(rows)] * z.chips,...  12.9 us
    ppermute x6, starting transfers between devices, along(): lax.ppermute(array, 'expert', [(i, (i + d) % layers) for i in range(layer...  12.4 us
    unnamed x24, local copies, waits for them, and re-layouts  5.88 us
    pallas_call x4, Pallas kernels, mix(): call(functools.partial(mix_kernel, z, CORES, own), [shape(z.toks), shape(...  5.36 us
  transfers between devices with their start and end apart: 42, of which 25 were waited for; matrix products, arithmetic and copies ran while one was open for 0% of the time, Pallas kernels for 12%

profile of v10, /device:TPU:0, one launch (start us, length us, event | category | flops | bytes accessed | tf_op | source)
XLA Modules:
  0.0 159.2 jit_solution(17503145988972418284)
XLA Ops:
  0.0 2.0 %shard_map.64.refs_0_ = bf16[136,2048]{1,0:T(8,128)(2,1)} custom-call(bf16[128,2048]{1,0:T(8,128)(2,1)} %refs_0_.1, s32[8,128]{1,0:T(8,128)} %bitcast.17, bf16[32,256]{1,0:T(8,128)(2,1)} %bitcast.19), custom_call_target="tpu_custom_call" | custom-call | flops 1000 | bytes 1000 | tf_op jit(solution)/shard_map/pallas_call | solution.py:263
  2.6 2.6 %collective-permute-start.1 = (bf16[136,2048]{1,0:T(8,128)(2,1)}, bf16[136,2048]{1,0:T(8,128)(2,1)S(1)}, u32[]{:S(2)}, u32[]{:S(2)}) collective-permute-start(bf16[136,2048]{1,0:T(8,128)(2,1)} %shard_map.64.refs_0_), channel_id=1, source_target_pairs={{0,8},{8,16},{16,24},{24,0},{1,9},{9,17},{17,25},{25,1},{2,10},{10... | collective-permute-start | bytes 1671176 | tf_op jit(solution)/shard_map/ppermute | solution.py:212
  7.1 2.0 %collective-permute-start.2 = (bf16[80,2048]{1,0:T(8,128)(2,1)S(1)}, bf16[80,2048]{1,0:T(8,128)(2,1)S(1)}, u32[]{:S(2)}, u32[]{:S(2)}) collective-permute-start(bf16[80,2048]{1,0:T(8,128)(2,1)S(1)} %get-tuple-element.114), channel_id=1, source_target_pairs={{0,2},{1,3},{2,0},{3,1},{4,6},{5,7},{6,4},{7,5},{8,10},{9,11},{10,... | collective-permute-start | bytes 983048 | tf_op jit(solution)/shard_map/ppermute | solution.py:215
  10.6 10.1 %collective-permute-done.1.refs_0_ = bf16[136,2048]{1,0:T(8,128)(2,1)S(1)} collective-permute-done((bf16[136,2048]{1,0:T(8,128)(2,1)}, bf16[136,2048]{1,0:T(8,128)(2,1)S(1)}, u32[]{:S(2)}, u32[]{:S(2)}) %collective-permute-start.1) | collective-permute-done | bytes 557088 | tf_op jit(solution)/shard_map/ppermute | solution.py:212
  20.7 4.9 %collective-permute-done.4.refs_2_ = bf16[80,2048]{1,0:T(8,128)(2,1)S(1)} collective-permute-done((bf16[80,2048]{1,0:T(8,128)(2,1)S(1)}, bf16[80,2048]{1,0:T(8,128)(2,1)S(1)}, u32[]{:S(2)}, u32[]{:S(2)}) %collective-permute-start.4) | collective-permute-done | bytes 327712 | tf_op jit(solution)/shard_map/ppermute | solution.py:215
  27.5 1.8 %collective-permute-start.8 = (bf16[88,2048]{1,0:T(8,128)(2,1)S(1)}, bf16[88,2048]{1,0:T(8,128)(2,1)S(1)}, u32[]{:S(2)}, u32[]{:S(2)}) collective-permute-start(bf16[88,2048]{1,0:T(8,128)(2,1)S(1)} %get-tuple-element.125), channel_id=1, source_target_pairs={{0,6},{1,7},{2,4},{3,5},{4,2},{5,3},{6,0},{7,1},{8,14},{9,15},{10,... | collective-permute-start | bytes 1081352 | tf_op jit(solution)/shard_map/ppermute | solution.py:215
  29.7 1.9 %copy-done.1 = bf16[1,2048,768]{2,1,0:T(8,128)(2,1)S(1)} copy-done((bf16[1,2048,768]{2,1,0:T(8,128)(2,1)S(1)}, bf16[1,2048,768]{2,1,0:T(8,128)(2,1)}, u32[]{:S(2)}) %copy-start.1) | copy-done | bytes 3145752
  31.6 1.9 %copy-done.3 = bf16[1,768,2048]{2,1,0:T(8,128)(2,1)S(1)} copy-done((bf16[1,768,2048]{2,1,0:T(8,128)(2,1)S(1)}, bf16[1,768,2048]{2,1,0:T(8,128)(2,1)}, u32[]{:S(2)}) %copy-start.3) | copy-done | bytes 3145752
  33.5 3.2 %shard_map.67 = (bf16[80,2048]{1,0:T(8,128)(2,1)S(1)}, bf16[80,2048]{1,0:T(8,128)(2,1)S(1)}, bf16[80,2048]{1,0:T(8,128)(2,1)S(1)}, bf16[80,2048]{1,0:T(8,128)(2,1)S(1)}) custom-call(bf16[80,2048]{1,0:T(8,128)(2,1)S(1)} %get-tuple-element.127.refs_0_, bf16[80,2048]{1,0:T(8,128)(2,1)S(1)} %collective-permute-done.2.refs_1_, ...), custom_call_target="tpu_custom_call" | custom-call | flops 1000 | bytes 1000 | tf_op jit(solution)/shard_map/pallas_call | solution.py:238
  39.2 5.2 %collective-permute-done.8.refs_3_.refs_5_.refs_6_ = bf16[88,2048]{1,0:T(8,128)(2,1)S(1)} collective-permute-done((bf16[88,2048]{1,0:T(8,128)(2,1)S(1)}, bf16[88,2048]{1,0:T(8,128)(2,1)S(1)}, u32[]{:S(2)}, u32[]{:S(2)}) %collective-permute-start.8) | collective-permute-done | bytes 360480 | tf_op jit(solution)/shard_map/ppermute | solution.py:215
  49.9 4.6 %collective-permute-done.10.refs_0_ = bf16[136,2048]{1,0:T(8,128)(2,1)S(1)} collective-permute-done((bf16[136,2048]{1,0:T(8,128)(2,1)S(1)}, bf16[136,2048]{1,0:T(8,128)(2,1)S(1)}, u32[]{:S(2)}, u32[]{:S(2)}) %collective-permute-start.10) | collective-permute-done | bytes 557088 | tf_op jit(solution)/shard_map/ppermute | solution.py:212
  54.5 1.6 %collective-permute-done.12.refs_1_ = bf16[80,2048]{1,0:T(8,128)(2,1)S(1)} collective-permute-done((bf16[80,2048]{1,0:T(8,128)(2,1)S(1)}, bf16[80,2048]{1,0:T(8,128)(2,1)S(1)}, u32[]{:S(2)}, u32[]{:S(2)}) %collective-permute-start.12) | collective-permute-done | bytes 327712 | tf_op jit(solution)/shard_map/ppermute | solution.py:215
  56.2 3.2 %shard_map.69 = (bf16[80,2048]{1,0:T(8,128)(2,1)S(1)}, bf16[80,2048]{1,0:T(8,128)(2,1)S(1)}, bf16[80,2048]{1,0:T(8,128)(2,1)S(1)}, bf16[80,2048]{1,0:T(8,128)(2,1)S(1)}) custom-call(bf16[88,2048]{1,0:T(8,128)(2,1)S(1)} %get-tuple-element.137.refs_0_.refs_2_.refs_3_, bf16[88,2048]{1,0:T(8,128)(2,1)S(1)} %collective-permute-done.6.refs_1_.refs_3_.refs_4_, ...), custom_call_target="tpu_custom_call" | custom-call | flops 1000 | bytes 1000 | tf_op jit(solution)/shard_map/pallas_call | solution.py:238
  61.6 1.6 %collective-permute-start.16 = (bf16[80,2048]{1,0:T(8,128)(2,1)S(1)}, bf16[80,2048]{1,0:T(8,128)(2,1)S(1)}, u32[]{:S(2)}, u32[]{:S(2)}) collective-permute-start(bf16[80,2048]{1,0:T(8,128)(2,1)S(1)} %get-tuple-element.149), channel_id=1, source_target_pairs={{0,4},{1,5},{2,6},{3,7},{4,0},{5,1},{6,2},{7,3},{8,12},{9,13},{10,... | collective-permute-start | bytes 983048 | tf_op jit(solution)/shard_map/ppermute | solution.py:215
  63.6 3.2 %shard_map.70 = (bf16[80,2048]{1,0:T(8,128)(2,1)S(1)}, bf16[80,2048]{1,0:T(8,128)(2,1)S(1)}, bf16[80,2048]{1,0:T(8,128)(2,1)S(1)}, bf16[80,2048]{1,0:T(8,128)(2,1)S(1)}) custom-call(bf16[80,2048]{1,0:T(8,128)(2,1)S(1)} %get-tuple-element.154.refs_0_, bf16[80,2048]{1,0:T(8,128)(2,1)S(1)} %collective-permute-done.12.refs_1_, ...), custom_call_target="tpu_custom_call" | custom-call | flops 1000 | bytes 1000 | tf_op jit(solution)/shard_map/pallas_call | solution.py:238
  66.8 4.8 %collective-permute-done.18.refs_9_ = bf16[80,2048]{1,0:T(8,128)(2,1)S(1)} collective-permute-done((bf16[80,2048]{1,0:T(8,128)(2,1)S(1)}, bf16[80,2048]{1,0:T(8,128)(2,1)S(1)}, u32[]{:S(2)}, u32[]{:S(2)}) %collective-permute-start.18) | collective-permute-done | bytes 327712 | tf_op jit(solution)/shard_map/ppermute | solution.py:215
  71.6 5.9 %collective-permute-done.16.refs_8_ = bf16[80,2048]{1,0:T(8,128)(2,1)S(1)} collective-permute-done((bf16[80,2048]{1,0:T(8,128)(2,1)S(1)}, bf16[80,2048]{1,0:T(8,128)(2,1)S(1)}, u32[]{:S(2)}, u32[]{:S(2)}) %collective-permute-start.16) | collective-permute-done | bytes 327712 | tf_op jit(solution)/shard_map/ppermute | solution.py:215
  79.4 1.7 %collective-permute-start.25 = (bf16[80,2048]{1,0:T(8,128)(2,1)S(1)}, bf16[80,2048]{1,0:T(8,128)(2,1)S(1)}, u32[]{:S(2)}, u32[]{:S(2)}) collective-permute-start(bf16[80,2048]{1,0:T(8,128)(2,1)S(1)} %get-tuple-element.181), channel_id=1, source_target_pairs={{0,6},{1,7},{2,4},{3,5},{4,2},{5,3},{6,0},{7,1},{8,14},{9,15},{10,... | collective-permute-start | bytes 983048 | tf_op jit(solution)/shard_map/ppermute | solution.py:215
  83.1 3.8 %collective-permute-start.27 = (bf16[128,2048]{1,0:T(8,128)(2,1)S(1)}, bf16[128,2048]{1,0:T(8,128)(2,1)S(1)}, u32[]{:S(2)}, u32[]{:S(2)}) collective-permute-start(bf16[128,2048]{1,0:T(8,128)(2,1)S(1)} %shard_map.72), channel_id=1, source_target_pairs={{0,24},{8,0},{16,8},{24,16},{1,25},{9,1},{17,9},{25,17},{2,26},{10... | collective-permute-start | bytes 1572872 | tf_op jit(solution)/shard_map/ppermute | solution.py:212
  87.5 8.9 %collective-permute-done.21.refs_7_ = bf16[80,2048]{1,0:T(8,128)(2,1)S(1)} collective-permute-done((bf16[80,2048]{1,0:T(8,128)(2,1)S(1)}, bf16[80,2048]{1,0:T(8,128)(2,1)S(1)}, u32[]{:S(2)}, u32[]{:S(2)}) %collective-permute-start.21) | collective-permute-done | bytes 327712 | tf_op jit(solution)/shard_map/ppermute | solution.py:215
  97.1 1.7 %collective-permute-start.26 = (bf16[80,2048]{1,0:T(8,128)(2,1)S(1)}, bf16[80,2048]{1,0:T(8,128)(2,1)S(1)}, u32[]{:S(2)}, u32[]{:S(2)}) collective-permute-start(bf16[80,2048]{1,0:T(8,128)(2,1)S(1)} %get-tuple-element.182), channel_id=1, source_target_pairs={{0,6},{1,7},{2,4},{3,5},{4,2},{5,3},{6,0},{7,1},{8,14},{9,15},{10,... | collective-permute-start | bytes 983048 | tf_op jit(solution)/shard_map/ppermute | solution.py:215
  104.8 2.7 %collective-permute-start.36 = (bf16[128,2048]{1,0:T(8,128)(2,1)S(1)}, bf16[128,2048]{1,0:T(8,128)(2,1)S(1)}, u32[]{:S(2)}, u32[]{:S(2)}) collective-permute-start(bf16[128,2048]{1,0:T(8,128)(2,1)S(1)} %shard_map.75), channel_id=1, source_target_pairs={{0,16},{8,24},{16,0},{24,8},{1,17},{9,25},{17,1},{25,9},{2,18},{10... | collective-permute-start | bytes 1572872 | tf_op jit(solution)/shard_map/ppermute | solution.py:212
  108.6 6.0 %collective-permute-done.24.refs_2_ = bf16[80,2048]{1,0:T(8,128)(2,1)S(1)} collective-permute-done((bf16[80,2048]{1,0:T(8,128)(2,1)S(1)}, bf16[80,2048]{1,0:T(8,128)(2,1)S(1)}, u32[]{:S(2)}, u32[]{:S(2)}) %collective-permute-start.24) | collective-permute-done | bytes 327712 | tf_op jit(solution)/shard_map/ppermute | solution.py:215
  114.6 3.2 %shard_map.76 = (bf16[80,2048]{1,0:T(8,128)(2,1)S(1)}, bf16[80,2048]{1,0:T(8,128)(2,1)S(1)}, bf16[80,2048]{1,0:T(8,128)(2,1)S(1)}, bf16[80,2048]{1,0:T(8,128)(2,1)S(1)}) custom-call(bf16[80,2048]{1,0:T(8,128)(2,1)S(1)} %get-tuple-element.190.refs_0_, bf16[80,2048]{1,0:T(8,128)(2,1)S(1)} %collective-permute-done.22.refs_1_, ...), custom_call_target="tpu_custom_call" | custom-call | flops 49999998976 | bytes 1000 | tf_op jit(solution)/shard_map/pallas_call | solution.py:238
  117.8 1.8 %collective-permute-start.34 = (bf16[80,2048]{1,0:T(8,128)(2,1)S(1)}, bf16[80,2048]{1,0:T(8,128)(2,1)S(1)}, u32[]{:S(2)}, u32[]{:S(2)}) collective-permute-start(bf16[80,2048]{1,0:T(8,128)(2,1)S(1)} %get-tuple-element.207), channel_id=1, source_target_pairs={{0,6},{1,7},{2,4},{3,5},{4,2},{5,3},{6,0},{7,1},{8,14},{9,15},{10,... | collective-permute-start | bytes 983048 | tf_op jit(solution)/shard_map/ppermute | solution.py:215
  121.4 8.0 %collective-permute-done.34.refs_9_ = bf16[80,2048]{1,0:T(8,128)(2,1)S(1)} collective-permute-done((bf16[80,2048]{1,0:T(8,128)(2,1)S(1)}, bf16[80,2048]{1,0:T(8,128)(2,1)S(1)}, u32[]{:S(2)}, u32[]{:S(2)}) %collective-permute-start.34) | collective-permute-done | bytes 327712 | tf_op jit(solution)/shard_map/ppermute | solution.py:215
  129.4 1.7 %collective-permute-start.35 = (bf16[80,2048]{1,0:T(8,128)(2,1)S(1)}, bf16[80,2048]{1,0:T(8,128)(2,1)S(1)}, u32[]{:S(2)}, u32[]{:S(2)}) collective-permute-start(bf16[80,2048]{1,0:T(8,128)(2,1)S(1)} %get-tuple-element.208), channel_id=1, source_target_pairs={{0,6},{1,7},{2,4},{3,5},{4,2},{5,3},{6,0},{7,1},{8,14},{9,15},{10,... | collective-permute-start | bytes 983048 | tf_op jit(solution)/shard_map/ppermute | solution.py:215
  131.2 5.2 %collective-permute-done.32.refs_8_ = bf16[80,2048]{1,0:T(8,128)(2,1)S(1)} collective-permute-done((bf16[80,2048]{1,0:T(8,128)(2,1)S(1)}, bf16[80,2048]{1,0:T(8,128)(2,1)S(1)}, u32[]{:S(2)}, u32[]{:S(2)}) %collective-permute-start.32) | collective-permute-done | bytes 327712 | tf_op jit(solution)/shard_map/ppermute | solution.py:215
  137.1 1.6 %collective-permute-start.31 = (bf16[80,2048]{1,0:T(8,128)(2,1)S(1)}, bf16[80,2048]{1,0:T(8,128)(2,1)S(1)}, u32[]{:S(2)}, u32[]{:S(2)}) collective-permute-start(bf16[80,2048]{1,0:T(8,128)(2,1)S(1)} %get-tuple-element.200), channel_id=1, source_target_pairs={{0,2},{1,3},{2,0},{3,1},{4,6},{5,7},{6,4},{7,5},{8,10},{9,11},{10,... | collective-permute-start | bytes 983048 | tf_op jit(solution)/shard_map/ppermute | solution.py:215
  142.2 1.6 %collective-permute-start.41 = (bf16[128,2048]{1,0:T(8,128)(2,1)S(1)}, bf16[128,2048]{1,0:T(8,128)(2,1)S(1)}, u32[]{:S(2)}, u32[]{:S(2)}) collective-permute-start(bf16[128,2048]{1,0:T(8,128)(2,1)S(1)} %shard_map.78), channel_id=1, source_target_pairs={{0,8},{8,16},{16,24},{24,0},{1,9},{9,17},{17,25},{25,1},{2,10},{10... | collective-permute-start | bytes 1572872 | tf_op jit(solution)/shard_map/ppermute | solution.py:212
  143.9 5.7 %collective-permute-done.33.refs_9_ = bf16[80,2048]{1,0:T(8,128)(2,1)S(1)} collective-permute-done((bf16[80,2048]{1,0:T(8,128)(2,1)S(1)}, bf16[80,2048]{1,0:T(8,128)(2,1)S(1)}, u32[]{:S(2)}, u32[]{:S(2)}) %collective-permute-start.33) | collective-permute-done | bytes 327712 | tf_op jit(solution)/shard_map/ppermute | solution.py:215
  152.9 5.2 %collective-permute-done.41.refs_5_ = bf16[128,2048]{1,0:T(8,128)(2,1)S(1)} collective-permute-done((bf16[128,2048]{1,0:T(8,128)(2,1)S(1)}, bf16[128,2048]{1,0:T(8,128)(2,1)S(1)}, u32[]{:S(2)}, u32[]{:S(2)}) %collective-permute-start.41) | collective-permute-done | bytes 524320 | tf_op jit(solution)/shard_map/ppermute | solution.py:212
  (93 shorter events, 39.4 us)
Async XLA Ops:
  2.6 18.1 %collective-permute-start.1 = (bf16[136,2048]{1,0:T(8,128)(2,1)}, bf16[136,2048]{1,0:T(8,128)(2,1)S(1)}, u32[]{:S(2)}, u32[]{:S(2)}) collective-permute-start(bf16[136,2048]{1,0:T(8,128)(2,1)} %shard_map.64.refs_0_), channel_id=1, source_target_pairs={{0,8},{8,16},{16,24},{24,0},{1,9},{9,17},{17,25},{25,1},{2,10},{10... | collective-permute-start | bytes 1671176 | tf_op jit(solution)/shard_map/ppermute | solution.py:212
  7.1 13.6 %collective-permute-start.2 = (bf16[80,2048]{1,0:T(8,128)(2,1)S(1)}, bf16[80,2048]{1,0:T(8,128)(2,1)S(1)}, u32[]{:S(2)}, u32[]{:S(2)}) collective-permute-start(bf16[80,2048]{1,0:T(8,128)(2,1)S(1)} %get-tuple-element.114), channel_id=1, source_target_pairs={{0,2},{1,3},{2,0},{3,1},{4,6},{5,7},{6,4},{7,5},{8,10},{9,11},{10,... | collective-permute-start | bytes 983048 | tf_op jit(solution)/shard_map/ppermute | solution.py:215
  9.1 16.5 %collective-permute-start.4 = (bf16[80,2048]{1,0:T(8,128)(2,1)S(1)}, bf16[80,2048]{1,0:T(8,128)(2,1)S(1)}, u32[]{:S(2)}, u32[]{:S(2)}) collective-permute-start(bf16[80,2048]{1,0:T(8,128)(2,1)S(1)} %get-tuple-element.117), channel_id=1, source_target_pairs={{0,4},{1,5},{2,6},{3,7},{4,0},{5,1},{6,2},{7,3},{8,12},{9,13},{10,... | collective-permute-start | bytes 983048 | tf_op jit(solution)/shard_map/ppermute | solution.py:215
  10.6 15.0 %collective-permute-start.5 = (bf16[80,2048]{1,0:T(8,128)(2,1)S(1)}, bf16[80,2048]{1,0:T(8,128)(2,1)S(1)}, u32[]{:S(2)}, u32[]{:S(2)}) collective-permute-start(bf16[80,2048]{1,0:T(8,128)(2,1)S(1)} %get-tuple-element.118), channel_id=1, source_target_pairs={{0,6},{1,7},{2,4},{3,5},{4,2},{5,3},{6,0},{7,1},{8,14},{9,15},{10,... | collective-permute-start | bytes 983048 | tf_op jit(solution)/shard_map/ppermute | solution.py:215
  20.7 16.2 %collective-permute-start.9 = (bf16[136,2048]{1,0:T(8,128)(2,1)S(1)}, bf16[136,2048]{1,0:T(8,128)(2,1)S(1)}, u32[]{:S(2)}, u32[]{:S(2)}) collective-permute-start(bf16[136,2048]{1,0:T(8,128)(2,1)S(1)} %collective-permute-done.1.refs_0_), channel_id=1, source_target_pairs={{0,8},{8,16},{16,24},{24,0},{1,9},{9,17},{17,25},{25,1},{2,10},{10... | collective-permute-start | bytes 1671176 | tf_op jit(solution)/shard_map/ppermute | solution.py:212
  26.2 11.4 %collective-permute-start.6 = (bf16[88,2048]{1,0:T(8,128)(2,1)S(1)}, bf16[88,2048]{1,0:T(8,128)(2,1)S(1)}, u32[]{:S(2)}, u32[]{:S(2)}) collective-permute-start(bf16[88,2048]{1,0:T(8,128)(2,1)S(1)} %get-tuple-element.121), channel_id=1, source_target_pairs={{0,2},{1,3},{2,0},{3,1},{4,6},{5,7},{6,4},{7,5},{8,10},{9,11},{10,... | collective-permute-start | bytes 1081352 | tf_op jit(solution)/shard_map/ppermute | solution.py:215
  27.5 16.9 %collective-permute-start.8 = (bf16[88,2048]{1,0:T(8,128)(2,1)S(1)}, bf16[88,2048]{1,0:T(8,128)(2,1)S(1)}, u32[]{:S(2)}, u32[]{:S(2)}) collective-permute-start(bf16[88,2048]{1,0:T(8,128)(2,1)S(1)} %get-tuple-element.125), channel_id=1, source_target_pairs={{0,6},{1,7},{2,4},{3,5},{4,2},{5,3},{6,0},{7,1},{8,14},{9,15},{10,... | collective-permute-start | bytes 1081352 | tf_op jit(solution)/shard_map/ppermute | solution.py:215
  29.2 16.5 %collective-permute-start.7 = (bf16[88,2048]{1,0:T(8,128)(2,1)S(1)}, bf16[88,2048]{1,0:T(8,128)(2,1)S(1)}, u32[]{:S(2)}, u32[]{:S(2)}) collective-permute-start(bf16[88,2048]{1,0:T(8,128)(2,1)S(1)} %get-tuple-element.123), channel_id=1, source_target_pairs={{0,4},{1,5},{2,6},{3,7},{4,0},{5,1},{6,2},{7,3},{8,12},{9,13},{10,... | collective-permute-start | bytes 1081352 | tf_op jit(solution)/shard_map/ppermute | solution.py:215
  37.6 8.1 %collective-permute-start.11 = (bf16[136,2048]{1,0:T(8,128)(2,1)S(1)}, bf16[136,2048]{1,0:T(8,128)(2,1)S(1)}, u32[]{:S(2)}, u32[]{:S(2)}) collective-permute-start(bf16[136,2048]{1,0:T(8,128)(2,1)S(1)} %collective-permute-done.9.refs_0_), channel_id=1, source_target_pairs={{0,1},{1,0},{2,3},{3,2},{4,5},{5,4},{6,7},{7,6},{8,9},{9,8},{10,11... | collective-permute-start | bytes 1671176 | tf_op jit(solution)/shard_map/ppermute | solution.py:215
  37.6 16.9 %collective-permute-start.10 = (bf16[136,2048]{1,0:T(8,128)(2,1)S(1)}, bf16[136,2048]{1,0:T(8,128)(2,1)S(1)}, u32[]{:S(2)}, u32[]{:S(2)}) collective-permute-start(bf16[136,2048]{1,0:T(8,128)(2,1)S(1)} %collective-permute-done.9.refs_0_), channel_id=1, source_target_pairs={{0,8},{8,16},{16,24},{24,0},{1,9},{9,17},{17,25},{25,1},{2,10},{10... | collective-permute-start | bytes 1671176 | tf_op jit(solution)/shard_map/ppermute | solution.py:212
  46.3 9.8 %collective-permute-start.12 = (bf16[80,2048]{1,0:T(8,128)(2,1)S(1)}, bf16[80,2048]{1,0:T(8,128)(2,1)S(1)}, u32[]{:S(2)}, u32[]{:S(2)}) collective-permute-start(bf16[80,2048]{1,0:T(8,128)(2,1)S(1)} %get-tuple-element.134), channel_id=1, source_target_pairs={{0,2},{1,3},{2,0},{3,1},{4,6},{5,7},{6,4},{7,5},{8,10},{9,11},{10,... | collective-permute-start | bytes 983048 | tf_op jit(solution)/shard_map/ppermute | solution.py:215
  47.0 13.1 %collective-permute-start.15 = (bf16[80,2048]{1,0:T(8,128)(2,1)S(1)}, bf16[80,2048]{1,0:T(8,128)(2,1)S(1)}, u32[]{:S(2)}, u32[]{:S(2)}) collective-permute-start(bf16[80,2048]{1,0:T(8,128)(2,1)S(1)} %get-tuple-element.148), channel_id=1, source_target_pairs={{0,4},{1,5},{2,6},{3,7},{4,0},{5,1},{6,2},{7,3},{8,12},{9,13},{10,... | collective-permute-start | bytes 983048 | tf_op jit(solution)/shard_map/ppermute | solution.py:215
  48.5 11.6 %collective-permute-start.17 = (bf16[80,2048]{1,0:T(8,128)(2,1)S(1)}, bf16[80,2048]{1,0:T(8,128)(2,1)S(1)}, u32[]{:S(2)}, u32[]{:S(2)}) collective-permute-start(bf16[80,2048]{1,0:T(8,128)(2,1)S(1)} %get-tuple-element.152), channel_id=1, source_target_pairs={{0,6},{1,7},{2,4},{3,5},{4,2},{5,3},{6,0},{7,1},{8,14},{9,15},{10,... | collective-permute-start | bytes 983048 | tf_op jit(solution)/shard_map/ppermute | solution.py:215
  56.2 7.4 %collective-permute-start.13 = (bf16[136,2048]{1,0:T(8,128)(2,1)S(1)}, bf16[136,2048]{1,0:T(8,128)(2,1)S(1)}, u32[]{:S(2)}, u32[]{:S(2)}) collective-permute-start(bf16[136,2048]{1,0:T(8,128)(2,1)S(1)} %collective-permute-done.10.refs_0_), channel_id=1, source_target_pairs={{0,1},{1,0},{2,3},{3,2},{4,5},{5,4},{6,7},{7,6},{8,9},{9,8},{10,11... | collective-permute-start | bytes 1671176 | tf_op jit(solution)/shard_map/ppermute | solution.py:215
  60.1 11.5 %collective-permute-start.18 = (bf16[80,2048]{1,0:T(8,128)(2,1)S(1)}, bf16[80,2048]{1,0:T(8,128)(2,1)S(1)}, u32[]{:S(2)}, u32[]{:S(2)}) collective-permute-start(bf16[80,2048]{1,0:T(8,128)(2,1)S(1)} %get-tuple-element.153), channel_id=1, source_target_pairs={{0,6},{1,7},{2,4},{3,5},{4,2},{5,3},{6,0},{7,1},{8,14},{9,15},{10,... | collective-permute-start | bytes 983048 | tf_op jit(solution)/shard_map/ppermute | solution.py:215
  61.6 15.9 %collective-permute-start.16 = (bf16[80,2048]{1,0:T(8,128)(2,1)S(1)}, bf16[80,2048]{1,0:T(8,128)(2,1)S(1)}, u32[]{:S(2)}, u32[]{:S(2)}) collective-permute-start(bf16[80,2048]{1,0:T(8,128)(2,1)S(1)} %get-tuple-element.149), channel_id=1, source_target_pairs={{0,4},{1,5},{2,6},{3,7},{4,0},{5,1},{6,2},{7,3},{8,12},{9,13},{10,... | collective-permute-start | bytes 983048 | tf_op jit(solution)/shard_map/ppermute | solution.py:215
  63.2 14.3 %collective-permute-start.14 = (bf16[80,2048]{1,0:T(8,128)(2,1)S(1)}, bf16[80,2048]{1,0:T(8,128)(2,1)S(1)}, u32[]{:S(2)}, u32[]{:S(2)}) collective-permute-start(bf16[80,2048]{1,0:T(8,128)(2,1)S(1)} %get-tuple-element.145), channel_id=1, source_target_pairs={{0,2},{1,3},{2,0},{3,1},{4,6},{5,7},{6,4},{7,5},{8,10},{9,11},{10,... | collective-permute-start | bytes 983048 | tf_op jit(solution)/shard_map/ppermute | solution.py:215
  79.4 17.6 %collective-permute-start.25 = (bf16[80,2048]{1,0:T(8,128)(2,1)S(1)}, bf16[80,2048]{1,0:T(8,128)(2,1)S(1)}, u32[]{:S(2)}, u32[]{:S(2)}) collective-permute-start(bf16[80,2048]{1,0:T(8,128)(2,1)S(1)} %get-tuple-element.181), channel_id=1, source_target_pairs={{0,6},{1,7},{2,4},{3,5},{4,2},{5,3},{6,0},{7,1},{8,14},{9,15},{10,... | collective-permute-start | bytes 983048 | tf_op jit(solution)/shard_map/ppermute | solution.py:215
  81.2 15.9 %collective-permute-start.23 = (bf16[80,2048]{1,0:T(8,128)(2,1)S(1)}, bf16[80,2048]{1,0:T(8,128)(2,1)S(1)}, u32[]{:S(2)}, u32[]{:S(2)}) collective-permute-start(bf16[80,2048]{1,0:T(8,128)(2,1)S(1)} %get-tuple-element.177), channel_id=1, source_target_pairs={{0,4},{1,5},{2,6},{3,7},{4,0},{5,1},{6,2},{7,3},{8,12},{9,13},{10,... | collective-permute-start | bytes 983048 | tf_op jit(solution)/shard_map/ppermute | solution.py:215
  81.9 14.5 %collective-permute-start.21 = (bf16[80,2048]{1,0:T(8,128)(2,1)S(1)}, bf16[80,2048]{1,0:T(8,128)(2,1)S(1)}, u32[]{:S(2)}, u32[]{:S(2)}) collective-permute-start(bf16[80,2048]{1,0:T(8,128)(2,1)S(1)} %get-tuple-element.173), channel_id=1, source_target_pairs={{0,2},{1,3},{2,0},{3,1},{4,6},{5,7},{6,4},{7,5},{8,10},{9,11},{10,... | collective-permute-start | bytes 983048 | tf_op jit(solution)/shard_map/ppermute | solution.py:215
  83.1 17.5 %collective-permute-start.27 = (bf16[128,2048]{1,0:T(8,128)(2,1)S(1)}, bf16[128,2048]{1,0:T(8,128)(2,1)S(1)}, u32[]{:S(2)}, u32[]{:S(2)}) collective-permute-start(bf16[128,2048]{1,0:T(8,128)(2,1)S(1)} %shard_map.72), channel_id=1, source_target_pairs={{0,24},{8,0},{16,8},{24,16},{1,25},{9,1},{17,9},{25,17},{2,26},{10... | collective-permute-start | bytes 1572872 | tf_op jit(solution)/shard_map/ppermute | solution.py:212
  97.1 11.5 %collective-permute-start.26 = (bf16[80,2048]{1,0:T(8,128)(2,1)S(1)}, bf16[80,2048]{1,0:T(8,128)(2,1)S(1)}, u32[]{:S(2)}, u32[]{:S(2)}) collective-permute-start(bf16[80,2048]{1,0:T(8,128)(2,1)S(1)} %get-tuple-element.182), channel_id=1, source_target_pairs={{0,6},{1,7},{2,4},{3,5},{4,2},{5,3},{6,0},{7,1},{8,14},{9,15},{10,... | collective-permute-start | bytes 983048 | tf_op jit(solution)/shard_map/ppermute | solution.py:215
  98.8 15.8 %collective-permute-start.24 = (bf16[80,2048]{1,0:T(8,128)(2,1)S(1)}, bf16[80,2048]{1,0:T(8,128)(2,1)S(1)}, u32[]{:S(2)}, u32[]{:S(2)}) collective-permute-start(bf16[80,2048]{1,0:T(8,128)(2,1)S(1)} %get-tuple-element.178), channel_id=1, source_target_pairs={{0,4},{1,5},{2,6},{3,7},{4,0},{5,1},{6,2},{7,3},{8,12},{9,13},{10,... | collective-permute-start | bytes 983048 | tf_op jit(solution)/shard_map/ppermute | solution.py:215
  99.5 15.1 %collective-permute-start.22 = (bf16[80,2048]{1,0:T(8,128)(2,1)S(1)}, bf16[80,2048]{1,0:T(8,128)(2,1)S(1)}, u32[]{:S(2)}, u32[]{:S(2)}) collective-permute-start(bf16[80,2048]{1,0:T(8,128)(2,1)S(1)} %get-tuple-element.174), channel_id=1, source_target_pairs={{0,2},{1,3},{2,0},{3,1},{4,6},{5,7},{6,4},{7,5},{8,10},{9,11},{10,... | collective-permute-start | bytes 983048 | tf_op jit(solution)/shard_map/ppermute | solution.py:215
  104.8 34.0 %collective-permute-start.36 = (bf16[128,2048]{1,0:T(8,128)(2,1)S(1)}, bf16[128,2048]{1,0:T(8,128)(2,1)S(1)}, u32[]{:S(2)}, u32[]{:S(2)}) collective-permute-start(bf16[128,2048]{1,0:T(8,128)(2,1)S(1)} %shard_map.75), channel_id=1, source_target_pairs={{0,16},{8,24},{16,0},{24,8},{1,17},{9,25},{17,1},{25,9},{2,18},{10... | collective-permute-start | bytes 1572872 | tf_op jit(solution)/shard_map/ppermute | solution.py:212
  117.8 11.6 %collective-permute-start.34 = (bf16[80,2048]{1,0:T(8,128)(2,1)S(1)}, bf16[80,2048]{1,0:T(8,128)(2,1)S(1)}, u32[]{:S(2)}, u32[]{:S(2)}) collective-permute-start(bf16[80,2048]{1,0:T(8,128)(2,1)S(1)} %get-tuple-element.207), channel_id=1, source_target_pairs={{0,6},{1,7},{2,4},{3,5},{4,2},{5,3},{6,0},{7,1},{8,14},{9,15},{10,... | collective-permute-start | bytes 983048 | tf_op jit(solution)/shard_map/ppermute | solution.py:215
  119.7 16.7 %collective-permute-start.32 = (bf16[80,2048]{1,0:T(8,128)(2,1)S(1)}, bf16[80,2048]{1,0:T(8,128)(2,1)S(1)}, u32[]{:S(2)}, u32[]{:S(2)}) collective-permute-start(bf16[80,2048]{1,0:T(8,128)(2,1)S(1)} %get-tuple-element.203), channel_id=1, source_target_pairs={{0,4},{1,5},{2,6},{3,7},{4,0},{5,1},{6,2},{7,3},{8,12},{9,13},{10,... | collective-permute-start | bytes 983048 | tf_op jit(solution)/shard_map/ppermute | solution.py:215
  120.4 16.7 %collective-permute-start.30 = (bf16[80,2048]{1,0:T(8,128)(2,1)S(1)}, bf16[80,2048]{1,0:T(8,128)(2,1)S(1)}, u32[]{:S(2)}, u32[]{:S(2)}) collective-permute-start(bf16[80,2048]{1,0:T(8,128)(2,1)S(1)} %get-tuple-element.199), channel_id=1, source_target_pairs={{0,2},{1,3},{2,0},{3,1},{4,6},{5,7},{6,4},{7,5},{8,10},{9,11},{10,... | collective-permute-start | bytes 983048 | tf_op jit(solution)/shard_map/ppermute | solution.py:215
  129.4 14.4 %collective-permute-start.35 = (bf16[80,2048]{1,0:T(8,128)(2,1)S(1)}, bf16[80,2048]{1,0:T(8,128)(2,1)S(1)}, u32[]{:S(2)}, u32[]{:S(2)}) collective-permute-start(bf16[80,2048]{1,0:T(8,128)(2,1)S(1)} %get-tuple-element.208), channel_id=1, source_target_pairs={{0,6},{1,7},{2,4},{3,5},{4,2},{5,3},{6,0},{7,1},{8,14},{9,15},{10,... | collective-permute-start | bytes 983048 | tf_op jit(solution)/shard_map/ppermute | solution.py:215
  136.4 13.2 %collective-permute-start.33 = (bf16[80,2048]{1,0:T(8,128)(2,1)S(1)}, bf16[80,2048]{1,0:T(8,128)(2,1)S(1)}, u32[]{:S(2)}, u32[]{:S(2)}) collective-permute-start(bf16[80,2048]{1,0:T(8,128)(2,1)S(1)} %get-tuple-element.204), channel_id=1, source_target_pairs={{0,4},{1,5},{2,6},{3,7},{4,0},{5,1},{6,2},{7,3},{8,12},{9,13},{10,... | collective-permute-start | bytes 983048 | tf_op jit(solution)/shard_map/ppermute | solution.py:215
  137.1 12.5 %collective-permute-start.31 = (bf16[80,2048]{1,0:T(8,128)(2,1)S(1)}, bf16[80,2048]{1,0:T(8,128)(2,1)S(1)}, u32[]{:S(2)}, u32[]{:S(2)}) collective-permute-start(bf16[80,2048]{1,0:T(8,128)(2,1)S(1)} %get-tuple-element.200), channel_id=1, source_target_pairs={{0,2},{1,3},{2,0},{3,1},{4,6},{5,7},{6,4},{7,5},{8,10},{9,11},{10,... | collective-permute-start | bytes 983048 | tf_op jit(solution)/shard_map/ppermute | solution.py:215
  142.2 15.9 %collective-permute-start.41 = (bf16[128,2048]{1,0:T(8,128)(2,1)S(1)}, bf16[128,2048]{1,0:T(8,128)(2,1)S(1)}, u32[]{:S(2)}, u32[]{:S(2)}) collective-permute-start(bf16[128,2048]{1,0:T(8,128)(2,1)S(1)} %shard_map.78), channel_id=1, source_target_pairs={{0,8},{8,16},{16,24},{24,0},{1,9},{9,17},{17,25},{25,1},{2,10},{10... | collective-permute-start | bytes 1572872 | tf_op jit(solution)/shard_map/ppermute | solution.py:212
  (22 other events, 156.3 us)

commit v11 on v8

--- a/solution.py
+++ b/solution.py
@@ -75,11 +75,11 @@
     return block_ref[z.toks : z.toks + 8, 0 : z.toks].astype(F32).astype(jnp.int32)
 
 
-def slot_marks(z, ids_t):
+def slot_marks(z, ids_t, offsets):
     has = jnp.concatenate(
         [
             jnp.max((ids_t == served_expert(z, q)).astype(F32), axis=0, keepdims=True)
-            for q in range(z.chips)
+            for q in offsets
         ]
         * 2,
         axis=0,
@@ -94,9 +94,9 @@
     return [jnp.where(row == slot[q : q + 1, :], 1.0, 0.0) for q in range(z.chips)]
 
 
-def pick_kernel(z, n, ride, *refs):
+def pick_kernel(z, n, offsets, ride, *refs):
     blocks, outs = refs[:n], refs[n:]
-    marks = [jnp.concatenate(slot_marks(z, ids_of(z, b)), axis=0).astype(BF16) for b in blocks]
+    marks = [jnp.concatenate(slot_marks(z, ids_of(z, b), offsets), axis=0).astype(BF16) for b in blocks]
     part = z.width // PARTS
     for c in range(PARTS):
         cols = slice(c * part, (c + 1) * part)
@@ -131,19 +131,19 @@
             outs[q][:, c : c + tile] = y[q * rows : (q + 1) * rows].astype(BF16)
 
 
-def mix_kernel(z, n, *refs):
+def mix_kernel(z, n, offsets, ride_offsets, *refs):
     blocks, refs = refs[:n], refs[n:]
     riders, backs, outs = refs[: z.chips], refs[z.chips : 2 * z.chips], refs[2 * z.chips :]
     number = lax.broadcasted_iota(jnp.int32, (z.experts, z.toks), 0)
-    routers = []
-    for q in range(z.chips):
+    routers = {}
+    for i, q in enumerate(ride_offsets):
         for r in range(CORES):
             base = CORES * z.cap
             pieces = []
             for g in range(z.experts // 8):
                 rows, cols = z.tile(r * (z.experts // 8) + g)
-                pieces.append(riders[q][base + rows.start : base + rows.stop, cols].astype(F32))
-            routers.append(jnp.concatenate(pieces, axis=0).astype(BF16))
+                pieces.append(riders[i][base + rows.start : base + rows.stop, cols].astype(F32))
+            routers[CORES * q + r] = jnp.concatenate(pieces, axis=0).astype(BF16)
     for b, block in enumerate(blocks):
         ids_t = ids_of(z, block)
         logits = None
@@ -161,11 +161,11 @@
             chosen = chosen | (number == ids_t[k : k + 1, :])
         weights = jnp.where(chosen, jnp.exp(jnp.where(chosen, logits, 0.0)), 0.0)
         gates = weights / jnp.sum(weights, axis=0, keepdims=True)
-        marks = slot_marks(z, ids_t)
+        marks = slot_marks(z, ids_t, offsets)
         mix = []
-        for q in range(z.chips):
+        for mark, q in zip(marks, offsets):
             gate = jnp.sum(jnp.where(number == served_expert(z, q), gates, 0.0), axis=0, keepdims=True)
-            mix.append(marks[q] * gate)
+            mix.append(mark * gate)
         mix = jnp.concatenate(mix, axis=0).astype(BF16)
         part = z.width // PARTS
         for c in range(PARTS):
@@ -208,22 +208,29 @@
     def shape(rows):
         return jax.ShapeDtypeStruct((rows, z.width), BF16)
 
-    def pick(blocks, ride, flops=1000):
+    forward = list(range(z.chips))
+    backward = [0] + forward[:0:-1]
+    out_order = {0: forward, 1: forward[:-2] + forward[:-3:-1]}
+    ride_order = out_order[1]
+
+    def pick(blocks, d, flops=1000):
         n = len(blocks)
-        rows = n * z.cap + (z.ride if ride else 0)
-        body = functools.partial(pick_kernel, z, n, ride)
-        return call(body, [shape(rows)] * z.chips, n, flops=flops)(*blocks)
+        offsets = out_order.get(d, backward)
+        rows = n * z.cap + (z.ride if d == 1 else 0)
+        body = functools.partial(pick_kernel, z, n, offsets, d == 1)
+        return dict(zip(offsets, call(body, [shape(rows)] * z.chips, n, flops=flops)(*blocks)))
 
     def arrived(arrays):
         out = jax.ShapeDtypeStruct((8, 128), BF16)
         return call(arrived_kernel, out, len(arrays), flops=PHASE_FLOPS)(*arrays)
 
     def slabs_across(slabs):
-        return [across(s, CORES * q) for q, s in enumerate(slabs)]
-
-    def expert(slabs, n, flops=1000):
-        rows = n * z.cap
-        return call(
+        return {q: across(s, CORES * q) for q, s in slabs.items()}
+
+    def expert(slabs, *first, flops=1000):
+        rows = CORES * z.cap
+        offsets = list(slabs)
+        outs = call(
             functools.partial(expert_kernel, z, rows),
             [shape(rows)] * z.chips,
             z.chips + 3,
@@ -232,16 +239,18 @@
                 pltpu.VMEM((z.chips * rows, gate_weight.shape[2]), BF16),
             ],
             flops,
-        )(*slabs, gate_weight[0], up_weight[0], down_weight[0])
-
-    def mix(blocks, backs):
-        riders = slots[1]
+        )(*after(list(slabs.values()), *first), gate_weight[0], up_weight[0], down_weight[0])
+        return dict(zip(offsets, outs))
+
+    def mix(blocks, backs, *first):
+        riders = [slots[1][q] for q in ride_order]
+        n = len(blocks)
         mine, *other = call(
-            functools.partial(mix_kernel, z, CORES),
+            functools.partial(mix_kernel, z, n, list(backs), ride_order),
             [shape(z.toks), shape(z.toks // 2), shape(z.toks // 2)],
-            CORES + 2 * z.chips,
+            n + 2 * z.chips,
             flops=PHASE_FLOPS,
-        )(*blocks, *riders, *backs)
+        )(*blocks, *riders, *after(list(backs.values()), *first))
         return [mine] + [across(part, 1) for part in other]
 
     def join(parts):
@@ -261,24 +270,25 @@
             if d:
                 blocks[d] = after([along(blocks[d - 1], 1)], slots[d - 1][1])[0]
             pairs[d] = [blocks[d], across(blocks[d], 1)]
-            rows = slabs = pick(pairs[d], d == 1, PHASE_FLOPS if d == end else 1000)
+            rows = slabs = pick(pairs[d], d, PHASE_FLOPS if d == end else 1000)
             if 0 < d < end:
-                gate = arrived(slots[d - 1][1:] + ([results[d - 2][0]] if d > 1 else []))
-                rows = [after([s], gate)[0] for s in slabs]
-                results[d - 1] = expert(after(slots[d - 1], slabs[0]), 2)
+                gate = [slots[d - 1][q] for q in forward[1:]] + ([results[d - 2][0]] if d > 1 else [])
+                gate = arrived(gate)
+                rows = {q: after([s], gate)[0] for q, s in slabs.items()}
+                results[d - 1] = expert(slots[d - 1], slabs[0])
             if d == end:
-                rows = [after([r], b)[0] for r, b in zip(slabs, seen)]
+                rows = {q: after([s], seen[q])[0] for q, s in slabs.items()}
             seen = slots[d] = slabs_across(rows)
             if d == end - 1:
-                results[d] = expert(slots[d], 2)
+                results[d] = expert(slots[d])
             if d == end:
                 first = [leaving[e] for e in range(1, end)]
-                results[d] = expert(after(slots[d], *first), 2, PHASE_FLOPS)
+                results[d] = expert(slots[d], *first, flops=PHASE_FLOPS)
         else:
-            rows = [after([r], b)[0] for r, b in zip(results[d], seen)]
+            rows = {q: after([results[d][q]], seen[q])[0] for q in backward}
             seen = backs = slabs_across(rows)
             first = [(home if d else leaving)[waiting]] if waiting else [results[end - 1][0]]
-            sums = mix(pairs[d], after(backs, *first))
+            sums = mix(pairs[d], backs, *first)
             if d:
                 leaving[d] = join(sums)
                 home[d] = along(leaving[d], layers - d)

time: 153 us -> 152 us (level)
  waiting for transfers between devices: 77.6 us -> 71.2 us
  starting transfers between devices: 44.7 us -> 49.8 us
    ppermute x36, waiting for transfers between devices: 61 us -> 54.1 us  [across(): lax.ppermute(array, 'zero', [(i, i ^ o) for i in range(near)])]
    ppermute x36, starting transfers between devices: 32.4 us -> 37.4 us  [across(): lax.ppermute(array, 'zero', [(i, i ^ o) for i in range(near)])]
  transfers between devices with their start and end apart: 42 -> 42, of which waited for: 21 -> 24; matrix products, arithmetic and copies ran while one was open for 0% -> 0% of each run, Pallas kernels for 13% -> 13%
where the time goes in v11:
time: 152 us; the launch traced here: 151 us
  waiting for transfers between devices  71.2 us (47%)
  starting transfers between devices  49.8 us (33%)
  Pallas kernels  22.2 us (15%)
  local copies, waits for them, and re-layouts  7.99 us (5%)
    ppermute x36, waiting for transfers between devices, across(): lax.ppermute(array, 'zero', [(i, i ^ o) for i in range(near)])  54.1 us
    ppermute x36, starting transfers between devices, across(): lax.ppermute(array, 'zero', [(i, i ^ o) for i in range(near)])  37.4 us
    ppermute x6, waiting for transfers between devices, along(): lax.ppermute(array, 'expert', [(i, (i + d) % layers) for i in range(layer...  17 us
    pallas_call x4, Pallas kernels, expert(): call(functools.partial(expert_kernel, z, rows), [shape(rows)] * z.chips,...  12.9 us
    ppermute x6, starting transfers between devices, along(): lax.ppermute(array, 'expert', [(i, (i + d) % layers) for i in range(layer...  12.5 us
    unnamed x28, local copies, waits for them, and re-layouts  7.99 us
    pallas_call x4, Pallas kernels, mix(): call(functools.partial(mix_kernel, z, n, list(backs), ride_order), [shape...  5.36 us
  transfers between devices with their start and end apart: 42, of which 24 were waited for; matrix products, arithmetic and copies ran while one was open for 0% of the time, Pallas kernels for 13%

profile of v11, /device:TPU:0, one launch (start us, length us, event | category | flops | bytes accessed | tf_op | source)
XLA Modules:
  0.0 151.4 jit_solution(451323987227539964)
XLA Ops:
  3.2 2.6 %collective-permute-start.1 = (bf16[136,2048]{1,0:T(8,128)(2,1)S(1)}, bf16[136,2048]{1,0:T(8,128)(2,1)S(1)}, u32[]{:S(2)}, u32[]{:S(2)}) collective-permute-start(bf16[136,2048]{1,0:T(8,128)(2,1)S(1)} %shard_map.64.refs_0_), channel_id=1, source_target_pairs={{0,8},{8,16},{16,24},{24,0},{1,9},{9,17},{17,25},{25,1},{2,10},{10... | collective-permute-start | bytes 1671176 | tf_op jit(solution)/shard_map/ppermute | solution.py:200
  7.2 1.8 %collective-permute-start.2 = (bf16[80,2048]{1,0:T(8,128)(2,1)S(1)}, bf16[80,2048]{1,0:T(8,128)(2,1)S(1)}, u32[]{:S(2)}, u32[]{:S(2)}) collective-permute-start(bf16[80,2048]{1,0:T(8,128)(2,1)S(1)} %get-tuple-element.112), channel_id=1, source_target_pairs={{0,2},{1,3},{2,0},{3,1},{4,6},{5,7},{6,4},{7,5},{8,10},{9,11},{10,... | collective-permute-start | bytes 983048 | tf_op jit(solution)/shard_map/ppermute | solution.py:203
  9.0 1.5 %collective-permute-start.4 = (bf16[80,2048]{1,0:T(8,128)(2,1)S(1)}, bf16[80,2048]{1,0:T(8,128)(2,1)S(1)}, u32[]{:S(2)}, u32[]{:S(2)}) collective-permute-start(bf16[80,2048]{1,0:T(8,128)(2,1)S(1)} %get-tuple-element.115), channel_id=1, source_target_pairs={{0,4},{1,5},{2,6},{3,7},{4,0},{5,1},{6,2},{7,3},{8,12},{9,13},{10,... | collective-permute-start | bytes 983048 | tf_op jit(solution)/shard_map/ppermute | solution.py:203
  10.7 10.3 %collective-permute-done.1.refs_0_ = bf16[136,2048]{1,0:T(8,128)(2,1)S(1)} collective-permute-done((bf16[136,2048]{1,0:T(8,128)(2,1)S(1)}, bf16[136,2048]{1,0:T(8,128)(2,1)S(1)}, u32[]{:S(2)}, u32[]{:S(2)}) %collective-permute-start.1) | collective-permute-done | bytes 557088 | tf_op jit(solution)/shard_map/ppermute | solution.py:200
  21.1 4.4 %collective-permute-done.4.refs_2_ = bf16[80,2048]{1,0:T(8,128)(2,1)S(1)} collective-permute-done((bf16[80,2048]{1,0:T(8,128)(2,1)S(1)}, bf16[80,2048]{1,0:T(8,128)(2,1)S(1)}, u32[]{:S(2)}, u32[]{:S(2)}) %collective-permute-start.4) | collective-permute-done | bytes 327712 | tf_op jit(solution)/shard_map/ppermute | solution.py:203
  29.7 1.9 %copy-done.1 = bf16[1,2048,768]{2,1,0:T(8,128)(2,1)S(1)} copy-done((bf16[1,2048,768]{2,1,0:T(8,128)(2,1)S(1)}, bf16[1,2048,768]{2,1,0:T(8,128)(2,1)}, u32[]{:S(2)}) %copy-start.1) | copy-done | bytes 3145752
  31.6 1.9 %copy-done.3 = bf16[1,768,2048]{2,1,0:T(8,128)(2,1)S(1)} copy-done((bf16[1,768,2048]{2,1,0:T(8,128)(2,1)S(1)}, bf16[1,768,2048]{2,1,0:T(8,128)(2,1)}, u32[]{:S(2)}) %copy-start.3) | copy-done | bytes 3145752
  33.5 3.2 %shard_map.67 = (bf16[80,2048]{1,0:T(8,128)(2,1)S(1)}, bf16[80,2048]{1,0:T(8,128)(2,1)S(1)}, bf16[80,2048]{1,0:T(8,128)(2,1)S(1)}, bf16[80,2048]{1,0:T(8,128)(2,1)S(1)}) custom-call(bf16[80,2048]{1,0:T(8,128)(2,1)S(1)} %get-tuple-element.125.refs_0_, bf16[80,2048]{1,0:T(8,128)(2,1)S(1)} %collective-permute-done.2.refs_1_, ...), custom_call_target="tpu_custom_call" | custom-call | flops 1000 | bytes 1000 | tf_op jit(solution)/shard_map/pallas_call | solution.py:233
  37.9 6.6 %collective-permute-done.8.refs_3_.refs_5_ = bf16[88,2048]{1,0:T(8,128)(2,1)S(1)} collective-permute-done((bf16[88,2048]{1,0:T(8,128)(2,1)S(1)}, bf16[88,2048]{1,0:T(8,128)(2,1)S(1)}, u32[]{:S(2)}, u32[]{:S(2)}) %collective-permute-start.8) | collective-permute-done | bytes 360480 | tf_op jit(solution)/shard_map/ppermute | solution.py:203
  48.7 1.6 %collective-permute-start.10 = (bf16[136,2048]{1,0:T(8,128)(2,1)S(1)}, bf16[136,2048]{1,0:T(8,128)(2,1)S(1)}, u32[]{:S(2)}, u32[]{:S(2)}) collective-permute-start(bf16[136,2048]{1,0:T(8,128)(2,1)S(1)} %collective-permute-done.9.refs_0_), channel_id=1, source_target_pairs={{0,8},{8,16},{16,24},{24,0},{1,9},{9,17},{17,25},{25,1},{2,10},{10... | collective-permute-start | bytes 1671176 | tf_op jit(solution)/shard_map/ppermute | solution.py:200
  50.2 3.2 %shard_map.71 = (bf16[80,2048]{1,0:T(8,128)(2,1)S(1)}, bf16[80,2048]{1,0:T(8,128)(2,1)S(1)}, bf16[80,2048]{1,0:T(8,128)(2,1)S(1)}, bf16[80,2048]{1,0:T(8,128)(2,1)S(1)}) custom-call(bf16[88,2048]{1,0:T(8,128)(2,1)S(1)} %get-tuple-element.146.refs_0_.refs_2_, bf16[88,2048]{1,0:T(8,128)(2,1)S(1)} %collective-permute-done.6.refs_1_.refs_3_, ...), custom_call_target="tpu_custom_call" | custom-call | flops 1000 | bytes 1000 | tf_op jit(solution)/shard_map/pallas_call | solution.py:233
  53.5 2.4 %collective-permute-done.12.refs_3_ = bf16[80,2048]{1,0:T(8,128)(2,1)S(1)} collective-permute-done((bf16[80,2048]{1,0:T(8,128)(2,1)S(1)}, bf16[80,2048]{1,0:T(8,128)(2,1)S(1)}, u32[]{:S(2)}, u32[]{:S(2)}) %collective-permute-start.12) | collective-permute-done | bytes 327712 | tf_op jit(solution)/shard_map/ppermute | solution.py:203
  56.4 3.5 %collective-permute-done.15.refs_2_ = bf16[80,2048]{1,0:T(8,128)(2,1)S(1)} collective-permute-done((bf16[80,2048]{1,0:T(8,128)(2,1)S(1)}, bf16[80,2048]{1,0:T(8,128)(2,1)S(1)}, u32[]{:S(2)}, u32[]{:S(2)}) %collective-permute-start.15) | collective-permute-done | bytes 327712 | tf_op jit(solution)/shard_map/ppermute | solution.py:203
  59.9 2.6 %collective-permute-start.19 = (bf16[80,2048]{1,0:T(8,128)(2,1)S(1)}, bf16[80,2048]{1,0:T(8,128)(2,1)S(1)}, u32[]{:S(2)}, u32[]{:S(2)}) collective-permute-start(bf16[80,2048]{1,0:T(8,128)(2,1)S(1)} %get-tuple-element.163), channel_id=1, source_target_pairs={{0,4},{1,5},{2,6},{3,7},{4,0},{5,1},{6,2},{7,3},{8,12},{9,13},{10,... | collective-permute-start | bytes 983048 | tf_op jit(solution)/shard_map/ppermute | solution.py:203
  62.8 1.5 collective-permute-start.16
  64.3 3.2 %shard_map.70 = (bf16[80,2048]{1,0:T(8,128)(2,1)S(1)}, bf16[80,2048]{1,0:T(8,128)(2,1)S(1)}, bf16[80,2048]{1,0:T(8,128)(2,1)S(1)}, bf16[80,2048]{1,0:T(8,128)(2,1)S(1)}) custom-call(bf16[80,2048]{1,0:T(8,128)(2,1)S(1)} %get-tuple-element.141.refs_0_, bf16[80,2048]{1,0:T(8,128)(2,1)S(1)} %collective-permute-done.14.refs_1_, ...), custom_call_target="tpu_custom_call" | custom-call | flops 1000 | bytes 1000 | tf_op jit(solution)/shard_map/pallas_call | solution.py:233
  67.6 2.3 %collective-permute-done.22.refs_9_ = bf16[80,2048]{1,0:T(8,128)(2,1)S(1)} collective-permute-done((bf16[80,2048]{1,0:T(8,128)(2,1)S(1)}, bf16[80,2048]{1,0:T(8,128)(2,1)S(1)}, u32[]{:S(2)}, u32[]{:S(2)}) %collective-permute-start.22) | collective-permute-done | bytes 327712 | tf_op jit(solution)/shard_map/ppermute | solution.py:203
  69.9 4.5 %collective-permute-done.19.refs_8_ = bf16[80,2048]{1,0:T(8,128)(2,1)S(1)} collective-permute-done((bf16[80,2048]{1,0:T(8,128)(2,1)S(1)}, bf16[80,2048]{1,0:T(8,128)(2,1)S(1)}, u32[]{:S(2)}, u32[]{:S(2)}) %collective-permute-start.19) | collective-permute-done | bytes 327712 | tf_op jit(solution)/shard_map/ppermute | solution.py:203
  78.2 1.6 %collective-permute-start.17 = (bf16[80,2048]{1,0:T(8,128)(2,1)S(1)}, bf16[80,2048]{1,0:T(8,128)(2,1)S(1)}, u32[]{:S(2)}, u32[]{:S(2)}) collective-permute-start(bf16[80,2048]{1,0:T(8,128)(2,1)S(1)} %get-tuple-element.158), channel_id=1, source_target_pairs={{0,6},{1,7},{2,4},{3,5},{4,2},{5,3},{6,0},{7,1},{8,14},{9,15},{10,... | collective-permute-start | bytes 983048 | tf_op jit(solution)/shard_map/ppermute | solution.py:203
  79.9 3.9 %collective-permute-start.27 = (bf16[128,2048]{1,0:T(8,128)(2,1)S(1)}, bf16[128,2048]{1,0:T(8,128)(2,1)S(1)}, u32[]{:S(2)}, u32[]{:S(2)}) collective-permute-start(bf16[128,2048]{1,0:T(8,128)(2,1)S(1)} %shard_map.73), channel_id=1, source_target_pairs={{0,24},{8,0},{16,8},{24,16},{1,25},{9,1},{17,9},{25,17},{2,26},{10... | collective-permute-start | bytes 1572872 | tf_op jit(solution)/shard_map/ppermute | solution.py:200
  84.4 2.4 %collective-permute-done.23.refs_9_ = bf16[80,2048]{1,0:T(8,128)(2,1)S(1)} collective-permute-done((bf16[80,2048]{1,0:T(8,128)(2,1)S(1)}, bf16[80,2048]{1,0:T(8,128)(2,1)S(1)}, u32[]{:S(2)}, u32[]{:S(2)}) %collective-permute-start.23) | collective-permute-done | bytes 327712 | tf_op jit(solution)/shard_map/ppermute | solution.py:203
  88.0 5.9 %collective-permute-start.21 = (bf16[80,2048]{1,0:T(8,128)(2,1)S(1)}, bf16[80,2048]{1,0:T(8,128)(2,1)S(1)}, u32[]{:S(2)}, u32[]{:S(2)}) collective-permute-start(bf16[80,2048]{1,0:T(8,128)(2,1)S(1)} %get-tuple-element.165), channel_id=1, source_target_pairs={{0,4},{1,5},{2,6},{3,7},{4,0},{5,1},{6,2},{7,3},{8,12},{9,13},{10,... | collective-permute-start | bytes 983048 | tf_op jit(solution)/shard_map/ppermute | solution.py:203
  95.0 1.5 %collective-permute-start.18 = (bf16[80,2048]{1,0:T(8,128)(2,1)S(1)}, bf16[80,2048]{1,0:T(8,128)(2,1)S(1)}, u32[]{:S(2)}, u32[]{:S(2)}) collective-permute-start(bf16[80,2048]{1,0:T(8,128)(2,1)S(1)} %get-tuple-element.159), channel_id=1, source_target_pairs={{0,6},{1,7},{2,4},{3,5},{4,2},{5,3},{6,0},{7,1},{8,14},{9,15},{10,... | collective-permute-start | bytes 983048 | tf_op jit(solution)/shard_map/ppermute | solution.py:203
  100.7 2.7 %collective-permute-start.36 = (bf16[128,2048]{1,0:T(8,128)(2,1)S(1)}, bf16[128,2048]{1,0:T(8,128)(2,1)S(1)}, u32[]{:S(2)}, u32[]{:S(2)}) collective-permute-start(bf16[128,2048]{1,0:T(8,128)(2,1)S(1)} %shard_map.75), channel_id=1, source_target_pairs={{0,16},{8,24},{16,0},{24,8},{1,17},{9,25},{17,1},{25,9},{2,18},{10... | collective-permute-start | bytes 1572872 | tf_op jit(solution)/shard_map/ppermute | solution.py:200
  103.4 4.7 %collective-permute-done.18.refs_1_ = bf16[80,2048]{1,0:T(8,128)(2,1)S(1)} collective-permute-done((bf16[80,2048]{1,0:T(8,128)(2,1)S(1)}, bf16[80,2048]{1,0:T(8,128)(2,1)S(1)}, u32[]{:S(2)}, u32[]{:S(2)}) %collective-permute-start.18) | collective-permute-done | bytes 327712 | tf_op jit(solution)/shard_map/ppermute | solution.py:203
  108.2 3.2 %shard_map.76 = (bf16[80,2048]{1,0:T(8,128)(2,1)S(1)}, bf16[80,2048]{1,0:T(8,128)(2,1)S(1)}, bf16[80,2048]{1,0:T(8,128)(2,1)S(1)}, bf16[80,2048]{1,0:T(8,128)(2,1)S(1)}) custom-call(bf16[80,2048]{1,0:T(8,128)(2,1)S(1)} %get-tuple-element.186.refs_0_, bf16[80,2048]{1,0:T(8,128)(2,1)S(1)} %collective-permute-done.18.refs_1_, ...), custom_call_target="tpu_custom_call" | custom-call | flops 49999998976 | bytes 1000 | tf_op jit(solution)/shard_map/pallas_call | solution.py:233
  112.4 2.0 %collective-permute-start.32 = (bf16[80,2048]{1,0:T(8,128)(2,1)S(1)}, bf16[80,2048]{1,0:T(8,128)(2,1)S(1)}, u32[]{:S(2)}, u32[]{:S(2)}) collective-permute-start(bf16[80,2048]{1,0:T(8,128)(2,1)S(1)} %get-tuple-element.199), channel_id=1, source_target_pairs={{0,4},{1,5},{2,6},{3,7},{4,0},{5,1},{6,2},{7,3},{8,12},{9,13},{10,... | collective-permute-start | bytes 983048 | tf_op jit(solution)/shard_map/ppermute | solution.py:203
  114.9 7.2 %collective-permute-done.34.refs_9_ = bf16[80,2048]{1,0:T(8,128)(2,1)S(1)} collective-permute-done((bf16[80,2048]{1,0:T(8,128)(2,1)S(1)}, bf16[80,2048]{1,0:T(8,128)(2,1)S(1)}, u32[]{:S(2)}, u32[]{:S(2)}) %collective-permute-start.34) | collective-permute-done | bytes 327712 | tf_op jit(solution)/shard_map/ppermute | solution.py:203
  123.0 3.7 %collective-permute-done.32.refs_8_ = bf16[80,2048]{1,0:T(8,128)(2,1)S(1)} collective-permute-done((bf16[80,2048]{1,0:T(8,128)(2,1)S(1)}, bf16[80,2048]{1,0:T(8,128)(2,1)S(1)}, u32[]{:S(2)}, u32[]{:S(2)}) %collective-permute-start.32) | collective-permute-done | bytes 327712 | tf_op jit(solution)/shard_map/ppermute | solution.py:203
  134.4 1.6 %collective-permute-start.41 = (bf16[128,2048]{1,0:T(8,128)(2,1)S(1)}, bf16[128,2048]{1,0:T(8,128)(2,1)S(1)}, u32[]{:S(2)}, u32[]{:S(2)}) collective-permute-start(bf16[128,2048]{1,0:T(8,128)(2,1)S(1)} %shard_map.78), channel_id=1, source_target_pairs={{0,8},{8,16},{16,24},{24,0},{1,9},{9,17},{17,25},{25,1},{2,10},{10... | collective-permute-start | bytes 1572872 | tf_op jit(solution)/shard_map/ppermute | solution.py:200
  136.2 5.3 %collective-permute-done.33.refs_8_ = bf16[80,2048]{1,0:T(8,128)(2,1)S(1)} collective-permute-done((bf16[80,2048]{1,0:T(8,128)(2,1)S(1)}, bf16[80,2048]{1,0:T(8,128)(2,1)S(1)}, u32[]{:S(2)}, u32[]{:S(2)}) %collective-permute-start.33) | collective-permute-done | bytes 327712 | tf_op jit(solution)/shard_map/ppermute | solution.py:203
  144.8 5.5 %collective-permute-done.41.refs_5_ = bf16[128,2048]{1,0:T(8,128)(2,1)S(1)} collective-permute-done((bf16[128,2048]{1,0:T(8,128)(2,1)S(1)}, bf16[128,2048]{1,0:T(8,128)(2,1)S(1)}, u32[]{:S(2)}, u32[]{:S(2)}) %collective-permute-start.41) | collective-permute-done | bytes 524320 | tf_op jit(solution)/shard_map/ppermute | solution.py:200
  (97 shorter events, 40.8 us)
Async XLA Ops:
  3.2 17.9 %collective-permute-start.1 = (bf16[136,2048]{1,0:T(8,128)(2,1)S(1)}, bf16[136,2048]{1,0:T(8,128)(2,1)S(1)}, u32[]{:S(2)}, u32[]{:S(2)}) collective-permute-start(bf16[136,2048]{1,0:T(8,128)(2,1)S(1)} %shard_map.64.refs_0_), channel_id=1, source_target_pairs={{0,8},{8,16},{16,24},{24,0},{1,9},{9,17},{17,25},{25,1},{2,10},{10... | collective-permute-start | bytes 1671176 | tf_op jit(solution)/shard_map/ppermute | solution.py:200
  7.2 13.8 %collective-permute-start.2 = (bf16[80,2048]{1,0:T(8,128)(2,1)S(1)}, bf16[80,2048]{1,0:T(8,128)(2,1)S(1)}, u32[]{:S(2)}, u32[]{:S(2)}) collective-permute-start(bf16[80,2048]{1,0:T(8,128)(2,1)S(1)} %get-tuple-element.112), channel_id=1, source_target_pairs={{0,2},{1,3},{2,0},{3,1},{4,6},{5,7},{6,4},{7,5},{8,10},{9,11},{10,... | collective-permute-start | bytes 983048 | tf_op jit(solution)/shard_map/ppermute | solution.py:203
  9.0 16.5 %collective-permute-start.4 = (bf16[80,2048]{1,0:T(8,128)(2,1)S(1)}, bf16[80,2048]{1,0:T(8,128)(2,1)S(1)}, u32[]{:S(2)}, u32[]{:S(2)}) collective-permute-start(bf16[80,2048]{1,0:T(8,128)(2,1)S(1)} %get-tuple-element.115), channel_id=1, source_target_pairs={{0,4},{1,5},{2,6},{3,7},{4,0},{5,1},{6,2},{7,3},{8,12},{9,13},{10,... | collective-permute-start | bytes 983048 | tf_op jit(solution)/shard_map/ppermute | solution.py:203
  10.5 15.0 %collective-permute-start.5 = (bf16[80,2048]{1,0:T(8,128)(2,1)S(1)}, bf16[80,2048]{1,0:T(8,128)(2,1)S(1)}, u32[]{:S(2)}, u32[]{:S(2)}) collective-permute-start(bf16[80,2048]{1,0:T(8,128)(2,1)S(1)} %get-tuple-element.116), channel_id=1, source_target_pairs={{0,6},{1,7},{2,4},{3,5},{4,2},{5,3},{6,0},{7,1},{8,14},{9,15},{10,... | collective-permute-start | bytes 983048 | tf_op jit(solution)/shard_map/ppermute | solution.py:203
  21.1 16.8 %collective-permute-start.9 = (bf16[136,2048]{1,0:T(8,128)(2,1)S(1)}, bf16[136,2048]{1,0:T(8,128)(2,1)S(1)}, u32[]{:S(2)}, u32[]{:S(2)}) collective-permute-start(bf16[136,2048]{1,0:T(8,128)(2,1)S(1)} %collective-permute-done.1.refs_0_), channel_id=1, source_target_pairs={{0,8},{8,16},{16,24},{24,0},{1,9},{9,17},{17,25},{25,1},{2,10},{10... | collective-permute-start | bytes 1671176 | tf_op jit(solution)/shard_map/ppermute | solution.py:200
  26.1 11.8 %collective-permute-start.6 = (bf16[88,2048]{1,0:T(8,128)(2,1)S(1)}, bf16[88,2048]{1,0:T(8,128)(2,1)S(1)}, u32[]{:S(2)}, u32[]{:S(2)}) collective-permute-start(bf16[88,2048]{1,0:T(8,128)(2,1)S(1)} %get-tuple-element.119), channel_id=1, source_target_pairs={{0,2},{1,3},{2,0},{3,1},{4,6},{5,7},{6,4},{7,5},{8,10},{9,11},{10,... | collective-permute-start | bytes 1081352 | tf_op jit(solution)/shard_map/ppermute | solution.py:203
  27.4 17.1 %collective-permute-start.8 = (bf16[88,2048]{1,0:T(8,128)(2,1)S(1)}, bf16[88,2048]{1,0:T(8,128)(2,1)S(1)}, u32[]{:S(2)}, u32[]{:S(2)}) collective-permute-start(bf16[88,2048]{1,0:T(8,128)(2,1)S(1)} %get-tuple-element.123), channel_id=1, source_target_pairs={{0,4},{1,5},{2,6},{3,7},{4,0},{5,1},{6,2},{7,3},{8,12},{9,13},{10,... | collective-permute-start | bytes 1081352 | tf_op jit(solution)/shard_map/ppermute | solution.py:203
  28.3 16.2 %collective-permute-start.7 = (bf16[88,2048]{1,0:T(8,128)(2,1)S(1)}, bf16[88,2048]{1,0:T(8,128)(2,1)S(1)}, u32[]{:S(2)}, u32[]{:S(2)}) collective-permute-start(bf16[88,2048]{1,0:T(8,128)(2,1)S(1)} %get-tuple-element.121), channel_id=1, source_target_pairs={{0,6},{1,7},{2,4},{3,5},{4,2},{5,3},{6,0},{7,1},{8,14},{9,15},{10,... | collective-permute-start | bytes 1081352 | tf_op jit(solution)/shard_map/ppermute | solution.py:203
  37.9 6.6 %collective-permute-start.11 = (bf16[136,2048]{1,0:T(8,128)(2,1)S(1)}, bf16[136,2048]{1,0:T(8,128)(2,1)S(1)}, u32[]{:S(2)}, u32[]{:S(2)}) collective-permute-start(bf16[136,2048]{1,0:T(8,128)(2,1)S(1)} %collective-permute-done.9.refs_0_), channel_id=1, source_target_pairs={{0,1},{1,0},{2,3},{3,2},{4,5},{5,4},{6,7},{7,6},{8,9},{9,8},{10,11... | collective-permute-start | bytes 1671176 | tf_op jit(solution)/shard_map/ppermute | solution.py:203
  45.1 10.7 %collective-permute-start.12 = (bf16[80,2048]{1,0:T(8,128)(2,1)S(1)}, bf16[80,2048]{1,0:T(8,128)(2,1)S(1)}, u32[]{:S(2)}, u32[]{:S(2)}) collective-permute-start(bf16[80,2048]{1,0:T(8,128)(2,1)S(1)} %get-tuple-element.132), channel_id=1, source_target_pairs={{0,2},{1,3},{2,0},{3,1},{4,6},{5,7},{6,4},{7,5},{8,10},{9,11},{10,... | collective-permute-start | bytes 983048 | tf_op jit(solution)/shard_map/ppermute | solution.py:203
  45.8 14.2 %collective-permute-start.15 = (bf16[80,2048]{1,0:T(8,128)(2,1)S(1)}, bf16[80,2048]{1,0:T(8,128)(2,1)S(1)}, u32[]{:S(2)}, u32[]{:S(2)}) collective-permute-start(bf16[80,2048]{1,0:T(8,128)(2,1)S(1)} %get-tuple-element.140), channel_id=1, source_target_pairs={{0,4},{1,5},{2,6},{3,7},{4,0},{5,1},{6,2},{7,3},{8,12},{9,13},{10,... | collective-permute-start | bytes 983048 | tf_op jit(solution)/shard_map/ppermute | solution.py:203
  47.2 15.7 %collective-permute-start.14 = (bf16[80,2048]{1,0:T(8,128)(2,1)S(1)}, bf16[80,2048]{1,0:T(8,128)(2,1)S(1)}, u32[]{:S(2)}, u32[]{:S(2)}) collective-permute-start(bf16[80,2048]{1,0:T(8,128)(2,1)S(1)} %get-tuple-element.138), channel_id=1, source_target_pairs={{0,6},{1,7},{2,4},{3,5},{4,2},{5,3},{6,0},{7,1},{8,14},{9,15},{10,... | collective-permute-start | bytes 983048 | tf_op jit(solution)/shard_map/ppermute | solution.py:203
  48.7 15.7 %collective-permute-start.10 = (bf16[136,2048]{1,0:T(8,128)(2,1)S(1)}, bf16[136,2048]{1,0:T(8,128)(2,1)S(1)}, u32[]{:S(2)}, u32[]{:S(2)}) collective-permute-start(bf16[136,2048]{1,0:T(8,128)(2,1)S(1)} %collective-permute-done.9.refs_0_), channel_id=1, source_target_pairs={{0,8},{8,16},{16,24},{24,0},{1,9},{9,17},{17,25},{25,1},{2,10},{10... | collective-permute-start | bytes 1671176 | tf_op jit(solution)/shard_map/ppermute | solution.py:200
  55.8 14.0 %collective-permute-start.22 = (bf16[80,2048]{1,0:T(8,128)(2,1)S(1)}, bf16[80,2048]{1,0:T(8,128)(2,1)S(1)}, u32[]{:S(2)}, u32[]{:S(2)}) collective-permute-start(bf16[80,2048]{1,0:T(8,128)(2,1)S(1)} %get-tuple-element.169), channel_id=1, source_target_pairs={{0,2},{1,3},{2,0},{3,1},{4,6},{5,7},{6,4},{7,5},{8,10},{9,11},{10,... | collective-permute-start | bytes 983048 | tf_op jit(solution)/shard_map/ppermute | solution.py:203
  59.9 14.4 %collective-permute-start.19 = (bf16[80,2048]{1,0:T(8,128)(2,1)S(1)}, bf16[80,2048]{1,0:T(8,128)(2,1)S(1)}, u32[]{:S(2)}, u32[]{:S(2)}) collective-permute-start(bf16[80,2048]{1,0:T(8,128)(2,1)S(1)} %get-tuple-element.163), channel_id=1, source_target_pairs={{0,4},{1,5},{2,6},{3,7},{4,0},{5,1},{6,2},{7,3},{8,12},{9,13},{10,... | collective-permute-start | bytes 983048 | tf_op jit(solution)/shard_map/ppermute | solution.py:203
  62.8 11.6 %collective-permute-start.16 = (bf16[80,2048]{1,0:T(8,128)(2,1)S(1)}, bf16[80,2048]{1,0:T(8,128)(2,1)S(1)}, u32[]{:S(2)}, u32[]{:S(2)}) collective-permute-start(bf16[80,2048]{1,0:T(8,128)(2,1)S(1)} %get-tuple-element.157), channel_id=1, source_target_pairs={{0,6},{1,7},{2,4},{3,5},{4,2},{5,3},{6,0},{7,1},{8,14},{9,15},{10,... | collective-permute-start | bytes 983048 | tf_op jit(solution)/shard_map/ppermute | solution.py:203
  64.3 19.5 %collective-permute-start.13 = (bf16[136,2048]{1,0:T(8,128)(2,1)S(1)}, bf16[136,2048]{1,0:T(8,128)(2,1)S(1)}, u32[]{:S(2)}, u32[]{:S(2)}) collective-permute-start(bf16[136,2048]{1,0:T(8,128)(2,1)S(1)} %collective-permute-done.10.refs_0_), channel_id=1, source_target_pairs={{0,1},{1,0},{2,3},{3,2},{4,5},{5,4},{6,7},{7,6},{8,9},{9,8},{10,11... | collective-permute-start | bytes 1671176 | tf_op jit(solution)/shard_map/ppermute | solution.py:203
  76.3 10.6 %collective-permute-start.23 = (bf16[80,2048]{1,0:T(8,128)(2,1)S(1)}, bf16[80,2048]{1,0:T(8,128)(2,1)S(1)}, u32[]{:S(2)}, u32[]{:S(2)}) collective-permute-start(bf16[80,2048]{1,0:T(8,128)(2,1)S(1)} %get-tuple-element.170), channel_id=1, source_target_pairs={{0,2},{1,3},{2,0},{3,1},{4,6},{5,7},{6,4},{7,5},{8,10},{9,11},{10,... | collective-permute-start | bytes 983048 | tf_op jit(solution)/shard_map/ppermute | solution.py:203
  77.4 10.6 %collective-permute-start.20 = (bf16[80,2048]{1,0:T(8,128)(2,1)S(1)}, bf16[80,2048]{1,0:T(8,128)(2,1)S(1)}, u32[]{:S(2)}, u32[]{:S(2)}) collective-permute-start(bf16[80,2048]{1,0:T(8,128)(2,1)S(1)} %get-tuple-element.164), channel_id=1, source_target_pairs={{0,4},{1,5},{2,6},{3,7},{4,0},{5,1},{6,2},{7,3},{8,12},{9,13},{10,... | collective-permute-start | bytes 983048 | tf_op jit(solution)/shard_map/ppermute | solution.py:203
  78.2 16.8 %collective-permute-start.17 = (bf16[80,2048]{1,0:T(8,128)(2,1)S(1)}, bf16[80,2048]{1,0:T(8,128)(2,1)S(1)}, u32[]{:S(2)}, u32[]{:S(2)}) collective-permute-start(bf16[80,2048]{1,0:T(8,128)(2,1)S(1)} %get-tuple-element.158), channel_id=1, source_target_pairs={{0,6},{1,7},{2,4},{3,5},{4,2},{5,3},{6,0},{7,1},{8,14},{9,15},{10,... | collective-permute-start | bytes 983048 | tf_op jit(solution)/shard_map/ppermute | solution.py:203
  79.9 16.6 %collective-permute-start.27 = (bf16[128,2048]{1,0:T(8,128)(2,1)S(1)}, bf16[128,2048]{1,0:T(8,128)(2,1)S(1)}, u32[]{:S(2)}, u32[]{:S(2)}) collective-permute-start(bf16[128,2048]{1,0:T(8,128)(2,1)S(1)} %shard_map.73), channel_id=1, source_target_pairs={{0,24},{8,0},{16,8},{24,16},{1,25},{9,1},{17,9},{25,17},{2,26},{10... | collective-permute-start | bytes 1572872 | tf_op jit(solution)/shard_map/ppermute | solution.py:200
  86.9 16.5 %collective-permute-start.24 = (bf16[80,2048]{1,0:T(8,128)(2,1)S(1)}, bf16[80,2048]{1,0:T(8,128)(2,1)S(1)}, u32[]{:S(2)}, u32[]{:S(2)}) collective-permute-start(bf16[80,2048]{1,0:T(8,128)(2,1)S(1)} %get-tuple-element.171), channel_id=1, source_target_pairs={{0,2},{1,3},{2,0},{3,1},{4,6},{5,7},{6,4},{7,5},{8,10},{9,11},{10,... | collective-permute-start | bytes 983048 | tf_op jit(solution)/shard_map/ppermute | solution.py:203
  88.0 15.4 %collective-permute-start.21 = (bf16[80,2048]{1,0:T(8,128)(2,1)S(1)}, bf16[80,2048]{1,0:T(8,128)(2,1)S(1)}, u32[]{:S(2)}, u32[]{:S(2)}) collective-permute-start(bf16[80,2048]{1,0:T(8,128)(2,1)S(1)} %get-tuple-element.165), channel_id=1, source_target_pairs={{0,4},{1,5},{2,6},{3,7},{4,0},{5,1},{6,2},{7,3},{8,12},{9,13},{10,... | collective-permute-start | bytes 983048 | tf_op jit(solution)/shard_map/ppermute | solution.py:203
  95.0 13.2 %collective-permute-start.18 = (bf16[80,2048]{1,0:T(8,128)(2,1)S(1)}, bf16[80,2048]{1,0:T(8,128)(2,1)S(1)}, u32[]{:S(2)}, u32[]{:S(2)}) collective-permute-start(bf16[80,2048]{1,0:T(8,128)(2,1)S(1)} %get-tuple-element.159), channel_id=1, source_target_pairs={{0,6},{1,7},{2,4},{3,5},{4,2},{5,3},{6,0},{7,1},{8,14},{9,15},{10,... | collective-permute-start | bytes 983048 | tf_op jit(solution)/shard_map/ppermute | solution.py:203
  100.7 30.2 %collective-permute-start.36 = (bf16[128,2048]{1,0:T(8,128)(2,1)S(1)}, bf16[128,2048]{1,0:T(8,128)(2,1)S(1)}, u32[]{:S(2)}, u32[]{:S(2)}) collective-permute-start(bf16[128,2048]{1,0:T(8,128)(2,1)S(1)} %shard_map.75), channel_id=1, source_target_pairs={{0,16},{8,24},{16,0},{24,8},{1,17},{9,25},{17,1},{25,9},{2,18},{10... | collective-permute-start | bytes 1572872 | tf_op jit(solution)/shard_map/ppermute | solution.py:200
  111.4 10.7 %collective-permute-start.34 = (bf16[80,2048]{1,0:T(8,128)(2,1)S(1)}, bf16[80,2048]{1,0:T(8,128)(2,1)S(1)}, u32[]{:S(2)}, u32[]{:S(2)}) collective-permute-start(bf16[80,2048]{1,0:T(8,128)(2,1)S(1)} %get-tuple-element.203), channel_id=1, source_target_pairs={{0,2},{1,3},{2,0},{3,1},{4,6},{5,7},{6,4},{7,5},{8,10},{9,11},{10,... | collective-permute-start | bytes 983048 | tf_op jit(solution)/shard_map/ppermute | solution.py:203
  112.4 14.4 %collective-permute-start.32 = (bf16[80,2048]{1,0:T(8,128)(2,1)S(1)}, bf16[80,2048]{1,0:T(8,128)(2,1)S(1)}, u32[]{:S(2)}, u32[]{:S(2)}) collective-permute-start(bf16[80,2048]{1,0:T(8,128)(2,1)S(1)} %get-tuple-element.199), channel_id=1, source_target_pairs={{0,4},{1,5},{2,6},{3,7},{4,0},{5,1},{6,2},{7,3},{8,12},{9,13},{10,... | collective-permute-start | bytes 983048 | tf_op jit(solution)/shard_map/ppermute | solution.py:203
  114.4 15.1 %collective-permute-start.30 = (bf16[80,2048]{1,0:T(8,128)(2,1)S(1)}, bf16[80,2048]{1,0:T(8,128)(2,1)S(1)}, u32[]{:S(2)}, u32[]{:S(2)}) collective-permute-start(bf16[80,2048]{1,0:T(8,128)(2,1)S(1)} %get-tuple-element.195), channel_id=1, source_target_pairs={{0,6},{1,7},{2,4},{3,5},{4,2},{5,3},{6,0},{7,1},{8,14},{9,15},{10,... | collective-permute-start | bytes 983048 | tf_op jit(solution)/shard_map/ppermute | solution.py:203
  122.1 14.1 %collective-permute-start.35 = (bf16[80,2048]{1,0:T(8,128)(2,1)S(1)}, bf16[80,2048]{1,0:T(8,128)(2,1)S(1)}, u32[]{:S(2)}, u32[]{:S(2)}) collective-permute-start(bf16[80,2048]{1,0:T(8,128)(2,1)S(1)} %get-tuple-element.204), channel_id=1, source_target_pairs={{0,2},{1,3},{2,0},{3,1},{4,6},{5,7},{6,4},{7,5},{8,10},{9,11},{10,... | collective-permute-start | bytes 983048 | tf_op jit(solution)/shard_map/ppermute | solution.py:203
  126.8 14.7 %collective-permute-start.33 = (bf16[80,2048]{1,0:T(8,128)(2,1)S(1)}, bf16[80,2048]{1,0:T(8,128)(2,1)S(1)}, u32[]{:S(2)}, u32[]{:S(2)}) collective-permute-start(bf16[80,2048]{1,0:T(8,128)(2,1)S(1)} %get-tuple-element.200), channel_id=1, source_target_pairs={{0,4},{1,5},{2,6},{3,7},{4,0},{5,1},{6,2},{7,3},{8,12},{9,13},{10,... | collective-permute-start | bytes 983048 | tf_op jit(solution)/shard_map/ppermute | solution.py:203
  129.5 11.9 %collective-permute-start.31 = (bf16[80,2048]{1,0:T(8,128)(2,1)S(1)}, bf16[80,2048]{1,0:T(8,128)(2,1)S(1)}, u32[]{:S(2)}, u32[]{:S(2)}) collective-permute-start(bf16[80,2048]{1,0:T(8,128)(2,1)S(1)} %get-tuple-element.196), channel_id=1, source_target_pairs={{0,6},{1,7},{2,4},{3,5},{4,2},{5,3},{6,0},{7,1},{8,14},{9,15},{10,... | collective-permute-start | bytes 983048 | tf_op jit(solution)/shard_map/ppermute | solution.py:203
  134.4 15.8 %collective-permute-start.41 = (bf16[128,2048]{1,0:T(8,128)(2,1)S(1)}, bf16[128,2048]{1,0:T(8,128)(2,1)S(1)}, u32[]{:S(2)}, u32[]{:S(2)}) collective-permute-start(bf16[128,2048]{1,0:T(8,128)(2,1)S(1)} %shard_map.78), channel_id=1, source_target_pairs={{0,8},{8,16},{16,24},{24,0},{1,9},{9,17},{17,25},{25,1},{2,10},{10... | collective-permute-start | bytes 1572872 | tf_op jit(solution)/shard_map/ppermute | solution.py:200
  (24 other events, 147.1 us)

commit v12 on v11

--- a/solution.py
+++ b/solution.py
@@ -12,7 +12,7 @@
 VMEM_LIMIT = 32 * 1024 * 1024
 PARTS = 4
 CORES = 2
-PHASE_FLOPS = 50_000_000_000
+PHASE_FLOPS = 20_000_000_000
 VMEM = pl.BlockSpec(memory_space=pltpu.VMEM)
 
 

time: 152 us -> 151 us (level)
  waiting for transfers between devices: 71.2 us -> 78.4 us
  starting transfers between devices: 49.8 us -> 43.8 us
  local copies, waits for them, and re-layouts: 7.99 us -> 6.38 us
    ppermute x36, waiting for transfers between devices: 54.1 us -> 59.6 us  [across(): lax.ppermute(array, 'zero', [(i, i ^ o) for i in range(near)])]
    ppermute x36, starting transfers between devices: 37.4 us -> 32.1 us  [across(): lax.ppermute(array, 'zero', [(i, i ^ o) for i in range(near)])]
    ppermute x6, waiting for transfers between devices: 17 us -> 18.8 us  [along(): lax.ppermute(array, 'expert', [(i, (i + d) % layers) for i in range(layer...]
    unnamed x28 -> x16, local copies, waits for them, and re-layouts: 7.99 us -> 6.38 us
  transfers between devices with their start and end apart: 42 -> 42, of which waited for: 24 -> 25; matrix products, arithmetic and copies ran while one was open for 0% -> 0% of each run, Pallas kernels for 13% -> 14%
where the time goes in v12:
time: 151 us
  waiting for transfers between devices  78.4 us (52%)
  starting transfers between devices  43.8 us (29%)
  Pallas kernels  22.2 us (15%)
  local copies, waits for them, and re-layouts  6.38 us (4%)
    ppermute x36, waiting for transfers between devices, across(): lax.ppermute(array, 'zero', [(i, i ^ o) for i in range(near)])  59.6 us
    ppermute x36, starting transfers between devices, across(): lax.ppermute(array, 'zero', [(i, i ^ o) for i in range(near)])  32.1 us
    ppermute x6, waiting for transfers between devices, along(): lax.ppermute(array, 'expert', [(i, (i + d) % layers) for i in range(layer...  18.8 us
    pallas_call x4, Pallas kernels, expert(): call(functools.partial(expert_kernel, z, rows), [shape(rows)] * z.chips,...  12.9 us
    ppermute x6, starting transfers between devices, along(): lax.ppermute(array, 'expert', [(i, (i + d) % layers) for i in range(layer...  11.7 us
    unnamed x16, local copies, waits for them, and re-layouts  6.38 us
    pallas_call x4, Pallas kernels, mix(): call(functools.partial(mix_kernel, z, n, list(backs), ride_order), [shape...  5.35 us
  transfers between devices with their start and end apart: 42, of which 25 were waited for; matrix products, arithmetic and copies ran while one was open for 0% of the time, Pallas kernels for 14%

profile of v12, /device:TPU:0, one launch (start us, length us, event | category | flops | bytes accessed | tf_op | source)
XLA Modules:
  0.0 150.9 jit_solution(11869430574621027705)
XLA Ops:
  3.2 2.6 %collective-permute-start.1 = (bf16[136,2048]{1,0:T(8,128)(2,1)S(1)}, bf16[136,2048]{1,0:T(8,128)(2,1)S(1)}, u32[]{:S(2)}, u32[]{:S(2)}) collective-permute-start(bf16[136,2048]{1,0:T(8,128)(2,1)S(1)} %shard_map.64.refs_0_), channel_id=1, source_target_pairs={{0,8},{8,16},{16,24},{24,0},{1,9},{9,17},{17,25},{25,1},{2,10},{10... | collective-permute-start | bytes 1671176 | tf_op jit(solution)/shard_map/ppermute | solution.py:200
  6.4 1.9 %collective-permute-start.2 = (bf16[80,2048]{1,0:T(8,128)(2,1)S(1)}, bf16[80,2048]{1,0:T(8,128)(2,1)S(1)}, u32[]{:S(2)}, u32[]{:S(2)}) collective-permute-start(bf16[80,2048]{1,0:T(8,128)(2,1)S(1)} %get-tuple-element.112), channel_id=1, source_target_pairs={{0,2},{1,3},{2,0},{3,1},{4,6},{5,7},{6,4},{7,5},{8,10},{9,11},{10,... | collective-permute-start | bytes 983048 | tf_op jit(solution)/shard_map/ppermute | solution.py:203
  10.0 11.1 %collective-permute-done.1.refs_0_ = bf16[136,2048]{1,0:T(8,128)(2,1)S(1)} collective-permute-done((bf16[136,2048]{1,0:T(8,128)(2,1)S(1)}, bf16[136,2048]{1,0:T(8,128)(2,1)S(1)}, u32[]{:S(2)}, u32[]{:S(2)}) %collective-permute-start.1) | collective-permute-done | bytes 557088 | tf_op jit(solution)/shard_map/ppermute | solution.py:200
  21.1 3.7 %collective-permute-done.4.refs_2_ = bf16[80,2048]{1,0:T(8,128)(2,1)S(1)} collective-permute-done((bf16[80,2048]{1,0:T(8,128)(2,1)S(1)}, bf16[80,2048]{1,0:T(8,128)(2,1)S(1)}, u32[]{:S(2)}, u32[]{:S(2)}) %collective-permute-start.4) | collective-permute-done | bytes 327712 | tf_op jit(solution)/shard_map/ppermute | solution.py:203
  28.9 1.9 %copy-done.1 = bf16[1,2048,768]{2,1,0:T(8,128)(2,1)S(1)} copy-done((bf16[1,2048,768]{2,1,0:T(8,128)(2,1)S(1)}, bf16[1,2048,768]{2,1,0:T(8,128)(2,1)}, u32[]{:S(2)}) %copy-start.1) | copy-done | bytes 3145752
  30.8 1.9 %copy-done.3 = bf16[1,768,2048]{2,1,0:T(8,128)(2,1)S(1)} copy-done((bf16[1,768,2048]{2,1,0:T(8,128)(2,1)S(1)}, bf16[1,768,2048]{2,1,0:T(8,128)(2,1)}, u32[]{:S(2)}) %copy-start.3) | copy-done | bytes 3145752
  32.7 3.2 %shard_map.67 = (bf16[80,2048]{1,0:T(8,128)(2,1)S(1)}, bf16[80,2048]{1,0:T(8,128)(2,1)S(1)}, bf16[80,2048]{1,0:T(8,128)(2,1)S(1)}, bf16[80,2048]{1,0:T(8,128)(2,1)S(1)}) custom-call(bf16[80,2048]{1,0:T(8,128)(2,1)S(1)} %get-tuple-element.125.refs_0_, bf16[80,2048]{1,0:T(8,128)(2,1)S(1)} %collective-permute-done.2.refs_1_, ...), custom_call_target="tpu_custom_call" | custom-call | flops 1000 | bytes 1000 | tf_op jit(solution)/shard_map/pallas_call | solution.py:233
  36.0 1.9 %collective-permute-done.9.refs_0_ = bf16[136,2048]{1,0:T(8,128)(2,1)S(1)} collective-permute-done((bf16[136,2048]{1,0:T(8,128)(2,1)S(1)}, bf16[136,2048]{1,0:T(8,128)(2,1)S(1)}, u32[]{:S(2)}, u32[]{:S(2)}) %collective-permute-start.9) | collective-permute-done | bytes 557088 | tf_op jit(solution)/shard_map/ppermute | solution.py:200
  37.9 5.8 %collective-permute-done.8.refs_3_.refs_5_ = bf16[88,2048]{1,0:T(8,128)(2,1)S(1)} collective-permute-done((bf16[88,2048]{1,0:T(8,128)(2,1)S(1)}, bf16[88,2048]{1,0:T(8,128)(2,1)S(1)}, u32[]{:S(2)}, u32[]{:S(2)}) %collective-permute-start.8) | collective-permute-done | bytes 360480 | tf_op jit(solution)/shard_map/ppermute | solution.py:203
  47.9 1.6 %collective-permute-start.10 = (bf16[136,2048]{1,0:T(8,128)(2,1)S(1)}, bf16[136,2048]{1,0:T(8,128)(2,1)S(1)}, u32[]{:S(2)}, u32[]{:S(2)}) collective-permute-start(bf16[136,2048]{1,0:T(8,128)(2,1)S(1)} %collective-permute-done.9.refs_0_), channel_id=1, source_target_pairs={{0,8},{8,16},{16,24},{24,0},{1,9},{9,17},{17,25},{25,1},{2,10},{10... | collective-permute-start | bytes 1671176 | tf_op jit(solution)/shard_map/ppermute | solution.py:200
  49.5 3.2 %shard_map.71 = (bf16[80,2048]{1,0:T(8,128)(2,1)S(1)}, bf16[80,2048]{1,0:T(8,128)(2,1)S(1)}, bf16[80,2048]{1,0:T(8,128)(2,1)S(1)}, bf16[80,2048]{1,0:T(8,128)(2,1)S(1)}) custom-call(bf16[88,2048]{1,0:T(8,128)(2,1)S(1)} %get-tuple-element.146.refs_0_.refs_2_, bf16[88,2048]{1,0:T(8,128)(2,1)S(1)} %collective-permute-done.6.refs_1_.refs_3_, ...), custom_call_target="tpu_custom_call" | custom-call | flops 1000 | bytes 1000 | tf_op jit(solution)/shard_map/pallas_call | solution.py:233
  52.7 2.3 %collective-permute-done.12.refs_3_ = bf16[80,2048]{1,0:T(8,128)(2,1)S(1)} collective-permute-done((bf16[80,2048]{1,0:T(8,128)(2,1)S(1)}, bf16[80,2048]{1,0:T(8,128)(2,1)S(1)}, u32[]{:S(2)}, u32[]{:S(2)}) %collective-permute-start.12) | collective-permute-done | bytes 327712 | tf_op jit(solution)/shard_map/ppermute | solution.py:203
  55.7 4.5 %collective-permute-done.15.refs_2_ = bf16[80,2048]{1,0:T(8,128)(2,1)S(1)} collective-permute-done((bf16[80,2048]{1,0:T(8,128)(2,1)S(1)}, bf16[80,2048]{1,0:T(8,128)(2,1)S(1)}, u32[]{:S(2)}, u32[]{:S(2)}) %collective-permute-start.15) | collective-permute-done | bytes 327712 | tf_op jit(solution)/shard_map/ppermute | solution.py:203
  60.1 1.6 %collective-permute-start.19 = (bf16[80,2048]{1,0:T(8,128)(2,1)S(1)}, bf16[80,2048]{1,0:T(8,128)(2,1)S(1)}, u32[]{:S(2)}, u32[]{:S(2)}) collective-permute-start(bf16[80,2048]{1,0:T(8,128)(2,1)S(1)} %get-tuple-element.163), channel_id=1, source_target_pairs={{0,4},{1,5},{2,6},{3,7},{4,0},{5,1},{6,2},{7,3},{8,12},{9,13},{10,... | collective-permute-start | bytes 983048 | tf_op jit(solution)/shard_map/ppermute | solution.py:203
  63.6 3.2 %shard_map.70 = (bf16[80,2048]{1,0:T(8,128)(2,1)S(1)}, bf16[80,2048]{1,0:T(8,128)(2,1)S(1)}, bf16[80,2048]{1,0:T(8,128)(2,1)S(1)}, bf16[80,2048]{1,0:T(8,128)(2,1)S(1)}) custom-call(bf16[80,2048]{1,0:T(8,128)(2,1)S(1)} %get-tuple-element.141.refs_0_, bf16[80,2048]{1,0:T(8,128)(2,1)S(1)} %collective-permute-done.14.refs_1_, ...), custom_call_target="tpu_custom_call" | custom-call | flops 1000 | bytes 1000 | tf_op jit(solution)/shard_map/pallas_call | solution.py:233
  66.9 2.2 %collective-permute-done.22.refs_9_ = bf16[80,2048]{1,0:T(8,128)(2,1)S(1)} collective-permute-done((bf16[80,2048]{1,0:T(8,128)(2,1)S(1)}, bf16[80,2048]{1,0:T(8,128)(2,1)S(1)}, u32[]{:S(2)}, u32[]{:S(2)}) %collective-permute-start.22) | collective-permute-done | bytes 327712 | tf_op jit(solution)/shard_map/ppermute | solution.py:203
  69.1 4.7 %collective-permute-done.19.refs_8_ = bf16[80,2048]{1,0:T(8,128)(2,1)S(1)} collective-permute-done((bf16[80,2048]{1,0:T(8,128)(2,1)S(1)}, bf16[80,2048]{1,0:T(8,128)(2,1)S(1)}, u32[]{:S(2)}, u32[]{:S(2)}) %collective-permute-start.19) | collective-permute-done | bytes 327712 | tf_op jit(solution)/shard_map/ppermute | solution.py:203
  77.5 1.7 %collective-permute-start.17 = (bf16[80,2048]{1,0:T(8,128)(2,1)S(1)}, bf16[80,2048]{1,0:T(8,128)(2,1)S(1)}, u32[]{:S(2)}, u32[]{:S(2)}) collective-permute-start(bf16[80,2048]{1,0:T(8,128)(2,1)S(1)} %get-tuple-element.158), channel_id=1, source_target_pairs={{0,6},{1,7},{2,4},{3,5},{4,2},{5,3},{6,0},{7,1},{8,14},{9,15},{10,... | collective-permute-start | bytes 983048 | tf_op jit(solution)/shard_map/ppermute | solution.py:203
  79.4 3.7 %collective-permute-start.27 = (bf16[128,2048]{1,0:T(8,128)(2,1)S(1)}, bf16[128,2048]{1,0:T(8,128)(2,1)S(1)}, u32[]{:S(2)}, u32[]{:S(2)}) collective-permute-start(bf16[128,2048]{1,0:T(8,128)(2,1)S(1)} %shard_map.73), channel_id=1, source_target_pairs={{0,24},{8,0},{16,8},{24,16},{1,25},{9,1},{17,9},{25,17},{2,26},{10... | collective-permute-start | bytes 1572872 | tf_op jit(solution)/shard_map/ppermute | solution.py:200
  83.7 2.6 %collective-permute-done.23.refs_9_ = bf16[80,2048]{1,0:T(8,128)(2,1)S(1)} collective-permute-done((bf16[80,2048]{1,0:T(8,128)(2,1)S(1)}, bf16[80,2048]{1,0:T(8,128)(2,1)S(1)}, u32[]{:S(2)}, u32[]{:S(2)}) %collective-permute-start.23) | collective-permute-done | bytes 327712 | tf_op jit(solution)/shard_map/ppermute | solution.py:203
  88.1 6.1 %collective-permute-done.17.refs_7_ = bf16[80,2048]{1,0:T(8,128)(2,1)S(1)} collective-permute-done((bf16[80,2048]{1,0:T(8,128)(2,1)S(1)}, bf16[80,2048]{1,0:T(8,128)(2,1)S(1)}, u32[]{:S(2)}, u32[]{:S(2)}) %collective-permute-start.17) | collective-permute-done | bytes 327712 | tf_op jit(solution)/shard_map/ppermute | solution.py:203
  94.2 1.8 %collective-permute-start.18 = (bf16[80,2048]{1,0:T(8,128)(2,1)S(1)}, bf16[80,2048]{1,0:T(8,128)(2,1)S(1)}, u32[]{:S(2)}, u32[]{:S(2)}) collective-permute-start(bf16[80,2048]{1,0:T(8,128)(2,1)S(1)} %get-tuple-element.159), channel_id=1, source_target_pairs={{0,6},{1,7},{2,4},{3,5},{4,2},{5,3},{6,0},{7,1},{8,14},{9,15},{10,... | collective-permute-start | bytes 983048 | tf_op jit(solution)/shard_map/ppermute | solution.py:203
  99.4 2.5 %collective-permute-start.36 = (bf16[128,2048]{1,0:T(8,128)(2,1)S(1)}, bf16[128,2048]{1,0:T(8,128)(2,1)S(1)}, u32[]{:S(2)}, u32[]{:S(2)}) collective-permute-start(bf16[128,2048]{1,0:T(8,128)(2,1)S(1)} %shard_map.75), channel_id=1, source_target_pairs={{0,16},{8,24},{16,0},{24,8},{1,17},{9,25},{17,1},{25,9},{2,18},{10... | collective-permute-start | bytes 1572872 | tf_op jit(solution)/shard_map/ppermute | solution.py:200
  101.9 5.5 %collective-permute-done.18.refs_1_ = bf16[80,2048]{1,0:T(8,128)(2,1)S(1)} collective-permute-done((bf16[80,2048]{1,0:T(8,128)(2,1)S(1)}, bf16[80,2048]{1,0:T(8,128)(2,1)S(1)}, u32[]{:S(2)}, u32[]{:S(2)}) %collective-permute-start.18) | collective-permute-done | bytes 327712 | tf_op jit(solution)/shard_map/ppermute | solution.py:203
  107.4 3.2 %shard_map.76 = (bf16[80,2048]{1,0:T(8,128)(2,1)S(1)}, bf16[80,2048]{1,0:T(8,128)(2,1)S(1)}, bf16[80,2048]{1,0:T(8,128)(2,1)S(1)}, bf16[80,2048]{1,0:T(8,128)(2,1)S(1)}) custom-call(bf16[80,2048]{1,0:T(8,128)(2,1)S(1)} %get-tuple-element.186.refs_0_, bf16[80,2048]{1,0:T(8,128)(2,1)S(1)} %collective-permute-done.18.refs_1_, ...), custom_call_target="tpu_custom_call" | custom-call | flops 20000000000 | bytes 1000 | tf_op jit(solution)/shard_map/pallas_call | solution.py:233
  111.9 1.7 %collective-permute-start.32 = (bf16[80,2048]{1,0:T(8,128)(2,1)S(1)}, bf16[80,2048]{1,0:T(8,128)(2,1)S(1)}, u32[]{:S(2)}, u32[]{:S(2)}) collective-permute-start(bf16[80,2048]{1,0:T(8,128)(2,1)S(1)} %get-tuple-element.199), channel_id=1, source_target_pairs={{0,4},{1,5},{2,6},{3,7},{4,0},{5,1},{6,2},{7,3},{8,12},{9,13},{10,... | collective-permute-start | bytes 983048 | tf_op jit(solution)/shard_map/ppermute | solution.py:203
  114.2 7.2 %collective-permute-done.34.refs_9_ = bf16[80,2048]{1,0:T(8,128)(2,1)S(1)} collective-permute-done((bf16[80,2048]{1,0:T(8,128)(2,1)S(1)}, bf16[80,2048]{1,0:T(8,128)(2,1)S(1)}, u32[]{:S(2)}, u32[]{:S(2)}) %collective-permute-start.34) | collective-permute-done | bytes 327712 | tf_op jit(solution)/shard_map/ppermute | solution.py:203
  122.6 3.4 %collective-permute-done.32.refs_8_ = bf16[80,2048]{1,0:T(8,128)(2,1)S(1)} collective-permute-done((bf16[80,2048]{1,0:T(8,128)(2,1)S(1)}, bf16[80,2048]{1,0:T(8,128)(2,1)S(1)}, u32[]{:S(2)}, u32[]{:S(2)}) %collective-permute-start.32) | collective-permute-done | bytes 327712 | tf_op jit(solution)/shard_map/ppermute | solution.py:203
  125.9 1.6 %collective-permute-start.33 = (bf16[80,2048]{1,0:T(8,128)(2,1)S(1)}, bf16[80,2048]{1,0:T(8,128)(2,1)S(1)}, u32[]{:S(2)}, u32[]{:S(2)}) collective-permute-start(bf16[80,2048]{1,0:T(8,128)(2,1)S(1)} %get-tuple-element.200), channel_id=1, source_target_pairs={{0,4},{1,5},{2,6},{3,7},{4,0},{5,1},{6,2},{7,3},{8,12},{9,13},{10,... | collective-permute-start | bytes 983048 | tf_op jit(solution)/shard_map/ppermute | solution.py:203
  128.7 1.8 %collective-permute-start.31 = (bf16[80,2048]{1,0:T(8,128)(2,1)S(1)}, bf16[80,2048]{1,0:T(8,128)(2,1)S(1)}, u32[]{:S(2)}, u32[]{:S(2)}) collective-permute-start(bf16[80,2048]{1,0:T(8,128)(2,1)S(1)} %get-tuple-element.196), channel_id=1, source_target_pairs={{0,6},{1,7},{2,4},{3,5},{4,2},{5,3},{6,0},{7,1},{8,14},{9,15},{10,... | collective-permute-start | bytes 983048 | tf_op jit(solution)/shard_map/ppermute | solution.py:203
  135.8 4.9 %collective-permute-done.31.refs_7_ = bf16[80,2048]{1,0:T(8,128)(2,1)S(1)} collective-permute-done((bf16[80,2048]{1,0:T(8,128)(2,1)S(1)}, bf16[80,2048]{1,0:T(8,128)(2,1)S(1)}, u32[]{:S(2)}, u32[]{:S(2)}) %collective-permute-start.31) | collective-permute-done | bytes 327712 | tf_op jit(solution)/shard_map/ppermute | solution.py:203
  144.1 5.7 %collective-permute-done.41.refs_5_ = bf16[128,2048]{1,0:T(8,128)(2,1)S(1)} collective-permute-done((bf16[128,2048]{1,0:T(8,128)(2,1)S(1)}, bf16[128,2048]{1,0:T(8,128)(2,1)S(1)}, u32[]{:S(2)}, u32[]{:S(2)}) %collective-permute-start.41) | collective-permute-done | bytes 524320 | tf_op jit(solution)/shard_map/ppermute | solution.py:200
  (85 shorter events, 39.9 us)
Async XLA Ops:
  3.2 17.9 %collective-permute-start.1 = (bf16[136,2048]{1,0:T(8,128)(2,1)S(1)}, bf16[136,2048]{1,0:T(8,128)(2,1)S(1)}, u32[]{:S(2)}, u32[]{:S(2)}) collective-permute-start(bf16[136,2048]{1,0:T(8,128)(2,1)S(1)} %shard_map.64.refs_0_), channel_id=1, source_target_pairs={{0,8},{8,16},{16,24},{24,0},{1,9},{9,17},{17,25},{25,1},{2,10},{10... | collective-permute-start | bytes 1671176 | tf_op jit(solution)/shard_map/ppermute | solution.py:200
  6.4 14.7 %collective-permute-start.2 = (bf16[80,2048]{1,0:T(8,128)(2,1)S(1)}, bf16[80,2048]{1,0:T(8,128)(2,1)S(1)}, u32[]{:S(2)}, u32[]{:S(2)}) collective-permute-start(bf16[80,2048]{1,0:T(8,128)(2,1)S(1)} %get-tuple-element.112), channel_id=1, source_target_pairs={{0,2},{1,3},{2,0},{3,1},{4,6},{5,7},{6,4},{7,5},{8,10},{9,11},{10,... | collective-permute-start | bytes 983048 | tf_op jit(solution)/shard_map/ppermute | solution.py:203
  8.3 16.5 %collective-permute-start.4 = (bf16[80,2048]{1,0:T(8,128)(2,1)S(1)}, bf16[80,2048]{1,0:T(8,128)(2,1)S(1)}, u32[]{:S(2)}, u32[]{:S(2)}) collective-permute-start(bf16[80,2048]{1,0:T(8,128)(2,1)S(1)} %get-tuple-element.115), channel_id=1, source_target_pairs={{0,4},{1,5},{2,6},{3,7},{4,0},{5,1},{6,2},{7,3},{8,12},{9,13},{10,... | collective-permute-start | bytes 983048 | tf_op jit(solution)/shard_map/ppermute | solution.py:203
  9.8 15.0 %collective-permute-start.5 = (bf16[80,2048]{1,0:T(8,128)(2,1)S(1)}, bf16[80,2048]{1,0:T(8,128)(2,1)S(1)}, u32[]{:S(2)}, u32[]{:S(2)}) collective-permute-start(bf16[80,2048]{1,0:T(8,128)(2,1)S(1)} %get-tuple-element.116), channel_id=1, source_target_pairs={{0,6},{1,7},{2,4},{3,5},{4,2},{5,3},{6,0},{7,1},{8,14},{9,15},{10,... | collective-permute-start | bytes 983048 | tf_op jit(solution)/shard_map/ppermute | solution.py:203
  21.1 16.8 %collective-permute-start.9 = (bf16[136,2048]{1,0:T(8,128)(2,1)S(1)}, bf16[136,2048]{1,0:T(8,128)(2,1)S(1)}, u32[]{:S(2)}, u32[]{:S(2)}) collective-permute-start(bf16[136,2048]{1,0:T(8,128)(2,1)S(1)} %collective-permute-done.1.refs_0_), channel_id=1, source_target_pairs={{0,8},{8,16},{16,24},{24,0},{1,9},{9,17},{17,25},{25,1},{2,10},{10... | collective-permute-start | bytes 1671176 | tf_op jit(solution)/shard_map/ppermute | solution.py:200
  25.4 12.5 %collective-permute-start.6 = (bf16[88,2048]{1,0:T(8,128)(2,1)S(1)}, bf16[88,2048]{1,0:T(8,128)(2,1)S(1)}, u32[]{:S(2)}, u32[]{:S(2)}) collective-permute-start(bf16[88,2048]{1,0:T(8,128)(2,1)S(1)} %get-tuple-element.119), channel_id=1, source_target_pairs={{0,2},{1,3},{2,0},{3,1},{4,6},{5,7},{6,4},{7,5},{8,10},{9,11},{10,... | collective-permute-start | bytes 1081352 | tf_op jit(solution)/shard_map/ppermute | solution.py:203
  26.7 17.1 %collective-permute-start.8 = (bf16[88,2048]{1,0:T(8,128)(2,1)S(1)}, bf16[88,2048]{1,0:T(8,128)(2,1)S(1)}, u32[]{:S(2)}, u32[]{:S(2)}) collective-permute-start(bf16[88,2048]{1,0:T(8,128)(2,1)S(1)} %get-tuple-element.123), channel_id=1, source_target_pairs={{0,4},{1,5},{2,6},{3,7},{4,0},{5,1},{6,2},{7,3},{8,12},{9,13},{10,... | collective-permute-start | bytes 1081352 | tf_op jit(solution)/shard_map/ppermute | solution.py:203
  27.5 16.2 %collective-permute-start.7 = (bf16[88,2048]{1,0:T(8,128)(2,1)S(1)}, bf16[88,2048]{1,0:T(8,128)(2,1)S(1)}, u32[]{:S(2)}, u32[]{:S(2)}) collective-permute-start(bf16[88,2048]{1,0:T(8,128)(2,1)S(1)} %get-tuple-element.121), channel_id=1, source_target_pairs={{0,6},{1,7},{2,4},{3,5},{4,2},{5,3},{6,0},{7,1},{8,14},{9,15},{10,... | collective-permute-start | bytes 1081352 | tf_op jit(solution)/shard_map/ppermute | solution.py:203
  37.9 5.8 %collective-permute-start.11 = (bf16[136,2048]{1,0:T(8,128)(2,1)S(1)}, bf16[136,2048]{1,0:T(8,128)(2,1)S(1)}, u32[]{:S(2)}, u32[]{:S(2)}) collective-permute-start(bf16[136,2048]{1,0:T(8,128)(2,1)S(1)} %collective-permute-done.9.refs_0_), channel_id=1, source_target_pairs={{0,1},{1,0},{2,3},{3,2},{4,5},{5,4},{6,7},{7,6},{8,9},{9,8},{10,11... | collective-permute-start | bytes 1671176 | tf_op jit(solution)/shard_map/ppermute | solution.py:203
  44.4 10.7 %collective-permute-start.12 = (bf16[80,2048]{1,0:T(8,128)(2,1)S(1)}, bf16[80,2048]{1,0:T(8,128)(2,1)S(1)}, u32[]{:S(2)}, u32[]{:S(2)}) collective-permute-start(bf16[80,2048]{1,0:T(8,128)(2,1)S(1)} %get-tuple-element.132), channel_id=1, source_target_pairs={{0,2},{1,3},{2,0},{3,1},{4,6},{5,7},{6,4},{7,5},{8,10},{9,11},{10,... | collective-permute-start | bytes 983048 | tf_op jit(solution)/shard_map/ppermute | solution.py:203
  45.0 15.1 %collective-permute-start.15 = (bf16[80,2048]{1,0:T(8,128)(2,1)S(1)}, bf16[80,2048]{1,0:T(8,128)(2,1)S(1)}, u32[]{:S(2)}, u32[]{:S(2)}) collective-permute-start(bf16[80,2048]{1,0:T(8,128)(2,1)S(1)} %get-tuple-element.140), channel_id=1, source_target_pairs={{0,4},{1,5},{2,6},{3,7},{4,0},{5,1},{6,2},{7,3},{8,12},{9,13},{10,... | collective-permute-start | bytes 983048 | tf_op jit(solution)/shard_map/ppermute | solution.py:203
  46.4 16.0 %collective-permute-start.14 = (bf16[80,2048]{1,0:T(8,128)(2,1)S(1)}, bf16[80,2048]{1,0:T(8,128)(2,1)S(1)}, u32[]{:S(2)}, u32[]{:S(2)}) collective-permute-start(bf16[80,2048]{1,0:T(8,128)(2,1)S(1)} %get-tuple-element.138), channel_id=1, source_target_pairs={{0,6},{1,7},{2,4},{3,5},{4,2},{5,3},{6,0},{7,1},{8,14},{9,15},{10,... | collective-permute-start | bytes 983048 | tf_op jit(solution)/shard_map/ppermute | solution.py:203
  47.9 15.7 %collective-permute-start.10 = (bf16[136,2048]{1,0:T(8,128)(2,1)S(1)}, bf16[136,2048]{1,0:T(8,128)(2,1)S(1)}, u32[]{:S(2)}, u32[]{:S(2)}) collective-permute-start(bf16[136,2048]{1,0:T(8,128)(2,1)S(1)} %collective-permute-done.9.refs_0_), channel_id=1, source_target_pairs={{0,8},{8,16},{16,24},{24,0},{1,9},{9,17},{17,25},{25,1},{2,10},{10... | collective-permute-start | bytes 1671176 | tf_op jit(solution)/shard_map/ppermute | solution.py:200
  55.1 14.0 %collective-permute-start.22 = (bf16[80,2048]{1,0:T(8,128)(2,1)S(1)}, bf16[80,2048]{1,0:T(8,128)(2,1)S(1)}, u32[]{:S(2)}, u32[]{:S(2)}) collective-permute-start(bf16[80,2048]{1,0:T(8,128)(2,1)S(1)} %get-tuple-element.169), channel_id=1, source_target_pairs={{0,2},{1,3},{2,0},{3,1},{4,6},{5,7},{6,4},{7,5},{8,10},{9,11},{10,... | collective-permute-start | bytes 983048 | tf_op jit(solution)/shard_map/ppermute | solution.py:203
  60.1 13.7 %collective-permute-start.19 = (bf16[80,2048]{1,0:T(8,128)(2,1)S(1)}, bf16[80,2048]{1,0:T(8,128)(2,1)S(1)}, u32[]{:S(2)}, u32[]{:S(2)}) collective-permute-start(bf16[80,2048]{1,0:T(8,128)(2,1)S(1)} %get-tuple-element.163), channel_id=1, source_target_pairs={{0,4},{1,5},{2,6},{3,7},{4,0},{5,1},{6,2},{7,3},{8,12},{9,13},{10,... | collective-permute-start | bytes 983048 | tf_op jit(solution)/shard_map/ppermute | solution.py:203
  62.4 11.4 %collective-permute-start.16 = (bf16[80,2048]{1,0:T(8,128)(2,1)S(1)}, bf16[80,2048]{1,0:T(8,128)(2,1)S(1)}, u32[]{:S(2)}, u32[]{:S(2)}) collective-permute-start(bf16[80,2048]{1,0:T(8,128)(2,1)S(1)} %get-tuple-element.157), channel_id=1, source_target_pairs={{0,6},{1,7},{2,4},{3,5},{4,2},{5,3},{6,0},{7,1},{8,14},{9,15},{10,... | collective-permute-start | bytes 983048 | tf_op jit(solution)/shard_map/ppermute | solution.py:203
  63.6 19.4 %collective-permute-start.13 = (bf16[136,2048]{1,0:T(8,128)(2,1)S(1)}, bf16[136,2048]{1,0:T(8,128)(2,1)S(1)}, u32[]{:S(2)}, u32[]{:S(2)}) collective-permute-start(bf16[136,2048]{1,0:T(8,128)(2,1)S(1)} %collective-permute-done.10.refs_0_), channel_id=1, source_target_pairs={{0,1},{1,0},{2,3},{3,2},{4,5},{5,4},{6,7},{7,6},{8,9},{9,8},{10,11... | collective-permute-start | bytes 1671176 | tf_op jit(solution)/shard_map/ppermute | solution.py:203
  75.7 10.6 %collective-permute-start.23 = (bf16[80,2048]{1,0:T(8,128)(2,1)S(1)}, bf16[80,2048]{1,0:T(8,128)(2,1)S(1)}, u32[]{:S(2)}, u32[]{:S(2)}) collective-permute-start(bf16[80,2048]{1,0:T(8,128)(2,1)S(1)} %get-tuple-element.170), channel_id=1, source_target_pairs={{0,2},{1,3},{2,0},{3,1},{4,6},{5,7},{6,4},{7,5},{8,10},{9,11},{10,... | collective-permute-start | bytes 983048 | tf_op jit(solution)/shard_map/ppermute | solution.py:203
  76.7 10.6 %collective-permute-start.20 = (bf16[80,2048]{1,0:T(8,128)(2,1)S(1)}, bf16[80,2048]{1,0:T(8,128)(2,1)S(1)}, u32[]{:S(2)}, u32[]{:S(2)}) collective-permute-start(bf16[80,2048]{1,0:T(8,128)(2,1)S(1)} %get-tuple-element.164), channel_id=1, source_target_pairs={{0,4},{1,5},{2,6},{3,7},{4,0},{5,1},{6,2},{7,3},{8,12},{9,13},{10,... | collective-permute-start | bytes 983048 | tf_op jit(solution)/shard_map/ppermute | solution.py:203
  77.5 16.7 %collective-permute-start.17 = (bf16[80,2048]{1,0:T(8,128)(2,1)S(1)}, bf16[80,2048]{1,0:T(8,128)(2,1)S(1)}, u32[]{:S(2)}, u32[]{:S(2)}) collective-permute-start(bf16[80,2048]{1,0:T(8,128)(2,1)S(1)} %get-tuple-element.158), channel_id=1, source_target_pairs={{0,6},{1,7},{2,4},{3,5},{4,2},{5,3},{6,0},{7,1},{8,14},{9,15},{10,... | collective-permute-start | bytes 983048 | tf_op jit(solution)/shard_map/ppermute | solution.py:203
  79.4 16.6 %collective-permute-start.27 = (bf16[128,2048]{1,0:T(8,128)(2,1)S(1)}, bf16[128,2048]{1,0:T(8,128)(2,1)S(1)}, u32[]{:S(2)}, u32[]{:S(2)}) collective-permute-start(bf16[128,2048]{1,0:T(8,128)(2,1)S(1)} %shard_map.73), channel_id=1, source_target_pairs={{0,24},{8,0},{16,8},{24,16},{1,25},{9,1},{17,9},{25,17},{2,26},{10... | collective-permute-start | bytes 1572872 | tf_op jit(solution)/shard_map/ppermute | solution.py:200
  86.3 15.6 %collective-permute-start.24 = (bf16[80,2048]{1,0:T(8,128)(2,1)S(1)}, bf16[80,2048]{1,0:T(8,128)(2,1)S(1)}, u32[]{:S(2)}, u32[]{:S(2)}) collective-permute-start(bf16[80,2048]{1,0:T(8,128)(2,1)S(1)} %get-tuple-element.171), channel_id=1, source_target_pairs={{0,2},{1,3},{2,0},{3,1},{4,6},{5,7},{6,4},{7,5},{8,10},{9,11},{10,... | collective-permute-start | bytes 983048 | tf_op jit(solution)/shard_map/ppermute | solution.py:203
  87.3 14.7 %collective-permute-start.21 = (bf16[80,2048]{1,0:T(8,128)(2,1)S(1)}, bf16[80,2048]{1,0:T(8,128)(2,1)S(1)}, u32[]{:S(2)}, u32[]{:S(2)}) collective-permute-start(bf16[80,2048]{1,0:T(8,128)(2,1)S(1)} %get-tuple-element.165), channel_id=1, source_target_pairs={{0,4},{1,5},{2,6},{3,7},{4,0},{5,1},{6,2},{7,3},{8,12},{9,13},{10,... | collective-permute-start | bytes 983048 | tf_op jit(solution)/shard_map/ppermute | solution.py:203
  94.2 13.2 %collective-permute-start.18 = (bf16[80,2048]{1,0:T(8,128)(2,1)S(1)}, bf16[80,2048]{1,0:T(8,128)(2,1)S(1)}, u32[]{:S(2)}, u32[]{:S(2)}) collective-permute-start(bf16[80,2048]{1,0:T(8,128)(2,1)S(1)} %get-tuple-element.159), channel_id=1, source_target_pairs={{0,6},{1,7},{2,4},{3,5},{4,2},{5,3},{6,0},{7,1},{8,14},{9,15},{10,... | collective-permute-start | bytes 983048 | tf_op jit(solution)/shard_map/ppermute | solution.py:203
  99.4 31.1 %collective-permute-start.36 = (bf16[128,2048]{1,0:T(8,128)(2,1)S(1)}, bf16[128,2048]{1,0:T(8,128)(2,1)S(1)}, u32[]{:S(2)}, u32[]{:S(2)}) collective-permute-start(bf16[128,2048]{1,0:T(8,128)(2,1)S(1)} %shard_map.75), channel_id=1, source_target_pairs={{0,16},{8,24},{16,0},{24,8},{1,17},{9,25},{17,1},{25,9},{2,18},{10... | collective-permute-start | bytes 1572872 | tf_op jit(solution)/shard_map/ppermute | solution.py:200
  110.6 10.7 %collective-permute-start.34 = (bf16[80,2048]{1,0:T(8,128)(2,1)S(1)}, bf16[80,2048]{1,0:T(8,128)(2,1)S(1)}, u32[]{:S(2)}, u32[]{:S(2)}) collective-permute-start(bf16[80,2048]{1,0:T(8,128)(2,1)S(1)} %get-tuple-element.203), channel_id=1, source_target_pairs={{0,2},{1,3},{2,0},{3,1},{4,6},{5,7},{6,4},{7,5},{8,10},{9,11},{10,... | collective-permute-start | bytes 983048 | tf_op jit(solution)/shard_map/ppermute | solution.py:203
  111.9 14.0 %collective-permute-start.32 = (bf16[80,2048]{1,0:T(8,128)(2,1)S(1)}, bf16[80,2048]{1,0:T(8,128)(2,1)S(1)}, u32[]{:S(2)}, u32[]{:S(2)}) collective-permute-start(bf16[80,2048]{1,0:T(8,128)(2,1)S(1)} %get-tuple-element.199), channel_id=1, source_target_pairs={{0,4},{1,5},{2,6},{3,7},{4,0},{5,1},{6,2},{7,3},{8,12},{9,13},{10,... | collective-permute-start | bytes 983048 | tf_op jit(solution)/shard_map/ppermute | solution.py:203
  113.6 15.1 %collective-permute-start.30 = (bf16[80,2048]{1,0:T(8,128)(2,1)S(1)}, bf16[80,2048]{1,0:T(8,128)(2,1)S(1)}, u32[]{:S(2)}, u32[]{:S(2)}) collective-permute-start(bf16[80,2048]{1,0:T(8,128)(2,1)S(1)} %get-tuple-element.195), channel_id=1, source_target_pairs={{0,6},{1,7},{2,4},{3,5},{4,2},{5,3},{6,0},{7,1},{8,14},{9,15},{10,... | collective-permute-start | bytes 983048 | tf_op jit(solution)/shard_map/ppermute | solution.py:203
  121.3 14.1 %collective-permute-start.35 = (bf16[80,2048]{1,0:T(8,128)(2,1)S(1)}, bf16[80,2048]{1,0:T(8,128)(2,1)S(1)}, u32[]{:S(2)}, u32[]{:S(2)}) collective-permute-start(bf16[80,2048]{1,0:T(8,128)(2,1)S(1)} %get-tuple-element.204), channel_id=1, source_target_pairs={{0,2},{1,3},{2,0},{3,1},{4,6},{5,7},{6,4},{7,5},{8,10},{9,11},{10,... | collective-permute-start | bytes 983048 | tf_op jit(solution)/shard_map/ppermute | solution.py:203
  125.9 9.9 %collective-permute-start.33 = (bf16[80,2048]{1,0:T(8,128)(2,1)S(1)}, bf16[80,2048]{1,0:T(8,128)(2,1)S(1)}, u32[]{:S(2)}, u32[]{:S(2)}) collective-permute-start(bf16[80,2048]{1,0:T(8,128)(2,1)S(1)} %get-tuple-element.200), channel_id=1, source_target_pairs={{0,4},{1,5},{2,6},{3,7},{4,0},{5,1},{6,2},{7,3},{8,12},{9,13},{10,... | collective-permute-start | bytes 983048 | tf_op jit(solution)/shard_map/ppermute | solution.py:203
  128.7 12.0 %collective-permute-start.31 = (bf16[80,2048]{1,0:T(8,128)(2,1)S(1)}, bf16[80,2048]{1,0:T(8,128)(2,1)S(1)}, u32[]{:S(2)}, u32[]{:S(2)}) collective-permute-start(bf16[80,2048]{1,0:T(8,128)(2,1)S(1)} %get-tuple-element.196), channel_id=1, source_target_pairs={{0,6},{1,7},{2,4},{3,5},{4,2},{5,3},{6,0},{7,1},{8,14},{9,15},{10,... | collective-permute-start | bytes 983048 | tf_op jit(solution)/shard_map/ppermute | solution.py:203
  134.0 15.8 %collective-permute-start.41 = (bf16[128,2048]{1,0:T(8,128)(2,1)S(1)}, bf16[128,2048]{1,0:T(8,128)(2,1)S(1)}, u32[]{:S(2)}, u32[]{:S(2)}) collective-permute-start(bf16[128,2048]{1,0:T(8,128)(2,1)S(1)} %shard_map.78), channel_id=1, source_target_pairs={{0,8},{8,16},{16,24},{24,0},{1,9},{9,17},{17,25},{25,1},{2,10},{10... | collective-permute-start | bytes 1572872 | tf_op jit(solution)/shard_map/ppermute | solution.py:200
  (18 other events, 89.0 us)

commit v13 on v12

--- a/solution.py
+++ b/solution.py
@@ -286,6 +286,8 @@
                 results[d] = expert(slots[d], *first, flops=PHASE_FLOPS)
         else:
             rows = {q: after([results[d][q]], seen[q])[0] for q in backward}
+            if d == 0:
+                rows[forward[-1]] = after([rows[forward[-1]]], sums[0])[0]
             seen = backs = slabs_across(rows)
             first = [(home if d else leaving)[waiting]] if waiting else [results[end - 1][0]]
             sums = mix(pairs[d], backs, *first)

time: 151 us -> 151 us (level)
  no operation moved by 1% of the time
where the time goes in v13:
time: 151 us
  waiting for transfers between devices  78.4 us (52%)
  starting transfers between devices  43.8 us (29%)
  Pallas kernels  22.2 us (15%)
  local copies, waits for them, and re-layouts  6.38 us (4%)
    ppermute x36, waiting for transfers between devices, across(): lax.ppermute(array, 'zero', [(i, i ^ o) for i in range(near)])  59.6 us
    ppermute x36, starting transfers between devices, across(): lax.ppermute(array, 'zero', [(i, i ^ o) for i in range(near)])  32.1 us
    ppermute x6, waiting for transfers between devices, along(): lax.ppermute(array, 'expert', [(i, (i + d) % layers) for i in range(layer...  18.8 us
    pallas_call x4, Pallas kernels, expert(): call(functools.partial(expert_kernel, z, rows), [shape(rows)] * z.chips,...  12.9 us
    ppermute x6, starting transfers between devices, along(): lax.ppermute(array, 'expert', [(i, (i + d) % layers) for i in range(layer...  11.7 us
    unnamed x16, local copies, waits for them, and re-layouts  6.38 us
    pallas_call x4, Pallas kernels, mix(): call(functools.partial(mix_kernel, z, n, list(backs), ride_order), [shape...  5.35 us
  transfers between devices with their start and end apart: 42, of which 25 were waited for; matrix products, arithmetic and copies ran while one was open for 0% of the time, Pallas kernels for 14%

profile of v13, /device:TPU:0, one launch (start us, length us, event | category | flops | bytes accessed | tf_op | source)
XLA Modules:
  0.0 150.9 jit_solution(2865484031760300478)
XLA Ops:
  3.2 2.6 %collective-permute-start.1 = (bf16[136,2048]{1,0:T(8,128)(2,1)S(1)}, bf16[136,2048]{1,0:T(8,128)(2,1)S(1)}, u32[]{:S(2)}, u32[]{:S(2)}) collective-permute-start(bf16[136,2048]{1,0:T(8,128)(2,1)S(1)} %shard_map.64.refs_0_), channel_id=1, source_target_pairs={{0,8},{8,16},{16,24},{24,0},{1,9},{9,17},{17,25},{25,1},{2,10},{10... | collective-permute-start | bytes 1671176 | tf_op jit(solution)/shard_map/ppermute | solution.py:200
  6.4 1.9 %collective-permute-start.2 = (bf16[80,2048]{1,0:T(8,128)(2,1)S(1)}, bf16[80,2048]{1,0:T(8,128)(2,1)S(1)}, u32[]{:S(2)}, u32[]{:S(2)}) collective-permute-start(bf16[80,2048]{1,0:T(8,128)(2,1)S(1)} %get-tuple-element.113), channel_id=1, source_target_pairs={{0,2},{1,3},{2,0},{3,1},{4,6},{5,7},{6,4},{7,5},{8,10},{9,11},{10,... | collective-permute-start | bytes 983048 | tf_op jit(solution)/shard_map/ppermute | solution.py:203
  10.0 11.1 %collective-permute-done.1.refs_0_ = bf16[136,2048]{1,0:T(8,128)(2,1)S(1)} collective-permute-done((bf16[136,2048]{1,0:T(8,128)(2,1)S(1)}, bf16[136,2048]{1,0:T(8,128)(2,1)S(1)}, u32[]{:S(2)}, u32[]{:S(2)}) %collective-permute-start.1) | collective-permute-done | bytes 557088 | tf_op jit(solution)/shard_map/ppermute | solution.py:200
  21.1 3.7 %collective-permute-done.4.refs_2_ = bf16[80,2048]{1,0:T(8,128)(2,1)S(1)} collective-permute-done((bf16[80,2048]{1,0:T(8,128)(2,1)S(1)}, bf16[80,2048]{1,0:T(8,128)(2,1)S(1)}, u32[]{:S(2)}, u32[]{:S(2)}) %collective-permute-start.4) | collective-permute-done | bytes 327712 | tf_op jit(solution)/shard_map/ppermute | solution.py:203
  28.9 1.9 %copy-done.1 = bf16[1,2048,768]{2,1,0:T(8,128)(2,1)S(1)} copy-done((bf16[1,2048,768]{2,1,0:T(8,128)(2,1)S(1)}, bf16[1,2048,768]{2,1,0:T(8,128)(2,1)}, u32[]{:S(2)}) %copy-start.1) | copy-done | bytes 3145752
  30.8 1.9 %copy-done.3 = bf16[1,768,2048]{2,1,0:T(8,128)(2,1)S(1)} copy-done((bf16[1,768,2048]{2,1,0:T(8,128)(2,1)S(1)}, bf16[1,768,2048]{2,1,0:T(8,128)(2,1)}, u32[]{:S(2)}) %copy-start.3) | copy-done | bytes 3145752
  32.7 3.2 %shard_map.67 = (bf16[80,2048]{1,0:T(8,128)(2,1)S(1)}, bf16[80,2048]{1,0:T(8,128)(2,1)S(1)}, bf16[80,2048]{1,0:T(8,128)(2,1)S(1)}, bf16[80,2048]{1,0:T(8,128)(2,1)S(1)}) custom-call(bf16[80,2048]{1,0:T(8,128)(2,1)S(1)} %get-tuple-element.126.refs_0_, bf16[80,2048]{1,0:T(8,128)(2,1)S(1)} %collective-permute-done.2.refs_1_, ...), custom_call_target="tpu_custom_call" | custom-call | flops 1000 | bytes 1000 | tf_op jit(solution)/shard_map/pallas_call | solution.py:233
  36.0 1.9 %collective-permute-done.9.refs_0_ = bf16[136,2048]{1,0:T(8,128)(2,1)S(1)} collective-permute-done((bf16[136,2048]{1,0:T(8,128)(2,1)S(1)}, bf16[136,2048]{1,0:T(8,128)(2,1)S(1)}, u32[]{:S(2)}, u32[]{:S(2)}) %collective-permute-start.9) | collective-permute-done | bytes 557088 | tf_op jit(solution)/shard_map/ppermute | solution.py:200
  37.9 5.8 %collective-permute-done.8.refs_3_.refs_5_ = bf16[88,2048]{1,0:T(8,128)(2,1)S(1)} collective-permute-done((bf16[88,2048]{1,0:T(8,128)(2,1)S(1)}, bf16[88,2048]{1,0:T(8,128)(2,1)S(1)}, u32[]{:S(2)}, u32[]{:S(2)}) %collective-permute-start.8) | collective-permute-done | bytes 360480 | tf_op jit(solution)/shard_map/ppermute | solution.py:203
  47.9 1.6 %collective-permute-start.10 = (bf16[136,2048]{1,0:T(8,128)(2,1)S(1)}, bf16[136,2048]{1,0:T(8,128)(2,1)S(1)}, u32[]{:S(2)}, u32[]{:S(2)}) collective-permute-start(bf16[136,2048]{1,0:T(8,128)(2,1)S(1)} %collective-permute-done.9.refs_0_), channel_id=1, source_target_pairs={{0,8},{8,16},{16,24},{24,0},{1,9},{9,17},{17,25},{25,1},{2,10},{10... | collective-permute-start | bytes 1671176 | tf_op jit(solution)/shard_map/ppermute | solution.py:200
  49.5 3.2 %shard_map.71 = (bf16[80,2048]{1,0:T(8,128)(2,1)S(1)}, bf16[80,2048]{1,0:T(8,128)(2,1)S(1)}, bf16[80,2048]{1,0:T(8,128)(2,1)S(1)}, bf16[80,2048]{1,0:T(8,128)(2,1)S(1)}) custom-call(bf16[88,2048]{1,0:T(8,128)(2,1)S(1)} %get-tuple-element.147.refs_0_.refs_2_, bf16[88,2048]{1,0:T(8,128)(2,1)S(1)} %collective-permute-done.6.refs_1_.refs_3_, ...), custom_call_target="tpu_custom_call" | custom-call | flops 1000 | bytes 1000 | tf_op jit(solution)/shard_map/pallas_call | solution.py:233
  52.7 2.3 %collective-permute-done.12.refs_3_ = bf16[80,2048]{1,0:T(8,128)(2,1)S(1)} collective-permute-done((bf16[80,2048]{1,0:T(8,128)(2,1)S(1)}, bf16[80,2048]{1,0:T(8,128)(2,1)S(1)}, u32[]{:S(2)}, u32[]{:S(2)}) %collective-permute-start.12) | collective-permute-done | bytes 327712 | tf_op jit(solution)/shard_map/ppermute | solution.py:203
  55.7 4.5 %collective-permute-done.15.refs_2_ = bf16[80,2048]{1,0:T(8,128)(2,1)S(1)} collective-permute-done((bf16[80,2048]{1,0:T(8,128)(2,1)S(1)}, bf16[80,2048]{1,0:T(8,128)(2,1)S(1)}, u32[]{:S(2)}, u32[]{:S(2)}) %collective-permute-start.15) | collective-permute-done | bytes 327712 | tf_op jit(solution)/shard_map/ppermute | solution.py:203
  60.1 1.6 %collective-permute-start.19 = (bf16[80,2048]{1,0:T(8,128)(2,1)S(1)}, bf16[80,2048]{1,0:T(8,128)(2,1)S(1)}, u32[]{:S(2)}, u32[]{:S(2)}) collective-permute-start(bf16[80,2048]{1,0:T(8,128)(2,1)S(1)} %get-tuple-element.164), channel_id=1, source_target_pairs={{0,4},{1,5},{2,6},{3,7},{4,0},{5,1},{6,2},{7,3},{8,12},{9,13},{10,... | collective-permute-start | bytes 983048 | tf_op jit(solution)/shard_map/ppermute | solution.py:203
  63.6 3.2 %shard_map.70 = (bf16[80,2048]{1,0:T(8,128)(2,1)S(1)}, bf16[80,2048]{1,0:T(8,128)(2,1)S(1)}, bf16[80,2048]{1,0:T(8,128)(2,1)S(1)}, bf16[80,2048]{1,0:T(8,128)(2,1)S(1)}) custom-call(bf16[80,2048]{1,0:T(8,128)(2,1)S(1)} %get-tuple-element.142.refs_0_, bf16[80,2048]{1,0:T(8,128)(2,1)S(1)} %collective-permute-done.14.refs_1_, ...), custom_call_target="tpu_custom_call" | custom-call | flops 1000 | bytes 1000 | tf_op jit(solution)/shard_map/pallas_call | solution.py:233
  66.9 2.2 %collective-permute-done.22.refs_9_ = bf16[80,2048]{1,0:T(8,128)(2,1)S(1)} collective-permute-done((bf16[80,2048]{1,0:T(8,128)(2,1)S(1)}, bf16[80,2048]{1,0:T(8,128)(2,1)S(1)}, u32[]{:S(2)}, u32[]{:S(2)}) %collective-permute-start.22) | collective-permute-done | bytes 327712 | tf_op jit(solution)/shard_map/ppermute | solution.py:203
  69.1 4.7 %collective-permute-done.19.refs_8_ = bf16[80,2048]{1,0:T(8,128)(2,1)S(1)} collective-permute-done((bf16[80,2048]{1,0:T(8,128)(2,1)S(1)}, bf16[80,2048]{1,0:T(8,128)(2,1)S(1)}, u32[]{:S(2)}, u32[]{:S(2)}) %collective-permute-start.19) | collective-permute-done | bytes 327712 | tf_op jit(solution)/shard_map/ppermute | solution.py:203
  77.5 1.7 %collective-permute-start.17 = (bf16[80,2048]{1,0:T(8,128)(2,1)S(1)}, bf16[80,2048]{1,0:T(8,128)(2,1)S(1)}, u32[]{:S(2)}, u32[]{:S(2)}) collective-permute-start(bf16[80,2048]{1,0:T(8,128)(2,1)S(1)} %get-tuple-element.159), channel_id=1, source_target_pairs={{0,6},{1,7},{2,4},{3,5},{4,2},{5,3},{6,0},{7,1},{8,14},{9,15},{10,... | collective-permute-start | bytes 983048 | tf_op jit(solution)/shard_map/ppermute | solution.py:203
  79.4 3.7 %collective-permute-start.27 = (bf16[128,2048]{1,0:T(8,128)(2,1)S(1)}, bf16[128,2048]{1,0:T(8,128)(2,1)S(1)}, u32[]{:S(2)}, u32[]{:S(2)}) collective-permute-start(bf16[128,2048]{1,0:T(8,128)(2,1)S(1)} %shard_map.73), channel_id=1, source_target_pairs={{0,24},{8,0},{16,8},{24,16},{1,25},{9,1},{17,9},{25,17},{2,26},{10... | collective-permute-start | bytes 1572872 | tf_op jit(solution)/shard_map/ppermute | solution.py:200
  83.7 2.6 %collective-permute-done.23.refs_9_ = bf16[80,2048]{1,0:T(8,128)(2,1)S(1)} collective-permute-done((bf16[80,2048]{1,0:T(8,128)(2,1)S(1)}, bf16[80,2048]{1,0:T(8,128)(2,1)S(1)}, u32[]{:S(2)}, u32[]{:S(2)}) %collective-permute-start.23) | collective-permute-done | bytes 327712 | tf_op jit(solution)/shard_map/ppermute | solution.py:203
  88.1 6.1 %collective-permute-done.17.refs_7_ = bf16[80,2048]{1,0:T(8,128)(2,1)S(1)} collective-permute-done((bf16[80,2048]{1,0:T(8,128)(2,1)S(1)}, bf16[80,2048]{1,0:T(8,128)(2,1)S(1)}, u32[]{:S(2)}, u32[]{:S(2)}) %collective-permute-start.17) | collective-permute-done | bytes 327712 | tf_op jit(solution)/shard_map/ppermute | solution.py:203
  94.2 1.8 %collective-permute-start.18 = (bf16[80,2048]{1,0:T(8,128)(2,1)S(1)}, bf16[80,2048]{1,0:T(8,128)(2,1)S(1)}, u32[]{:S(2)}, u32[]{:S(2)}) collective-permute-start(bf16[80,2048]{1,0:T(8,128)(2,1)S(1)} %get-tuple-element.160), channel_id=1, source_target_pairs={{0,6},{1,7},{2,4},{3,5},{4,2},{5,3},{6,0},{7,1},{8,14},{9,15},{10,... | collective-permute-start | bytes 983048 | tf_op jit(solution)/shard_map/ppermute | solution.py:203
  99.4 2.5 %collective-permute-start.33 = (bf16[128,2048]{1,0:T(8,128)(2,1)S(1)}, bf16[128,2048]{1,0:T(8,128)(2,1)S(1)}, u32[]{:S(2)}, u32[]{:S(2)}) collective-permute-start(bf16[128,2048]{1,0:T(8,128)(2,1)S(1)} %shard_map.75), channel_id=1, source_target_pairs={{0,16},{8,24},{16,0},{24,8},{1,17},{9,25},{17,1},{25,9},{2,18},{10... | collective-permute-start | bytes 1572872 | tf_op jit(solution)/shard_map/ppermute | solution.py:200
  101.9 5.5 %collective-permute-done.18.refs_1_ = bf16[80,2048]{1,0:T(8,128)(2,1)S(1)} collective-permute-done((bf16[80,2048]{1,0:T(8,128)(2,1)S(1)}, bf16[80,2048]{1,0:T(8,128)(2,1)S(1)}, u32[]{:S(2)}, u32[]{:S(2)}) %collective-permute-start.18) | collective-permute-done | bytes 327712 | tf_op jit(solution)/shard_map/ppermute | solution.py:203
  107.4 3.2 %shard_map.76 = (bf16[80,2048]{1,0:T(8,128)(2,1)S(1)}, bf16[80,2048]{1,0:T(8,128)(2,1)S(1)}, bf16[80,2048]{1,0:T(8,128)(2,1)S(1)}, bf16[80,2048]{1,0:T(8,128)(2,1)S(1)}) custom-call(bf16[80,2048]{1,0:T(8,128)(2,1)S(1)} %get-tuple-element.187.refs_0_, bf16[80,2048]{1,0:T(8,128)(2,1)S(1)} %collective-permute-done.18.refs_1_, ...), custom_call_target="tpu_custom_call" | custom-call | flops 20000000000 | bytes 1000 | tf_op jit(solution)/shard_map/pallas_call | solution.py:233
  111.9 1.7 %collective-permute-start.31 = (bf16[80,2048]{1,0:T(8,128)(2,1)S(1)}, bf16[80,2048]{1,0:T(8,128)(2,1)S(1)}, u32[]{:S(2)}, u32[]{:S(2)}) collective-permute-start(bf16[80,2048]{1,0:T(8,128)(2,1)S(1)} %get-tuple-element.199), channel_id=1, source_target_pairs={{0,4},{1,5},{2,6},{3,7},{4,0},{5,1},{6,2},{7,3},{8,12},{9,13},{10,... | collective-permute-start | bytes 983048 | tf_op jit(solution)/shard_map/ppermute | solution.py:203
  114.2 7.2 %collective-permute-done.32.refs_9_ = bf16[80,2048]{1,0:T(8,128)(2,1)S(1)} collective-permute-done((bf16[80,2048]{1,0:T(8,128)(2,1)S(1)}, bf16[80,2048]{1,0:T(8,128)(2,1)S(1)}, u32[]{:S(2)}, u32[]{:S(2)}) %collective-permute-start.32) | collective-permute-done | bytes 327712 | tf_op jit(solution)/shard_map/ppermute | solution.py:203
  122.6 3.4 %collective-permute-done.31.refs_8_ = bf16[80,2048]{1,0:T(8,128)(2,1)S(1)} collective-permute-done((bf16[80,2048]{1,0:T(8,128)(2,1)S(1)}, bf16[80,2048]{1,0:T(8,128)(2,1)S(1)}, u32[]{:S(2)}, u32[]{:S(2)}) %collective-permute-start.31) | collective-permute-done | bytes 327712 | tf_op jit(solution)/shard_map/ppermute | solution.py:203
  125.9 1.6 %collective-permute-start.35 = (bf16[80,2048]{1,0:T(8,128)(2,1)S(1)}, bf16[80,2048]{1,0:T(8,128)(2,1)S(1)}, u32[]{:S(2)}, u32[]{:S(2)}) collective-permute-start(bf16[80,2048]{1,0:T(8,128)(2,1)S(1)} %get-tuple-element.209), channel_id=1, source_target_pairs={{0,4},{1,5},{2,6},{3,7},{4,0},{5,1},{6,2},{7,3},{8,12},{9,13},{10,... | collective-permute-start | bytes 983048 | tf_op jit(solution)/shard_map/ppermute | solution.py:203
  130.1 1.8 %collective-permute-start.34 = (bf16[80,2048]{1,0:T(8,128)(2,1)S(1)}, bf16[80,2048]{1,0:T(8,128)(2,1)S(1)}, u32[]{:S(2)}, u32[]{:S(2)}) collective-permute-start(bf16[80,2048]{1,0:T(8,128)(2,1)S(1)} %get-tuple-element.207), channel_id=1, source_target_pairs={{0,6},{1,7},{2,4},{3,5},{4,2},{5,3},{6,0},{7,1},{8,14},{9,15},{10,... | collective-permute-start | bytes 983048 | tf_op jit(solution)/shard_map/ppermute | solution.py:203
  135.8 4.9 %collective-permute-done.34.refs_7_ = bf16[80,2048]{1,0:T(8,128)(2,1)S(1)} collective-permute-done((bf16[80,2048]{1,0:T(8,128)(2,1)S(1)}, bf16[80,2048]{1,0:T(8,128)(2,1)S(1)}, u32[]{:S(2)}, u32[]{:S(2)}) %collective-permute-start.34) | collective-permute-done | bytes 327712 | tf_op jit(solution)/shard_map/ppermute | solution.py:203
  144.1 5.7 %collective-permute-done.41.refs_5_ = bf16[128,2048]{1,0:T(8,128)(2,1)S(1)} collective-permute-done((bf16[128,2048]{1,0:T(8,128)(2,1)S(1)}, bf16[128,2048]{1,0:T(8,128)(2,1)S(1)}, u32[]{:S(2)}, u32[]{:S(2)}) %collective-permute-start.41) | collective-permute-done | bytes 524320 | tf_op jit(solution)/shard_map/ppermute | solution.py:200
  (85 shorter events, 39.8 us)
Async XLA Ops:
  3.2 17.9 %collective-permute-start.1 = (bf16[136,2048]{1,0:T(8,128)(2,1)S(1)}, bf16[136,2048]{1,0:T(8,128)(2,1)S(1)}, u32[]{:S(2)}, u32[]{:S(2)}) collective-permute-start(bf16[136,2048]{1,0:T(8,128)(2,1)S(1)} %shard_map.64.refs_0_), channel_id=1, source_target_pairs={{0,8},{8,16},{16,24},{24,0},{1,9},{9,17},{17,25},{25,1},{2,10},{10... | collective-permute-start | bytes 1671176 | tf_op jit(solution)/shard_map/ppermute | solution.py:200
  6.4 14.7 %collective-permute-start.2 = (bf16[80,2048]{1,0:T(8,128)(2,1)S(1)}, bf16[80,2048]{1,0:T(8,128)(2,1)S(1)}, u32[]{:S(2)}, u32[]{:S(2)}) collective-permute-start(bf16[80,2048]{1,0:T(8,128)(2,1)S(1)} %get-tuple-element.113), channel_id=1, source_target_pairs={{0,2},{1,3},{2,0},{3,1},{4,6},{5,7},{6,4},{7,5},{8,10},{9,11},{10,... | collective-permute-start | bytes 983048 | tf_op jit(solution)/shard_map/ppermute | solution.py:203
  8.3 16.5 %collective-permute-start.4 = (bf16[80,2048]{1,0:T(8,128)(2,1)S(1)}, bf16[80,2048]{1,0:T(8,128)(2,1)S(1)}, u32[]{:S(2)}, u32[]{:S(2)}) collective-permute-start(bf16[80,2048]{1,0:T(8,128)(2,1)S(1)} %get-tuple-element.116), channel_id=1, source_target_pairs={{0,4},{1,5},{2,6},{3,7},{4,0},{5,1},{6,2},{7,3},{8,12},{9,13},{10,... | collective-permute-start | bytes 983048 | tf_op jit(solution)/shard_map/ppermute | solution.py:203
  9.8 15.0 %collective-permute-start.5 = (bf16[80,2048]{1,0:T(8,128)(2,1)S(1)}, bf16[80,2048]{1,0:T(8,128)(2,1)S(1)}, u32[]{:S(2)}, u32[]{:S(2)}) collective-permute-start(bf16[80,2048]{1,0:T(8,128)(2,1)S(1)} %get-tuple-element.117), channel_id=1, source_target_pairs={{0,6},{1,7},{2,4},{3,5},{4,2},{5,3},{6,0},{7,1},{8,14},{9,15},{10,... | collective-permute-start | bytes 983048 | tf_op jit(solution)/shard_map/ppermute | solution.py:203
  21.1 16.8 %collective-permute-start.9 = (bf16[136,2048]{1,0:T(8,128)(2,1)S(1)}, bf16[136,2048]{1,0:T(8,128)(2,1)S(1)}, u32[]{:S(2)}, u32[]{:S(2)}) collective-permute-start(bf16[136,2048]{1,0:T(8,128)(2,1)S(1)} %collective-permute-done.1.refs_0_), channel_id=1, source_target_pairs={{0,8},{8,16},{16,24},{24,0},{1,9},{9,17},{17,25},{25,1},{2,10},{10... | collective-permute-start | bytes 1671176 | tf_op jit(solution)/shard_map/ppermute | solution.py:200
  25.4 12.5 %collective-permute-start.6 = (bf16[88,2048]{1,0:T(8,128)(2,1)S(1)}, bf16[88,2048]{1,0:T(8,128)(2,1)S(1)}, u32[]{:S(2)}, u32[]{:S(2)}) collective-permute-start(bf16[88,2048]{1,0:T(8,128)(2,1)S(1)} %get-tuple-element.120), channel_id=1, source_target_pairs={{0,2},{1,3},{2,0},{3,1},{4,6},{5,7},{6,4},{7,5},{8,10},{9,11},{10,... | collective-permute-start | bytes 1081352 | tf_op jit(solution)/shard_map/ppermute | solution.py:203
  26.7 17.1 %collective-permute-start.8 = (bf16[88,2048]{1,0:T(8,128)(2,1)S(1)}, bf16[88,2048]{1,0:T(8,128)(2,1)S(1)}, u32[]{:S(2)}, u32[]{:S(2)}) collective-permute-start(bf16[88,2048]{1,0:T(8,128)(2,1)S(1)} %get-tuple-element.124), channel_id=1, source_target_pairs={{0,4},{1,5},{2,6},{3,7},{4,0},{5,1},{6,2},{7,3},{8,12},{9,13},{10,... | collective-permute-start | bytes 1081352 | tf_op jit(solution)/shard_map/ppermute | solution.py:203
  27.5 16.2 %collective-permute-start.7 = (bf16[88,2048]{1,0:T(8,128)(2,1)S(1)}, bf16[88,2048]{1,0:T(8,128)(2,1)S(1)}, u32[]{:S(2)}, u32[]{:S(2)}) collective-permute-start(bf16[88,2048]{1,0:T(8,128)(2,1)S(1)} %get-tuple-element.122), channel_id=1, source_target_pairs={{0,6},{1,7},{2,4},{3,5},{4,2},{5,3},{6,0},{7,1},{8,14},{9,15},{10,... | collective-permute-start | bytes 1081352 | tf_op jit(solution)/shard_map/ppermute | solution.py:203
  37.9 5.8 %collective-permute-start.11 = (bf16[136,2048]{1,0:T(8,128)(2,1)S(1)}, bf16[136,2048]{1,0:T(8,128)(2,1)S(1)}, u32[]{:S(2)}, u32[]{:S(2)}) collective-permute-start(bf16[136,2048]{1,0:T(8,128)(2,1)S(1)} %collective-permute-done.9.refs_0_), channel_id=1, source_target_pairs={{0,1},{1,0},{2,3},{3,2},{4,5},{5,4},{6,7},{7,6},{8,9},{9,8},{10,11... | collective-permute-start | bytes 1671176 | tf_op jit(solution)/shard_map/ppermute | solution.py:203
  44.4 10.7 %collective-permute-start.12 = (bf16[80,2048]{1,0:T(8,128)(2,1)S(1)}, bf16[80,2048]{1,0:T(8,128)(2,1)S(1)}, u32[]{:S(2)}, u32[]{:S(2)}) collective-permute-start(bf16[80,2048]{1,0:T(8,128)(2,1)S(1)} %get-tuple-element.133), channel_id=1, source_target_pairs={{0,2},{1,3},{2,0},{3,1},{4,6},{5,7},{6,4},{7,5},{8,10},{9,11},{10,... | collective-permute-start | bytes 983048 | tf_op jit(solution)/shard_map/ppermute | solution.py:203
  45.0 15.1 %collective-permute-start.15 = (bf16[80,2048]{1,0:T(8,128)(2,1)S(1)}, bf16[80,2048]{1,0:T(8,128)(2,1)S(1)}, u32[]{:S(2)}, u32[]{:S(2)}) collective-permute-start(bf16[80,2048]{1,0:T(8,128)(2,1)S(1)} %get-tuple-element.141), channel_id=1, source_target_pairs={{0,4},{1,5},{2,6},{3,7},{4,0},{5,1},{6,2},{7,3},{8,12},{9,13},{10,... | collective-permute-start | bytes 983048 | tf_op jit(solution)/shard_map/ppermute | solution.py:203
  46.4 16.0 %collective-permute-start.14 = (bf16[80,2048]{1,0:T(8,128)(2,1)S(1)}, bf16[80,2048]{1,0:T(8,128)(2,1)S(1)}, u32[]{:S(2)}, u32[]{:S(2)}) collective-permute-start(bf16[80,2048]{1,0:T(8,128)(2,1)S(1)} %get-tuple-element.139), channel_id=1, source_target_pairs={{0,6},{1,7},{2,4},{3,5},{4,2},{5,3},{6,0},{7,1},{8,14},{9,15},{10,... | collective-permute-start | bytes 983048 | tf_op jit(solution)/shard_map/ppermute | solution.py:203
  47.9 15.7 %collective-permute-start.10 = (bf16[136,2048]{1,0:T(8,128)(2,1)S(1)}, bf16[136,2048]{1,0:T(8,128)(2,1)S(1)}, u32[]{:S(2)}, u32[]{:S(2)}) collective-permute-start(bf16[136,2048]{1,0:T(8,128)(2,1)S(1)} %collective-permute-done.9.refs_0_), channel_id=1, source_target_pairs={{0,8},{8,16},{16,24},{24,0},{1,9},{9,17},{17,25},{25,1},{2,10},{10... | collective-permute-start | bytes 1671176 | tf_op jit(solution)/shard_map/ppermute | solution.py:200
  55.1 14.0 %collective-permute-start.22 = (bf16[80,2048]{1,0:T(8,128)(2,1)S(1)}, bf16[80,2048]{1,0:T(8,128)(2,1)S(1)}, u32[]{:S(2)}, u32[]{:S(2)}) collective-permute-start(bf16[80,2048]{1,0:T(8,128)(2,1)S(1)} %get-tuple-element.170), channel_id=1, source_target_pairs={{0,2},{1,3},{2,0},{3,1},{4,6},{5,7},{6,4},{7,5},{8,10},{9,11},{10,... | collective-permute-start | bytes 983048 | tf_op jit(solution)/shard_map/ppermute | solution.py:203
  60.1 13.7 %collective-permute-start.19 = (bf16[80,2048]{1,0:T(8,128)(2,1)S(1)}, bf16[80,2048]{1,0:T(8,128)(2,1)S(1)}, u32[]{:S(2)}, u32[]{:S(2)}) collective-permute-start(bf16[80,2048]{1,0:T(8,128)(2,1)S(1)} %get-tuple-element.164), channel_id=1, source_target_pairs={{0,4},{1,5},{2,6},{3,7},{4,0},{5,1},{6,2},{7,3},{8,12},{9,13},{10,... | collective-permute-start | bytes 983048 | tf_op jit(solution)/shard_map/ppermute | solution.py:203
  62.4 11.4 %collective-permute-start.16 = (bf16[80,2048]{1,0:T(8,128)(2,1)S(1)}, bf16[80,2048]{1,0:T(8,128)(2,1)S(1)}, u32[]{:S(2)}, u32[]{:S(2)}) collective-permute-start(bf16[80,2048]{1,0:T(8,128)(2,1)S(1)} %get-tuple-element.158), channel_id=1, source_target_pairs={{0,6},{1,7},{2,4},{3,5},{4,2},{5,3},{6,0},{7,1},{8,14},{9,15},{10,... | collective-permute-start | bytes 983048 | tf_op jit(solution)/shard_map/ppermute | solution.py:203
  63.6 19.4 %collective-permute-start.13 = (bf16[136,2048]{1,0:T(8,128)(2,1)S(1)}, bf16[136,2048]{1,0:T(8,128)(2,1)S(1)}, u32[]{:S(2)}, u32[]{:S(2)}) collective-permute-start(bf16[136,2048]{1,0:T(8,128)(2,1)S(1)} %collective-permute-done.10.refs_0_), channel_id=1, source_target_pairs={{0,1},{1,0},{2,3},{3,2},{4,5},{5,4},{6,7},{7,6},{8,9},{9,8},{10,11... | collective-permute-start | bytes 1671176 | tf_op jit(solution)/shard_map/ppermute | solution.py:203
  75.7 10.6 %collective-permute-start.23 = (bf16[80,2048]{1,0:T(8,128)(2,1)S(1)}, bf16[80,2048]{1,0:T(8,128)(2,1)S(1)}, u32[]{:S(2)}, u32[]{:S(2)}) collective-permute-start(bf16[80,2048]{1,0:T(8,128)(2,1)S(1)} %get-tuple-element.171), channel_id=1, source_target_pairs={{0,2},{1,3},{2,0},{3,1},{4,6},{5,7},{6,4},{7,5},{8,10},{9,11},{10,... | collective-permute-start | bytes 983048 | tf_op jit(solution)/shard_map/ppermute | solution.py:203
  76.7 10.6 %collective-permute-start.20 = (bf16[80,2048]{1,0:T(8,128)(2,1)S(1)}, bf16[80,2048]{1,0:T(8,128)(2,1)S(1)}, u32[]{:S(2)}, u32[]{:S(2)}) collective-permute-start(bf16[80,2048]{1,0:T(8,128)(2,1)S(1)} %get-tuple-element.165), channel_id=1, source_target_pairs={{0,4},{1,5},{2,6},{3,7},{4,0},{5,1},{6,2},{7,3},{8,12},{9,13},{10,... | collective-permute-start | bytes 983048 | tf_op jit(solution)/shard_map/ppermute | solution.py:203
  77.5 16.7 %collective-permute-start.17 = (bf16[80,2048]{1,0:T(8,128)(2,1)S(1)}, bf16[80,2048]{1,0:T(8,128)(2,1)S(1)}, u32[]{:S(2)}, u32[]{:S(2)}) collective-permute-start(bf16[80,2048]{1,0:T(8,128)(2,1)S(1)} %get-tuple-element.159), channel_id=1, source_target_pairs={{0,6},{1,7},{2,4},{3,5},{4,2},{5,3},{6,0},{7,1},{8,14},{9,15},{10,... | collective-permute-start | bytes 983048 | tf_op jit(solution)/shard_map/ppermute | solution.py:203
  79.4 16.6 %collective-permute-start.27 = (bf16[128,2048]{1,0:T(8,128)(2,1)S(1)}, bf16[128,2048]{1,0:T(8,128)(2,1)S(1)}, u32[]{:S(2)}, u32[]{:S(2)}) collective-permute-start(bf16[128,2048]{1,0:T(8,128)(2,1)S(1)} %shard_map.73), channel_id=1, source_target_pairs={{0,24},{8,0},{16,8},{24,16},{1,25},{9,1},{17,9},{25,17},{2,26},{10... | collective-permute-start | bytes 1572872 | tf_op jit(solution)/shard_map/ppermute | solution.py:200
  86.3 15.6 %collective-permute-start.24 = (bf16[80,2048]{1,0:T(8,128)(2,1)S(1)}, bf16[80,2048]{1,0:T(8,128)(2,1)S(1)}, u32[]{:S(2)}, u32[]{:S(2)}) collective-permute-start(bf16[80,2048]{1,0:T(8,128)(2,1)S(1)} %get-tuple-element.172), channel_id=1, source_target_pairs={{0,2},{1,3},{2,0},{3,1},{4,6},{5,7},{6,4},{7,5},{8,10},{9,11},{10,... | collective-permute-start | bytes 983048 | tf_op jit(solution)/shard_map/ppermute | solution.py:203
  87.3 14.7 %collective-permute-start.21 = (bf16[80,2048]{1,0:T(8,128)(2,1)S(1)}, bf16[80,2048]{1,0:T(8,128)(2,1)S(1)}, u32[]{:S(2)}, u32[]{:S(2)}) collective-permute-start(bf16[80,2048]{1,0:T(8,128)(2,1)S(1)} %get-tuple-element.166), channel_id=1, source_target_pairs={{0,4},{1,5},{2,6},{3,7},{4,0},{5,1},{6,2},{7,3},{8,12},{9,13},{10,... | collective-permute-start | bytes 983048 | tf_op jit(solution)/shard_map/ppermute | solution.py:203
  94.2 13.2 %collective-permute-start.18 = (bf16[80,2048]{1,0:T(8,128)(2,1)S(1)}, bf16[80,2048]{1,0:T(8,128)(2,1)S(1)}, u32[]{:S(2)}, u32[]{:S(2)}) collective-permute-start(bf16[80,2048]{1,0:T(8,128)(2,1)S(1)} %get-tuple-element.160), channel_id=1, source_target_pairs={{0,6},{1,7},{2,4},{3,5},{4,2},{5,3},{6,0},{7,1},{8,14},{9,15},{10,... | collective-permute-start | bytes 983048 | tf_op jit(solution)/shard_map/ppermute | solution.py:203
  99.4 29.3 %collective-permute-start.33 = (bf16[128,2048]{1,0:T(8,128)(2,1)S(1)}, bf16[128,2048]{1,0:T(8,128)(2,1)S(1)}, u32[]{:S(2)}, u32[]{:S(2)}) collective-permute-start(bf16[128,2048]{1,0:T(8,128)(2,1)S(1)} %shard_map.75), channel_id=1, source_target_pairs={{0,16},{8,24},{16,0},{24,8},{1,17},{9,25},{17,1},{25,9},{2,18},{10... | collective-permute-start | bytes 1572872 | tf_op jit(solution)/shard_map/ppermute | solution.py:200
  110.6 10.7 %collective-permute-start.32 = (bf16[80,2048]{1,0:T(8,128)(2,1)S(1)}, bf16[80,2048]{1,0:T(8,128)(2,1)S(1)}, u32[]{:S(2)}, u32[]{:S(2)}) collective-permute-start(bf16[80,2048]{1,0:T(8,128)(2,1)S(1)} %get-tuple-element.201), channel_id=1, source_target_pairs={{0,2},{1,3},{2,0},{3,1},{4,6},{5,7},{6,4},{7,5},{8,10},{9,11},{10,... | collective-permute-start | bytes 983048 | tf_op jit(solution)/shard_map/ppermute | solution.py:203
  111.9 14.0 %collective-permute-start.31 = (bf16[80,2048]{1,0:T(8,128)(2,1)S(1)}, bf16[80,2048]{1,0:T(8,128)(2,1)S(1)}, u32[]{:S(2)}, u32[]{:S(2)}) collective-permute-start(bf16[80,2048]{1,0:T(8,128)(2,1)S(1)} %get-tuple-element.199), channel_id=1, source_target_pairs={{0,4},{1,5},{2,6},{3,7},{4,0},{5,1},{6,2},{7,3},{8,12},{9,13},{10,... | collective-permute-start | bytes 983048 | tf_op jit(solution)/shard_map/ppermute | solution.py:203
  113.6 15.1 %collective-permute-start.30 = (bf16[80,2048]{1,0:T(8,128)(2,1)S(1)}, bf16[80,2048]{1,0:T(8,128)(2,1)S(1)}, u32[]{:S(2)}, u32[]{:S(2)}) collective-permute-start(bf16[80,2048]{1,0:T(8,128)(2,1)S(1)} %get-tuple-element.196), channel_id=1, source_target_pairs={{0,6},{1,7},{2,4},{3,5},{4,2},{5,3},{6,0},{7,1},{8,14},{9,15},{10,... | collective-permute-start | bytes 983048 | tf_op jit(solution)/shard_map/ppermute | solution.py:203
  121.3 14.1 %collective-permute-start.36 = (bf16[80,2048]{1,0:T(8,128)(2,1)S(1)}, bf16[80,2048]{1,0:T(8,128)(2,1)S(1)}, u32[]{:S(2)}, u32[]{:S(2)}) collective-permute-start(bf16[80,2048]{1,0:T(8,128)(2,1)S(1)} %get-tuple-element.211), channel_id=1, source_target_pairs={{0,2},{1,3},{2,0},{3,1},{4,6},{5,7},{6,4},{7,5},{8,10},{9,11},{10,... | collective-permute-start | bytes 983048 | tf_op jit(solution)/shard_map/ppermute | solution.py:203
  125.9 9.9 %collective-permute-start.35 = (bf16[80,2048]{1,0:T(8,128)(2,1)S(1)}, bf16[80,2048]{1,0:T(8,128)(2,1)S(1)}, u32[]{:S(2)}, u32[]{:S(2)}) collective-permute-start(bf16[80,2048]{1,0:T(8,128)(2,1)S(1)} %get-tuple-element.209), channel_id=1, source_target_pairs={{0,4},{1,5},{2,6},{3,7},{4,0},{5,1},{6,2},{7,3},{8,12},{9,13},{10,... | collective-permute-start | bytes 983048 | tf_op jit(solution)/shard_map/ppermute | solution.py:203
  130.1 10.7 %collective-permute-start.34 = (bf16[80,2048]{1,0:T(8,128)(2,1)S(1)}, bf16[80,2048]{1,0:T(8,128)(2,1)S(1)}, u32[]{:S(2)}, u32[]{:S(2)}) collective-permute-start(bf16[80,2048]{1,0:T(8,128)(2,1)S(1)} %get-tuple-element.207), channel_id=1, source_target_pairs={{0,6},{1,7},{2,4},{3,5},{4,2},{5,3},{6,0},{7,1},{8,14},{9,15},{10,... | collective-permute-start | bytes 983048 | tf_op jit(solution)/shard_map/ppermute | solution.py:203
  134.0 15.8 %collective-permute-start.41 = (bf16[128,2048]{1,0:T(8,128)(2,1)S(1)}, bf16[128,2048]{1,0:T(8,128)(2,1)S(1)}, u32[]{:S(2)}, u32[]{:S(2)}) collective-permute-start(bf16[128,2048]{1,0:T(8,128)(2,1)S(1)} %shard_map.78), channel_id=1, source_target_pairs={{0,8},{8,16},{16,24},{24,0},{1,9},{9,17},{17,25},{25,1},{2,10},{10... | collective-permute-start | bytes 1572872 | tf_op jit(solution)/shard_map/ppermute | solution.py:200
  (18 other events, 89.0 us)

commit v14 on v12

--- a/solution.py
+++ b/solution.py
@@ -120,11 +120,12 @@
     for q in range(z.chips):
         x[q * rows : (q + 1) * rows, :] = slabs[q][0:rows, :]
     ff = gate_ref.shape[1]
-    tile = 256
+    tile = ff
     for f in range(0, ff, tile):
         gate = jnp.dot(x[...], gate_ref[:, f : f + tile], preferred_element_type=F32)
         upper = jnp.dot(x[...], up_ref[:, f : f + tile], preferred_element_type=F32)
         hidden[:, f : f + tile] = (gate / (1.0 + jnp.exp(-gate)) * upper).astype(BF16)
+    tile = z.width // PARTS
     for c in range(0, z.width, tile):
         y = jnp.dot(hidden[...], down_ref[:, c : c + tile], preferred_element_type=F32)
         for q in range(z.chips):

time: 151 us -> 151 us (level)
  transfers between devices with their start and end apart: 42 -> 42, of which waited for: 25 -> 25; matrix products, arithmetic and copies ran while one was open for 0% -> 0% of each run, Pallas kernels for 14% -> 13%
where the time goes in v14:
time: 151 us
  waiting for transfers between devices  78.4 us (52%)
  starting transfers between devices  43.8 us (29%)
  Pallas kernels  22.1 us (15%)
  local copies, waits for them, and re-layouts  6.38 us (4%)
    ppermute x36, waiting for transfers between devices, across(): lax.ppermute(array, 'zero', [(i, i ^ o) for i in range(near)])  59.6 us
    ppermute x36, starting transfers between devices, across(): lax.ppermute(array, 'zero', [(i, i ^ o) for i in range(near)])  32.1 us
    ppermute x6, waiting for transfers between devices, along(): lax.ppermute(array, 'expert', [(i, (i + d) % layers) for i in range(layer...  18.8 us
    pallas_call x4, Pallas kernels, expert(): call(functools.partial(expert_kernel, z, rows), [shape(rows)] * z.chips,...  12.8 us
    ppermute x6, starting transfers between devices, along(): lax.ppermute(array, 'expert', [(i, (i + d) % layers) for i in range(layer...  11.7 us
    unnamed x16, local copies, waits for them, and re-layouts  6.38 us
    pallas_call x4, Pallas kernels, mix(): call(functools.partial(mix_kernel, z, n, list(backs), ride_order), [shape...  5.35 us
  transfers between devices with their start and end apart: 42, of which 25 were waited for; matrix products, arithmetic and copies ran while one was open for 0% of the time, Pallas kernels for 13%

profile of v14, /device:TPU:0, one launch (start us, length us, event | category | flops | bytes accessed | tf_op | source)
XLA Modules:
  0.0 150.9 jit_solution(5779290260755385043)
XLA Ops:
  3.2 2.6 %collective-permute-start.1 = (bf16[136,2048]{1,0:T(8,128)(2,1)S(1)}, bf16[136,2048]{1,0:T(8,128)(2,1)S(1)}, u32[]{:S(2)}, u32[]{:S(2)}) collective-permute-start(bf16[136,2048]{1,0:T(8,128)(2,1)S(1)} %shard_map.64.refs_0_), channel_id=1, source_target_pairs={{0,8},{8,16},{16,24},{24,0},{1,9},{9,17},{17,25},{25,1},{2,10},{10... | collective-permute-start | bytes 1671176 | tf_op jit(solution)/shard_map/ppermute | solution.py:201
  6.4 1.9 %collective-permute-start.2 = (bf16[80,2048]{1,0:T(8,128)(2,1)S(1)}, bf16[80,2048]{1,0:T(8,128)(2,1)S(1)}, u32[]{:S(2)}, u32[]{:S(2)}) collective-permute-start(bf16[80,2048]{1,0:T(8,128)(2,1)S(1)} %get-tuple-element.112), channel_id=1, source_target_pairs={{0,2},{1,3},{2,0},{3,1},{4,6},{5,7},{6,4},{7,5},{8,10},{9,11},{10,... | collective-permute-start | bytes 983048 | tf_op jit(solution)/shard_map/ppermute | solution.py:204
  10.0 11.1 %collective-permute-done.1.refs_0_ = bf16[136,2048]{1,0:T(8,128)(2,1)S(1)} collective-permute-done((bf16[136,2048]{1,0:T(8,128)(2,1)S(1)}, bf16[136,2048]{1,0:T(8,128)(2,1)S(1)}, u32[]{:S(2)}, u32[]{:S(2)}) %collective-permute-start.1) | collective-permute-done | bytes 557088 | tf_op jit(solution)/shard_map/ppermute | solution.py:201
  21.1 3.7 %collective-permute-done.4.refs_2_ = bf16[80,2048]{1,0:T(8,128)(2,1)S(1)} collective-permute-done((bf16[80,2048]{1,0:T(8,128)(2,1)S(1)}, bf16[80,2048]{1,0:T(8,128)(2,1)S(1)}, u32[]{:S(2)}, u32[]{:S(2)}) %collective-permute-start.4) | collective-permute-done | bytes 327712 | tf_op jit(solution)/shard_map/ppermute | solution.py:204
  28.9 1.9 %copy-done.1 = bf16[1,2048,768]{2,1,0:T(8,128)(2,1)S(1)} copy-done((bf16[1,2048,768]{2,1,0:T(8,128)(2,1)S(1)}, bf16[1,2048,768]{2,1,0:T(8,128)(2,1)}, u32[]{:S(2)}) %copy-start.1) | copy-done | bytes 3145752
  30.8 1.9 %copy-done.3 = bf16[1,768,2048]{2,1,0:T(8,128)(2,1)S(1)} copy-done((bf16[1,768,2048]{2,1,0:T(8,128)(2,1)S(1)}, bf16[1,768,2048]{2,1,0:T(8,128)(2,1)}, u32[]{:S(2)}) %copy-start.3) | copy-done | bytes 3145752
  32.7 3.2 %shard_map.67 = (bf16[80,2048]{1,0:T(8,128)(2,1)S(1)}, bf16[80,2048]{1,0:T(8,128)(2,1)S(1)}, bf16[80,2048]{1,0:T(8,128)(2,1)S(1)}, bf16[80,2048]{1,0:T(8,128)(2,1)S(1)}) custom-call(bf16[80,2048]{1,0:T(8,128)(2,1)S(1)} %get-tuple-element.125.refs_0_, bf16[80,2048]{1,0:T(8,128)(2,1)S(1)} %collective-permute-done.2.refs_1_, ...), custom_call_target="tpu_custom_call" | custom-call | flops 1000 | bytes 1000 | tf_op jit(solution)/shard_map/pallas_call | solution.py:234
  35.9 2.0 %collective-permute-done.9.refs_0_ = bf16[136,2048]{1,0:T(8,128)(2,1)S(1)} collective-permute-done((bf16[136,2048]{1,0:T(8,128)(2,1)S(1)}, bf16[136,2048]{1,0:T(8,128)(2,1)S(1)}, u32[]{:S(2)}, u32[]{:S(2)}) %collective-permute-start.9) | collective-permute-done | bytes 557088 | tf_op jit(solution)/shard_map/ppermute | solution.py:201
  37.9 5.8 %collective-permute-done.8.refs_3_.refs_5_ = bf16[88,2048]{1,0:T(8,128)(2,1)S(1)} collective-permute-done((bf16[88,2048]{1,0:T(8,128)(2,1)S(1)}, bf16[88,2048]{1,0:T(8,128)(2,1)S(1)}, u32[]{:S(2)}, u32[]{:S(2)}) %collective-permute-start.8) | collective-permute-done | bytes 360480 | tf_op jit(solution)/shard_map/ppermute | solution.py:204
  47.9 1.6 %collective-permute-start.10 = (bf16[136,2048]{1,0:T(8,128)(2,1)S(1)}, bf16[136,2048]{1,0:T(8,128)(2,1)S(1)}, u32[]{:S(2)}, u32[]{:S(2)}) collective-permute-start(bf16[136,2048]{1,0:T(8,128)(2,1)S(1)} %collective-permute-done.9.refs_0_), channel_id=1, source_target_pairs={{0,8},{8,16},{16,24},{24,0},{1,9},{9,17},{17,25},{25,1},{2,10},{10... | collective-permute-start | bytes 1671176 | tf_op jit(solution)/shard_map/ppermute | solution.py:201
  49.5 3.2 %shard_map.71 = (bf16[80,2048]{1,0:T(8,128)(2,1)S(1)}, bf16[80,2048]{1,0:T(8,128)(2,1)S(1)}, bf16[80,2048]{1,0:T(8,128)(2,1)S(1)}, bf16[80,2048]{1,0:T(8,128)(2,1)S(1)}) custom-call(bf16[88,2048]{1,0:T(8,128)(2,1)S(1)} %get-tuple-element.146.refs_0_.refs_2_, bf16[88,2048]{1,0:T(8,128)(2,1)S(1)} %collective-permute-done.6.refs_1_.refs_3_, ...), custom_call_target="tpu_custom_call" | custom-call | flops 1000 | bytes 1000 | tf_op jit(solution)/shard_map/pallas_call | solution.py:234
  52.7 2.3 %collective-permute-done.12.refs_3_ = bf16[80,2048]{1,0:T(8,128)(2,1)S(1)} collective-permute-done((bf16[80,2048]{1,0:T(8,128)(2,1)S(1)}, bf16[80,2048]{1,0:T(8,128)(2,1)S(1)}, u32[]{:S(2)}, u32[]{:S(2)}) %collective-permute-start.12) | collective-permute-done | bytes 327712 | tf_op jit(solution)/shard_map/ppermute | solution.py:204
  55.7 4.5 %collective-permute-done.15.refs_2_ = bf16[80,2048]{1,0:T(8,128)(2,1)S(1)} collective-permute-done((bf16[80,2048]{1,0:T(8,128)(2,1)S(1)}, bf16[80,2048]{1,0:T(8,128)(2,1)S(1)}, u32[]{:S(2)}, u32[]{:S(2)}) %collective-permute-start.15) | collective-permute-done | bytes 327712 | tf_op jit(solution)/shard_map/ppermute | solution.py:204
  60.1 1.6 %collective-permute-start.19 = (bf16[80,2048]{1,0:T(8,128)(2,1)S(1)}, bf16[80,2048]{1,0:T(8,128)(2,1)S(1)}, u32[]{:S(2)}, u32[]{:S(2)}) collective-permute-start(bf16[80,2048]{1,0:T(8,128)(2,1)S(1)} %get-tuple-element.163), channel_id=1, source_target_pairs={{0,4},{1,5},{2,6},{3,7},{4,0},{5,1},{6,2},{7,3},{8,12},{9,13},{10,... | collective-permute-start | bytes 983048 | tf_op jit(solution)/shard_map/ppermute | solution.py:204
  63.6 3.2 %shard_map.70 = (bf16[80,2048]{1,0:T(8,128)(2,1)S(1)}, bf16[80,2048]{1,0:T(8,128)(2,1)S(1)}, bf16[80,2048]{1,0:T(8,128)(2,1)S(1)}, bf16[80,2048]{1,0:T(8,128)(2,1)S(1)}) custom-call(bf16[80,2048]{1,0:T(8,128)(2,1)S(1)} %get-tuple-element.141.refs_0_, bf16[80,2048]{1,0:T(8,128)(2,1)S(1)} %collective-permute-done.14.refs_1_, ...), custom_call_target="tpu_custom_call" | custom-call | flops 1000 | bytes 1000 | tf_op jit(solution)/shard_map/pallas_call | solution.py:234
  66.9 2.3 %collective-permute-done.22.refs_9_ = bf16[80,2048]{1,0:T(8,128)(2,1)S(1)} collective-permute-done((bf16[80,2048]{1,0:T(8,128)(2,1)S(1)}, bf16[80,2048]{1,0:T(8,128)(2,1)S(1)}, u32[]{:S(2)}, u32[]{:S(2)}) %collective-permute-start.22) | collective-permute-done | bytes 327712 | tf_op jit(solution)/shard_map/ppermute | solution.py:204
  69.1 4.7 %collective-permute-done.19.refs_8_ = bf16[80,2048]{1,0:T(8,128)(2,1)S(1)} collective-permute-done((bf16[80,2048]{1,0:T(8,128)(2,1)S(1)}, bf16[80,2048]{1,0:T(8,128)(2,1)S(1)}, u32[]{:S(2)}, u32[]{:S(2)}) %collective-permute-start.19) | collective-permute-done | bytes 327712 | tf_op jit(solution)/shard_map/ppermute | solution.py:204
  77.5 1.7 %collective-permute-start.17 = (bf16[80,2048]{1,0:T(8,128)(2,1)S(1)}, bf16[80,2048]{1,0:T(8,128)(2,1)S(1)}, u32[]{:S(2)}, u32[]{:S(2)}) collective-permute-start(bf16[80,2048]{1,0:T(8,128)(2,1)S(1)} %get-tuple-element.158), channel_id=1, source_target_pairs={{0,6},{1,7},{2,4},{3,5},{4,2},{5,3},{6,0},{7,1},{8,14},{9,15},{10,... | collective-permute-start | bytes 983048 | tf_op jit(solution)/shard_map/ppermute | solution.py:204
  79.4 3.7 %collective-permute-start.27 = (bf16[128,2048]{1,0:T(8,128)(2,1)S(1)}, bf16[128,2048]{1,0:T(8,128)(2,1)S(1)}, u32[]{:S(2)}, u32[]{:S(2)}) collective-permute-start(bf16[128,2048]{1,0:T(8,128)(2,1)S(1)} %shard_map.73), channel_id=1, source_target_pairs={{0,24},{8,0},{16,8},{24,16},{1,25},{9,1},{17,9},{25,17},{2,26},{10... | collective-permute-start | bytes 1572872 | tf_op jit(solution)/shard_map/ppermute | solution.py:201
  83.7 2.6 %collective-permute-done.23.refs_9_ = bf16[80,2048]{1,0:T(8,128)(2,1)S(1)} collective-permute-done((bf16[80,2048]{1,0:T(8,128)(2,1)S(1)}, bf16[80,2048]{1,0:T(8,128)(2,1)S(1)}, u32[]{:S(2)}, u32[]{:S(2)}) %collective-permute-start.23) | collective-permute-done | bytes 327712 | tf_op jit(solution)/shard_map/ppermute | solution.py:204
  88.1 6.1 %collective-permute-done.17.refs_7_ = bf16[80,2048]{1,0:T(8,128)(2,1)S(1)} collective-permute-done((bf16[80,2048]{1,0:T(8,128)(2,1)S(1)}, bf16[80,2048]{1,0:T(8,128)(2,1)S(1)}, u32[]{:S(2)}, u32[]{:S(2)}) %collective-permute-start.17) | collective-permute-done | bytes 327712 | tf_op jit(solution)/shard_map/ppermute | solution.py:204
  94.2 1.8 %collective-permute-start.18 = (bf16[80,2048]{1,0:T(8,128)(2,1)S(1)}, bf16[80,2048]{1,0:T(8,128)(2,1)S(1)}, u32[]{:S(2)}, u32[]{:S(2)}) collective-permute-start(bf16[80,2048]{1,0:T(8,128)(2,1)S(1)} %get-tuple-element.159), channel_id=1, source_target_pairs={{0,6},{1,7},{2,4},{3,5},{4,2},{5,3},{6,0},{7,1},{8,14},{9,15},{10,... | collective-permute-start | bytes 983048 | tf_op jit(solution)/shard_map/ppermute | solution.py:204
  99.4 2.5 %collective-permute-start.36 = (bf16[128,2048]{1,0:T(8,128)(2,1)S(1)}, bf16[128,2048]{1,0:T(8,128)(2,1)S(1)}, u32[]{:S(2)}, u32[]{:S(2)}) collective-permute-start(bf16[128,2048]{1,0:T(8,128)(2,1)S(1)} %shard_map.75), channel_id=1, source_target_pairs={{0,16},{8,24},{16,0},{24,8},{1,17},{9,25},{17,1},{25,9},{2,18},{10... | collective-permute-start | bytes 1572872 | tf_op jit(solution)/shard_map/ppermute | solution.py:201
  101.9 5.5 %collective-permute-done.18.refs_1_ = bf16[80,2048]{1,0:T(8,128)(2,1)S(1)} collective-permute-done((bf16[80,2048]{1,0:T(8,128)(2,1)S(1)}, bf16[80,2048]{1,0:T(8,128)(2,1)S(1)}, u32[]{:S(2)}, u32[]{:S(2)}) %collective-permute-start.18) | collective-permute-done | bytes 327712 | tf_op jit(solution)/shard_map/ppermute | solution.py:204
  107.4 3.2 %shard_map.76 = (bf16[80,2048]{1,0:T(8,128)(2,1)S(1)}, bf16[80,2048]{1,0:T(8,128)(2,1)S(1)}, bf16[80,2048]{1,0:T(8,128)(2,1)S(1)}, bf16[80,2048]{1,0:T(8,128)(2,1)S(1)}) custom-call(bf16[80,2048]{1,0:T(8,128)(2,1)S(1)} %get-tuple-element.186.refs_0_, bf16[80,2048]{1,0:T(8,128)(2,1)S(1)} %collective-permute-done.18.refs_1_, ...), custom_call_target="tpu_custom_call" | custom-call | flops 20000000000 | bytes 1000 | tf_op jit(solution)/shard_map/pallas_call | solution.py:234
  111.9 1.7 %collective-permute-start.32 = (bf16[80,2048]{1,0:T(8,128)(2,1)S(1)}, bf16[80,2048]{1,0:T(8,128)(2,1)S(1)}, u32[]{:S(2)}, u32[]{:S(2)}) collective-permute-start(bf16[80,2048]{1,0:T(8,128)(2,1)S(1)} %get-tuple-element.199), channel_id=1, source_target_pairs={{0,4},{1,5},{2,6},{3,7},{4,0},{5,1},{6,2},{7,3},{8,12},{9,13},{10,... | collective-permute-start | bytes 983048 | tf_op jit(solution)/shard_map/ppermute | solution.py:204
  114.2 7.2 %collective-permute-done.34.refs_9_ = bf16[80,2048]{1,0:T(8,128)(2,1)S(1)} collective-permute-done((bf16[80,2048]{1,0:T(8,128)(2,1)S(1)}, bf16[80,2048]{1,0:T(8,128)(2,1)S(1)}, u32[]{:S(2)}, u32[]{:S(2)}) %collective-permute-start.34) | collective-permute-done | bytes 327712 | tf_op jit(solution)/shard_map/ppermute | solution.py:204
  122.5 3.4 %collective-permute-done.32.refs_8_ = bf16[80,2048]{1,0:T(8,128)(2,1)S(1)} collective-permute-done((bf16[80,2048]{1,0:T(8,128)(2,1)S(1)}, bf16[80,2048]{1,0:T(8,128)(2,1)S(1)}, u32[]{:S(2)}, u32[]{:S(2)}) %collective-permute-start.32) | collective-permute-done | bytes 327712 | tf_op jit(solution)/shard_map/ppermute | solution.py:204
  125.9 1.6 %collective-permute-start.33 = (bf16[80,2048]{1,0:T(8,128)(2,1)S(1)}, bf16[80,2048]{1,0:T(8,128)(2,1)S(1)}, u32[]{:S(2)}, u32[]{:S(2)}) collective-permute-start(bf16[80,2048]{1,0:T(8,128)(2,1)S(1)} %get-tuple-element.200), channel_id=1, source_target_pairs={{0,4},{1,5},{2,6},{3,7},{4,0},{5,1},{6,2},{7,3},{8,12},{9,13},{10,... | collective-permute-start | bytes 983048 | tf_op jit(solution)/shard_map/ppermute | solution.py:204
  128.7 1.8 %collective-permute-start.31 = (bf16[80,2048]{1,0:T(8,128)(2,1)S(1)}, bf16[80,2048]{1,0:T(8,128)(2,1)S(1)}, u32[]{:S(2)}, u32[]{:S(2)}) collective-permute-start(bf16[80,2048]{1,0:T(8,128)(2,1)S(1)} %get-tuple-element.196), channel_id=1, source_target_pairs={{0,6},{1,7},{2,4},{3,5},{4,2},{5,3},{6,0},{7,1},{8,14},{9,15},{10,... | collective-permute-start | bytes 983048 | tf_op jit(solution)/shard_map/ppermute | solution.py:204
  135.8 4.9 %collective-permute-done.31.refs_7_ = bf16[80,2048]{1,0:T(8,128)(2,1)S(1)} collective-permute-done((bf16[80,2048]{1,0:T(8,128)(2,1)S(1)}, bf16[80,2048]{1,0:T(8,128)(2,1)S(1)}, u32[]{:S(2)}, u32[]{:S(2)}) %collective-permute-start.31) | collective-permute-done | bytes 327712 | tf_op jit(solution)/shard_map/ppermute | solution.py:204
  144.1 5.7 %collective-permute-done.41.refs_5_ = bf16[128,2048]{1,0:T(8,128)(2,1)S(1)} collective-permute-done((bf16[128,2048]{1,0:T(8,128)(2,1)S(1)}, bf16[128,2048]{1,0:T(8,128)(2,1)S(1)}, u32[]{:S(2)}, u32[]{:S(2)}) %collective-permute-start.41) | collective-permute-done | bytes 524320 | tf_op jit(solution)/shard_map/ppermute | solution.py:201
  (85 shorter events, 39.9 us)
Async XLA Ops:
  3.2 17.9 %collective-permute-start.1 = (bf16[136,2048]{1,0:T(8,128)(2,1)S(1)}, bf16[136,2048]{1,0:T(8,128)(2,1)S(1)}, u32[]{:S(2)}, u32[]{:S(2)}) collective-permute-start(bf16[136,2048]{1,0:T(8,128)(2,1)S(1)} %shard_map.64.refs_0_), channel_id=1, source_target_pairs={{0,8},{8,16},{16,24},{24,0},{1,9},{9,17},{17,25},{25,1},{2,10},{10... | collective-permute-start | bytes 1671176 | tf_op jit(solution)/shard_map/ppermute | solution.py:201
  6.4 14.7 %collective-permute-start.2 = (bf16[80,2048]{1,0:T(8,128)(2,1)S(1)}, bf16[80,2048]{1,0:T(8,128)(2,1)S(1)}, u32[]{:S(2)}, u32[]{:S(2)}) collective-permute-start(bf16[80,2048]{1,0:T(8,128)(2,1)S(1)} %get-tuple-element.112), channel_id=1, source_target_pairs={{0,2},{1,3},{2,0},{3,1},{4,6},{5,7},{6,4},{7,5},{8,10},{9,11},{10,... | collective-permute-start | bytes 983048 | tf_op jit(solution)/shard_map/ppermute | solution.py:204
  8.3 16.5 %collective-permute-start.4 = (bf16[80,2048]{1,0:T(8,128)(2,1)S(1)}, bf16[80,2048]{1,0:T(8,128)(2,1)S(1)}, u32[]{:S(2)}, u32[]{:S(2)}) collective-permute-start(bf16[80,2048]{1,0:T(8,128)(2,1)S(1)} %get-tuple-element.115), channel_id=1, source_target_pairs={{0,4},{1,5},{2,6},{3,7},{4,0},{5,1},{6,2},{7,3},{8,12},{9,13},{10,... | collective-permute-start | bytes 983048 | tf_op jit(solution)/shard_map/ppermute | solution.py:204
  9.8 15.0 %collective-permute-start.5 = (bf16[80,2048]{1,0:T(8,128)(2,1)S(1)}, bf16[80,2048]{1,0:T(8,128)(2,1)S(1)}, u32[]{:S(2)}, u32[]{:S(2)}) collective-permute-start(bf16[80,2048]{1,0:T(8,128)(2,1)S(1)} %get-tuple-element.116), channel_id=1, source_target_pairs={{0,6},{1,7},{2,4},{3,5},{4,2},{5,3},{6,0},{7,1},{8,14},{9,15},{10,... | collective-permute-start | bytes 983048 | tf_op jit(solution)/shard_map/ppermute | solution.py:204
  21.1 16.8 %collective-permute-start.9 = (bf16[136,2048]{1,0:T(8,128)(2,1)S(1)}, bf16[136,2048]{1,0:T(8,128)(2,1)S(1)}, u32[]{:S(2)}, u32[]{:S(2)}) collective-permute-start(bf16[136,2048]{1,0:T(8,128)(2,1)S(1)} %collective-permute-done.1.refs_0_), channel_id=1, source_target_pairs={{0,8},{8,16},{16,24},{24,0},{1,9},{9,17},{17,25},{25,1},{2,10},{10... | collective-permute-start | bytes 1671176 | tf_op jit(solution)/shard_map/ppermute | solution.py:201
  25.4 12.5 %collective-permute-start.6 = (bf16[88,2048]{1,0:T(8,128)(2,1)S(1)}, bf16[88,2048]{1,0:T(8,128)(2,1)S(1)}, u32[]{:S(2)}, u32[]{:S(2)}) collective-permute-start(bf16[88,2048]{1,0:T(8,128)(2,1)S(1)} %get-tuple-element.119), channel_id=1, source_target_pairs={{0,2},{1,3},{2,0},{3,1},{4,6},{5,7},{6,4},{7,5},{8,10},{9,11},{10,... | collective-permute-start | bytes 1081352 | tf_op jit(solution)/shard_map/ppermute | solution.py:204
  26.7 17.1 %collective-permute-start.8 = (bf16[88,2048]{1,0:T(8,128)(2,1)S(1)}, bf16[88,2048]{1,0:T(8,128)(2,1)S(1)}, u32[]{:S(2)}, u32[]{:S(2)}) collective-permute-start(bf16[88,2048]{1,0:T(8,128)(2,1)S(1)} %get-tuple-element.123), channel_id=1, source_target_pairs={{0,4},{1,5},{2,6},{3,7},{4,0},{5,1},{6,2},{7,3},{8,12},{9,13},{10,... | collective-permute-start | bytes 1081352 | tf_op jit(solution)/shard_map/ppermute | solution.py:204
  27.5 16.2 %collective-permute-start.7 = (bf16[88,2048]{1,0:T(8,128)(2,1)S(1)}, bf16[88,2048]{1,0:T(8,128)(2,1)S(1)}, u32[]{:S(2)}, u32[]{:S(2)}) collective-permute-start(bf16[88,2048]{1,0:T(8,128)(2,1)S(1)} %get-tuple-element.121), channel_id=1, source_target_pairs={{0,6},{1,7},{2,4},{3,5},{4,2},{5,3},{6,0},{7,1},{8,14},{9,15},{10,... | collective-permute-start | bytes 1081352 | tf_op jit(solution)/shard_map/ppermute | solution.py:204
  37.9 5.8 %collective-permute-start.11 = (bf16[136,2048]{1,0:T(8,128)(2,1)S(1)}, bf16[136,2048]{1,0:T(8,128)(2,1)S(1)}, u32[]{:S(2)}, u32[]{:S(2)}) collective-permute-start(bf16[136,2048]{1,0:T(8,128)(2,1)S(1)} %collective-permute-done.9.refs_0_), channel_id=1, source_target_pairs={{0,1},{1,0},{2,3},{3,2},{4,5},{5,4},{6,7},{7,6},{8,9},{9,8},{10,11... | collective-permute-start | bytes 1671176 | tf_op jit(solution)/shard_map/ppermute | solution.py:204
  44.4 10.7 %collective-permute-start.12 = (bf16[80,2048]{1,0:T(8,128)(2,1)S(1)}, bf16[80,2048]{1,0:T(8,128)(2,1)S(1)}, u32[]{:S(2)}, u32[]{:S(2)}) collective-permute-start(bf16[80,2048]{1,0:T(8,128)(2,1)S(1)} %get-tuple-element.132), channel_id=1, source_target_pairs={{0,2},{1,3},{2,0},{3,1},{4,6},{5,7},{6,4},{7,5},{8,10},{9,11},{10,... | collective-permute-start | bytes 983048 | tf_op jit(solution)/shard_map/ppermute | solution.py:204
  45.0 15.1 %collective-permute-start.15 = (bf16[80,2048]{1,0:T(8,128)(2,1)S(1)}, bf16[80,2048]{1,0:T(8,128)(2,1)S(1)}, u32[]{:S(2)}, u32[]{:S(2)}) collective-permute-start(bf16[80,2048]{1,0:T(8,128)(2,1)S(1)} %get-tuple-element.140), channel_id=1, source_target_pairs={{0,4},{1,5},{2,6},{3,7},{4,0},{5,1},{6,2},{7,3},{8,12},{9,13},{10,... | collective-permute-start | bytes 983048 | tf_op jit(solution)/shard_map/ppermute | solution.py:204
  46.4 16.0 %collective-permute-start.14 = (bf16[80,2048]{1,0:T(8,128)(2,1)S(1)}, bf16[80,2048]{1,0:T(8,128)(2,1)S(1)}, u32[]{:S(2)}, u32[]{:S(2)}) collective-permute-start(bf16[80,2048]{1,0:T(8,128)(2,1)S(1)} %get-tuple-element.138), channel_id=1, source_target_pairs={{0,6},{1,7},{2,4},{3,5},{4,2},{5,3},{6,0},{7,1},{8,14},{9,15},{10,... | collective-permute-start | bytes 983048 | tf_op jit(solution)/shard_map/ppermute | solution.py:204
  47.9 15.7 %collective-permute-start.10 = (bf16[136,2048]{1,0:T(8,128)(2,1)S(1)}, bf16[136,2048]{1,0:T(8,128)(2,1)S(1)}, u32[]{:S(2)}, u32[]{:S(2)}) collective-permute-start(bf16[136,2048]{1,0:T(8,128)(2,1)S(1)} %collective-permute-done.9.refs_0_), channel_id=1, source_target_pairs={{0,8},{8,16},{16,24},{24,0},{1,9},{9,17},{17,25},{25,1},{2,10},{10... | collective-permute-start | bytes 1671176 | tf_op jit(solution)/shard_map/ppermute | solution.py:201
  55.1 14.0 %collective-permute-start.22 = (bf16[80,2048]{1,0:T(8,128)(2,1)S(1)}, bf16[80,2048]{1,0:T(8,128)(2,1)S(1)}, u32[]{:S(2)}, u32[]{:S(2)}) collective-permute-start(bf16[80,2048]{1,0:T(8,128)(2,1)S(1)} %get-tuple-element.169), channel_id=1, source_target_pairs={{0,2},{1,3},{2,0},{3,1},{4,6},{5,7},{6,4},{7,5},{8,10},{9,11},{10,... | collective-permute-start | bytes 983048 | tf_op jit(solution)/shard_map/ppermute | solution.py:204
  60.1 13.7 %collective-permute-start.19 = (bf16[80,2048]{1,0:T(8,128)(2,1)S(1)}, bf16[80,2048]{1,0:T(8,128)(2,1)S(1)}, u32[]{:S(2)}, u32[]{:S(2)}) collective-permute-start(bf16[80,2048]{1,0:T(8,128)(2,1)S(1)} %get-tuple-element.163), channel_id=1, source_target_pairs={{0,4},{1,5},{2,6},{3,7},{4,0},{5,1},{6,2},{7,3},{8,12},{9,13},{10,... | collective-permute-start | bytes 983048 | tf_op jit(solution)/shard_map/ppermute | solution.py:204
  62.4 11.4 %collective-permute-start.16 = (bf16[80,2048]{1,0:T(8,128)(2,1)S(1)}, bf16[80,2048]{1,0:T(8,128)(2,1)S(1)}, u32[]{:S(2)}, u32[]{:S(2)}) collective-permute-start(bf16[80,2048]{1,0:T(8,128)(2,1)S(1)} %get-tuple-element.157), channel_id=1, source_target_pairs={{0,6},{1,7},{2,4},{3,5},{4,2},{5,3},{6,0},{7,1},{8,14},{9,15},{10,... | collective-permute-start | bytes 983048 | tf_op jit(solution)/shard_map/ppermute | solution.py:204
  63.6 19.4 %collective-permute-start.13 = (bf16[136,2048]{1,0:T(8,128)(2,1)S(1)}, bf16[136,2048]{1,0:T(8,128)(2,1)S(1)}, u32[]{:S(2)}, u32[]{:S(2)}) collective-permute-start(bf16[136,2048]{1,0:T(8,128)(2,1)S(1)} %collective-permute-done.10.refs_0_), channel_id=1, source_target_pairs={{0,1},{1,0},{2,3},{3,2},{4,5},{5,4},{6,7},{7,6},{8,9},{9,8},{10,11... | collective-permute-start | bytes 1671176 | tf_op jit(solution)/shard_map/ppermute | solution.py:204
  75.7 10.6 %collective-permute-start.23 = (bf16[80,2048]{1,0:T(8,128)(2,1)S(1)}, bf16[80,2048]{1,0:T(8,128)(2,1)S(1)}, u32[]{:S(2)}, u32[]{:S(2)}) collective-permute-start(bf16[80,2048]{1,0:T(8,128)(2,1)S(1)} %get-tuple-element.170), channel_id=1, source_target_pairs={{0,2},{1,3},{2,0},{3,1},{4,6},{5,7},{6,4},{7,5},{8,10},{9,11},{10,... | collective-permute-start | bytes 983048 | tf_op jit(solution)/shard_map/ppermute | solution.py:204
  76.7 10.6 %collective-permute-start.20 = (bf16[80,2048]{1,0:T(8,128)(2,1)S(1)}, bf16[80,2048]{1,0:T(8,128)(2,1)S(1)}, u32[]{:S(2)}, u32[]{:S(2)}) collective-permute-start(bf16[80,2048]{1,0:T(8,128)(2,1)S(1)} %get-tuple-element.164), channel_id=1, source_target_pairs={{0,4},{1,5},{2,6},{3,7},{4,0},{5,1},{6,2},{7,3},{8,12},{9,13},{10,... | collective-permute-start | bytes 983048 | tf_op jit(solution)/shard_map/ppermute | solution.py:204
  77.5 16.7 %collective-permute-start.17 = (bf16[80,2048]{1,0:T(8,128)(2,1)S(1)}, bf16[80,2048]{1,0:T(8,128)(2,1)S(1)}, u32[]{:S(2)}, u32[]{:S(2)}) collective-permute-start(bf16[80,2048]{1,0:T(8,128)(2,1)S(1)} %get-tuple-element.158), channel_id=1, source_target_pairs={{0,6},{1,7},{2,4},{3,5},{4,2},{5,3},{6,0},{7,1},{8,14},{9,15},{10,... | collective-permute-start | bytes 983048 | tf_op jit(solution)/shard_map/ppermute | solution.py:204
  79.4 16.6 %collective-permute-start.27 = (bf16[128,2048]{1,0:T(8,128)(2,1)S(1)}, bf16[128,2048]{1,0:T(8,128)(2,1)S(1)}, u32[]{:S(2)}, u32[]{:S(2)}) collective-permute-start(bf16[128,2048]{1,0:T(8,128)(2,1)S(1)} %shard_map.73), channel_id=1, source_target_pairs={{0,24},{8,0},{16,8},{24,16},{1,25},{9,1},{17,9},{25,17},{2,26},{10... | collective-permute-start | bytes 1572872 | tf_op jit(solution)/shard_map/ppermute | solution.py:201
  86.3 15.6 %collective-permute-start.24 = (bf16[80,2048]{1,0:T(8,128)(2,1)S(1)}, bf16[80,2048]{1,0:T(8,128)(2,1)S(1)}, u32[]{:S(2)}, u32[]{:S(2)}) collective-permute-start(bf16[80,2048]{1,0:T(8,128)(2,1)S(1)} %get-tuple-element.171), channel_id=1, source_target_pairs={{0,2},{1,3},{2,0},{3,1},{4,6},{5,7},{6,4},{7,5},{8,10},{9,11},{10,... | collective-permute-start | bytes 983048 | tf_op jit(solution)/shard_map/ppermute | solution.py:204
  87.3 14.7 %collective-permute-start.21 = (bf16[80,2048]{1,0:T(8,128)(2,1)S(1)}, bf16[80,2048]{1,0:T(8,128)(2,1)S(1)}, u32[]{:S(2)}, u32[]{:S(2)}) collective-permute-start(bf16[80,2048]{1,0:T(8,128)(2,1)S(1)} %get-tuple-element.165), channel_id=1, source_target_pairs={{0,4},{1,5},{2,6},{3,7},{4,0},{5,1},{6,2},{7,3},{8,12},{9,13},{10,... | collective-permute-start | bytes 983048 | tf_op jit(solution)/shard_map/ppermute | solution.py:204
  94.2 13.2 %collective-permute-start.18 = (bf16[80,2048]{1,0:T(8,128)(2,1)S(1)}, bf16[80,2048]{1,0:T(8,128)(2,1)S(1)}, u32[]{:S(2)}, u32[]{:S(2)}) collective-permute-start(bf16[80,2048]{1,0:T(8,128)(2,1)S(1)} %get-tuple-element.159), channel_id=1, source_target_pairs={{0,6},{1,7},{2,4},{3,5},{4,2},{5,3},{6,0},{7,1},{8,14},{9,15},{10,... | collective-permute-start | bytes 983048 | tf_op jit(solution)/shard_map/ppermute | solution.py:204
  99.4 31.1 %collective-permute-start.36 = (bf16[128,2048]{1,0:T(8,128)(2,1)S(1)}, bf16[128,2048]{1,0:T(8,128)(2,1)S(1)}, u32[]{:S(2)}, u32[]{:S(2)}) collective-permute-start(bf16[128,2048]{1,0:T(8,128)(2,1)S(1)} %shard_map.75), channel_id=1, source_target_pairs={{0,16},{8,24},{16,0},{24,8},{1,17},{9,25},{17,1},{25,9},{2,18},{10... | collective-permute-start | bytes 1572872 | tf_op jit(solution)/shard_map/ppermute | solution.py:201
  110.6 10.7 %collective-permute-start.34 = (bf16[80,2048]{1,0:T(8,128)(2,1)S(1)}, bf16[80,2048]{1,0:T(8,128)(2,1)S(1)}, u32[]{:S(2)}, u32[]{:S(2)}) collective-permute-start(bf16[80,2048]{1,0:T(8,128)(2,1)S(1)} %get-tuple-element.203), channel_id=1, source_target_pairs={{0,2},{1,3},{2,0},{3,1},{4,6},{5,7},{6,4},{7,5},{8,10},{9,11},{10,... | collective-permute-start | bytes 983048 | tf_op jit(solution)/shard_map/ppermute | solution.py:204
  111.9 14.0 %collective-permute-start.32 = (bf16[80,2048]{1,0:T(8,128)(2,1)S(1)}, bf16[80,2048]{1,0:T(8,128)(2,1)S(1)}, u32[]{:S(2)}, u32[]{:S(2)}) collective-permute-start(bf16[80,2048]{1,0:T(8,128)(2,1)S(1)} %get-tuple-element.199), channel_id=1, source_target_pairs={{0,4},{1,5},{2,6},{3,7},{4,0},{5,1},{6,2},{7,3},{8,12},{9,13},{10,... | collective-permute-start | bytes 983048 | tf_op jit(solution)/shard_map/ppermute | solution.py:204
  113.6 15.1 %collective-permute-start.30 = (bf16[80,2048]{1,0:T(8,128)(2,1)S(1)}, bf16[80,2048]{1,0:T(8,128)(2,1)S(1)}, u32[]{:S(2)}, u32[]{:S(2)}) collective-permute-start(bf16[80,2048]{1,0:T(8,128)(2,1)S(1)} %get-tuple-element.195), channel_id=1, source_target_pairs={{0,6},{1,7},{2,4},{3,5},{4,2},{5,3},{6,0},{7,1},{8,14},{9,15},{10,... | collective-permute-start | bytes 983048 | tf_op jit(solution)/shard_map/ppermute | solution.py:204
  121.3 14.1 %collective-permute-start.35 = (bf16[80,2048]{1,0:T(8,128)(2,1)S(1)}, bf16[80,2048]{1,0:T(8,128)(2,1)S(1)}, u32[]{:S(2)}, u32[]{:S(2)}) collective-permute-start(bf16[80,2048]{1,0:T(8,128)(2,1)S(1)} %get-tuple-element.204), channel_id=1, source_target_pairs={{0,2},{1,3},{2,0},{3,1},{4,6},{5,7},{6,4},{7,5},{8,10},{9,11},{10,... | collective-permute-start | bytes 983048 | tf_op jit(solution)/shard_map/ppermute | solution.py:204
  125.9 9.9 %collective-permute-start.33 = (bf16[80,2048]{1,0:T(8,128)(2,1)S(1)}, bf16[80,2048]{1,0:T(8,128)(2,1)S(1)}, u32[]{:S(2)}, u32[]{:S(2)}) collective-permute-start(bf16[80,2048]{1,0:T(8,128)(2,1)S(1)} %get-tuple-element.200), channel_id=1, source_target_pairs={{0,4},{1,5},{2,6},{3,7},{4,0},{5,1},{6,2},{7,3},{8,12},{9,13},{10,... | collective-permute-start | bytes 983048 | tf_op jit(solution)/shard_map/ppermute | solution.py:204
  128.7 12.0 %collective-permute-start.31 = (bf16[80,2048]{1,0:T(8,128)(2,1)S(1)}, bf16[80,2048]{1,0:T(8,128)(2,1)S(1)}, u32[]{:S(2)}, u32[]{:S(2)}) collective-permute-start(bf16[80,2048]{1,0:T(8,128)(2,1)S(1)} %get-tuple-element.196), channel_id=1, source_target_pairs={{0,6},{1,7},{2,4},{3,5},{4,2},{5,3},{6,0},{7,1},{8,14},{9,15},{10,... | collective-permute-start | bytes 983048 | tf_op jit(solution)/shard_map/ppermute | solution.py:204
  134.0 15.8 %collective-permute-start.41 = (bf16[128,2048]{1,0:T(8,128)(2,1)S(1)}, bf16[128,2048]{1,0:T(8,128)(2,1)S(1)}, u32[]{:S(2)}, u32[]{:S(2)}) collective-permute-start(bf16[128,2048]{1,0:T(8,128)(2,1)S(1)} %shard_map.78), channel_id=1, source_target_pairs={{0,8},{8,16},{16,24},{24,0},{1,9},{9,17},{17,25},{25,1},{2,10},{10... | collective-permute-start | bytes 1572872 | tf_op jit(solution)/shard_map/ppermute | solution.py:201
  (18 other events, 89.0 us)
